TPU v7x, 32 devices: a whole 2x2x4 slice. The times are simulated.
32 devices in a mesh: parts: 2 (over y), blk: 4 (over z), grp: 4 (over x, core).
Axes of the slice: x: 2, y: 2, z: 4, core: 2. Of those that a mesh axis runs over, the one named last changes fastest.
Arguments:
- features: bfloat16 [512, 65536], P('grp', ('parts', 'blk')), parts along dimension 1, may hold values from -6 to 6
- tile_rows: int32 [8, 4, 20], P(('parts', 'blk')), parts along dimension 0, may hold values from 0 to 63, as said below
- tile_cols: int32 [8, 4, 20], P(('parts', 'blk')), parts along dimension 0, may hold values from 0 to 63, as said below
- tile_weights: bfloat16 [8, 4, 20, 128, 128], P(('parts', 'blk')), parts along dimension 0, may hold values from 0 to 3, as said below
- order: int32 [65536], P(('parts', 'blk')), parts along dimension 0, may hold values from 0 to 8191, as said below
- weight: bfloat16 [512, 512], replicated, may hold values from -0.25 to 0.25
- bias: float32 [512], replicated, may hold values from -3 to 3
Outputs:
- activations: bfloat16 [512, 65536], P(None, ('parts', 'blk', 'grp')), parts along dimension 1
There are 2 independent parts, one for each index of `parts`. A program takes and returns all parts, laid end to end along the dimension named above; an argument that names none is the same for every part. Nothing has to cross between parts.
Inputs may be any that keep to these rules, and one draw needn't show every extreme that they name: `tile_rows`: row tiles of a block. For each destination block and offset the slots hold distinct (row, column) pairs among their live slots; the slots after the live ones have zero weights and coordinates 0; offset 0 has all 20 slots live. `tile_cols`: column tiles of a block, as for tile_rows. `tile_weights`: whole numbers. `order`: the 8192 entries of each vertex block are a permutation of 0 to 8191.
All inputs are finite; a program needn't handle non-finite values.
Results may differ from a plain program's by a relative error of at most 0.0031.
Values may be sent and summed in bfloat16 or wider, within the bound.
No kernel may reach another device: no remote copies, remote signals or barrier semaphores. Data moves between devices by JAX's collectives and lax.ppermute only.
A program may use at most 64 MiB of HBM per device.

v0:
```python
import jax
import jax.numpy as jnp
from jax import lax
from jax.sharding import PartitionSpec as P


def shifted(value, axis, steps):
    count = lax.axis_size(axis)
    pairs = [(source, (source + steps) % count) for source in range(count)]
    return lax.ppermute(value, axis, pairs)


def on_device(features, tile_rows, tile_cols, tile_weights, order, weight, bias):
    width, rows_blk = features.shape
    tile = tile_weights.shape[-1]
    row_tiles = rows_blk // tile
    blocks = lax.axis_size("blk")
    rows = tile_rows[0]
    cols = tile_cols[0]
    counts = tile_weights[0]
    onehot = (rows[:, :, None] == jnp.arange(row_tiles, dtype=jnp.int32)[None, None, :]).astype(
        jnp.float32
    )
    degree = jnp.einsum(
        "sti,str->ri",
        jnp.sum(counts, axis=-1, dtype=jnp.float32),
        onehot,
        precision=lax.Precision.HIGHEST,
    )
    panel_tiles = features.reshape(width, row_tiles, tile)

    def contrib(panel, offset):
        cols_step = lax.dynamic_index_in_dim(cols, offset, 0, keepdims=False)
        counts_step = lax.dynamic_index_in_dim(counts, offset, 0, keepdims=False)
        onehot_step = lax.dynamic_index_in_dim(onehot, offset, 0, keepdims=False)
        gathered = jnp.take(panel.reshape(width, row_tiles, tile), cols_step, axis=1)
        product = jnp.einsum(
            "ftj,tij->fti", gathered, counts_step, preferred_element_type=jnp.float32
        )
        return jnp.einsum("fti,tr->fri", product, onehot_step, precision=lax.Precision.HIGHEST)

    def advance(step, carry):
        panel, running = carry
        moved = shifted(panel, "blk", 1)
        return (moved, running + contrib(panel, step))

    start = jnp.zeros((width, row_tiles, tile), jnp.float32)
    panel, total = lax.fori_loop(0, blocks - 1, advance, (features, start))
    total = total + contrib(panel, blocks - 1)
    own = panel_tiles.astype(jnp.float32)
    aggregated = ((total + own) / (degree + 1.0)[None]).reshape(width, rows_blk)
    reordered = jnp.take(aggregated, order, axis=1).astype(jnp.bfloat16)
    regrouped = lax.all_to_all(reordered, "grp", split_axis=1, concat_axis=0, tiled=True)
    mixed = (
        jnp.einsum("fh,fi->hi", weight, regrouped, preferred_element_type=jnp.float32)
        + bias[:, None]
    )
    return jnp.maximum(mixed, 0.0).astype(jnp.bfloat16)


def solution(mesh):
    in_specs = (
        P("grp", ("parts", "blk")),
        P(("parts", "blk"), None, None),
        P(("parts", "blk"), None, None),
        P(("parts", "blk"), None, None, None, None),
        P(("parts", "blk")),
        P(),
        P(),
    )
    out_specs = P(None, ("parts", "blk", "grp"))
    return jax.shard_map(
        on_device, mesh=mesh, in_specs=in_specs, out_specs=out_specs, check_vma=False
    )
```

profile of v0, /device:TPU:0, one launch (start us, length us, event | category | flops | bytes accessed | tf_op | source)
XLA Modules:
  0.0 248.5 jit_solution(8963870164869348281)
XLA Ops:
  0.0 0.0 copy-start
  0.0 4.2 %copy.15 = bf16[128,8192]{0,1:T(8,128)(2,1)} copy(bf16[128,8192]{1,0:T(8,128)(2,1)} %param.11) | data formatting | bytes 4194304
  4.2 0.0 copy-done.1
  4.2 0.0 copy-start.4
  4.2 2.4 convert_bitcast_fusion
  6.6 0.0 copy-done.2
  6.6 0.1 iota_compare_fusion
  6.8 2.5 %convert_reduce_fusion = f32[4,20,128]{2,1,0:T(8,128)S(1)} fusion(bf16[1,4,20,128,128]{4,3,2,1,0:T(8,128)(2,1)} %param.14), kind=kLoop, calls=%fused_computation.21 | loop fusion | flops 2611200 | bytes 2662400 | tf_op jit(solution)/shard_map/reduce_sum | solution.py:26
  9.3 152.1 %while.16 = (s32[]{:T(128)}, bf16[128,8192]{0,1:T(8,128)(2,1)}, f32[128,64,128]{2,1,0:T(8,128)}, f32[4,20,64]{2,1,0:T(8,128)S(1)}, bf16[4,20,128,128]{3,2,1,0:T(...) while((s32[]{:T(128)}, bf16[128,8192]{0,1:T(8,128)(2,1)}, f32[128,64,128]{2,1,0:T(8,128)}, ...), condition=%wide.region_1.3_spmd.clone, body=%wide.region_0.2_spmd.clone.sunk | while | flops 337970304 | bytes 33047040 | solution.py:48
  9.3 1.6 copy.33
  10.9 3.0 %collective-permute-start = (bf16[128,8192]{0,1:T(8,128)(2,1)S(1)}, bf16[128,8192]{0,1:T(8,128)(2,1)}, u32[]{:S(2)}, u32[]{:S(2)}) collective-permute-start(bf16[128,8192]{0,1:T(8,128)(2,1)S(1)} %copy.33), channel_id=1, source_target_pairs={{0,4},{4,8},{8,12},{12,0},{1,5},{5,9},{9,13},{13,1},{2,6},{6,10},{... | collective-permute-start | bytes 6291464 | tf_op jit(solution)/shard_map/while/body/eval_jaxpr/ppermute | solution.py:10
  13.9 2.9 %copy.27 = bf16[128,64,128]{2,0,1:T(8,128)(2,1)} copy(bf16[128,64,128]{0,2,1:T(8,128)(2,1)S(1)} %bitcast.81) | data formatting | bytes 4194304 | tf_op jit(solution)/shard_map/while/body/eval_jaxpr/reshape | solution.py:36
  16.8 2.3 gather_fusion
  19.1 2.8 %convolution_bitcast_fusion.4 = f32[128,20,128]{0,2,1:T(8,128)} fusion(bf16[20,128,128]{2,1,0:T(8,128)(2,1)S(1)} %gather_fusion, bf16[4,20,128,128]{3,2,1,0:T(8,128)(2,1)} %get-tuple-element.224, s32[]{:T(128)S(6)} %copy.32, pred[20]{0:T(512)(128)(4,1)S(1)} %get-tuple-element.203), kind=kOutput, calls=%fused_computation.4.clone.1 | convolution fusion | flops 84213760 | bytes 2621464 | tf_op jit(solution)/shard_map/while/body/eval_jaxpr/ftj,tij->fti/dot_general | solution.py:37
  21.9 2.9 %copy.28 = f32[128,20,128]{2,1,0:T(8,128)} copy(f32[128,20,128]{0,2,1:T(8,128)} %convolution_bitcast_fusion.4) | data formatting | bytes 2621440 | tf_op jit(solution)/shard_map/while/body/eval_jaxpr/ftj,tij->fti/transpose | solution.py:37
  24.8 7.0 %bitcast_add_fusion.4 = f32[128,64,128]{2,1,0:T(8,128)} fusion(f32[128,64,128]{2,1,0:T(8,128)} %get-tuple-element.214, f32[128,20,128]{2,1,0:T(8,128)} %copy.28, pred[]{:T(512)S(6)} %compare.3, f32[4,20,64]{2,1,0:T(8,128)S(1)} %get-tuple-element.223, s32[]{:T(128)S(6)} %copy.32), kind=kOutput, calls=%fused_computation.3.clone.1 | convolution fusion | flops 253755392 | bytes 9711621 | tf_op jit(solution)/shard_map/while/body/eval_jaxpr/fti,tr->fri/dot_general | solution.py:40
  31.8 29.8 %collective-permute-done = bf16[128,8192]{0,1:T(8,128)(2,1)} collective-permute-done((bf16[128,8192]{0,1:T(8,128)(2,1)S(1)}, bf16[128,8192]{0,1:T(8,128)(2,1)}, u32[]{:S(2)}, u32[]{:S(2)}) %collective-permute-start) | collective-permute-done | bytes 2097184 | tf_op jit(solution)/shard_map/while/body/eval_jaxpr/ppermute | solution.py:10
  61.7 1.6 copy.33
  63.2 0.0 collective-permute-start
  63.2 2.9 %copy.27 = bf16[128,64,128]{2,0,1:T(8,128)(2,1)} copy(bf16[128,64,128]{0,2,1:T(8,128)(2,1)S(1)} %bitcast.81) | data formatting | bytes 4194304 | tf_op jit(solution)/shard_map/while/body/eval_jaxpr/reshape | solution.py:36
  66.2 2.3 gather_fusion
  68.4 2.8 %convolution_bitcast_fusion.4 = f32[128,20,128]{0,2,1:T(8,128)} fusion(bf16[20,128,128]{2,1,0:T(8,128)(2,1)S(1)} %gather_fusion, bf16[4,20,128,128]{3,2,1,0:T(8,128)(2,1)} %get-tuple-element.224, s32[]{:T(128)S(6)} %copy.32, pred[20]{0:T(512)(128)(4,1)S(1)} %get-tuple-element.203), kind=kOutput, calls=%fused_computation.4.clone.1 | convolution fusion | flops 84213760 | bytes 2621464 | tf_op jit(solution)/shard_map/while/body/eval_jaxpr/ftj,tij->fti/dot_general | solution.py:37
  71.2 2.9 %copy.28 = f32[128,20,128]{2,1,0:T(8,128)} copy(f32[128,20,128]{0,2,1:T(8,128)} %convolution_bitcast_fusion.4) | data formatting | bytes 2621440 | tf_op jit(solution)/shard_map/while/body/eval_jaxpr/ftj,tij->fti/transpose | solution.py:37
  74.2 8.3 %bitcast_add_fusion.4 = f32[128,64,128]{2,1,0:T(8,128)} fusion(f32[128,64,128]{2,1,0:T(8,128)} %get-tuple-element.214, f32[128,20,128]{2,1,0:T(8,128)} %copy.28, pred[]{:T(512)S(6)} %compare.3, f32[4,20,64]{2,1,0:T(8,128)S(1)} %get-tuple-element.223, s32[]{:T(128)S(6)} %copy.32), kind=kOutput, calls=%fused_computation.3.clone.1 | convolution fusion | flops 253755392 | bytes 9711621 | tf_op jit(solution)/shard_map/while/body/eval_jaxpr/fti,tr->fri/dot_general | solution.py:40
  82.4 29.5 %collective-permute-done = bf16[128,8192]{0,1:T(8,128)(2,1)} collective-permute-done((bf16[128,8192]{0,1:T(8,128)(2,1)S(1)}, bf16[128,8192]{0,1:T(8,128)(2,1)}, u32[]{:S(2)}, u32[]{:S(2)}) %collective-permute-start) | collective-permute-done | bytes 2097184 | tf_op jit(solution)/shard_map/while/body/eval_jaxpr/ppermute | solution.py:10
  112.0 1.6 copy.33
  113.6 0.0 collective-permute-start
  113.6 2.9 %copy.27 = bf16[128,64,128]{2,0,1:T(8,128)(2,1)} copy(bf16[128,64,128]{0,2,1:T(8,128)(2,1)S(1)} %bitcast.81) | data formatting | bytes 4194304 | tf_op jit(solution)/shard_map/while/body/eval_jaxpr/reshape | solution.py:36
  116.5 2.3 gather_fusion
  118.7 2.8 %convolution_bitcast_fusion.4 = f32[128,20,128]{0,2,1:T(8,128)} fusion(bf16[20,128,128]{2,1,0:T(8,128)(2,1)S(1)} %gather_fusion, bf16[4,20,128,128]{3,2,1,0:T(8,128)(2,1)} %get-tuple-element.224, s32[]{:T(128)S(6)} %copy.32, pred[20]{0:T(512)(128)(4,1)S(1)} %get-tuple-element.203), kind=kOutput, calls=%fused_computation.4.clone.1 | convolution fusion | flops 84213760 | bytes 2621464 | tf_op jit(solution)/shard_map/while/body/eval_jaxpr/ftj,tij->fti/dot_general | solution.py:37
  121.6 2.9 %copy.28 = f32[128,20,128]{2,1,0:T(8,128)} copy(f32[128,20,128]{0,2,1:T(8,128)} %convolution_bitcast_fusion.4) | data formatting | bytes 2621440 | tf_op jit(solution)/shard_map/while/body/eval_jaxpr/ftj,tij->fti/transpose | solution.py:37
  124.5 8.3 %bitcast_add_fusion.4 = f32[128,64,128]{2,1,0:T(8,128)} fusion(f32[128,64,128]{2,1,0:T(8,128)} %get-tuple-element.214, f32[128,20,128]{2,1,0:T(8,128)} %copy.28, pred[]{:T(512)S(6)} %compare.3, f32[4,20,64]{2,1,0:T(8,128)S(1)} %get-tuple-element.223, s32[]{:T(128)S(6)} %copy.32), kind=kOutput, calls=%fused_computation.3.clone.1 | convolution fusion | flops 253755392 | bytes 9711621 | tf_op jit(solution)/shard_map/while/body/eval_jaxpr/fti,tr->fri/dot_general | solution.py:40
  132.8 28.6 %collective-permute-done = bf16[128,8192]{0,1:T(8,128)(2,1)} collective-permute-done((bf16[128,8192]{0,1:T(8,128)(2,1)S(1)}, bf16[128,8192]{0,1:T(8,128)(2,1)}, u32[]{:S(2)}, u32[]{:S(2)}) %collective-permute-start) | collective-permute-done | bytes 2097184 | tf_op jit(solution)/shard_map/while/body/eval_jaxpr/ppermute | solution.py:10
  161.4 3.2 %copy.16 = bf16[128,64,128]{2,0,1:T(8,128)(2,1)S(1)} copy(bf16[128,64,128]{0,2,1:T(8,128)(2,1)} %bitcast.6) | data formatting | bytes 4194304 | tf_op jit(solution)/shard_map/reshape | solution.py:36
  164.6 0.3 fusion.15
  164.9 4.9 %copy.22 = f32[16,8,64,128]{3,2,1,0:T(8,128)} copy(f32[16,8,64,128]{3,1,2,0:T(8,128)} %convert_bitcast_fusion) | data formatting | bytes 8388608
  169.8 0.7 gather_fusion.2
  170.5 1.7 convolution_bitcast_fusion.1
  172.2 8.1 %fusion.12 = bf16[128,64,128]{2,1,0:T(8,128)(2,1)} fusion(f32[16,8,64,128]{3,2,1,0:T(8,128)} %copy.22, f32[128,64,128]{2,1,0:T(8,128)} %get-tuple-element.116, f32[64,128]{1,0:T(8,128)S(1)} %fusion.15, f32[128,20,128]{2,0,1:T(8,128)S(1)} %convolution_bitcast_fusion.1, pred[4,20,64]{2,1,0:T(8,128)(4,1)S(1)} %get-tuple-element.161), kind=kOutput, calls=%fused_computation.23 | convolution fusion | flops 255852544 | bytes 11832320 | tf_op jit(solution)/shard_map/fti,tr->fri/dot_general | solution.py:40
  180.3 3.3 %copy.21 = bf16[128,64,128]{0,2,1:T(8,128)(2,1)S(1)} copy(bf16[128,64,128]{2,1,0:T(8,128)(2,1)} %fusion.12) | data formatting | bytes 4194304 | tf_op jit(solution)/shard_map/reshape | solution.py:51
  183.6 29.5 %gather_fusion.1 = bf16[8192,128]{1,0:T(8,128)(2,1)} fusion(bf16[128,8192]{0,1:T(8,128)(2,1)S(1)} %bitcast.82, s32[8192]{0:T(1024)S(1)} %fusion.22), kind=kCustom, calls=%fused_computation.2 | custom fusion | bytes 4227072 | tf_op jit(solution)/shard_map/jit(_take)/gather | solution.py:52
  213.1 2.9 %copy.19 = bf16[128,4,2048]{2,0,1:T(8,128)(2,1)S(1)} copy(bf16[128,4,2048]{0,2,1:T(8,128)(2,1)} %bitcast.83) | data formatting | bytes 4194304 | tf_op jit(solution)/shard_map/jit(_take)/gather | solution.py:52
  216.0 0.6 select_convert_fusion
  216.6 0.0 copy-start.5
  216.7 28.2 %all_to_all.16 = bf16[128,4,2048]{2,0,1:T(8,128)(2,1)S(1)} all-to-all(bf16[128,4,2048]{2,0,1:T(8,128)(2,1)S(1)} %select_convert_fusion), channel_id=1, replica_groups=mesh['parts'=2,'blk'=4,'grp'=4] {'grp'}, dimensions={1} | all-to-all | bytes 4194304 | tf_op jit(solution)/shard_map/all_to_all | solution.py:53
  244.8 0.0 copy-done
  244.8 1.3 fusion.13
  246.2 2.4 copy.20
  (18 shorter events, 0.1 us)
Async XLA Ops:
  0.0 244.8 %copy-start = (bf16[512,512]{1,0:T(8,128)(2,1)S(1)}, bf16[512,512]{1,0:T(8,128)(2,1)}, u32[]{:S(2)}) copy-start(bf16[512,512]{1,0:T(8,128)(2,1)} %param.16) | copy-start | bytes 1572868
  0.0 4.2 %copy-start.1 = (bf16[128,8192]{1,0:T(8,128)(2,1)S(1)}, bf16[128,8192]{1,0:T(8,128)(2,1)}, u32[]{:S(2)}) copy-start(bf16[128,8192]{1,0:T(8,128)(2,1)} %param.11) | copy-start | bytes 6291460
  4.2 2.4 copy-start.2
  4.2 2.4 copy-start.3
  4.2 2.5 %copy-start.4 = (s32[1,4,20]{2,1,0:T(4,128)S(1)}, s32[1,4,20]{2,1,0:T(4,128)}, u32[]{:S(2)}) copy-start(s32[1,4,20]{2,1,0:T(4,128)} %param.13) | copy-start | bytes 964
  10.9 50.8 %collective-permute-start = (bf16[128,8192]{0,1:T(8,128)(2,1)S(1)}, bf16[128,8192]{0,1:T(8,128)(2,1)}, u32[]{:S(2)}, u32[]{:S(2)}) collective-permute-start(bf16[128,8192]{0,1:T(8,128)(2,1)S(1)} %copy.33), channel_id=1, source_target_pairs={{0,4},{4,8},{8,12},{12,0},{1,5},{5,9},{9,13},{13,1},{2,6},{6,10},{... | collective-permute-start | bytes 6291464 | tf_op jit(solution)/shard_map/while/body/eval_jaxpr/ppermute | solution.py:10
  63.2 48.7 %collective-permute-start = (bf16[128,8192]{0,1:T(8,128)(2,1)S(1)}, bf16[128,8192]{0,1:T(8,128)(2,1)}, u32[]{:S(2)}, u32[]{:S(2)}) collective-permute-start(bf16[128,8192]{0,1:T(8,128)(2,1)S(1)} %copy.33), channel_id=1, source_target_pairs={{0,4},{4,8},{8,12},{12,0},{1,5},{5,9},{9,13},{13,1},{2,6},{6,10},{... | collective-permute-start | bytes 6291464 | tf_op jit(solution)/shard_map/while/body/eval_jaxpr/ppermute | solution.py:10
  113.6 47.8 %collective-permute-start = (bf16[128,8192]{0,1:T(8,128)(2,1)S(1)}, bf16[128,8192]{0,1:T(8,128)(2,1)}, u32[]{:S(2)}, u32[]{:S(2)}) collective-permute-start(bf16[128,8192]{0,1:T(8,128)(2,1)S(1)} %copy.33), channel_id=1, source_target_pairs={{0,4},{4,8},{8,12},{12,0},{1,5},{5,9},{9,13},{13,1},{2,6},{6,10},{... | collective-permute-start | bytes 6291464 | tf_op jit(solution)/shard_map/while/body/eval_jaxpr/ppermute | solution.py:10
  216.6 28.2 %copy-start.5 = (f32[512]{0:T(512)S(1)}, f32[512]{0:T(512)}, u32[]{:S(2)}) copy-start(f32[512]{0:T(512)} %param.17) | copy-start | bytes 6148
where the time goes:
time: 250 us; the launch traced here: 249 us
  waiting for transfers between devices  88 us (35%)
  local copies, waits for them, and re-layouts  80.1 us (32%)
  matrix products  43.4 us (17%)
  blocking collectives  28.2 us (11%)
  other arithmetic  5.62 us (2%)
  starting transfers between devices  3.04 us (1%)
    ppermute x3, waiting for transfers between devices, shifted(): return lax.ppermute(value, axis, pairs)  88 us
    gather x2, local copies, waits for them, and re-layouts, on_device(): reordered = jnp.take(aggregated, order, axis=1).astype(jnp.bfloat16)  32.4 us
    dot_general x4, matrix products, contrib(): jnp.einsum('fti,tr->fri', product, onehot_step, precision=lax.Precision.H...  31.7 us
    all_to_all x1, blocking collectives, on_device(): lax.all_to_all(reordered, 'grp', split_axis=1, concat_axis=0, tiled=True)  28.2 us
    reshape x4, local copies, waits for them, and re-layouts, contrib(): panel.reshape(width, row_tiles, tile)  11.8 us
    dot_general x4, matrix products, contrib(): jnp.einsum('ftj,tij->fti', gathered, counts_step, preferred_element_type=...  10.2 us
    unnamed x14, local copies, waits for them, and re-layouts  9.12 us
    transpose x3, local copies, waits for them, and re-layouts, contrib(): jnp.einsum('ftj,tij->fti', gathered, counts_step, preferred_element_type=...  8.79 us
  transfers between devices with their start and end apart: 3, of which 3 were waited for; matrix products, arithmetic and copies ran while one was open for 23% of the time, Pallas kernels for 0%

commit v1 on v0

v1 whole, which is shorter than its diff:
```python
import functools

import jax
import jax.numpy as jnp
from jax import lax
from jax.experimental import pallas as pl
from jax.experimental.pallas import tpu as pltpu
from jax.sharding import PartitionSpec as P

NT = (((1,), (1,)), ((), ()))
VMEM = pl.BlockSpec(memory_space=pltpu.VMEM)
SMEM = pl.BlockSpec(memory_space=pltpu.SMEM)
LIMIT = 48 * 2**20


def params():
    return pltpu.CompilerParams(vmem_limit_bytes=LIMIT)


def cost(flops, moved):
    return pl.CostEstimate(flops=flops, bytes_accessed=moved, transcendentals=0)


def shifted(value, axis, steps):
    count = lax.axis_size(axis)
    pairs = [(source, (source + steps) % count) for source in range(count)]
    return lax.ppermute(value, axis, pairs)


def partner(index, k, count):
    return index ^ k if count & (count - 1) == 0 else (k - index) % count


def traded(value, axis, k):
    count = lax.axis_size(axis)
    return lax.ppermute(value, axis, [(i, partner(i, k, count)) for i in range(count)])


def cuts(width):
    first = width // 2
    return ((0, first), (first, width - first))


def pack_kernel(ranges, offsets, slots, tile, *refs):
    asked, panel, outs = refs[:offsets], refs[offsets], refs[offsets + 1 :]
    for s in range(offsets):

        def body(t, carry, s=s):
            at = pl.multiple_of(asked[s][t] * tile, tile)
            for p, (low, size) in enumerate(ranges):
                outs[p * offsets + s][t] = panel[pl.ds(low, size), pl.ds(at, tile)]
            return carry

        lax.fori_loop(0, slots, body, 0, unroll=4)


def pack(panel, asked, ranges, tile):
    offsets, slots = len(asked), asked[0].shape[0]
    shapes = [
        jax.ShapeDtypeStruct((slots, size, tile), panel.dtype)
        for _, size in ranges
        for _ in range(offsets)
    ]
    outs = pl.pallas_call(
        functools.partial(pack_kernel, ranges, offsets, slots, tile),
        out_shape=shapes,
        in_specs=[SMEM] * offsets + [VMEM],
        out_specs=[VMEM] * len(shapes),
        compiler_params=params(),
        cost_estimate=cost(0, 4 * panel.size),
        name="pack",
    )(*asked, panel)
    return [outs[p * offsets : (p + 1) * offsets] for p in range(len(ranges))]


def own_kernel(ranges, blocks, slots, tile, rows, cols, panel, counts, *outs):
    accs, inverse = outs[:-1], outs[-1]
    lanes = inverse.shape[1]
    row_tiles = panel.shape[1] // tile
    eye = (
        lax.broadcasted_iota(jnp.int32, (tile, tile), 0)
        == lax.broadcasted_iota(jnp.int32, (tile, tile), 1)
    ).astype(jnp.float32).astype(jnp.bfloat16)
    ones = jnp.ones((lanes, tile), jnp.bfloat16)

    def start(r, carry):
        at = pl.multiple_of(r * tile, tile)
        for acc, (low, size) in zip(accs, ranges):
            acc[pl.ds(at, tile), :] = lax.dot_general(
                eye,
                panel[pl.ds(low, size), pl.ds(at, tile)],
                NT,
                preferred_element_type=jnp.float32,
            )
        inverse[pl.ds(at, tile), :] = jnp.ones((tile, lanes), jnp.float32)
        return carry

    lax.fori_loop(0, row_tiles, start, 0)

    def add(t, carry):
        at = pl.multiple_of(rows[0, t] * tile, tile)
        col = pl.multiple_of(cols[0, t] * tile, tile)
        for acc, (low, size) in zip(accs, ranges):
            acc[pl.ds(at, tile), :] += lax.dot_general(
                counts[t],
                panel[pl.ds(low, size), pl.ds(col, tile)],
                NT,
                preferred_element_type=jnp.float32,
            )
        return carry

    lax.fori_loop(0, slots, add, 0)

    for s in range(blocks):

        def degree(t, carry, s=s):
            at = pl.multiple_of(rows[s, t] * tile, tile)
            inverse[pl.ds(at, tile), :] += lax.dot_general(
                counts[s * slots + t], ones, NT, preferred_element_type=jnp.float32
            )
            return carry

        lax.fori_loop(0, slots, degree, 0)

    def invert(r, carry):
        at = pl.multiple_of(r * tile, tile)
        inverse[pl.ds(at, tile), :] = 1.0 / inverse[pl.ds(at, tile), :]
        return carry

    lax.fori_loop(0, row_tiles, invert, 0)


def own(panel, rows, cols, counts, ranges):
    blocks, slots = rows.shape
    nodes, tile = panel.shape[1], counts.shape[-1]
    lanes = max(size for _, size in ranges)
    shapes = [jax.ShapeDtypeStruct((nodes, size), jnp.float32) for _, size in ranges]
    shapes.append(jax.ShapeDtypeStruct((nodes, lanes), jnp.float32))
    outs = pl.pallas_call(
        functools.partial(own_kernel, ranges, blocks, slots, tile),
        out_shape=shapes,
        in_specs=[SMEM, SMEM, VMEM, VMEM],
        out_specs=[VMEM] * len(shapes),
        compiler_params=params(),
        cost_estimate=cost(2 * nodes * tile * tile, 16 * 2**20),
        name="own",
    )(rows, cols, panel, counts)
    return outs[:-1], outs[-1]


def pick(order, first, count, nodes_ref, stage, out, out_first):
    step = stage.shape[0]

    def chunk(c, carry):
        def group(i, inner):
            at = pl.multiple_of(i * 16, 16)
            for u in range(16):
                source = order[first + c * step + at + u]
                stage[pl.ds(at + u, 1), :] = nodes_ref[pl.ds(source, 1), :]
            return inner

        lax.fori_loop(0, step // 16, group, 0)
        to = pl.multiple_of(out_first + c * step, step)
        out[pl.ds(to, step), :] = stage[...].astype(out.dtype)
        return carry

    lax.fori_loop(0, count // step, chunk, 0)


def gather_kernel(offsets, slots, tile, far, rows, order, acc, inverse, counts, *refs):
    got, total, out, stage = refs[:offsets], refs[offsets], refs[offsets + 1], refs[offsets + 2]
    size = acc.shape[1]
    total[...] = acc[...]
    for s in range(offsets):

        def add(t, carry, s=s):
            at = pl.multiple_of(rows[s + 1, t] * tile, tile)
            total[pl.ds(at, tile), :] += lax.dot_general(
                counts[(s + 1) * slots + t], got[s][t], NT, preferred_element_type=jnp.float32
            )
            return carry

        lax.fori_loop(0, slots, add, 0, unroll=2)

    def scale(r, carry):
        at = pl.multiple_of(r * tile, tile)
        total[pl.ds(at, tile), :] = total[pl.ds(at, tile), :] * inverse[pl.ds(at, tile), :size]
        return carry

    lax.fori_loop(0, total.shape[0] // tile, scale, 0)
    pick(order, 0, far, total, stage, out, 0)


def gather_far(acc, inverse, rows, order, counts, got, far):
    nodes, size = acc.shape
    slots, tile = rows.shape[1], counts.shape[-1]
    return pl.pallas_call(
        functools.partial(gather_kernel, len(got), slots, tile, far),
        out_shape=[
            jax.ShapeDtypeStruct((nodes, size), jnp.float32),
            jax.ShapeDtypeStruct((far, size), jnp.bfloat16),
        ],
        in_specs=[SMEM, SMEM] + [VMEM] * (3 + len(got)),
        out_specs=[VMEM, VMEM],
        scratch_shapes=[pltpu.VMEM((256, size), jnp.float32)],
        compiler_params=params(),
        cost_estimate=cost(2 * nodes * tile * tile, 32 * 2**20),
        name="gather_far",
    )(rows, order, acc, inverse, counts, *got)


def near_kernel(first, count, order, total, out, stage):
    pick(order, first, count, total, stage, out, 0)


def gather_near(total, order, first):
    nodes, size = total.shape
    count = order.shape[0] - first
    return pl.pallas_call(
        functools.partial(near_kernel, first, count),
        out_shape=jax.ShapeDtypeStruct((count, size), jnp.bfloat16),
        in_specs=[SMEM, VMEM],
        out_specs=VMEM,
        scratch_shapes=[pltpu.VMEM((256, size), jnp.float32)],
        compiler_params=params(),
        cost_estimate=cost(0, 24 * 2**20),
        name="gather_near",
    )(order, total)


def mix_kernel(weight, bias, *refs):
    pieces, out = refs[:-1], refs[-1]
    nodes = jnp.concatenate([piece[...] for piece in pieces], axis=1)
    mixed = lax.dot_general(weight[...], nodes, NT, preferred_element_type=jnp.float32)
    out[...] = jnp.maximum(mixed + bias[...], 0.0).astype(out.dtype)


def mix(weight, bias, pieces):
    hidden = weight.shape[0]
    nodes = pieces[0].shape[0]
    step = min(512, nodes)
    return pl.pallas_call(
        mix_kernel,
        grid=(nodes // step,),
        out_shape=jax.ShapeDtypeStruct((hidden, nodes), jnp.bfloat16),
        in_specs=[
            pl.BlockSpec(weight.shape, lambda i: (0, 0)),
            pl.BlockSpec(bias.shape, lambda i: (0, 0)),
        ]
        + [pl.BlockSpec((step, piece.shape[1]), lambda i: (i, 0)) for piece in pieces],
        out_specs=pl.BlockSpec((hidden, step), lambda i: (0, i)),
        compiler_params=params(),
        cost_estimate=cost(2 * hidden * weight.shape[1] * nodes, 5 * 2**20),
        name="mix",
    )(weight, bias, *pieces)


def on_device(features, tile_rows, tile_cols, tile_weights, order, weight, bias):
    width, nodes = features.shape
    _, blocks, slots, tile, _ = tile_weights.shape
    groups = lax.axis_size("grp")
    me = lax.axis_index("grp")
    share = nodes // groups
    ranges = cuts(width)
    rows = tile_rows[0]
    cols = tile_cols[0]
    counts = tile_weights.reshape(blocks * slots, tile, tile)

    asked = [shifted(cols[s], "blk", -s) for s in range(1, blocks)]
    packed = pack(features, asked, ranges, tile)

    ranks = list(range(groups - 1, -1, -1))
    far = max(groups - 2, 1) * share
    whose = [partner(me, k, groups) for k in ranks]
    picks = jnp.concatenate([lax.dynamic_slice(order, (w * share,), (share,)) for w in whose])
    from_rank = {k: lax.dynamic_slice(weight, (w * width, 0), (width, weight.shape[1]))
                 for k, w in zip(ranks, whose)}
    mixing = jnp.concatenate(
        [from_rank[k][low : low + size] for low, size in ranges for k in ranks], axis=0
    ).T

    accs, inverse = own(features, rows, cols, counts, ranges)
    pieces = []
    got = None
    for p in range(len(ranges)):
        sent = packed[p]
        if got is not None:
            sent = [lax.optimization_barrier((a, b))[0] for a, b in zip(sent, got)]
        got = [shifted(value, "blk", s + 1) for s, value in enumerate(sent)]
        total, out_far = gather_far(accs[p], inverse, rows, picks, counts, got, far)
        near = gather_near(total, picks, far)
        both = (out_far, near)
        for position, k in enumerate(ranks):
            at = position * share
            source, at = (out_far, at) if at < far else (near, at - far)
            piece = lax.slice_in_dim(source, at, at + share, axis=0)
            pieces.append(piece if k == 0 else traded(piece, "grp", k))
    return mix(mixing, bias[:, None], pieces)


def solution(mesh):
    in_specs = (
        P("grp", ("parts", "blk")),
        P(("parts", "blk"), None, None),
        P(("parts", "blk"), None, None),
        P(("parts", "blk"), None, None, None, None),
        P(("parts", "blk")),
        P(),
        P(),
    )
    out_specs = P(None, ("parts", "blk", "grp"))
    return jax.shard_map(
        on_device, mesh=mesh, in_specs=in_specs, out_specs=out_specs, check_vma=False
    )
```

time: 250 us -> 142 us (0.57)
  Pallas kernels: 0 us -> 81.8 us
  waiting for transfers between devices: 88 us -> 18.5 us
  local copies, waits for them, and re-layouts: 80.1 us -> 23.9 us
  matrix products: 43.4 us -> 0 us
  blocking collectives: 28.2 us -> 0 us
  starting transfers between devices: 3.04 us -> 17.4 us
  other arithmetic: 5.62 us -> 0.01 us
    ppermute x3 -> x9, waiting for transfers between devices: 88 us -> 4.34 us  [shifted(): return lax.ppermute(value, axis, pairs)]
    pallas_call x0 -> x7, Pallas kernels: none -> 81.8 us  [the longest x2 32.1 us: gather_far(): pl.pallas_call(functools.partial(gather_kernel, len(got), slots, tile, fa...]
    dot_general x10 -> x0, matrix products: 43.4 us -> none  [the longest x4 31.7 us: contrib(): jnp.einsum('fti,tr->fri', product, onehot_step, precision=lax.Precision.H...]
    gather x6 -> x0, local copies, waits for them, and re-layouts: 39.9 us -> none  [the longest x2 32.4 us: on_device(): reordered = jnp.take(aggregated, order, axis=1).astype(jnp.bfloat16)]
    all_to_all x1 -> x0, blocking collectives: 28.2 us -> none  [on_device(): lax.all_to_all(reordered, 'grp', split_axis=1, concat_axis=0, tiled=True)]
    reshape x5 -> x0, local copies, waits for them, and re-layouts: 15.1 us -> none  [the longest x4 11.8 us: contrib(): panel.reshape(width, row_tiles, tile)]
    ppermute x0 -> x6, waiting for transfers between devices: none -> 14.2 us  [traded(): lax.ppermute(value, axis, [(i, partner(i, k, count)) for i in range(count)])]
    ppermute x3 -> x9, starting transfers between devices: 3.04 us -> 13.1 us  [shifted(): return lax.ppermute(value, axis, pairs)]
  transfers between devices with their start and end apart: 3 -> 15, of which waited for: 3 -> 5; matrix products, arithmetic and copies ran while one was open for 23% -> 9% of each run, Pallas kernels for 0% -> 53%
where the time goes in v1:
time: 142 us
  Pallas kernels  81.8 us (58%)
  local copies, waits for them, and re-layouts  23.9 us (17%)
  waiting for transfers between devices  18.5 us (13%)
  starting transfers between devices  17.4 us (12%)
    pallas_call x2, Pallas kernels, gather_far(): pl.pallas_call(functools.partial(gather_kernel, len(got), slots, tile, fa...  32.1 us
    pallas_call x1, Pallas kernels, own(): pl.pallas_call(functools.partial(own_kernel, ranges, blocks, slots, tile)...  31.3 us
    unnamed x30, local copies, waits for them, and re-layouts  17.8 us
    ppermute x6, waiting for transfers between devices, traded(): lax.ppermute(value, axis, [(i, partner(i, k, count)) for i in range(count)])  14.2 us
    ppermute x9, starting transfers between devices, shifted(): return lax.ppermute(value, axis, pairs)  13.1 us
    pallas_call x2, Pallas kernels, gather_near(): pl.pallas_call(functools.partial(near_kernel, first, count), out_shape=ja...  11.7 us
    pallas_call x1, Pallas kernels, mix(): pl.pallas_call(mix_kernel, grid=(nodes // step,), out_shape=jax.ShapeDtyp...  4.77 us
    ppermute x9, waiting for transfers between devices, shifted(): return lax.ppermute(value, axis, pairs)  4.34 us
  transfers between devices with their start and end apart: 15, of which 5 were waited for; matrix products, arithmetic and copies ran while one was open for 9% of the time, Pallas kernels for 53%

profile of v1, /device:TPU:0, one launch (start us, length us, event | category | flops | bytes accessed | tf_op | source)
XLA Modules:
  0.0 141.8 jit_solution(1260290846695472286)
XLA Ops:
  0.0 0.8 slice_bitcast_fusion
  0.8 5.0 %collective-permute-start = (s32[20]{0:T(128)S(1)}, s32[20]{0:T(128)S(1)}, u32[]{:S(2)}, u32[]{:S(2)}) collective-permute-start(s32[20]{0:T(128)S(1)} %get-tuple-element.58), channel_id=1, source_target_pairs={{0,12},{4,0},{8,4},{12,8},{1,13},{5,1},{9,5},{13,9},{2,14},{6,2},{... | collective-permute-start | bytes 248 | tf_op jit(solution)/shard_map/ppermute | solution.py:27
  5.8 1.0 collective-permute-start.2
  6.9 0.3 collective-permute-done.refs_0_
  7.1 3.1 %collective-permute-done.1.refs_1_ = s32[20]{0:T(128)S(1)} collective-permute-done((s32[20]{0:T(128)S(1)}, s32[20]{0:T(128)S(1)}, u32[]{:S(2)}, u32[]{:S(2)}) %collective-permute-start.1) | collective-permute-done | bytes 112 | tf_op jit(solution)/shard_map/ppermute | solution.py:27
  10.3 0.9 collective-permute-done.2.refs_2_
  11.2 1.6 %copy-done.2 = bf16[128,8192]{1,0:T(8,128)(2,1)S(1)} copy-done((bf16[128,8192]{1,0:T(8,128)(2,1)S(1)}, bf16[128,8192]{1,0:T(8,128)(2,1)}, u32[]{:S(2)}) %copy-start.2) | copy-done | bytes 2097176
  12.8 2.0 %pack.1 = (bf16[20,64,128]{2,1,0:T(8,128)(2,1)S(1)}, bf16[20,64,128]{2,1,0:T(8,128)(2,1)S(1)}, bf16[20,64,128]{2,1,0:T(8,128)(2,1)S(1)}, bf16[20,64,128]{2,1,0:T...) custom-call(s32[20]{0:T(128)S(1)} %collective-permute-done.refs_0_, ...), custom_call_target="tpu_custom_call" | custom-call | bytes 4194304 | tf_op jit(solution)/shard_map/pack/pallas_call | solution.py:64
  14.8 1.1 collective-permute-start.4
  15.9 0.7 collective-permute-start.5
  16.6 1.3 collective-permute-start.3
  17.9 1.7 %copy-done = bf16[1,4,20,128,128]{4,3,2,1,0:T(8,128)(2,1)S(1)} copy-done((bf16[1,4,20,128,128]{4,3,2,1,0:T(8,128)(2,1)S(1)}, bf16[1,4,20,128,128]{4,3,2,1,0:T(8,128)(2,1)}, u32[]{:S(2)}) %copy-start) | copy-done | bytes 2621464
  19.7 1.6 %copy-done.3 = bf16[128,8192]{1,0:T(8,128)(2,1)S(1)} copy-done((bf16[128,8192]{1,0:T(8,128)(2,1)S(1)}, bf16[128,8192]{1,0:T(8,128)(2,1)}, u32[]{:S(2)}) %copy-start.3) | copy-done | bytes 2097176
  21.3 0.7 copy-done.6
  21.9 0.7 copy-done.7
  22.6 31.3 %own.1 = (f32[8192,64]{1,0:T(8,128)}, f32[8192,64]{1,0:T(8,128)}, f32[8192,64]{1,0:T(8,128)}) custom-call(s32[4,20]{1,0:T(4,128)S(1)} %bitcast.15, s32[4,20]{1,0:T(4,128)S(1)} %bitcast.18, bf16[128,8192]{1,0:T(8,128)(2,1)S(1)} %copy-done.3, bf16[80,128,128]{2,1,0:T(8,128)(2,1)S(1)} %bitcast.11), custom_call_target="tpu_custom_call" | custom-call | flops 268435456 | bytes 16777216 | tf_op jit(solution)/shard_map/own/pallas_call | solution.py:139
  53.9 1.9 %collective-permute-start.10 = (bf16[20,64,128]{2,1,0:T(8,128)(2,1)S(1)}, bf16[20,64,128]{2,1,0:T(8,128)(2,1)S(1)}, u32[]{:S(2)}, u32[]{:S(2)}) collective-permute-start(bf16[20,64,128]{2,1,0:T(8,128)(2,1)S(1)} %get-tuple-element.32), channel_id=1, source_target_pairs={{0,8},{4,12},{8,0},{12,4},{1,9},{5,13},{9,1},{13,5},{2,10},{6,14},... | collective-permute-start | bytes 983048 | tf_op jit(solution)/shard_map/ppermute | solution.py:27
  55.8 0.9 collective-permute-start.11
  56.7 1.1 collective-permute-start.9
  57.8 16.0 %gather_far.2 = (f32[8192,64]{1,0:T(8,128)}, bf16[4096,64]{1,0:T(8,128)(2,1)S(1)}) custom-call(s32[4,20]{1,0:T(4,128)S(1)} %bitcast.16, s32[8192]{0:T(1024)S(1)} %pad_add_fusion.order, f32[8192,64]{1,0:T(8,128)} %get-tuple-element.21.acc, f32[8192,64]{1,0:T(8,128)} %get-tuple-element.22.inverse, bf16[80,128,128]{2,1,0:T(8,128)(2,1)S(1)} %bitcast.12, ...), custom_call_target="tpu_custom_call" | custom-call | flops 268435456 | bytes 33554432 | tf_op jit(solution)/shard_map/gather_far/pallas_call | solution.py:197
  73.8 2.2 %copy-done.5 = f32[8192,64]{1,0:T(8,128)S(1)} copy-done((f32[8192,64]{1,0:T(8,128)S(1)}, f32[8192,64]{1,0:T(8,128)}, u32[]{:S(2)}) %copy-start.5) | copy-done | bytes 2097176
  76.0 5.8 %gather_near.2 = bf16[4096,64]{1,0:T(8,128)(2,1)S(1)} custom-call(s32[8192]{0:T(1024)S(1)} %pad_add_fusion.order, f32[8192,64]{1,0:T(8,128)S(1)} %copy-done.5), custom_call_target="tpu_custom_call" | custom-call | bytes 25165824 | tf_op jit(solution)/shard_map/gather_near/pallas_call | solution.py:219
  81.9 0.1 fusion.2
  81.9 0.1 collective-permute-start.8
  82.0 1.1 fusion.3
  83.1 1.6 %collective-permute-start.6 = (bf16[2048,64]{1,0:T(8,128)(2,1)}, bf16[2048,64]{1,0:T(8,128)(2,1)S(1)}, u32[]{:S(2)}, u32[]{:S(2)}) collective-permute-start(bf16[2048,64]{1,0:T(8,128)(2,1)} %get-tuple-element.44), channel_id=1, source_target_pairs={{0,3},{1,2},{2,1},{3,0},{4,7},{5,6},{6,5},{7,4},{8,11},{9,10},{10,... | collective-permute-start | bytes 786440 | tf_op jit(solution)/shard_map/ppermute | solution.py:36
  84.7 0.5 collective-permute-start.7
  85.2 16.1 %gather_far.3 = (f32[8192,64]{1,0:T(8,128)}, bf16[4096,64]{1,0:T(8,128)(2,1)S(1)}) custom-call(s32[4,20]{1,0:T(4,128)S(1)} %bitcast.17, s32[8192]{0:T(1024)S(1)} %pad_add_fusion.order, f32[8192,64]{1,0:T(8,128)} %get-tuple-element.28.acc, f32[8192,64]{1,0:T(8,128)} %get-tuple-element.22.inverse, bf16[80,128,128]{2,1,0:T(8,128)(2,1)S(1)} %bitcast.13, ...), custom_call_target="tpu_custom_call" | custom-call | flops 268435456 | bytes 33554432 | tf_op jit(solution)/shard_map/gather_far/pallas_call | solution.py:197
  101.3 2.2 %copy-done.4 = f32[8192,64]{1,0:T(8,128)S(1)} copy-done((f32[8192,64]{1,0:T(8,128)S(1)}, f32[8192,64]{1,0:T(8,128)}, u32[]{:S(2)}) %copy-start.4) | copy-done | bytes 2097176
  103.5 5.8 %gather_near.3 = bf16[4096,64]{1,0:T(8,128)(2,1)S(1)} custom-call(s32[8192]{0:T(1024)S(1)} %pad_add_fusion.order, f32[8192,64]{1,0:T(8,128)S(1)} %copy-done.4), custom_call_target="tpu_custom_call" | custom-call | bytes 25165824 | tf_op jit(solution)/shard_map/gather_near/pallas_call | solution.py:219
  109.4 0.9 fusion
  110.2 1.1 fusion.1
  111.3 1.6 %collective-permute-start.12 = (bf16[2048,64]{1,0:T(8,128)(2,1)}, bf16[2048,64]{1,0:T(8,128)(2,1)}, u32[]{:S(2)}, u32[]{:S(2)}) collective-permute-start(bf16[2048,64]{1,0:T(8,128)(2,1)} %get-tuple-element.40), channel_id=1, source_target_pairs={{0,3},{1,2},{2,1},{3,0},{4,7},{5,6},{6,5},{7,4},{8,11},{9,10},{10,... | collective-permute-start | bytes 786440 | tf_op jit(solution)/shard_map/ppermute | solution.py:36
  112.9 0.5 collective-permute-start.13
  113.4 0.7 constant_dynamic-slice_fusion.4
  114.1 1.0 copy.18
  115.1 1.6 %copy.20 = bf16[64,512]{0,1:T(8,128)(2,1)} copy(bf16[64,512]{1,0:T(8,128)(2,1)} %get-tuple-element.48) | data formatting | bytes 131072
  116.7 0.8 copy.22
  117.5 0.8 copy.24
  118.2 0.8 copy.25
  119.0 0.8 copy.26
  119.7 0.8 copy.27
  120.5 0.8 copy.28
  121.3 0.1 copy.16.bias
  121.4 1.4 %concatenate.6 = bf16[512,512]{0,1:T(8,128)(2,1)S(1)} concatenate(bf16[64,512]{0,1:T(8,128)(2,1)S(1)} %copy.18, bf16[64,512]{0,1:T(8,128)(2,1)} %copy.20, bf16[64,512]{0,1:T(8,128)(2,1)} %copy.22, bf16[64,512]{0,1:T(8,128)(2,1)} %copy.24, bf16[64,512]{0,1:T(8,128)(2,1)} %copy.25, bf16[64,512]{0,1:T(8,128)(2,1)} %copy.26, bf16[64,512]{0,1:T(8,128)(2,1)} %copy.27, ...), dimensions={0} | concatenate | bytes 1048576 | tf_op jit(solution)/shard_map/concatenate | solution.py:278
  122.9 2.6 %collective-permute-done.12.refs_4_ = bf16[2048,64]{1,0:T(8,128)(2,1)} collective-permute-done((bf16[2048,64]{1,0:T(8,128)(2,1)}, bf16[2048,64]{1,0:T(8,128)(2,1)}, u32[]{:S(2)}, u32[]{:S(2)}) %collective-permute-start.12) | collective-permute-done | bytes 262176 | tf_op jit(solution)/shard_map/ppermute | solution.py:36
  125.5 11.6 %collective-permute-done.13.refs_5_ = bf16[2048,64]{1,0:T(8,128)(2,1)} collective-permute-done((bf16[2048,64]{1,0:T(8,128)(2,1)}, bf16[2048,64]{1,0:T(8,128)(2,1)}, u32[]{:S(2)}, u32[]{:S(2)}) %collective-permute-start.13) | collective-permute-done | bytes 262176 | tf_op jit(solution)/shard_map/ppermute | solution.py:36
  137.1 4.8 %mix.1 = bf16[512,2048]{1,0:T(8,128)(2,1)} custom-call(bf16[512,512]{1,0:T(8,128)(2,1)S(1)} %bitcast.14, f32[512,1]{1,0:T(8,128)S(1)} %copy.16.bias, bf16[2048,64]{1,0:T(8,128)(2,1)S(1)} %collective-permute-done.6.refs_0_, bf16[2048,64]{1,0:T(8,128)(2,1)S(1)} %collective-permute-done.7.refs_1_, bf16[2048,64]{1,0:T(8,128)(2,1)S(1)} %collective-permute-done.8.refs_2_, ...), custom_call_target="tpu_custom_call" | custom-call | flops 1073741824 | bytes 5242880 | tf_op jit(solution)/shard_map/mix/pallas_call | solution.py:242
  (29 shorter events, 0.1 us)
Async XLA Ops:
  0.8 6.3 %collective-permute-start = (s32[20]{0:T(128)S(1)}, s32[20]{0:T(128)S(1)}, u32[]{:S(2)}, u32[]{:S(2)}) collective-permute-start(s32[20]{0:T(128)S(1)} %get-tuple-element.58), channel_id=1, source_target_pairs={{0,12},{4,0},{8,4},{12,8},{1,13},{5,1},{9,5},{13,9},{2,14},{6,2},{... | collective-permute-start | bytes 248 | tf_op jit(solution)/shard_map/ppermute | solution.py:27
  5.8 4.4 %collective-permute-start.1 = (s32[20]{0:T(128)S(1)}, s32[20]{0:T(128)S(1)}, u32[]{:S(2)}, u32[]{:S(2)}) collective-permute-start(s32[20]{0:T(128)S(1)} %get-tuple-element.59), channel_id=1, source_target_pairs={{0,8},{4,12},{8,0},{12,4},{1,9},{5,13},{9,1},{13,5},{2,10},{6,14},... | collective-permute-start | bytes 248 | tf_op jit(solution)/shard_map/ppermute | solution.py:27
  5.8 5.3 %collective-permute-start.2 = (s32[20]{0:T(128)S(1)}, s32[20]{0:T(128)S(1)}, u32[]{:S(2)}, u32[]{:S(2)}) collective-permute-start(s32[20]{0:T(128)S(1)} %get-tuple-element.57), channel_id=1, source_target_pairs={{0,4},{4,8},{8,12},{12,0},{1,5},{5,9},{9,13},{13,1},{2,6},{6,10},{... | collective-permute-start | bytes 248 | tf_op jit(solution)/shard_map/ppermute | solution.py:27
  11.2 1.6 %copy-start.2 = (bf16[128,8192]{1,0:T(8,128)(2,1)S(1)}, bf16[128,8192]{1,0:T(8,128)(2,1)}, u32[]{:S(2)}) copy-start(bf16[128,8192]{1,0:T(8,128)(2,1)} %refs_3_.1) | copy-start | bytes 6291460
  12.8 41.1 %copy-start.9 = (s32[8192]{0:T(1024)S(1)}, s32[8192]{0:T(1024)}, u32[]{:S(2)}) copy-start(s32[8192]{0:T(1024)} %param.11) | copy-start | bytes 98308
  14.8 39.1 %collective-permute-start.4 = (bf16[20,64,128]{2,1,0:T(8,128)(2,1)S(1)}, bf16[20,64,128]{2,1,0:T(8,128)(2,1)S(1)}, u32[]{:S(2)}, u32[]{:S(2)}) collective-permute-start(bf16[20,64,128]{2,1,0:T(8,128)(2,1)S(1)} %get-tuple-element.24), channel_id=1, source_target_pairs={{0,8},{4,12},{8,0},{12,4},{1,9},{5,13},{9,1},{13,5},{2,10},{6,14},... | collective-permute-start | bytes 983048 | tf_op jit(solution)/shard_map/ppermute | solution.py:27
  15.9 39.9 %collective-permute-start.5 = (bf16[20,64,128]{2,1,0:T(8,128)(2,1)S(1)}, bf16[20,64,128]{2,1,0:T(8,128)(2,1)S(1)}, u32[]{:S(2)}, u32[]{:S(2)}) collective-permute-start(bf16[20,64,128]{2,1,0:T(8,128)(2,1)S(1)} %get-tuple-element.25), channel_id=1, source_target_pairs={{0,12},{4,0},{8,4},{12,8},{1,13},{5,1},{9,5},{13,9},{2,14},{6,2},{... | collective-permute-start | bytes 983048 | tf_op jit(solution)/shard_map/ppermute | solution.py:27
  16.6 40.1 %collective-permute-start.3 = (bf16[20,64,128]{2,1,0:T(8,128)(2,1)S(1)}, bf16[20,64,128]{2,1,0:T(8,128)(2,1)S(1)}, u32[]{:S(2)}, u32[]{:S(2)}) collective-permute-start(bf16[20,64,128]{2,1,0:T(8,128)(2,1)S(1)} %get-tuple-element.23), channel_id=1, source_target_pairs={{0,4},{4,8},{8,12},{12,0},{1,5},{5,9},{9,13},{13,1},{2,6},{6,10},{... | collective-permute-start | bytes 983048 | tf_op jit(solution)/shard_map/ppermute | solution.py:27
  17.9 1.7 %copy-start = (bf16[1,4,20,128,128]{4,3,2,1,0:T(8,128)(2,1)S(1)}, bf16[1,4,20,128,128]{4,3,2,1,0:T(8,128)(2,1)}, u32[]{:S(2)}) copy-start(bf16[1,4,20,128,128]{4,3,2,1,0:T(8,128)(2,1)} %param.10) | copy-start | bytes 7864324
  19.7 1.6 %copy-start.3 = (bf16[128,8192]{1,0:T(8,128)(2,1)S(1)}, bf16[128,8192]{1,0:T(8,128)(2,1)}, u32[]{:S(2)}) copy-start(bf16[128,8192]{1,0:T(8,128)(2,1)} %refs_3_.1) | copy-start | bytes 6291460
  21.3 0.7 copy-start.6
  21.9 0.7 copy-start.7
  22.6 35.2 %copy-start.1 = (bf16[1,4,20,128,128]{4,3,2,1,0:T(8,128)(2,1)S(1)}, bf16[1,4,20,128,128]{4,3,2,1,0:T(8,128)(2,1)}, u32[]{:S(2)}) copy-start(bf16[1,4,20,128,128]{4,3,2,1,0:T(8,128)(2,1)} %param.10) | copy-start | bytes 7864324
  53.9 30.8 %collective-permute-start.10 = (bf16[20,64,128]{2,1,0:T(8,128)(2,1)S(1)}, bf16[20,64,128]{2,1,0:T(8,128)(2,1)S(1)}, u32[]{:S(2)}, u32[]{:S(2)}) collective-permute-start(bf16[20,64,128]{2,1,0:T(8,128)(2,1)S(1)} %get-tuple-element.32), channel_id=1, source_target_pairs={{0,8},{4,12},{8,0},{12,4},{1,9},{5,13},{9,1},{13,5},{2,10},{6,14},... | collective-permute-start | bytes 983048 | tf_op jit(solution)/shard_map/ppermute | solution.py:27
  55.8 29.4 %collective-permute-start.11 = (bf16[20,64,128]{2,1,0:T(8,128)(2,1)}, bf16[20,64,128]{2,1,0:T(8,128)(2,1)S(1)}, u32[]{:S(2)}, u32[]{:S(2)}) collective-permute-start(bf16[20,64,128]{2,1,0:T(8,128)(2,1)} %get-tuple-element.34), channel_id=1, source_target_pairs={{0,12},{4,0},{8,4},{12,8},{1,13},{5,1},{9,5},{13,9},{2,14},{6,2},{... | collective-permute-start | bytes 983048 | tf_op jit(solution)/shard_map/ppermute | solution.py:27
  56.7 28.5 %collective-permute-start.9 = (bf16[20,64,128]{2,1,0:T(8,128)(2,1)}, bf16[20,64,128]{2,1,0:T(8,128)(2,1)S(1)}, u32[]{:S(2)}, u32[]{:S(2)}) collective-permute-start(bf16[20,64,128]{2,1,0:T(8,128)(2,1)} %get-tuple-element.30), channel_id=1, source_target_pairs={{0,4},{4,8},{8,12},{12,0},{1,5},{5,9},{9,13},{13,1},{2,6},{6,10},{... | collective-permute-start | bytes 983048 | tf_op jit(solution)/shard_map/ppermute | solution.py:27
  73.8 2.2 %copy-start.5 = (f32[8192,64]{1,0:T(8,128)S(1)}, f32[8192,64]{1,0:T(8,128)}, u32[]{:S(2)}) copy-start(f32[8192,64]{1,0:T(8,128)} %get-tuple-element.27.total) | copy-start | bytes 6291460
  81.9 31.0 %collective-permute-start.8 = (bf16[2048,64]{1,0:T(8,128)(2,1)S(1)}, bf16[2048,64]{1,0:T(8,128)(2,1)S(1)}, u32[]{:S(2)}, u32[]{:S(2)}) collective-permute-start(bf16[2048,64]{1,0:T(8,128)(2,1)S(1)} %get-tuple-element.42), channel_id=1, source_target_pairs={{0,1},{1,0},{2,3},{3,2},{4,5},{5,4},{6,7},{7,6},{8,9},{9,8},{10,11... | collective-permute-start | bytes 786440 | tf_op jit(solution)/shard_map/ppermute | solution.py:36
  83.1 39.8 %collective-permute-start.6 = (bf16[2048,64]{1,0:T(8,128)(2,1)}, bf16[2048,64]{1,0:T(8,128)(2,1)S(1)}, u32[]{:S(2)}, u32[]{:S(2)}) collective-permute-start(bf16[2048,64]{1,0:T(8,128)(2,1)} %get-tuple-element.44), channel_id=1, source_target_pairs={{0,3},{1,2},{2,1},{3,0},{4,7},{5,6},{6,5},{7,4},{8,11},{9,10},{10,... | collective-permute-start | bytes 786440 | tf_op jit(solution)/shard_map/ppermute | solution.py:36
  84.7 38.2 %collective-permute-start.7 = (bf16[2048,64]{1,0:T(8,128)(2,1)}, bf16[2048,64]{1,0:T(8,128)(2,1)S(1)}, u32[]{:S(2)}, u32[]{:S(2)}) collective-permute-start(bf16[2048,64]{1,0:T(8,128)(2,1)} %get-tuple-element.43), channel_id=1, source_target_pairs={{0,2},{1,3},{2,0},{3,1},{4,6},{5,7},{6,4},{7,5},{8,10},{9,11},{10,... | collective-permute-start | bytes 786440 | tf_op jit(solution)/shard_map/ppermute | solution.py:36
  101.3 2.2 %copy-start.4 = (f32[8192,64]{1,0:T(8,128)S(1)}, f32[8192,64]{1,0:T(8,128)}, u32[]{:S(2)}) copy-start(f32[8192,64]{1,0:T(8,128)} %get-tuple-element.36.total) | copy-start | bytes 6291460
  103.5 9.9 %copy-start.8 = (bf16[512,512]{1,0:T(8,128)(2,1)S(1)}, bf16[512,512]{1,0:T(8,128)(2,1)}, u32[]{:S(2)}) copy-start(bf16[512,512]{1,0:T(8,128)(2,1)} %param.12) | copy-start | bytes 1572868
  109.4 11.9 %copy-start.10 = (f32[512]{0:T(512)S(1)}, f32[512]{0:T(512)}, u32[]{:S(2)}) copy-start(f32[512]{0:T(512)} %param.13) | copy-start | bytes 6148
  110.2 12.6 %collective-permute-start.14 = (bf16[2048,64]{1,0:T(8,128)(2,1)}, bf16[2048,64]{1,0:T(8,128)(2,1)}, u32[]{:S(2)}, u32[]{:S(2)}) collective-permute-start(bf16[2048,64]{1,0:T(8,128)(2,1)} %get-tuple-element.38), channel_id=1, source_target_pairs={{0,1},{1,0},{2,3},{3,2},{4,5},{5,4},{6,7},{7,6},{8,9},{9,8},{10,11... | collective-permute-start | bytes 786440 | tf_op jit(solution)/shard_map/ppermute | solution.py:36
  111.3 14.2 %collective-permute-start.12 = (bf16[2048,64]{1,0:T(8,128)(2,1)}, bf16[2048,64]{1,0:T(8,128)(2,1)}, u32[]{:S(2)}, u32[]{:S(2)}) collective-permute-start(bf16[2048,64]{1,0:T(8,128)(2,1)} %get-tuple-element.40), channel_id=1, source_target_pairs={{0,3},{1,2},{2,1},{3,0},{4,7},{5,6},{6,5},{7,4},{8,11},{9,10},{10,... | collective-permute-start | bytes 786440 | tf_op jit(solution)/shard_map/ppermute | solution.py:36
  112.9 24.2 %collective-permute-start.13 = (bf16[2048,64]{1,0:T(8,128)(2,1)}, bf16[2048,64]{1,0:T(8,128)(2,1)}, u32[]{:S(2)}, u32[]{:S(2)}) collective-permute-start(bf16[2048,64]{1,0:T(8,128)(2,1)} %get-tuple-element.39), channel_id=1, source_target_pairs={{0,2},{1,3},{2,0},{3,1},{4,6},{5,7},{6,4},{7,5},{8,10},{9,11},{10,... | collective-permute-start | bytes 786440 | tf_op jit(solution)/shard_map/ppermute | solution.py:36

commit v2 on v0

v2 whole, which is shorter than its diff:
```python
import functools

import jax
import jax.numpy as jnp
from jax import lax
from jax.experimental import pallas as pl
from jax.experimental.pallas import tpu as pltpu
from jax.sharding import PartitionSpec as P

NN = (((1,), (0,)), ((), ()))
NT = (((1,), (1,)), ((), ()))
VMEM = pl.BlockSpec(memory_space=pltpu.VMEM)
SMEM = pl.BlockSpec(memory_space=pltpu.SMEM)
CHUNK = 256


def dot(a, b, dims):
    return lax.dot_general(a, b, dims, preferred_element_type=jnp.float32)


def padded(shape, dtype):
    rows = 1
    for extent in shape[:-1]:
        rows *= extent
    return rows * -(-shape[-1] // 128) * 128 * jnp.dtype(dtype).itemsize


def call(kernel, name, scalars, arrays, outs, scratch=(), flops=0, twice=False, **kwargs):
    held = sum(padded(a.shape, a.dtype) for a in list(arrays) + list(outs))
    held += sum(padded(shape, dtype) for shape, dtype in scratch)
    return pl.pallas_call(
        kernel,
        out_shape=list(outs),
        in_specs=[SMEM] * len(scalars) + [VMEM] * len(arrays),
        out_specs=[VMEM] * len(outs),
        scratch_shapes=[pltpu.VMEM(shape, dtype) for shape, dtype in scratch],
        compiler_params=pltpu.CompilerParams(vmem_limit_bytes=held + 4 * 2**20),
        cost_estimate=pl.CostEstimate(flops=flops, bytes_accessed=held, transcendentals=0),
        name=name,
        **kwargs,
    )(*scalars, *arrays)


def shifted(value, axis, steps):
    count = lax.axis_size(axis)
    pairs = [(source, (source + steps) % count) for source in range(count)]
    return lax.ppermute(value, axis, pairs)


def traded(value, axis, k):
    return lax.ppermute(value, axis, [(i, i ^ k) for i in range(lax.axis_size(axis))])


def cuts(width):
    first = width // 2
    return ((0, first), (first, width - first))


def identity(size):
    row = lax.broadcasted_iota(jnp.int32, (size, size), 0)
    col = lax.broadcasted_iota(jnp.int32, (size, size), 1)
    return (row == col).astype(jnp.float32).astype(jnp.bfloat16)


def pack_kernel(low, size, offsets, slots, tile, *refs):
    asked, panel, outs = refs[:offsets], refs[offsets], refs[offsets + 1 :]
    for s in range(offsets):

        def body(t, carry, s=s):
            at = pl.multiple_of(asked[s][s + 1, t] * tile, tile)
            outs[s][t] = panel[pl.ds(low, size), pl.ds(at, tile)]
            return carry

        lax.fori_loop(0, slots, body, 0, unroll=4)


def pack(panel, asked, low, size, tile):
    offsets, slots = len(asked), asked[0].shape[1]
    shape = jax.ShapeDtypeStruct((slots, size, tile), panel.dtype)
    return call(
        functools.partial(pack_kernel, low, size, offsets, slots, tile),
        "pack",
        asked,
        [panel],
        [shape] * offsets,
    )


def own_kernel(ranges, blocks, slots, tile, rows, cols, panel, counts, *refs):
    accs, inverse, product = refs[: len(ranges)], refs[len(ranges)], refs[len(ranges) + 1]
    lanes = inverse.shape[1]
    row_tiles = panel.shape[1] // tile
    eye = identity(tile)
    ones = jnp.ones((tile, lanes), jnp.bfloat16)

    def start(r, carry):
        at = pl.multiple_of(r * tile, tile)
        for acc, (low, size) in zip(accs, ranges):
            acc[pl.ds(at, tile), :] = dot(eye, panel[pl.ds(low, size), pl.ds(at, tile)], NT)
        inverse[pl.ds(at, tile), :] = jnp.ones((tile, lanes), jnp.float32)
        return carry

    lax.fori_loop(0, row_tiles, start, 0, unroll=4)

    for acc, (low, size) in zip(accs, ranges):

        def multiply(t, carry, low=low, size=size):
            col = pl.multiple_of(cols[0, t] * tile, tile)
            product[t, :, :size] = dot(counts[t], panel[pl.ds(low, size), pl.ds(col, tile)], NT)
            return carry

        def add(t, carry, acc=acc, size=size):
            at = pl.multiple_of(rows[0, t] * tile, tile)
            acc[pl.ds(at, tile), :] += product[t, :, :size]
            return carry

        lax.fori_loop(0, slots, multiply, 0, unroll=4)
        lax.fori_loop(0, slots, add, 0)

    def degree(s, carry):
        def multiply(t, inner):
            product[t] = dot(counts[s * slots + t], ones, NN)
            return inner

        def add(t, inner):
            at = pl.multiple_of(rows[s, t] * tile, tile)
            inverse[pl.ds(at, tile), :] += product[t]
            return inner

        lax.fori_loop(0, slots, multiply, 0, unroll=4)
        lax.fori_loop(0, slots, add, 0)
        return carry

    lax.fori_loop(0, blocks, degree, 0)

    def invert(r, carry):
        at = pl.multiple_of(r * tile, tile)
        inverse[pl.ds(at, tile), :] = 1.0 / inverse[pl.ds(at, tile), :]
        return carry

    lax.fori_loop(0, row_tiles, invert, 0, unroll=2)


def own(panel, rows, cols, counts, ranges):
    blocks, slots = rows.shape
    nodes, tile = panel.shape[1], counts.shape[-1]
    lanes = max(size for _, size in ranges)
    shapes = [jax.ShapeDtypeStruct((nodes, size), jnp.float32) for _, size in ranges]
    shapes.append(jax.ShapeDtypeStruct((nodes, lanes), jnp.float32))
    outs = call(
        functools.partial(own_kernel, ranges, blocks, slots, tile),
        "own",
        [rows, cols],
        [panel, counts],
        shapes,
        [((slots, tile, lanes), jnp.float32)],
    )
    return outs[:-1], outs[-1]


def pick(order, base, nodes, stage, out):
    size = nodes.shape[1]
    eye = identity(size)

    def chunk(c, carry):
        def group(i, inner):
            at = pl.multiple_of(i * 16, 16)
            for u in range(16):
                source = order[base + c * CHUNK + at + u]
                stage[pl.ds(at + u, 1), :] = nodes[pl.ds(source, 1), :]
            return inner

        lax.fori_loop(0, CHUNK // 16, group, 0)
        to = pl.multiple_of(c * CHUNK, CHUNK)
        turned = dot(eye, stage[...].astype(jnp.bfloat16), NT)
        out[:, pl.ds(to, CHUNK)] = turned.astype(out.dtype)
        return carry

    lax.fori_loop(0, out.shape[1] // CHUNK, chunk, 0)


def far_kernel(offsets, slots, tile, bases, rows, order, acc, inverse, counts, *refs):
    got, total, outs = refs[:offsets], refs[offsets], refs[offsets + 1 : -2]
    product, stage = refs[-2:]
    size = acc.shape[1]
    total[...] = acc[...]
    for s in range(offsets):

        def multiply(t, carry, s=s):
            product[t] = dot(counts[(s + 1) * slots + t], got[s][t], NT)
            return carry

        def add(t, carry, s=s):
            at = pl.multiple_of(rows[s + 1, t] * tile, tile)
            total[pl.ds(at, tile), :] += product[t]
            return carry

        lax.fori_loop(0, slots, multiply, 0, unroll=4)
        lax.fori_loop(0, slots, add, 0)

    def scale(r, carry):
        at = pl.multiple_of(r * tile, tile)
        total[pl.ds(at, tile), :] = total[pl.ds(at, tile), :] * inverse[pl.ds(at, tile), :size]
        return carry

    lax.fori_loop(0, total.shape[0] // tile, scale, 0, unroll=2)
    for i, out in enumerate(outs):
        pick(order, bases[i], total, stage, out)


def gather_far(acc, inverse, bases, rows, order, counts, got, share, ranks):
    nodes, size = acc.shape
    slots, tile = rows.shape[1], counts.shape[-1]
    piece = jax.ShapeDtypeStruct((size, share), jnp.bfloat16)
    outs = call(
        functools.partial(far_kernel, len(got), slots, tile),
        "gather_far",
        [bases, rows, order],
        [acc, inverse, counts, *got],
        [jax.ShapeDtypeStruct((nodes, size), jnp.float32)] + [piece] * ranks,
        [((slots, tile, size), jnp.float32), ((CHUNK, size), jnp.float32)],
    )
    return outs[0], outs[1:]


def near_kernel(skip, bases, order, total, *refs):
    outs, stage = refs[:-1], refs[-1]
    for i, out in enumerate(outs):
        pick(order, bases[skip + i], total, stage, out)


def gather_near(total, bases, order, share, skip, ranks):
    size = total.shape[1]
    return call(
        functools.partial(near_kernel, skip),
        "gather_near",
        [bases, order],
        [total],
        [jax.ShapeDtypeStruct((size, share), jnp.bfloat16)] * ranks,
        [((CHUNK, size), jnp.float32)],
    )


def mix_kernel(places, starts, weight, bias, *refs):
    pieces, out, nodes = refs[:-2], refs[-2], refs[-1]
    for piece, (i, low) in zip(pieces, places):
        at = pl.multiple_of(starts[i] + low, 16)
        nodes[pl.ds(at, piece.shape[0]), :] = piece[...]
    mixed = dot(weight[...], nodes[...], NN)
    out[...] = jnp.maximum(mixed + bias[...], 0.0).astype(out.dtype)


def mix(starts, weight, bias, pieces, places):
    hidden, width = weight.shape
    nodes = pieces[0].shape[1]
    step = min(512, nodes)
    return pl.pallas_call(
        functools.partial(mix_kernel, places),
        grid=(nodes // step,),
        out_shape=jax.ShapeDtypeStruct((hidden, nodes), jnp.bfloat16),
        in_specs=[
            SMEM,
            pl.BlockSpec(weight.shape, lambda i: (0, 0)),
            pl.BlockSpec(bias.shape, lambda i: (0, 0)),
        ]
        + [pl.BlockSpec((piece.shape[0], step), lambda i: (0, i)) for piece in pieces],
        out_specs=pl.BlockSpec((hidden, step), lambda i: (0, i)),
        scratch_shapes=[pltpu.VMEM((width, step), jnp.bfloat16)],
        compiler_params=pltpu.CompilerParams(vmem_limit_bytes=16 * 2**20),
        cost_estimate=pl.CostEstimate(
            flops=2 * hidden * width * nodes, bytes_accessed=5 * 2**20, transcendentals=0
        ),
        name="mix",
    )(starts, weight, bias, *pieces)


def on_device(features, tile_rows, tile_cols, tile_weights, order, weight, bias):
    width, nodes = features.shape
    _, blocks, slots, tile, _ = tile_weights.shape
    groups = lax.axis_size("grp")
    me = lax.axis_index("grp")
    share = nodes // groups
    ranges = cuts(width)
    rows = tile_rows.reshape(blocks, slots)
    cols = tile_cols.reshape(blocks, slots)
    counts = tile_weights.reshape(blocks * slots, tile, tile)

    asked = [shifted(cols, "blk", -s) for s in range(1, blocks)]
    got = []
    for low, size in ranges:
        sent = pack(features, asked, low, size, tile)
        asked = lax.optimization_barrier((*asked, sent[0]))[:-1]
        got.append([shifted(value, "blk", s + 1) for s, value in enumerate(sent)])

    ranks = list(range(groups - 1, -1, -1))
    whose = me ^ jnp.asarray(ranks, jnp.int32)
    bases = whose * share
    far = groups - 2

    accs, inverse = own(features, rows, cols, counts, ranges)
    pieces, places = [], []
    for p, (low, size) in enumerate(ranges):
        total, out_far = gather_far(
            accs[p], inverse, bases, rows, order, counts, got[p], share, far
        )
        near = gather_near(total, bases, order, share, far, groups - far)
        for i, (k, piece) in enumerate(zip(ranks, [*out_far, *near])):
            pieces.append(piece if k == 0 else traded(piece, "grp", k))
            places.append((i, low))
    return mix(whose * width, weight.T, bias[:, None], pieces, tuple(places))


def solution(mesh):
    in_specs = (
        P("grp", ("parts", "blk")),
        P(("parts", "blk"), None, None),
        P(("parts", "blk"), None, None),
        P(("parts", "blk"), None, None, None, None),
        P(("parts", "blk")),
        P(),
        P(),
    )
    out_specs = P(None, ("parts", "blk", "grp"))
    return jax.shard_map(
        on_device, mesh=mesh, in_specs=in_specs, out_specs=out_specs, check_vma=False
    )
```

time: 250 us -> 122 us (0.49)
  the two profiles are of different devices: /device:TPU:0 before, /device:TPU:16 now
where the time goes in v2:
time: 122 us
  Pallas kernels  61 us (50%)
  waiting for transfers between devices  34.7 us (28%)
  starting transfers between devices  20.3 us (17%)
  local copies, waits for them, and re-layouts  5.72 us (5%)
    pallas_call x7, Pallas kernels, call(): pl.pallas_call(kernel, out_shape=list(outs), in_specs=[SMEM] * len(scalar...  56.6 us
    ppermute x9, waiting for transfers between devices, shifted(): return lax.ppermute(value, axis, pairs)  22.7 us
    ppermute x9, starting transfers between devices, shifted(): return lax.ppermute(value, axis, pairs)  15.9 us
    ppermute x6, waiting for transfers between devices, traded(): lax.ppermute(value, axis, [(i, i ^ k) for i in range(lax.axis_size(axis))])  12 us
    unnamed x25, local copies, waits for them, and re-layouts  5.58 us
    pallas_call x1, Pallas kernels, mix(): pl.pallas_call(functools.partial(mix_kernel, places), grid=(nodes // step...  4.33 us
    ppermute x6, starting transfers between devices, traded(): lax.ppermute(value, axis, [(i, i ^ k) for i in range(lax.axis_size(axis))])  4.32 us
  transfers between devices with their start and end apart: 15, of which 7 were waited for; matrix products, arithmetic and copies ran while one was open for 0% of the time, Pallas kernels for 44%

profile of v2, /device:TPU:16, one launch (start us, length us, event | category | flops | bytes accessed | tf_op | source)
XLA Modules:
  0.0 121.7 jit_solution(16120944823425003713)
XLA Ops:
  0.0 0.4 collective-permute-start
  0.5 3.5 %collective-permute-start.1 = (s32[4,20]{1,0:T(4,128)}, s32[4,20]{1,0:T(4,128)S(1)}, u32[]{:S(2)}, u32[]{:S(2)}) collective-permute-start(s32[4,20]{1,0:T(4,128)} %bitcast.13), channel_id=1, source_target_pairs={{0,8},{4,12},{8,0},{12,4},{1,9},{5,13},{9,1},{13,5},{2,10},{6,14},... | collective-permute-start | bytes 968 | tf_op jit(solution)/shard_map/ppermute | solution.py:47
  3.9 0.0 collective-permute-start.2
  3.9 0.0 collective-permute-done.refs_0_
  3.9 1.8 %collective-permute-done.1.refs_1_ = s32[4,20]{1,0:T(4,128)S(1)} collective-permute-done((s32[4,20]{1,0:T(4,128)}, s32[4,20]{1,0:T(4,128)S(1)}, u32[]{:S(2)}, u32[]{:S(2)}) %collective-permute-start.1) | collective-permute-done | bytes 352 | tf_op jit(solution)/shard_map/ppermute | solution.py:47
  5.7 2.0 %collective-permute-done.2.refs_2_ = s32[4,20]{1,0:T(4,128)S(1)} collective-permute-done((s32[4,20]{1,0:T(4,128)}, s32[4,20]{1,0:T(4,128)S(1)}, u32[]{:S(2)}, u32[]{:S(2)}) %collective-permute-start.2) | collective-permute-done | bytes 352 | tf_op jit(solution)/shard_map/ppermute | solution.py:47
  7.7 1.6 %copy-done.1 = bf16[128,8192]{1,0:T(8,128)(2,1)S(1)} copy-done((bf16[128,8192]{1,0:T(8,128)(2,1)S(1)}, bf16[128,8192]{1,0:T(8,128)(2,1)}, u32[]{:S(2)}) %copy-start.1) | copy-done | bytes 2097176
  9.3 1.0 pack.2
  10.4 0.0 copy-start.6
  10.4 0.7 copy-done.6
  11.1 0.7 copy-done.7
  11.8 0.7 copy-done.8
  12.5 2.0 %pack.3 = (bf16[20,64,128]{2,1,0:T(8,128)(2,1)}, bf16[20,64,128]{2,1,0:T(8,128)(2,1)}, bf16[20,64,128]{2,1,0:T(8,128)(2,1)}) custom-call(s32[4,20]{1,0:T(4,128)S(1)} %collective-permute-done.refs_0_, s32[4,20]{1,0:T(4,128)S(1)} %collective-permute-done.1.refs_1_, s32[4,20]{1,0:T(4,128)S(1)} %collective-permute-done.2.refs_2_, bf16[128,8192]{1,0:T(8,128)(2,1)S(1)} %copy-done.1), custom_call_target="tpu_custom_call" | custom-call | bytes 3080192 | tf_op jit(solution)/shard_map/pack/pallas_call | solution.py:31
  14.5 1.8 %collective-permute-start.10 = (bf16[20,64,128]{2,1,0:T(8,128)(2,1)}, bf16[20,64,128]{2,1,0:T(8,128)(2,1)S(1)}, u32[]{:S(2)}, u32[]{:S(2)}) collective-permute-start(bf16[20,64,128]{2,1,0:T(8,128)(2,1)} %get-tuple-element.42), channel_id=1, source_target_pairs={{0,8},{4,12},{8,0},{12,4},{1,9},{5,13},{9,1},{13,5},{2,10},{6,14},... | collective-permute-start | bytes 983048 | tf_op jit(solution)/shard_map/ppermute | solution.py:47
  16.3 0.0 collective-permute-start.11
  16.3 2.0 %collective-permute-start.9 = (bf16[20,64,128]{2,1,0:T(8,128)(2,1)}, bf16[20,64,128]{2,1,0:T(8,128)(2,1)}, u32[]{:S(2)}, u32[]{:S(2)}) collective-permute-start(bf16[20,64,128]{2,1,0:T(8,128)(2,1)} %get-tuple-element.41), channel_id=1, source_target_pairs={{0,4},{4,8},{8,12},{12,0},{1,5},{5,9},{9,13},{13,1},{2,6},{6,10},{... | collective-permute-start | bytes 983048 | tf_op jit(solution)/shard_map/ppermute | solution.py:47
  18.3 1.2 collective-permute-start.3
  19.5 0.3 collective-permute-start.4
  19.8 10.8 %collective-permute-done.10.refs_1_ = bf16[20,64,128]{2,1,0:T(8,128)(2,1)S(1)} collective-permute-done((bf16[20,64,128]{2,1,0:T(8,128)(2,1)}, bf16[20,64,128]{2,1,0:T(8,128)(2,1)S(1)}, u32[]{:S(2)}, u32[]{:S(2)}) %collective-permute-start.10) | collective-permute-done | bytes 327712 | tf_op jit(solution)/shard_map/ppermute | solution.py:47
  30.5 6.7 %collective-permute-start.5 = (bf16[20,64,128]{2,1,0:T(8,128)(2,1)}, bf16[20,64,128]{2,1,0:T(8,128)(2,1)S(1)}, u32[]{:S(2)}, u32[]{:S(2)}) collective-permute-start(bf16[20,64,128]{2,1,0:T(8,128)(2,1)} %copy-done.6), channel_id=1, source_target_pairs={{0,12},{4,0},{8,4},{12,8},{1,13},{5,1},{9,5},{13,9},{2,14},{6,2},{... | collective-permute-start | bytes 983048 | tf_op jit(solution)/shard_map/ppermute | solution.py:47
  37.2 0.0 copy-done.4
  37.3 0.0 copy-start.2
  37.3 1.6 %copy-done.2 = bf16[128,8192]{1,0:T(8,128)(2,1)S(1)} copy-done((bf16[128,8192]{1,0:T(8,128)(2,1)S(1)}, bf16[128,8192]{1,0:T(8,128)(2,1)}, u32[]{:S(2)}) %copy-start.2) | copy-done | bytes 2097176
  38.9 11.7 %own.1 = (f32[8192,64]{1,0:T(8,128)S(1)}, f32[8192,64]{1,0:T(8,128)S(1)}, f32[8192,64]{1,0:T(8,128)S(1)}) custom-call(s32[4,20]{1,0:T(4,128)S(1)} %bitcast.9, s32[4,20]{1,0:T(4,128)S(1)} %bitcast.15, bf16[128,8192]{1,0:T(8,128)(2,1)S(1)} %copy-done.2, bf16[80,128,128]{2,1,0:T(8,128)(2,1)S(1)} %bitcast.5), custom_call_target="tpu_custom_call" | custom-call | bytes 18612224 | tf_op jit(solution)/shard_map/own/pallas_call | solution.py:31
  50.6 5.6 %collective-permute-done.11.refs_2_ = bf16[20,64,128]{2,1,0:T(8,128)(2,1)S(1)} collective-permute-done((bf16[20,64,128]{2,1,0:T(8,128)(2,1)}, bf16[20,64,128]{2,1,0:T(8,128)(2,1)S(1)}, u32[]{:S(2)}, u32[]{:S(2)}) %collective-permute-start.11) | collective-permute-done | bytes 327712 | tf_op jit(solution)/shard_map/ppermute | solution.py:47
  56.3 2.5 %collective-permute-done.9.refs_0_ = bf16[20,64,128]{2,1,0:T(8,128)(2,1)} collective-permute-done((bf16[20,64,128]{2,1,0:T(8,128)(2,1)}, bf16[20,64,128]{2,1,0:T(8,128)(2,1)}, u32[]{:S(2)}, u32[]{:S(2)}) %collective-permute-start.9) | collective-permute-done | bytes 327712 | tf_op jit(solution)/shard_map/ppermute | solution.py:47
  58.8 13.0 %gather_far.3 = (f32[8192,64]{1,0:T(8,128)S(1)}, bf16[64,2048]{1,0:T(8,128)(2,1)}, bf16[64,2048]{1,0:T(8,128)(2,1)}) custom-call(s32[4]{0:T(128)S(1)} %get-tuple-element.49.bases, s32[4,20]{1,0:T(4,128)S(1)} %bitcast.10, s32[8192]{0:T(1024)S(1)} %copy-done.3, f32[8192,64]{1,0:T(8,128)S(1)} %get-tuple-element.37.acc, ...), custom_call_target="tpu_custom_call" | custom-call | bytes 18153472 | tf_op jit(solution)/shard_map/gather_far/pallas_call | solution.py:31
  71.7 8.0 %gather_near.3 = (bf16[64,2048]{1,0:T(8,128)(2,1)S(1)}, bf16[64,2048]{1,0:T(8,128)(2,1)S(1)}) custom-call(s32[4]{0:T(128)S(1)} %get-tuple-element.49.bases, s32[8192]{0:T(1024)S(1)} %copy-done.3, f32[8192,64]{1,0:T(8,128)S(1)} %get-tuple-element.46.total), custom_call_target="tpu_custom_call" | custom-call | bytes 4849664 | tf_op jit(solution)/shard_map/gather_near/pallas_call | solution.py:31
  79.7 0.0 collective-permute-start.14
  79.8 1.6 %collective-permute-start.12 = (bf16[64,2048]{1,0:T(8,128)(2,1)}, bf16[64,2048]{1,0:T(8,128)(2,1)S(1)}, u32[]{:S(2)}, u32[]{:S(2)}) collective-permute-start(bf16[64,2048]{1,0:T(8,128)(2,1)} %get-tuple-element.44), channel_id=1, source_target_pairs={{0,3},{1,2},{2,1},{3,0},{4,7},{5,6},{6,5},{7,4},{8,11},{9,10},{10,... | collective-permute-start | bytes 786440 | tf_op jit(solution)/shard_map/ppermute | solution.py:51
  81.4 0.0 collective-permute-done.3.refs_0_
  81.4 0.5 collective-permute-start.13
  81.9 0.0 collective-permute-done.4.refs_1_
  81.9 0.0 collective-permute-done.5.refs_2_
  81.9 12.9 %gather_far.2 = (f32[8192,64]{1,0:T(8,128)S(1)}, bf16[64,2048]{1,0:T(8,128)(2,1)}, bf16[64,2048]{1,0:T(8,128)(2,1)}) custom-call(s32[4]{0:T(128)S(1)} %get-tuple-element.49.bases, s32[4,20]{1,0:T(4,128)S(1)} %bitcast.11, s32[8192]{0:T(1024)S(1)} %copy-done.3, f32[8192,64]{1,0:T(8,128)S(1)} %get-tuple-element.27.acc, ...), custom_call_target="tpu_custom_call" | custom-call | bytes 18153472 | tf_op jit(solution)/shard_map/gather_far/pallas_call | solution.py:31
  94.9 8.0 %gather_near.2 = (bf16[64,2048]{1,0:T(8,128)(2,1)S(1)}, bf16[64,2048]{1,0:T(8,128)(2,1)S(1)}) custom-call(s32[4]{0:T(128)S(1)} %get-tuple-element.49.bases, s32[8192]{0:T(1024)S(1)} %copy-done.3, f32[8192,64]{1,0:T(8,128)S(1)} %get-tuple-element.34.total), custom_call_target="tpu_custom_call" | custom-call | bytes 4849664 | tf_op jit(solution)/shard_map/gather_near/pallas_call | solution.py:31
  102.9 0.0 collective-permute-start.8
  102.9 1.6 %collective-permute-start.6 = (bf16[64,2048]{1,0:T(8,128)(2,1)}, bf16[64,2048]{1,0:T(8,128)(2,1)S(1)}, u32[]{:S(2)}, u32[]{:S(2)}) collective-permute-start(bf16[64,2048]{1,0:T(8,128)(2,1)} %get-tuple-element.32), channel_id=1, source_target_pairs={{0,3},{1,2},{2,1},{3,0},{4,7},{5,6},{6,5},{7,4},{8,11},{9,10},{10,... | collective-permute-start | bytes 786440 | tf_op jit(solution)/shard_map/ppermute | solution.py:51
  104.5 0.0 collective-permute-done.14.refs_6_
  104.5 0.5 collective-permute-start.7
  105.0 0.2 copy.10
  105.3 0.1 copy.11.bias
  105.4 0.0 collective-permute-done.12.refs_4_
  105.4 0.0 collective-permute-done.13.refs_5_
  105.4 0.0 collective-permute-done.8.refs_2_
  105.5 6.0 %collective-permute-done.6.refs_0_ = bf16[64,2048]{1,0:T(8,128)(2,1)S(1)} collective-permute-done((bf16[64,2048]{1,0:T(8,128)(2,1)}, bf16[64,2048]{1,0:T(8,128)(2,1)S(1)}, u32[]{:S(2)}, u32[]{:S(2)}) %collective-permute-start.6) | collective-permute-done | bytes 262176 | tf_op jit(solution)/shard_map/ppermute | solution.py:51
  111.5 5.9 %collective-permute-done.7.refs_1_ = bf16[64,2048]{1,0:T(8,128)(2,1)S(1)} collective-permute-done((bf16[64,2048]{1,0:T(8,128)(2,1)}, bf16[64,2048]{1,0:T(8,128)(2,1)S(1)}, u32[]{:S(2)}, u32[]{:S(2)}) %collective-permute-start.7) | collective-permute-done | bytes 262176 | tf_op jit(solution)/shard_map/ppermute | solution.py:51
  117.4 4.3 %mix.1 = bf16[512,2048]{1,0:T(8,128)(2,1)} custom-call(s32[4]{0:T(128)S(1)} %get-tuple-element.50.starts, bf16[512,512]{1,0:T(8,128)(2,1)S(1)} %bitcast.8, f32[512,1]{1,0:T(8,128)S(1)} %copy.11.bias, bf16[64,2048]{1,0:T(8,128)(2,1)S(1)} %collective-permute-done.6.refs_0_, bf16[64,2048]{1,0:T(8,128)(2,1)S(1)} %collective-permute-done.7.refs_1_, ...), custom_call_target="tpu_custom_call" | custom-call | flops 1073741824 | bytes 5242880 | tf_op jit(solution)/shard_map/mix/pallas_call | solution.py:257
  (17 shorter events, 0.0 us)
Async XLA Ops:
  0.0 37.2 %copy-start = (bf16[1,4,20,128,128]{4,3,2,1,0:T(8,128)(2,1)S(1)}, bf16[1,4,20,128,128]{4,3,2,1,0:T(8,128)(2,1)}, u32[]{:S(2)}) copy-start(bf16[1,4,20,128,128]{4,3,2,1,0:T(8,128)(2,1)} %param.11) | copy-start | bytes 7864324
  0.0 3.9 %collective-permute-start = (s32[4,20]{1,0:T(4,128)}, s32[4,20]{1,0:T(4,128)S(1)}, u32[]{:S(2)}, u32[]{:S(2)}) collective-permute-start(s32[4,20]{1,0:T(4,128)} %bitcast.12), channel_id=1, source_target_pairs={{0,12},{4,0},{8,4},{12,8},{1,13},{5,1},{9,5},{13,9},{2,14},{6,2},{... | collective-permute-start | bytes 968 | tf_op jit(solution)/shard_map/ppermute | solution.py:47
  0.5 5.3 %collective-permute-start.1 = (s32[4,20]{1,0:T(4,128)}, s32[4,20]{1,0:T(4,128)S(1)}, u32[]{:S(2)}, u32[]{:S(2)}) collective-permute-start(s32[4,20]{1,0:T(4,128)} %bitcast.13), channel_id=1, source_target_pairs={{0,8},{4,12},{8,0},{12,4},{1,9},{5,13},{9,1},{13,5},{2,10},{6,14},... | collective-permute-start | bytes 968 | tf_op jit(solution)/shard_map/ppermute | solution.py:47
  3.9 3.8 %collective-permute-start.2 = (s32[4,20]{1,0:T(4,128)}, s32[4,20]{1,0:T(4,128)S(1)}, u32[]{:S(2)}, u32[]{:S(2)}) collective-permute-start(s32[4,20]{1,0:T(4,128)} %bitcast.14), channel_id=1, source_target_pairs={{0,4},{4,8},{8,12},{12,0},{1,5},{5,9},{9,13},{13,1},{2,6},{6,10},{... | collective-permute-start | bytes 968 | tf_op jit(solution)/shard_map/ppermute | solution.py:47
  7.7 1.6 %copy-start.1 = (bf16[128,8192]{1,0:T(8,128)(2,1)S(1)}, bf16[128,8192]{1,0:T(8,128)(2,1)}, u32[]{:S(2)}) copy-start(bf16[128,8192]{1,0:T(8,128)(2,1)} %refs_3_.3) | copy-start | bytes 6291460
  9.3 27.9 %copy-start.11 = (s32[4]{0:T(128)S(1)}, s32[4]{0:T(128)}, u32[]{:S(2)}) copy-start(s32[4]{0:T(128)} %constant.10.clone) | copy-start | bytes 52
  9.3 27.9 %copy-start.4 = (s32[1,4,20]{2,1,0:T(4,128)S(1)}, s32[1,4,20]{2,1,0:T(4,128)}, u32[]{:S(2)}) copy-start(s32[1,4,20]{2,1,0:T(4,128)} %param.9) | copy-start | bytes 964
  9.3 27.9 %copy-start.5 = (s32[1,4,20]{2,1,0:T(4,128)S(1)}, s32[1,4,20]{2,1,0:T(4,128)}, u32[]{:S(2)}) copy-start(s32[1,4,20]{2,1,0:T(4,128)} %param.10) | copy-start | bytes 964
  9.3 49.4 %copy-start.3 = (s32[8192]{0:T(1024)S(1)}, s32[8192]{0:T(1024)}, u32[]{:S(2)}) copy-start(s32[8192]{0:T(1024)} %order.7) | copy-start | bytes 98308
  10.4 0.7 copy-start.6
  11.1 0.7 copy-start.7
  11.8 0.7 copy-start.8
  14.5 16.1 %collective-permute-start.10 = (bf16[20,64,128]{2,1,0:T(8,128)(2,1)}, bf16[20,64,128]{2,1,0:T(8,128)(2,1)S(1)}, u32[]{:S(2)}, u32[]{:S(2)}) collective-permute-start(bf16[20,64,128]{2,1,0:T(8,128)(2,1)} %get-tuple-element.42), channel_id=1, source_target_pairs={{0,8},{4,12},{8,0},{12,4},{1,9},{5,13},{9,1},{13,5},{2,10},{6,14},... | collective-permute-start | bytes 983048 | tf_op jit(solution)/shard_map/ppermute | solution.py:47
  16.3 40.0 %collective-permute-start.11 = (bf16[20,64,128]{2,1,0:T(8,128)(2,1)}, bf16[20,64,128]{2,1,0:T(8,128)(2,1)S(1)}, u32[]{:S(2)}, u32[]{:S(2)}) collective-permute-start(bf16[20,64,128]{2,1,0:T(8,128)(2,1)} %get-tuple-element.43), channel_id=1, source_target_pairs={{0,12},{4,0},{8,4},{12,8},{1,13},{5,1},{9,5},{13,9},{2,14},{6,2},{... | collective-permute-start | bytes 983048 | tf_op jit(solution)/shard_map/ppermute | solution.py:47
  16.3 42.5 %collective-permute-start.9 = (bf16[20,64,128]{2,1,0:T(8,128)(2,1)}, bf16[20,64,128]{2,1,0:T(8,128)(2,1)}, u32[]{:S(2)}, u32[]{:S(2)}) collective-permute-start(bf16[20,64,128]{2,1,0:T(8,128)(2,1)} %get-tuple-element.41), channel_id=1, source_target_pairs={{0,4},{4,8},{8,12},{12,0},{1,5},{5,9},{9,13},{13,1},{2,6},{6,10},{... | collective-permute-start | bytes 983048 | tf_op jit(solution)/shard_map/ppermute | solution.py:47
  18.3 63.1 %collective-permute-start.3 = (bf16[20,64,128]{2,1,0:T(8,128)(2,1)}, bf16[20,64,128]{2,1,0:T(8,128)(2,1)S(1)}, u32[]{:S(2)}, u32[]{:S(2)}) collective-permute-start(bf16[20,64,128]{2,1,0:T(8,128)(2,1)} %copy-done.8), channel_id=1, source_target_pairs={{0,4},{4,8},{8,12},{12,0},{1,5},{5,9},{9,13},{13,1},{2,6},{6,10},{... | collective-permute-start | bytes 983048 | tf_op jit(solution)/shard_map/ppermute | solution.py:47
  19.5 62.4 %collective-permute-start.4 = (bf16[20,64,128]{2,1,0:T(8,128)(2,1)}, bf16[20,64,128]{2,1,0:T(8,128)(2,1)S(1)}, u32[]{:S(2)}, u32[]{:S(2)}) collective-permute-start(bf16[20,64,128]{2,1,0:T(8,128)(2,1)} %copy-done.7), channel_id=1, source_target_pairs={{0,8},{4,12},{8,0},{12,4},{1,9},{5,13},{9,1},{13,5},{2,10},{6,14},... | collective-permute-start | bytes 983048 | tf_op jit(solution)/shard_map/ppermute | solution.py:47
  30.5 51.4 %collective-permute-start.5 = (bf16[20,64,128]{2,1,0:T(8,128)(2,1)}, bf16[20,64,128]{2,1,0:T(8,128)(2,1)S(1)}, u32[]{:S(2)}, u32[]{:S(2)}) collective-permute-start(bf16[20,64,128]{2,1,0:T(8,128)(2,1)} %copy-done.6), channel_id=1, source_target_pairs={{0,12},{4,0},{8,4},{12,8},{1,13},{5,1},{9,5},{13,9},{2,14},{6,2},{... | collective-permute-start | bytes 983048 | tf_op jit(solution)/shard_map/ppermute | solution.py:47
  37.3 1.6 %copy-start.2 = (bf16[128,8192]{1,0:T(8,128)(2,1)S(1)}, bf16[128,8192]{1,0:T(8,128)(2,1)}, u32[]{:S(2)}) copy-start(bf16[128,8192]{1,0:T(8,128)(2,1)} %refs_3_.3) | copy-start | bytes 6291460
  79.7 24.8 %collective-permute-start.14 = (bf16[64,2048]{1,0:T(8,128)(2,1)S(1)}, bf16[64,2048]{1,0:T(8,128)(2,1)S(1)}, u32[]{:S(2)}, u32[]{:S(2)}) collective-permute-start(bf16[64,2048]{1,0:T(8,128)(2,1)S(1)} %get-tuple-element.47), channel_id=1, source_target_pairs={{0,1},{1,0},{2,3},{3,2},{4,5},{5,4},{6,7},{7,6},{8,9},{9,8},{10,11... | collective-permute-start | bytes 786440 | tf_op jit(solution)/shard_map/ppermute | solution.py:51
  79.8 25.6 %collective-permute-start.12 = (bf16[64,2048]{1,0:T(8,128)(2,1)}, bf16[64,2048]{1,0:T(8,128)(2,1)S(1)}, u32[]{:S(2)}, u32[]{:S(2)}) collective-permute-start(bf16[64,2048]{1,0:T(8,128)(2,1)} %get-tuple-element.44), channel_id=1, source_target_pairs={{0,3},{1,2},{2,1},{3,0},{4,7},{5,6},{6,5},{7,4},{8,11},{9,10},{10,... | collective-permute-start | bytes 786440 | tf_op jit(solution)/shard_map/ppermute | solution.py:51
  81.4 24.1 %collective-permute-start.13 = (bf16[64,2048]{1,0:T(8,128)(2,1)}, bf16[64,2048]{1,0:T(8,128)(2,1)}, u32[]{:S(2)}, u32[]{:S(2)}) collective-permute-start(bf16[64,2048]{1,0:T(8,128)(2,1)} %get-tuple-element.45), channel_id=1, source_target_pairs={{0,2},{1,3},{2,0},{3,1},{4,6},{5,7},{6,4},{7,5},{8,10},{9,11},{10,... | collective-permute-start | bytes 786440 | tf_op jit(solution)/shard_map/ppermute | solution.py:51
  94.9 10.2 %copy-start.9 = (bf16[512,512]{1,0:T(8,128)(2,1)S(1)}, bf16[512,512]{1,0:T(8,128)(2,1)}, u32[]{:S(2)}) copy-start(bf16[512,512]{1,0:T(8,128)(2,1)} %param.13) | copy-start | bytes 1572868
  94.9 10.4 %copy-start.10 = (f32[512]{0:T(512)S(1)}, f32[512]{0:T(512)}, u32[]{:S(2)}) copy-start(f32[512]{0:T(512)} %param.14) | copy-start | bytes 6148
  102.9 2.6 %collective-permute-start.8 = (bf16[64,2048]{1,0:T(8,128)(2,1)S(1)}, bf16[64,2048]{1,0:T(8,128)(2,1)S(1)}, u32[]{:S(2)}, u32[]{:S(2)}) collective-permute-start(bf16[64,2048]{1,0:T(8,128)(2,1)S(1)} %get-tuple-element.35), channel_id=1, source_target_pairs={{0,1},{1,0},{2,3},{3,2},{4,5},{5,4},{6,7},{7,6},{8,9},{9,8},{10,11... | collective-permute-start | bytes 786440 | tf_op jit(solution)/shard_map/ppermute | solution.py:51
  102.9 8.6 %collective-permute-start.6 = (bf16[64,2048]{1,0:T(8,128)(2,1)}, bf16[64,2048]{1,0:T(8,128)(2,1)S(1)}, u32[]{:S(2)}, u32[]{:S(2)}) collective-permute-start(bf16[64,2048]{1,0:T(8,128)(2,1)} %get-tuple-element.32), channel_id=1, source_target_pairs={{0,3},{1,2},{2,1},{3,0},{4,7},{5,6},{6,5},{7,4},{8,11},{9,10},{10,... | collective-permute-start | bytes 786440 | tf_op jit(solution)/shard_map/ppermute | solution.py:51
  104.5 12.9 %collective-permute-start.7 = (bf16[64,2048]{1,0:T(8,128)(2,1)}, bf16[64,2048]{1,0:T(8,128)(2,1)S(1)}, u32[]{:S(2)}, u32[]{:S(2)}) collective-permute-start(bf16[64,2048]{1,0:T(8,128)(2,1)} %get-tuple-element.33), channel_id=1, source_target_pairs={{0,2},{1,3},{2,0},{3,1},{4,6},{5,7},{6,4},{7,5},{8,10},{9,11},{10,... | collective-permute-start | bytes 786440 | tf_op jit(solution)/shard_map/ppermute | solution.py:51

commit v3 on v2

v3 whole, which is shorter than its diff:
```python
import functools

import jax
import jax.numpy as jnp
from jax import lax
from jax.experimental import pallas as pl
from jax.experimental.pallas import tpu as pltpu
from jax.sharding import PartitionSpec as P

NN = (((1,), (0,)), ((), ()))
NT = (((1,), (1,)), ((), ()))
VMEM = pl.BlockSpec(memory_space=pltpu.VMEM)
SMEM = pl.BlockSpec(memory_space=pltpu.SMEM)
CHUNK = 256
UNROLL = 64


def dot(a, b, dims):
    return lax.dot_general(a, b, dims, preferred_element_type=jnp.float32)


def padded(shape, dtype):
    rows = 1
    for extent in shape[:-1]:
        rows *= extent
    return rows * -(-shape[-1] // 128) * 128 * jnp.dtype(dtype).itemsize


def call(kernel, name, scalars, arrays, outs, scratch=(), moved=2**16):
    held = sum(padded(a.shape, a.dtype) for a in list(arrays) + list(outs))
    held += sum(padded(shape, dtype) for shape, dtype in scratch)
    return pl.pallas_call(
        kernel,
        out_shape=list(outs),
        in_specs=[SMEM] * len(scalars) + [VMEM] * len(arrays),
        out_specs=[VMEM] * len(outs),
        scratch_shapes=[pltpu.VMEM(shape, dtype) for shape, dtype in scratch],
        compiler_params=pltpu.CompilerParams(vmem_limit_bytes=held + 4 * 2**20),
        cost_estimate=pl.CostEstimate(flops=0, bytes_accessed=moved, transcendentals=0),
        name=name,
    )(*scalars, *arrays)


def shifted(value, axis, steps):
    count = lax.axis_size(axis)
    pairs = [(source, (source + steps) % count) for source in range(count)]
    return lax.ppermute(value, axis, pairs)


def traded(value, axis, k):
    return lax.ppermute(value, axis, [(i, i ^ k) for i in range(lax.axis_size(axis))])


def cuts(width):
    first = width // 2
    return ((0, first), (first, width - first))


def identity(size):
    row = lax.broadcasted_iota(jnp.int32, (size, size), 0)
    col = lax.broadcasted_iota(jnp.int32, (size, size), 1)
    return (row == col).astype(jnp.float32).astype(jnp.bfloat16)


def pack_kernel(low, size, offsets, slots, tile, *refs):
    asked, panel, outs = refs[:offsets], refs[offsets], refs[offsets + 1 :]
    for s in range(offsets):

        def body(t, carry, s=s):
            at = pl.multiple_of(asked[s][s + 1, t] * tile, tile)
            outs[s][t] = panel[pl.ds(low, size), pl.ds(at, tile)]
            return carry

        lax.fori_loop(0, slots, body, 0, unroll=4)


def pack(panel, asked, low, size, tile):
    offsets, slots = len(asked), asked[0].shape[1]
    shape = jax.ShapeDtypeStruct((slots, size, tile), panel.dtype)
    return call(
        functools.partial(pack_kernel, low, size, offsets, slots, tile),
        "pack",
        asked,
        [panel],
        [shape] * offsets,
    )


def degree_kernel(blocks, slots, tile, rows, counts, inverse, product):
    lanes = inverse.shape[1]
    row_tiles = inverse.shape[0] // tile
    ones = jnp.ones((tile, lanes), jnp.bfloat16)
    inverse[...] = jnp.ones(inverse.shape, jnp.float32)

    def block(s, carry):
        def multiply(t, inner):
            product[t] = dot(counts[s * slots + t], ones, NN)
            return inner

        def add(t, inner):
            at = pl.multiple_of(rows[s, t] * tile, tile)
            inverse[pl.ds(at, tile), :] += product[t]
            return inner

        lax.fori_loop(0, slots, multiply, 0, unroll=10)
        lax.fori_loop(0, slots, add, 0)
        return carry

    lax.fori_loop(0, blocks, block, 0)

    def invert(r, carry):
        at = pl.multiple_of(r * tile, tile)
        inverse[pl.ds(at, tile), :] = 1.0 / inverse[pl.ds(at, tile), :]
        return carry

    lax.fori_loop(0, row_tiles, invert, 0, unroll=2)


def degrees(rows, counts, nodes, lanes):
    blocks, slots = rows.shape
    tile = counts.shape[-1]
    return call(
        functools.partial(degree_kernel, blocks, slots, tile),
        "degrees",
        [rows],
        [counts],
        [jax.ShapeDtypeStruct((nodes, lanes), jnp.float32)],
        [((slots, tile, lanes), jnp.float32)],
    )[0]


def own_kernel(ranges, slots, tile, rows, cols, panel, counts, inverse, *refs):
    accs, product = refs[:-1], refs[-1]
    row_tiles = panel.shape[1] // tile
    eye = identity(tile)

    def start(r, carry):
        at = pl.multiple_of(r * tile, tile)
        for acc, (low, size) in zip(accs, ranges):
            here = dot(eye, panel[pl.ds(low, size), pl.ds(at, tile)], NT)
            acc[pl.ds(at, tile), :] = here * inverse[pl.ds(at, tile), :size]
        return carry

    lax.fori_loop(0, row_tiles, start, 0, unroll=4)

    for acc, (low, size) in zip(accs, ranges):

        def multiply(t, carry, low=low, size=size):
            col = pl.multiple_of(cols[0, t] * tile, tile)
            product[t, :, :size] = dot(counts[t], panel[pl.ds(low, size), pl.ds(col, tile)], NT)
            return carry

        def add(t, carry, acc=acc, size=size):
            at = pl.multiple_of(rows[0, t] * tile, tile)
            acc[pl.ds(at, tile), :] += product[t, :, :size] * inverse[pl.ds(at, tile), :size]
            return carry

        lax.fori_loop(0, slots, multiply, 0, unroll=10)
        lax.fori_loop(0, slots, add, 0)


def own(panel, rows, cols, counts, inverse, ranges):
    slots = rows.shape[1]
    nodes, tile = panel.shape[1], counts.shape[-1]
    lanes = max(size for _, size in ranges)
    return call(
        functools.partial(own_kernel, ranges, slots, tile),
        "own",
        [rows, cols],
        [panel, counts, inverse],
        [jax.ShapeDtypeStruct((nodes, size), jnp.float32) for _, size in ranges],
        [((slots, tile, lanes), jnp.float32)],
    )


def pick(order, base, nodes, stage, outs):
    count, size = stage.shape
    eye = identity(size)

    def group(i, carry):
        at = pl.multiple_of(i * UNROLL, UNROLL)
        for u in range(UNROLL):
            source = order[base + at + u]
            stage[pl.ds(at + u, 1), :] = nodes[pl.ds(source, 1), :]
        return carry

    lax.fori_loop(0, count // UNROLL, group, 0)

    def turn(c, carry):
        at = pl.multiple_of(c * CHUNK, CHUNK)
        turned = dot(eye, stage[pl.ds(at, CHUNK), :].astype(jnp.bfloat16), NT)
        low = 0
        for out in outs:
            out[:, pl.ds(at, CHUNK)] = turned[low : low + out.shape[0]].astype(out.dtype)
            low += out.shape[0]
        return carry

    lax.fori_loop(0, count // CHUNK, turn, 0, unroll=4)


def far_kernel(offsets, slots, tile, bases, rows, order, acc, inverse, counts, *refs):
    got, total, outs = refs[:offsets], refs[offsets], refs[offsets + 1 : -2]
    product, stage = refs[-2:]
    size = acc.shape[1]
    total[...] = acc[...]
    for s in range(offsets):

        def multiply(t, carry, s=s):
            product[t] = dot(counts[(s + 1) * slots + t], got[s][t], NT)
            return carry

        def add(t, carry, s=s):
            at = pl.multiple_of(rows[s + 1, t] * tile, tile)
            total[pl.ds(at, tile), :] += product[t] * inverse[pl.ds(at, tile), :size]
            return carry

        lax.fori_loop(0, slots, multiply, 0, unroll=10)
        lax.fori_loop(0, slots, add, 0)

    for i, out in enumerate(outs):
        pick(order, bases[i], total, stage, [out])


def gather_far(acc, inverse, bases, rows, order, counts, got, share, ranks):
    nodes, size = acc.shape
    slots, tile = rows.shape[1], counts.shape[-1]
    piece = jax.ShapeDtypeStruct((size, share), jnp.bfloat16)
    outs = call(
        functools.partial(far_kernel, len(got), slots, tile),
        "gather_far",
        [bases, rows, order],
        [acc, inverse, counts, *got],
        [jax.ShapeDtypeStruct((nodes, size), jnp.float32)] + [piece] * ranks,
        [((slots, tile, size), jnp.float32), ((share, size), jnp.float32)],
    )
    return outs[0], outs[1:]


def near_kernel(rank, bases, order, total, *refs):
    pick(order, bases[rank], total, refs[-1], refs[:-1])


def gather_near(total, bases, order, share, rank, heights, moved):
    return call(
        functools.partial(near_kernel, rank),
        "gather_near",
        [bases, order],
        [total],
        [jax.ShapeDtypeStruct((height, share), jnp.bfloat16) for height in heights],
        [((share, total.shape[1]), jnp.float32)],
        moved,
    )


def mix_kernel(places, starts, weight, bias, *refs):
    pieces, out, nodes = refs[:-2], refs[-2], refs[-1]
    for piece, (i, low) in zip(pieces, places):
        at = pl.multiple_of(starts[i] + low, 16)
        nodes[pl.ds(at, piece.shape[0]), :] = piece[...]
    mixed = dot(weight[...], nodes[...], NN)
    out[...] = jnp.maximum(mixed + bias[...], 0.0).astype(out.dtype)


def mix(starts, weight, bias, placed):
    places, pieces = tuple(placed), list(placed.values())
    hidden, width = weight.shape
    nodes = pieces[0].shape[1]
    step = min(512, nodes)
    return pl.pallas_call(
        functools.partial(mix_kernel, places),
        grid=(nodes // step,),
        out_shape=jax.ShapeDtypeStruct((hidden, nodes), jnp.bfloat16),
        in_specs=[
            SMEM,
            pl.BlockSpec(weight.shape, lambda i: (0, 0)),
            pl.BlockSpec(bias.shape, lambda i: (0, 0)),
        ]
        + [pl.BlockSpec((piece.shape[0], step), lambda i: (0, i)) for piece in pieces],
        out_specs=pl.BlockSpec((hidden, step), lambda i: (0, i)),
        scratch_shapes=[pltpu.VMEM((width, step), jnp.bfloat16)],
        compiler_params=pltpu.CompilerParams(vmem_limit_bytes=16 * 2**20),
        cost_estimate=pl.CostEstimate(
            flops=2 * hidden * width * nodes, bytes_accessed=5 * 2**20, transcendentals=0
        ),
        name="mix",
    )(starts, weight, bias, *pieces)


def on_device(features, tile_rows, tile_cols, tile_weights, order, weight, bias):
    width, nodes = features.shape
    _, blocks, slots, tile, _ = tile_weights.shape
    groups = lax.axis_size("grp")
    me = lax.axis_index("grp")
    share = nodes // groups
    ranges = cuts(width)
    rows = tile_rows.reshape(blocks, slots)
    cols = tile_cols.reshape(blocks, slots)
    counts = tile_weights.reshape(blocks * slots, tile, tile)

    ranks = list(range(groups - 1, -1, -1))
    whose = me ^ jnp.asarray(ranks, jnp.int32)
    bases = whose * share
    far = groups - 2

    asked = [shifted(cols, "blk", -s) for s in range(1, blocks)]
    inverse = degrees(rows, counts, nodes, max(size for _, size in ranges))
    *asked, inverse = lax.optimization_barrier((*asked, inverse))
    sent = []
    for low, size in ranges:
        sent.append(list(pack(features, asked, low, size, tile)))
        *asked, sent[-1][0] = lax.optimization_barrier((*asked, sent[-1][0]))
    accs = list(own(features, rows, cols, counts, inverse, ranges))

    got = [[shifted(value, "blk", s + 1) for s, value in enumerate(sent[0])]]
    for later in sent[1:]:
        tied = [lax.optimization_barrier((a, b, accs)) for a, b in zip(later, got[-1])]
        got[-1] = [b for _, b, _ in tied]
        got.append([shifted(a, "blk", s + 1) for s, (a, _, _) in enumerate(tied)])

    pieces, waits = {}, {}
    for p, (low, size) in enumerate(ranges):
        last = p == len(ranges) - 1
        acc, waits = lax.optimization_barrier((accs[p], waits))
        pieces.update(waits)
        total, out_far = gather_far(
            acc, inverse, bases, rows, order, counts, got[p], share, far
        )
        waits = {
            (i, low): traded(piece, "grp", ranks[i]) for i, piece in enumerate(out_far)
        }
        waits[far + 1, low] = gather_near(
            total, bases, order, share, far + 1, (size,), 2**16
        )[0]
        half = size // 32 * 16
        heights = (half, size - half) if last else (size,)
        moved = 2**24 if last else 2**16
        for piece in gather_near(total, bases, order, share, far, heights, moved):
            pieces[far, low] = traded(piece, "grp", 1)
            low += piece.shape[0]
    pieces.update(waits)
    return mix(whose * width, weight.T, bias[:, None], pieces)


def solution(mesh):
    in_specs = (
        P("grp", ("parts", "blk")),
        P(("parts", "blk"), None, None),
        P(("parts", "blk"), None, None),
        P(("parts", "blk"), None, None, None, None),
        P(("parts", "blk")),
        P(),
        P(),
    )
    out_specs = P(None, ("parts", "blk", "grp"))
    return jax.shard_map(
        on_device, mesh=mesh, in_specs=in_specs, out_specs=out_specs, check_vma=False
    )
```

time: 122 us -> 107 us (0.88)
  the two profiles are of different devices: /device:TPU:16 before, /device:TPU:0 now
where the time goes in v3:
time: 107 us; the launch traced here: 106 us
  Pallas kernels  48.1 us (45%)
  waiting for transfers between devices  27.5 us (26%)
  starting transfers between devices  17.7 us (17%)
  local copies, waits for them, and re-layouts  12.7 us (12%)
    pallas_call x10, Pallas kernels, call(): pl.pallas_call(kernel, out_shape=list(outs), in_specs=[SMEM] * len(scalar...  43.8 us
    ppermute x9, waiting for transfers between devices, shifted(): return lax.ppermute(value, axis, pairs)  21.2 us
    ppermute x9, starting transfers between devices, shifted(): return lax.ppermute(value, axis, pairs)  13.6 us
    unnamed x33, local copies, waits for them, and re-layouts  12.5 us
    ppermute x7, waiting for transfers between devices, traded(): lax.ppermute(value, axis, [(i, i ^ k) for i in range(lax.axis_size(axis))])  6.37 us
    pallas_call x1, Pallas kernels, mix(): pl.pallas_call(functools.partial(mix_kernel, places), grid=(nodes // step...  4.25 us
    ppermute x7, starting transfers between devices, traded(): lax.ppermute(value, axis, [(i, i ^ k) for i in range(lax.axis_size(axis))])  4.02 us
  transfers between devices with their start and end apart: 16, of which 4 were waited for; matrix products, arithmetic and copies ran while one was open for 0% of the time, Pallas kernels for 39%

profile of v3, /device:TPU:0, one launch (start us, length us, event | category | flops | bytes accessed | tf_op | source)
XLA Modules:
  0.0 106.2 jit_solution(13382360209123192132)
XLA Ops:
  0.0 5.0 %collective-permute-start = (s32[4,20]{1,0:T(4,128)}, s32[4,20]{1,0:T(4,128)S(1)}, u32[]{:S(2)}, u32[]{:S(2)}) collective-permute-start(s32[4,20]{1,0:T(4,128)} %bitcast.14), channel_id=1, source_target_pairs={{0,12},{4,0},{8,4},{12,8},{1,13},{5,1},{9,5},{13,9},{2,14},{6,2},{... | collective-permute-start | bytes 968 | tf_op jit(solution)/shard_map/ppermute | solution.py:47
  5.0 0.0 collective-permute-start.1
  5.1 1.0 collective-permute-start.2
  6.1 1.7 %copy-done.3 = bf16[1,4,20,128,128]{4,3,2,1,0:T(8,128)(2,1)S(1)} copy-done((bf16[1,4,20,128,128]{4,3,2,1,0:T(8,128)(2,1)S(1)}, bf16[1,4,20,128,128]{4,3,2,1,0:T(8,128)(2,1)}, u32[]{:S(2)}) %copy-start.3) | copy-done | bytes 2621464
  7.8 0.7 copy-done.10
  8.5 4.5 %degrees.1.inverse = f32[8192,64]{1,0:T(8,128)S(1)} custom-call(s32[4,20]{1,0:T(4,128)S(1)} %bitcast.10, bf16[80,128,128]{2,1,0:T(8,128)(2,1)S(1)} %bitcast.5), custom_call_target="tpu_custom_call" | custom-call | bytes 65536 | tf_op jit(solution)/shard_map/degrees/pallas_call | solution.py:32
  13.0 2.0 %copy-done = f32[8192,64]{1,0:T(8,128)} copy-done((f32[8192,64]{1,0:T(8,128)}, f32[8192,64]{1,0:T(8,128)S(1)}, u32[]{:S(2)}) %copy-start) | copy-done | bytes 2097176
  15.0 0.0 collective-permute-done.refs_0_
  15.0 0.0 collective-permute-done.1.refs_1_
  15.0 0.0 collective-permute-done.2.refs_2_
  15.0 2.0 %pack.2 = (bf16[20,64,128]{2,1,0:T(8,128)(2,1)}, bf16[20,64,128]{2,1,0:T(8,128)(2,1)}, bf16[20,64,128]{2,1,0:T(8,128)(2,1)}) custom-call(s32[4,20]{1,0:T(4,128)S(1)} %collective-permute-done.refs_0_, s32[4,20]{1,0:T(4,128)S(1)} %collective-permute-done.1.refs_1_, s32[4,20]{1,0:T(4,128)S(1)} %collective-permute-done.2.refs_2_, bf16[128,8192]{1,0:T(8,128)(2,1)S(1)} %copy-done.5), custom_call_target="tpu_custom_call" | custom-call | bytes 65536 | tf_op jit(solution)/shard_map/pack/pallas_call | solution.py:32
  17.0 2.8 %collective-permute-start.5 = (bf16[20,64,128]{2,1,0:T(8,128)(2,1)}, bf16[20,64,128]{2,1,0:T(8,128)(2,1)S(1)}, u32[]{:S(2)}, u32[]{:S(2)}) collective-permute-start(bf16[20,64,128]{2,1,0:T(8,128)(2,1)} %get-tuple-element.58), channel_id=1, source_target_pairs={{0,12},{4,0},{8,4},{12,8},{1,13},{5,1},{9,5},{13,9},{2,14},{6,2},{... | collective-permute-start | bytes 983048 | tf_op jit(solution)/shard_map/ppermute | solution.py:47
  19.8 1.1 %collective-permute-start.4 = (bf16[20,64,128]{2,1,0:T(8,128)(2,1)}, bf16[20,64,128]{2,1,0:T(8,128)(2,1)S(1)}, u32[]{:S(2)}, u32[]{:S(2)}) collective-permute-start(bf16[20,64,128]{2,1,0:T(8,128)(2,1)} %get-tuple-element.55), channel_id=1, source_target_pairs={{0,8},{4,12},{8,0},{12,4},{1,9},{5,13},{9,1},{13,5},{2,10},{6,14},... | collective-permute-start | bytes 983048 | tf_op jit(solution)/shard_map/ppermute | solution.py:47
  20.9 0.0 collective-permute-start.3
  21.0 2.2 %copy-done.1 = f32[8192,64]{1,0:T(8,128)S(1)} copy-done((f32[8192,64]{1,0:T(8,128)S(1)}, f32[8192,64]{1,0:T(8,128)}, u32[]{:S(2)}) %copy-start.1) | copy-done | bytes 2097176
  23.1 1.6 %copy-done.6 = bf16[128,8192]{1,0:T(8,128)(2,1)S(1)} copy-done((bf16[128,8192]{1,0:T(8,128)(2,1)S(1)}, bf16[128,8192]{1,0:T(8,128)(2,1)}, u32[]{:S(2)}) %copy-start.6) | copy-done | bytes 2097176
  24.7 5.7 %own.1 = (f32[8192,64]{1,0:T(8,128)S(1)}, f32[8192,64]{1,0:T(8,128)S(1)}) custom-call(s32[4,20]{1,0:T(4,128)S(1)} %bitcast.11, s32[4,20]{1,0:T(4,128)S(1)} %bitcast.17, bf16[128,8192]{1,0:T(8,128)(2,1)S(1)} %copy-done.6, bf16[80,128,128]{2,1,0:T(8,128)(2,1)S(1)} %bitcast.6, f32[8192,64]{1,0:T(8,128)S(1)} %copy-done.1), custom_call_target="tpu_custom_call" | custom-call | bytes 65536 | tf_op jit(solution)/shard_map/own/pallas_call | solution.py:32
  30.5 1.0 pack.3
  31.5 0.0 collective-permute-done.5.refs_2_
  31.5 17.3 %collective-permute-done.4.refs_1_ = bf16[20,64,128]{2,1,0:T(8,128)(2,1)S(1)} collective-permute-done((bf16[20,64,128]{2,1,0:T(8,128)(2,1)}, bf16[20,64,128]{2,1,0:T(8,128)(2,1)S(1)}, u32[]{:S(2)}, u32[]{:S(2)}) %collective-permute-start.4) | collective-permute-done | bytes 327712 | tf_op jit(solution)/shard_map/ppermute | solution.py:47
  48.8 0.0 collective-permute-done.3.refs_0_
  48.8 0.0 collective-permute-start.11
  48.8 1.6 %collective-permute-start.10 = (bf16[20,64,128]{2,1,0:T(8,128)(2,1)S(1)}, bf16[20,64,128]{2,1,0:T(8,128)(2,1)S(1)}, u32[]{:S(2)}, u32[]{:S(2)}) collective-permute-start(bf16[20,64,128]{2,1,0:T(8,128)(2,1)S(1)} %get-tuple-element.68), channel_id=1, source_target_pairs={{0,8},{4,12},{8,0},{12,4},{1,9},{5,13},{9,1},{13,5},{2,10},{6,14},... | collective-permute-start | bytes 983048 | tf_op jit(solution)/shard_map/ppermute | solution.py:47
  50.4 2.0 %collective-permute-start.9 = (bf16[20,64,128]{2,1,0:T(8,128)(2,1)S(1)}, bf16[20,64,128]{2,1,0:T(8,128)(2,1)S(1)}, u32[]{:S(2)}, u32[]{:S(2)}) collective-permute-start(bf16[20,64,128]{2,1,0:T(8,128)(2,1)S(1)} %get-tuple-element.67), channel_id=1, source_target_pairs={{0,4},{4,8},{8,12},{12,0},{1,5},{5,9},{9,13},{13,1},{2,6},{6,10},{... | collective-permute-start | bytes 983048 | tf_op jit(solution)/shard_map/ppermute | solution.py:47
  52.4 8.0 %gather_far.2 = (f32[8192,64]{1,0:T(8,128)S(1)}, bf16[64,2048]{1,0:T(8,128)(2,1)S(1)}, bf16[64,2048]{1,0:T(8,128)(2,1)S(1)}) custom-call(s32[4]{0:T(128)S(1)} %get-tuple-element.75.bases, s32[4,20]{1,0:T(4,128)S(1)} %bitcast.12, s32[8192]{0:T(1024)S(1)} %copy-done.9, f32[8192,64]{1,0:T(8,128)S(1)} %get-tuple-element.41.acc, f32[8192,64]{1,0:T(8,128)S(1)} %copy-done.2, ...), custom_call_target="tpu_custom_call" | custom-call | bytes 65536 | tf_op jit(solution)/shard_map/gather_far/pallas_call | solution.py:32
  60.5 0.1 collective-permute-start.7
  60.6 1.6 %collective-permute-start.8 = (bf16[64,2048]{1,0:T(8,128)(2,1)S(1)}, bf16[64,2048]{1,0:T(8,128)(2,1)S(1)}, u32[]{:S(2)}, u32[]{:S(2)}) collective-permute-start(bf16[64,2048]{1,0:T(8,128)(2,1)S(1)} %get-tuple-element.62), channel_id=1, source_target_pairs={{0,2},{1,3},{2,0},{3,1},{4,6},{5,7},{6,4},{7,5},{8,10},{9,11},{10,... | collective-permute-start | bytes 786440 | tf_op jit(solution)/shard_map/ppermute | solution.py:51
  62.2 3.3 %gather_near.5.refs_3_ = bf16[64,2048]{1,0:T(8,128)(2,1)S(1)} custom-call(s32[4]{0:T(128)S(1)} %get-tuple-element.75.bases, s32[8192]{0:T(1024)S(1)} %copy-done.9, f32[8192,64]{1,0:T(8,128)S(1)} %get-tuple-element.60.total), custom_call_target="tpu_custom_call" | custom-call | bytes 65536 | tf_op jit(solution)/shard_map/gather_near/pallas_call | solution.py:32
  65.4 4.0 %gather_near.4 = bf16[64,2048]{1,0:T(8,128)(2,1)} custom-call(s32[4]{0:T(128)S(1)} %get-tuple-element.75.bases, s32[8192]{0:T(1024)S(1)} %copy-done.9, f32[8192,64]{1,0:T(8,128)S(1)} %get-tuple-element.60.total), custom_call_target="tpu_custom_call" | custom-call | bytes 65536 | tf_op jit(solution)/shard_map/gather_near/pallas_call | solution.py:32
  69.4 0.3 collective-permute-start.6
  69.7 5.1 %collective-permute-done.8.refs_2_ = bf16[64,2048]{1,0:T(8,128)(2,1)S(1)} collective-permute-done((bf16[64,2048]{1,0:T(8,128)(2,1)S(1)}, bf16[64,2048]{1,0:T(8,128)(2,1)S(1)}, u32[]{:S(2)}, u32[]{:S(2)}) %collective-permute-start.8) | collective-permute-done | bytes 262176 | tf_op jit(solution)/shard_map/ppermute | solution.py:51
  74.8 0.0 collective-permute-done.11.refs_2_
  74.8 3.9 %collective-permute-done.10.refs_1_ = bf16[20,64,128]{2,1,0:T(8,128)(2,1)S(1)} collective-permute-done((bf16[20,64,128]{2,1,0:T(8,128)(2,1)S(1)}, bf16[20,64,128]{2,1,0:T(8,128)(2,1)S(1)}, u32[]{:S(2)}, u32[]{:S(2)}) %collective-permute-start.10) | collective-permute-done | bytes 327712 | tf_op jit(solution)/shard_map/ppermute | solution.py:47
  78.7 8.8 %gather_far.3 = (f32[8192,64]{1,0:T(8,128)S(1)}, bf16[64,2048]{1,0:T(8,128)(2,1)}, bf16[64,2048]{1,0:T(8,128)(2,1)}) custom-call(s32[4]{0:T(128)S(1)} %get-tuple-element.75.bases, s32[4,20]{1,0:T(4,128)S(1)} %bitcast.13, s32[8192]{0:T(1024)S(1)} %copy-done.9, f32[8192,64]{1,0:T(8,128)S(1)} %get-tuple-element.66.acc, f32[8192,64]{1,0:T(8,128)S(1)} %copy-done.2, ...), custom_call_target="tpu_custom_call" | custom-call | bytes 65536 | tf_op jit(solution)/shard_map/gather_far/pallas_call | solution.py:32
  87.5 1.6 %collective-permute-start.15 = (bf16[64,2048]{1,0:T(8,128)(2,1)}, bf16[64,2048]{1,0:T(8,128)(2,1)S(1)}, u32[]{:S(2)}, u32[]{:S(2)}) collective-permute-start(bf16[64,2048]{1,0:T(8,128)(2,1)} %get-tuple-element.74), channel_id=1, source_target_pairs={{0,2},{1,3},{2,0},{3,1},{4,6},{5,7},{6,4},{7,5},{8,10},{9,11},{10,... | collective-permute-start | bytes 786440 | tf_op jit(solution)/shard_map/ppermute | solution.py:51
  89.1 3.2 %gather_near.6 = (bf16[32,2048]{1,0:T(8,128)(2,1)S(1)}, bf16[32,2048]{1,0:T(8,128)(2,1)S(1)}) custom-call(s32[4]{0:T(128)S(1)} %get-tuple-element.75.bases, s32[8192]{0:T(1024)S(1)} %copy-done.9, f32[8192,64]{1,0:T(8,128)S(1)} %get-tuple-element.70.total), custom_call_target="tpu_custom_call" | custom-call | bytes 16777216 | tf_op jit(solution)/shard_map/gather_near/pallas_call | solution.py:32
  92.3 2.0 %copy-done.7 = f32[8192,64]{1,0:T(8,128)} copy-done((f32[8192,64]{1,0:T(8,128)}, f32[8192,64]{1,0:T(8,128)S(1)}, u32[]{:S(2)}) %copy-start.7) | copy-done | bytes 2097176
  94.3 0.3 collective-permute-start.12
  94.6 0.2 collective-permute-start.13
  94.8 0.2 copy.10
  95.0 0.1 copy.11.bias
  95.2 2.2 %copy-done.8 = f32[8192,64]{1,0:T(8,128)S(1)} copy-done((f32[8192,64]{1,0:T(8,128)S(1)}, f32[8192,64]{1,0:T(8,128)}, u32[]{:S(2)}) %copy-start.8) | copy-done | bytes 2097176
  97.4 3.3 %gather_near.7.refs_8_ = bf16[64,2048]{1,0:T(8,128)(2,1)S(1)} custom-call(s32[4]{0:T(128)S(1)} %get-tuple-element.75.bases, s32[8192]{0:T(1024)S(1)} %copy-done.9, f32[8192,64]{1,0:T(8,128)S(1)} %copy-done.8), custom_call_target="tpu_custom_call" | custom-call | bytes 65536 | tf_op jit(solution)/shard_map/gather_near/pallas_call | solution.py:32
  100.6 0.0 collective-permute-done.6.refs_0_
  100.7 0.0 collective-permute-done.12.refs_4_
  100.7 0.0 collective-permute-done.14.refs_6_
  100.7 1.2 %collective-permute-done.15.refs_7_ = bf16[64,2048]{1,0:T(8,128)(2,1)S(1)} collective-permute-done((bf16[64,2048]{1,0:T(8,128)(2,1)}, bf16[64,2048]{1,0:T(8,128)(2,1)S(1)}, u32[]{:S(2)}, u32[]{:S(2)}) %collective-permute-start.15) | collective-permute-done | bytes 262176 | tf_op jit(solution)/shard_map/ppermute | solution.py:51
  101.9 4.3 %mix.1 = bf16[512,2048]{1,0:T(8,128)(2,1)} custom-call(s32[4]{0:T(128)S(1)} %get-tuple-element.76.starts, bf16[512,512]{1,0:T(8,128)(2,1)S(1)} %bitcast.9, f32[512,1]{1,0:T(8,128)S(1)} %copy.11.bias, bf16[64,2048]{1,0:T(8,128)(2,1)} %collective-permute-done.6.refs_0_, bf16[64,2048]{1,0:T(8,128)(2,1)S(1)} %collective-permute-done.7.refs_1_, ...), custom_call_target="tpu_custom_call" | custom-call | flops 1073741824 | bytes 5242880 | tf_op jit(solution)/shard_map/mix/pallas_call | solution.py:269
  (30 shorter events, 0.1 us)
Async XLA Ops:
  0.0 15.0 %collective-permute-start = (s32[4,20]{1,0:T(4,128)}, s32[4,20]{1,0:T(4,128)S(1)}, u32[]{:S(2)}, u32[]{:S(2)}) collective-permute-start(s32[4,20]{1,0:T(4,128)} %bitcast.14), channel_id=1, source_target_pairs={{0,12},{4,0},{8,4},{12,8},{1,13},{5,1},{9,5},{13,9},{2,14},{6,2},{... | collective-permute-start | bytes 968 | tf_op jit(solution)/shard_map/ppermute | solution.py:47
  5.0 9.9 %collective-permute-start.1 = (s32[4,20]{1,0:T(4,128)}, s32[4,20]{1,0:T(4,128)S(1)}, u32[]{:S(2)}, u32[]{:S(2)}) collective-permute-start(s32[4,20]{1,0:T(4,128)} %bitcast.15), channel_id=1, source_target_pairs={{0,8},{4,12},{8,0},{12,4},{1,9},{5,13},{9,1},{13,5},{2,10},{6,14},... | collective-permute-start | bytes 968 | tf_op jit(solution)/shard_map/ppermute | solution.py:47
  5.1 9.9 %collective-permute-start.2 = (s32[4,20]{1,0:T(4,128)}, s32[4,20]{1,0:T(4,128)S(1)}, u32[]{:S(2)}, u32[]{:S(2)}) collective-permute-start(s32[4,20]{1,0:T(4,128)} %bitcast.16), channel_id=1, source_target_pairs={{0,4},{4,8},{8,12},{12,0},{1,5},{5,9},{9,13},{13,1},{2,6},{6,10},{... | collective-permute-start | bytes 968 | tf_op jit(solution)/shard_map/ppermute | solution.py:47
  6.1 1.7 %copy-start.3 = (bf16[1,4,20,128,128]{4,3,2,1,0:T(8,128)(2,1)S(1)}, bf16[1,4,20,128,128]{4,3,2,1,0:T(8,128)(2,1)}, u32[]{:S(2)}) copy-start(bf16[1,4,20,128,128]{4,3,2,1,0:T(8,128)(2,1)} %param.11) | copy-start | bytes 7864324
  7.8 0.7 copy-start.10
  8.5 6.5 %copy-start.5 = (bf16[128,8192]{1,0:T(8,128)(2,1)S(1)}, bf16[128,8192]{1,0:T(8,128)(2,1)}, u32[]{:S(2)}) copy-start(bf16[128,8192]{1,0:T(8,128)(2,1)} %refs_3_.3) | copy-start | bytes 6291460
  8.5 12.4 %copy-start.4 = (bf16[1,4,20,128,128]{4,3,2,1,0:T(8,128)(2,1)S(1)}, bf16[1,4,20,128,128]{4,3,2,1,0:T(8,128)(2,1)}, u32[]{:S(2)}) copy-start(bf16[1,4,20,128,128]{4,3,2,1,0:T(8,128)(2,1)} %param.11) | copy-start | bytes 7864324
  8.5 12.4 %copy-start.11 = (s32[1,4,20]{2,1,0:T(4,128)S(1)}, s32[1,4,20]{2,1,0:T(4,128)}, u32[]{:S(2)}) copy-start(s32[1,4,20]{2,1,0:T(4,128)} %param.9) | copy-start | bytes 964
  8.5 12.4 %copy-start.12 = (s32[1,4,20]{2,1,0:T(4,128)S(1)}, s32[1,4,20]{2,1,0:T(4,128)}, u32[]{:S(2)}) copy-start(s32[1,4,20]{2,1,0:T(4,128)} %param.10) | copy-start | bytes 964
  13.0 2.0 %copy-start = (f32[8192,64]{1,0:T(8,128)}, f32[8192,64]{1,0:T(8,128)S(1)}, u32[]{:S(2)}) copy-start(f32[8192,64]{1,0:T(8,128)S(1)} %degrees.1.inverse) | copy-start | bytes 6291460
  17.0 14.5 %collective-permute-start.5 = (bf16[20,64,128]{2,1,0:T(8,128)(2,1)}, bf16[20,64,128]{2,1,0:T(8,128)(2,1)S(1)}, u32[]{:S(2)}, u32[]{:S(2)}) collective-permute-start(bf16[20,64,128]{2,1,0:T(8,128)(2,1)} %get-tuple-element.58), channel_id=1, source_target_pairs={{0,12},{4,0},{8,4},{12,8},{1,13},{5,1},{9,5},{13,9},{2,14},{6,2},{... | collective-permute-start | bytes 983048 | tf_op jit(solution)/shard_map/ppermute | solution.py:47
  19.8 29.0 %collective-permute-start.4 = (bf16[20,64,128]{2,1,0:T(8,128)(2,1)}, bf16[20,64,128]{2,1,0:T(8,128)(2,1)S(1)}, u32[]{:S(2)}, u32[]{:S(2)}) collective-permute-start(bf16[20,64,128]{2,1,0:T(8,128)(2,1)} %get-tuple-element.55), channel_id=1, source_target_pairs={{0,8},{4,12},{8,0},{12,4},{1,9},{5,13},{9,1},{13,5},{2,10},{6,14},... | collective-permute-start | bytes 983048 | tf_op jit(solution)/shard_map/ppermute | solution.py:47
  20.9 27.9 %collective-permute-start.3 = (bf16[20,64,128]{2,1,0:T(8,128)(2,1)}, bf16[20,64,128]{2,1,0:T(8,128)(2,1)}, u32[]{:S(2)}, u32[]{:S(2)}) collective-permute-start(bf16[20,64,128]{2,1,0:T(8,128)(2,1)} %get-tuple-element.51), channel_id=1, source_target_pairs={{0,4},{4,8},{8,12},{12,0},{1,5},{5,9},{9,13},{13,1},{2,6},{6,10},{... | collective-permute-start | bytes 983048 | tf_op jit(solution)/shard_map/ppermute | solution.py:47
  20.9 2.2 %copy-start.1 = (f32[8192,64]{1,0:T(8,128)S(1)}, f32[8192,64]{1,0:T(8,128)}, u32[]{:S(2)}) copy-start(f32[8192,64]{1,0:T(8,128)} %copy-done) | copy-start | bytes 6291460
  23.1 1.6 %copy-start.6 = (bf16[128,8192]{1,0:T(8,128)(2,1)S(1)}, bf16[128,8192]{1,0:T(8,128)(2,1)}, u32[]{:S(2)}) copy-start(bf16[128,8192]{1,0:T(8,128)(2,1)} %refs_3_.3) | copy-start | bytes 6291460
  24.7 27.7 %copy-start.15 = (s32[4]{0:T(128)S(1)}, s32[4]{0:T(128)}, u32[]{:S(2)}) copy-start(s32[4]{0:T(128)} %constant.10.clone) | copy-start | bytes 52
  24.7 27.7 %copy-start.2 = (f32[8192,64]{1,0:T(8,128)S(1)}, f32[8192,64]{1,0:T(8,128)}, u32[]{:S(2)}) copy-start(f32[8192,64]{1,0:T(8,128)} %copy-done) | copy-start | bytes 6291460
  24.7 27.7 %copy-start.9 = (s32[8192]{0:T(1024)S(1)}, s32[8192]{0:T(1024)}, u32[]{:S(2)}) copy-start(s32[8192]{0:T(1024)} %order.11) | copy-start | bytes 98308
  48.8 26.0 %collective-permute-start.11 = (bf16[20,64,128]{2,1,0:T(8,128)(2,1)S(1)}, bf16[20,64,128]{2,1,0:T(8,128)(2,1)S(1)}, u32[]{:S(2)}, u32[]{:S(2)}) collective-permute-start(bf16[20,64,128]{2,1,0:T(8,128)(2,1)S(1)} %get-tuple-element.69), channel_id=1, source_target_pairs={{0,12},{4,0},{8,4},{12,8},{1,13},{5,1},{9,5},{13,9},{2,14},{6,2},{... | collective-permute-start | bytes 983048 | tf_op jit(solution)/shard_map/ppermute | solution.py:47
  48.8 29.9 %collective-permute-start.10 = (bf16[20,64,128]{2,1,0:T(8,128)(2,1)S(1)}, bf16[20,64,128]{2,1,0:T(8,128)(2,1)S(1)}, u32[]{:S(2)}, u32[]{:S(2)}) collective-permute-start(bf16[20,64,128]{2,1,0:T(8,128)(2,1)S(1)} %get-tuple-element.68), channel_id=1, source_target_pairs={{0,8},{4,12},{8,0},{12,4},{1,9},{5,13},{9,1},{13,5},{2,10},{6,14},... | collective-permute-start | bytes 983048 | tf_op jit(solution)/shard_map/ppermute | solution.py:47
  50.4 28.3 %collective-permute-start.9 = (bf16[20,64,128]{2,1,0:T(8,128)(2,1)S(1)}, bf16[20,64,128]{2,1,0:T(8,128)(2,1)S(1)}, u32[]{:S(2)}, u32[]{:S(2)}) collective-permute-start(bf16[20,64,128]{2,1,0:T(8,128)(2,1)S(1)} %get-tuple-element.67), channel_id=1, source_target_pairs={{0,4},{4,8},{8,12},{12,0},{1,5},{5,9},{9,13},{13,1},{2,6},{6,10},{... | collective-permute-start | bytes 983048 | tf_op jit(solution)/shard_map/ppermute | solution.py:47
  60.5 8.9 %collective-permute-start.7 = (bf16[64,2048]{1,0:T(8,128)(2,1)S(1)}, bf16[64,2048]{1,0:T(8,128)(2,1)S(1)}, u32[]{:S(2)}, u32[]{:S(2)}) collective-permute-start(bf16[64,2048]{1,0:T(8,128)(2,1)S(1)} %get-tuple-element.61), channel_id=1, source_target_pairs={{0,3},{1,2},{2,1},{3,0},{4,7},{5,6},{6,5},{7,4},{8,11},{9,10},{10,... | collective-permute-start | bytes 786440 | tf_op jit(solution)/shard_map/ppermute | solution.py:51
  60.6 14.2 %collective-permute-start.8 = (bf16[64,2048]{1,0:T(8,128)(2,1)S(1)}, bf16[64,2048]{1,0:T(8,128)(2,1)S(1)}, u32[]{:S(2)}, u32[]{:S(2)}) collective-permute-start(bf16[64,2048]{1,0:T(8,128)(2,1)S(1)} %get-tuple-element.62), channel_id=1, source_target_pairs={{0,2},{1,3},{2,0},{3,1},{4,6},{5,7},{6,4},{7,5},{8,10},{9,11},{10,... | collective-permute-start | bytes 786440 | tf_op jit(solution)/shard_map/ppermute | solution.py:51
  69.4 31.3 %collective-permute-start.6 = (bf16[64,2048]{1,0:T(8,128)(2,1)}, bf16[64,2048]{1,0:T(8,128)(2,1)}, u32[]{:S(2)}, u32[]{:S(2)}) collective-permute-start(bf16[64,2048]{1,0:T(8,128)(2,1)} %gather_near.4), channel_id=1, source_target_pairs={{0,1},{1,0},{2,3},{3,2},{4,5},{5,4},{6,7},{7,6},{8,9},{9,8},{10,11... | collective-permute-start | bytes 786440 | tf_op jit(solution)/shard_map/ppermute | solution.py:51
  87.5 7.3 %copy-start.13 = (bf16[512,512]{1,0:T(8,128)(2,1)S(1)}, bf16[512,512]{1,0:T(8,128)(2,1)}, u32[]{:S(2)}) copy-start(bf16[512,512]{1,0:T(8,128)(2,1)} %param.13) | copy-start | bytes 1572868
  87.5 7.5 %copy-start.14 = (f32[512]{0:T(512)S(1)}, f32[512]{0:T(512)}, u32[]{:S(2)}) copy-start(f32[512]{0:T(512)} %param.14) | copy-start | bytes 6148
  87.5 13.2 %collective-permute-start.14 = (bf16[64,2048]{1,0:T(8,128)(2,1)}, bf16[64,2048]{1,0:T(8,128)(2,1)S(1)}, u32[]{:S(2)}, u32[]{:S(2)}) collective-permute-start(bf16[64,2048]{1,0:T(8,128)(2,1)} %get-tuple-element.73), channel_id=1, source_target_pairs={{0,3},{1,2},{2,1},{3,0},{4,7},{5,6},{6,5},{7,4},{8,11},{9,10},{10,... | collective-permute-start | bytes 786440 | tf_op jit(solution)/shard_map/ppermute | solution.py:51
  87.5 14.4 %collective-permute-start.15 = (bf16[64,2048]{1,0:T(8,128)(2,1)}, bf16[64,2048]{1,0:T(8,128)(2,1)S(1)}, u32[]{:S(2)}, u32[]{:S(2)}) collective-permute-start(bf16[64,2048]{1,0:T(8,128)(2,1)} %get-tuple-element.74), channel_id=1, source_target_pairs={{0,2},{1,3},{2,0},{3,1},{4,6},{5,7},{6,4},{7,5},{8,10},{9,11},{10,... | collective-permute-start | bytes 786440 | tf_op jit(solution)/shard_map/ppermute | solution.py:51
  92.3 2.0 %copy-start.7 = (f32[8192,64]{1,0:T(8,128)}, f32[8192,64]{1,0:T(8,128)S(1)}, u32[]{:S(2)}) copy-start(f32[8192,64]{1,0:T(8,128)S(1)} %get-tuple-element.70.total) | copy-start | bytes 6291460
  94.3 6.4 %collective-permute-start.12 = (bf16[32,2048]{1,0:T(8,128)(2,1)S(1)}, bf16[32,2048]{1,0:T(8,128)(2,1)S(1)}, u32[]{:S(2)}, u32[]{:S(2)}) collective-permute-start(bf16[32,2048]{1,0:T(8,128)(2,1)S(1)} %get-tuple-element.71), channel_id=1, source_target_pairs={{0,1},{1,0},{2,3},{3,2},{4,5},{5,4},{6,7},{7,6},{8,9},{9,8},{10,11... | collective-permute-start | bytes 393224 | tf_op jit(solution)/shard_map/ppermute | solution.py:51
  94.6 6.1 %collective-permute-start.13 = (bf16[32,2048]{1,0:T(8,128)(2,1)S(1)}, bf16[32,2048]{1,0:T(8,128)(2,1)S(1)}, u32[]{:S(2)}, u32[]{:S(2)}) collective-permute-start(bf16[32,2048]{1,0:T(8,128)(2,1)S(1)} %get-tuple-element.72), channel_id=1, source_target_pairs={{0,1},{1,0},{2,3},{3,2},{4,5},{5,4},{6,7},{7,6},{8,9},{9,8},{10,11... | collective-permute-start | bytes 393224 | tf_op jit(solution)/shard_map/ppermute | solution.py:51
  95.2 2.2 %copy-start.8 = (f32[8192,64]{1,0:T(8,128)S(1)}, f32[8192,64]{1,0:T(8,128)}, u32[]{:S(2)}) copy-start(f32[8192,64]{1,0:T(8,128)} %copy-done.7) | copy-start | bytes 6291460

commit v4 on v3

--- a/solution.py
+++ b/solution.py
@@ -52,7 +52,7 @@
 
 
 def cuts(width):
-    first = width // 2
+    first = width * 5 // 8 // 16 * 16
     return ((0, first), (first, width - first))
 
 
@@ -60,6 +60,24 @@
     row = lax.broadcasted_iota(jnp.int32, (size, size), 0)
     col = lax.broadcasted_iota(jnp.int32, (size, size), 1)
     return (row == col).astype(jnp.float32).astype(jnp.bfloat16)
+
+
+def stage_kernel(panel, bias, out, column):
+    out[...] = panel[...]
+    column[...] = jnp.broadcast_to(bias[...], column.shape[::-1]).T
+
+
+def staged(panel, bias):
+    return call(
+        stage_kernel,
+        "stage",
+        [],
+        [panel, bias[None, :]],
+        [
+            jax.ShapeDtypeStruct(panel.shape, panel.dtype),
+            jax.ShapeDtypeStruct((bias.shape[0], 128), bias.dtype),
+        ],
+    )
 
 
 def pack_kernel(low, size, offsets, slots, tile, *refs):
@@ -185,22 +203,17 @@
         return carry
 
     lax.fori_loop(0, count // UNROLL, group, 0)
-
-    def turn(c, carry):
-        at = pl.multiple_of(c * CHUNK, CHUNK)
-        turned = dot(eye, stage[pl.ds(at, CHUNK), :].astype(jnp.bfloat16), NT)
-        low = 0
-        for out in outs:
-            out[:, pl.ds(at, CHUNK)] = turned[low : low + out.shape[0]].astype(out.dtype)
-            low += out.shape[0]
-        return carry
-
-    lax.fori_loop(0, count // CHUNK, turn, 0, unroll=4)
-
-
-def far_kernel(offsets, slots, tile, bases, rows, order, acc, inverse, counts, *refs):
-    got, total, outs = refs[:offsets], refs[offsets], refs[offsets + 1 : -2]
-    product, stage = refs[-2:]
+    first = 0
+    for out in outs:
+        columns = out.shape[1]
+        for at in range(0, columns, CHUNK):
+            chunk = stage[pl.ds(first + at, CHUNK), :].astype(jnp.bfloat16)
+            out[:, pl.ds(at, CHUNK)] = dot(eye, chunk, NT).astype(out.dtype)
+        first += columns
+
+
+def first_kernel(offsets, slots, tile, bases, rows, order, acc, inverse, counts, *refs):
+    got, total, out, product, stage = refs[:offsets], *refs[offsets:]
     size = acc.shape[1]
     total[...] = acc[...]
     for s in range(offsets):
@@ -216,68 +229,75 @@
 
         lax.fori_loop(0, slots, multiply, 0, unroll=10)
         lax.fori_loop(0, slots, add, 0)
-
-    for i, out in enumerate(outs):
-        pick(order, bases[i], total, stage, [out])
-
-
-def gather_far(acc, inverse, bases, rows, order, counts, got, share, ranks):
+    pick(order, bases[0], total, stage, [out])
+
+
+def gather_first(acc, inverse, bases, rows, order, counts, got, share):
     nodes, size = acc.shape
     slots, tile = rows.shape[1], counts.shape[-1]
-    piece = jax.ShapeDtypeStruct((size, share), jnp.bfloat16)
-    outs = call(
-        functools.partial(far_kernel, len(got), slots, tile),
-        "gather_far",
+    return call(
+        functools.partial(first_kernel, len(got), slots, tile),
+        "gather_first",
         [bases, rows, order],
         [acc, inverse, counts, *got],
-        [jax.ShapeDtypeStruct((nodes, size), jnp.float32)] + [piece] * ranks,
+        [
+            jax.ShapeDtypeStruct((nodes, size), jnp.float32),
+            jax.ShapeDtypeStruct((size, share), jnp.bfloat16),
+        ],
         [((slots, tile, size), jnp.float32), ((share, size), jnp.float32)],
-    )
-    return outs[0], outs[1:]
-
-
-def near_kernel(rank, bases, order, total, *refs):
+        2**22,
+    )
+
+
+def next_kernel(rank, bases, order, total, *refs):
     pick(order, bases[rank], total, refs[-1], refs[:-1])
 
 
-def gather_near(total, bases, order, share, rank, heights, moved):
-    return call(
-        functools.partial(near_kernel, rank),
-        "gather_near",
+def gather_next(total, bases, order, rank, widths):
+    size = total.shape[1]
+    return call(
+        functools.partial(next_kernel, rank),
+        "gather_next",
         [bases, order],
         [total],
-        [jax.ShapeDtypeStruct((height, share), jnp.bfloat16) for height in heights],
-        [((share, total.shape[1]), jnp.float32)],
-        moved,
+        [jax.ShapeDtypeStruct((size, width), jnp.bfloat16) for width in widths],
+        [((sum(widths), size), jnp.float32)],
     )
 
 
 def mix_kernel(places, starts, weight, bias, *refs):
-    pieces, out, nodes = refs[:-2], refs[-2], refs[-1]
-    for piece, (i, low) in zip(pieces, places):
+    pieces, (out, nodes, ready, sems) = refs[:-4], refs[-4:]
+    for piece, (i, low, first) in zip(pieces, places):
+        height, columns = piece.shape
         at = pl.multiple_of(starts[i] + low, 16)
-        nodes[pl.ds(at, piece.shape[0]), :] = piece[...]
-    mixed = dot(weight[...], nodes[...], NN)
-    out[...] = jnp.maximum(mixed + bias[...], 0.0).astype(out.dtype)
-
-
-def mix(starts, weight, bias, placed):
+        nodes[pl.ds(at, height), pl.ds(first, columns)] = piece[...]
+    copies = []
+    for c in range(ready.shape[0]):
+        step = ready.shape[2]
+        mixed = dot(weight[...], nodes[:, pl.ds(c * step, step)], NN)
+        ready[c] = jnp.maximum(mixed + bias[:, :1], 0.0).astype(out.dtype)
+        copies.append(
+            pltpu.make_async_copy(ready.at[c], out.at[:, pl.ds(c * step, step)], sems.at[c])
+        )
+        copies[-1].start()
+    for copy in copies:
+        copy.wait()
+
+
+def mix(starts, weight, bias, placed, nodes):
     places, pieces = tuple(placed), list(placed.values())
     hidden, width = weight.shape
-    nodes = pieces[0].shape[1]
     step = min(512, nodes)
     return pl.pallas_call(
         functools.partial(mix_kernel, places),
-        grid=(nodes // step,),
         out_shape=jax.ShapeDtypeStruct((hidden, nodes), jnp.bfloat16),
-        in_specs=[
-            SMEM,
-            pl.BlockSpec(weight.shape, lambda i: (0, 0)),
-            pl.BlockSpec(bias.shape, lambda i: (0, 0)),
-        ]
-        + [pl.BlockSpec((piece.shape[0], step), lambda i: (0, i)) for piece in pieces],
-        out_specs=pl.BlockSpec((hidden, step), lambda i: (0, i)),
-        scratch_shapes=[pltpu.VMEM((width, step), jnp.bfloat16)],
+        in_specs=[SMEM] + [VMEM] * (2 + len(pieces)),
+        out_specs=pl.BlockSpec(memory_space=pl.ANY),
+        scratch_shapes=[
+            pltpu.VMEM((width, nodes), jnp.bfloat16),
+            pltpu.VMEM((nodes // step, hidden, step), jnp.bfloat16),
+            pltpu.SemaphoreType.DMA((nodes // step,)),
+        ],
         compiler_params=pltpu.CompilerParams(vmem_limit_bytes=16 * 2**20),
         cost_estimate=pl.CostEstimate(
             flops=2 * hidden * width * nodes, bytes_accessed=5 * 2**20, transcendentals=0
@@ -303,13 +323,14 @@
     far = groups - 2
 
     asked = [shifted(cols, "blk", -s) for s in range(1, blocks)]
-    inverse = degrees(rows, counts, nodes, max(size for _, size in ranges))
-    *asked, inverse = lax.optimization_barrier((*asked, inverse))
+    *asked, panel, column = lax.optimization_barrier((*asked, *staged(features, bias)))
     sent = []
     for low, size in ranges:
-        sent.append(list(pack(features, asked, low, size, tile)))
+        sent.append(list(pack(panel, asked, low, size, tile)))
         *asked, sent[-1][0] = lax.optimization_barrier((*asked, sent[-1][0]))
-    accs = list(own(features, rows, cols, counts, inverse, ranges))
+    inverse = degrees(rows, counts, nodes, max(size for _, size in ranges))
+    accs = own(panel, rows, cols, counts, inverse, ranges)
+    accs, across = lax.optimization_barrier((accs, weight.T))
 
     got = [[shifted(value, "blk", s + 1) for s, value in enumerate(sent[0])]]
     for later in sent[1:]:
@@ -317,28 +338,32 @@
         got[-1] = [b for _, b, _ in tied]
         got.append([shifted(a, "blk", s + 1) for s, (a, _, _) in enumerate(tied)])
 
-    pieces, waits = {}, {}
+    pieces, waits, kept = {}, {}, {}
     for p, (low, size) in enumerate(ranges):
         last = p == len(ranges) - 1
-        acc, waits = lax.optimization_barrier((accs[p], waits))
-        pieces.update(waits)
-        total, out_far = gather_far(
-            acc, inverse, bases, rows, order, counts, got[p], share, far
-        )
-        waits = {
-            (i, low): traded(piece, "grp", ranks[i]) for i, piece in enumerate(out_far)
-        }
-        waits[far + 1, low] = gather_near(
-            total, bases, order, share, far + 1, (size,), 2**16
-        )[0]
-        half = size // 32 * 16
-        heights = (half, size - half) if last else (size,)
-        moved = 2**24 if last else 2**16
-        for piece in gather_near(total, bases, order, share, far, heights, moved):
-            pieces[far, low] = traded(piece, "grp", 1)
-            low += piece.shape[0]
+        acc, kept = lax.optimization_barrier((accs[p], kept))
+        pieces.update(kept)
+        total, piece = gather_first(acc, inverse, bases, rows, order, counts, got[p], share)
+        now = {(0, low, 0): traded(piece, "grp", ranks[0])}
+        for i in range(1, groups - 1):
+            widths = (share,)
+            if last and i == far:
+                total, waits = lax.optimization_barrier((total, waits))
+                pieces.update(waits)
+                widths = (share // 2, share // 2)
+            elif last and i == far - 1:
+                widths = (share // 4 * 3, share // 4)
+            first = 0
+            for piece in gather_next(total, bases, order, i, widths):
+                if i == far and not last:
+                    piece, got[p + 1][0] = lax.optimization_barrier((piece, got[p + 1][0]))
+                now[i, low, first] = traded(piece, "grp", ranks[i])
+                first += piece.shape[1]
+        kept = {(groups - 1, low, 0): gather_next(total, bases, order, groups - 1, (share,))[0]}
+        waits = now
     pieces.update(waits)
-    return mix(whose * width, weight.T, bias[:, None], pieces)
+    pieces.update(kept)
+    return mix(whose * width, across, column, pieces, share)
 
 
 def solution(mesh):

time: 107 us -> 106 us (level)
  waiting for transfers between devices: 27.5 us -> 20.4 us
  starting transfers between devices: 17.7 us -> 22.4 us
  local copies, waits for them, and re-layouts: 12.7 us -> 14.7 us
    ppermute x7 -> x8, waiting for transfers between devices: 6.37 us -> 0.02 us  [traded(): lax.ppermute(value, axis, [(i, i ^ k) for i in range(lax.axis_size(axis))])]
    ppermute x7 -> x8, starting transfers between devices: 4.02 us -> 6.7 us  [traded(): lax.ppermute(value, axis, [(i, i ^ k) for i in range(lax.axis_size(axis))])]
    unnamed x33 -> x37, local copies, waits for them, and re-layouts: 12.5 us -> 14.7 us
    ppermute x9, starting transfers between devices: 13.6 us -> 15.7 us  [shifted(): return lax.ppermute(value, axis, pairs)]
    pallas_call x10 -> x13, Pallas kernels: 43.8 us -> 45.3 us  [call(): pl.pallas_call(kernel, out_shape=list(outs), in_specs=[SMEM] * len(scalar...]
    pallas_call x1, Pallas kernels: 4.25 us -> 2.78 us  [mix(): pl.pallas_call(functools.partial(mix_kernel, places), out_shape=jax.Shape...]
  transfers between devices with their start and end apart: 16 -> 17, of which waited for: 4 -> 1; matrix products, arithmetic and copies ran while one was open for 0% -> 1% of each run, Pallas kernels for 39% -> 41%
where the time goes in v4:
time: 106 us
  Pallas kernels  48.1 us (45%)
  starting transfers between devices  22.4 us (21%)
  waiting for transfers between devices  20.4 us (19%)
  local copies, waits for them, and re-layouts  14.7 us (14%)
    pallas_call x13, Pallas kernels, call(): pl.pallas_call(kernel, out_shape=list(outs), in_specs=[SMEM] * len(scalar...  45.3 us
    ppermute x9, waiting for transfers between devices, shifted(): return lax.ppermute(value, axis, pairs)  20.4 us
    ppermute x9, starting transfers between devices, shifted(): return lax.ppermute(value, axis, pairs)  15.7 us
    unnamed x37, local copies, waits for them, and re-layouts  14.7 us
    ppermute x8, starting transfers between devices, traded(): lax.ppermute(value, axis, [(i, i ^ k) for i in range(lax.axis_size(axis))])  6.7 us
    pallas_call x1, Pallas kernels, mix(): pl.pallas_call(functools.partial(mix_kernel, places), out_shape=jax.Shape...  2.78 us
  transfers between devices with their start and end apart: 17, of which 1 were waited for; matrix products, arithmetic and copies ran while one was open for 1% of the time, Pallas kernels for 41%

profile of v4, /device:TPU:0, one launch (start us, length us, event | category | flops | bytes accessed | tf_op | source)
XLA Modules:
  0.0 105.9 jit_solution(6428337945924698311)
XLA Ops:
  0.0 3.0 %collective-permute-start.2 = (s32[4,20]{1,0:T(4,128)}, s32[4,20]{1,0:T(4,128)S(1)}, u32[]{:S(2)}, u32[]{:S(2)}) collective-permute-start(s32[4,20]{1,0:T(4,128)} %bitcast.15), channel_id=1, source_target_pairs={{0,4},{4,8},{8,12},{12,0},{1,5},{5,9},{9,13},{13,1},{2,6},{6,10},{... | collective-permute-start | bytes 968 | tf_op jit(solution)/shard_map/ppermute | solution.py:47
  3.0 2.6 %collective-permute-start.1 = (s32[4,20]{1,0:T(4,128)}, s32[4,20]{1,0:T(4,128)S(1)}, u32[]{:S(2)}, u32[]{:S(2)}) collective-permute-start(s32[4,20]{1,0:T(4,128)} %bitcast.16), channel_id=1, source_target_pairs={{0,8},{4,12},{8,0},{12,4},{1,9},{5,13},{9,1},{13,5},{2,10},{6,14},... | collective-permute-start | bytes 968 | tf_op jit(solution)/shard_map/ppermute | solution.py:47
  5.6 1.3 %collective-permute-start = (s32[4,20]{1,0:T(4,128)}, s32[4,20]{1,0:T(4,128)S(1)}, u32[]{:S(2)}, u32[]{:S(2)}) collective-permute-start(s32[4,20]{1,0:T(4,128)} %bitcast.17), channel_id=1, source_target_pairs={{0,12},{4,0},{8,4},{12,8},{1,13},{5,1},{9,5},{13,9},{2,14},{6,2},{... | collective-permute-start | bytes 968 | tf_op jit(solution)/shard_map/ppermute | solution.py:47
  7.0 1.6 %copy-done.11 = bf16[128,8192]{1,0:T(8,128)(2,1)S(1)} copy-done((bf16[128,8192]{1,0:T(8,128)(2,1)S(1)}, bf16[128,8192]{1,0:T(8,128)(2,1)}, u32[]{:S(2)}) %copy-start.11) | copy-done | bytes 2097176
  8.6 0.7 copy-done.13
  9.2 0.2 stage.1
  9.4 0.0 collective-permute-done.2.refs_2_
  9.4 2.1 %pack.2 = (bf16[20,80,128]{2,1,0:T(8,128)(2,1)}, bf16[20,80,128]{2,1,0:T(8,128)(2,1)}, bf16[20,80,128]{2,1,0:T(8,128)(2,1)}) custom-call(s32[4,20]{1,0:T(4,128)S(1)} %collective-permute-done.refs_0_, s32[4,20]{1,0:T(4,128)S(1)} %collective-permute-done.1.refs_1_, s32[4,20]{1,0:T(4,128)S(1)} %collective-permute-done.2.refs_2_, ...), custom_call_target="tpu_custom_call" | custom-call | bytes 65536 | tf_op jit(solution)/shard_map/pack/pallas_call | solution.py:32
  11.6 1.3 %copy-done.4 = bf16[128,8192]{1,0:T(8,128)(2,1)} copy-done((bf16[128,8192]{1,0:T(8,128)(2,1)}, bf16[128,8192]{1,0:T(8,128)(2,1)S(1)}, u32[]{:S(2)}) %copy-start.4) | copy-done | bytes 2097176
  12.9 0.7 collective-permute-start.3
  13.6 3.1 %collective-permute-start.5 = (bf16[20,80,128]{2,1,0:T(8,128)(2,1)}, bf16[20,80,128]{2,1,0:T(8,128)(2,1)}, u32[]{:S(2)}, u32[]{:S(2)}) collective-permute-start(bf16[20,80,128]{2,1,0:T(8,128)(2,1)} %get-tuple-element.74), channel_id=1, source_target_pairs={{0,12},{4,0},{8,4},{12,8},{1,13},{5,1},{9,5},{13,9},{2,14},{6,2},{... | collective-permute-start | bytes 1228808 | tf_op jit(solution)/shard_map/ppermute | solution.py:47
  16.7 1.3 %copy.9 = bf16[512,512]{0,1:T(8,128)(2,1)S(1)} copy(bf16[512,512]{1,0:T(8,128)(2,1)} %param.13) | data formatting | bytes 1048576 | tf_op args[5]
  18.0 0.0 copy-start.5
  18.0 0.0 copy-start.14
  18.0 4.5 %degrees.1.inverse = f32[8192,80]{1,0:T(8,128)S(1)} custom-call(s32[4,20]{1,0:T(4,128)S(1)} %bitcast.10, bf16[80,128,128]{2,1,0:T(8,128)(2,1)S(1)} %bitcast.5), custom_call_target="tpu_custom_call" | custom-call | bytes 65536 | tf_op jit(solution)/shard_map/degrees/pallas_call | solution.py:32
  22.5 2.1 %pack.3 = (bf16[20,48,128]{2,1,0:T(8,128)(2,1)}, bf16[20,48,128]{2,1,0:T(8,128)(2,1)S(1)}, bf16[20,48,128]{2,1,0:T(8,128)(2,1)S(1)}) custom-call(s32[4,20]{1,0:T(4,128)S(1)} %collective-permute-done.refs_0_, s32[4,20]{1,0:T(4,128)S(1)} %collective-permute-done.1.refs_1_, s32[4,20]{1,0:T(4,128)S(1)} %collective-permute-done.2.refs_2_, ...), custom_call_target="tpu_custom_call" | custom-call | bytes 65536 | tf_op jit(solution)/shard_map/pack/pallas_call | solution.py:32
  24.6 0.7 copy-done.15
  25.3 0.7 copy-done.16
  26.0 5.9 %own.1 = (f32[8192,80]{1,0:T(8,128)S(1)}, f32[8192,48]{1,0:T(8,128)S(1)}) custom-call(s32[4,20]{1,0:T(4,128)S(1)} %bitcast.11, s32[4,20]{1,0:T(4,128)S(1)} %bitcast.18, bf16[128,8192]{1,0:T(8,128)(2,1)S(1)} %copy-done.5, bf16[80,128,128]{2,1,0:T(8,128)(2,1)S(1)} %bitcast.6, f32[8192,80]{1,0:T(8,128)S(1)} %degrees.1.inverse), custom_call_target="tpu_custom_call" | custom-call | bytes 65536 | tf_op jit(solution)/shard_map/own/pallas_call | solution.py:32
  31.9 2.0 %copy-done.6 = f32[8192,48]{1,0:T(8,128)} copy-done((f32[8192,48]{1,0:T(8,128)}, f32[8192,48]{1,0:T(8,128)S(1)}, u32[]{:S(2)}) %copy-start.6) | copy-done | bytes 1572888
  33.9 2.0 %copy-done.8 = f32[8192,80]{1,0:T(8,128)} copy-done((f32[8192,80]{1,0:T(8,128)}, f32[8192,80]{1,0:T(8,128)S(1)}, u32[]{:S(2)}) %copy-start.8) | copy-done | bytes 2621464
  36.0 4.9 %collective-permute-start.6 = (bf16[20,48,128]{2,1,0:T(8,128)(2,1)}, bf16[20,48,128]{2,1,0:T(8,128)(2,1)}, u32[]{:S(2)}, u32[]{:S(2)}) collective-permute-start(bf16[20,48,128]{2,1,0:T(8,128)(2,1)} %get-tuple-element.79), channel_id=1, source_target_pairs={{0,4},{4,8},{8,12},{12,0},{1,5},{5,9},{9,13},{13,1},{2,6},{6,10},{... | collective-permute-start | bytes 737288 | tf_op jit(solution)/shard_map/ppermute | solution.py:47
  40.8 0.0 collective-permute-done.5.refs_2_
  40.8 20.4 %collective-permute-done.4.refs_1_ = bf16[20,80,128]{2,1,0:T(8,128)(2,1)} collective-permute-done((bf16[20,80,128]{2,1,0:T(8,128)(2,1)}, bf16[20,80,128]{2,1,0:T(8,128)(2,1)}, u32[]{:S(2)}, u32[]{:S(2)}) %collective-permute-start.4) | collective-permute-done | bytes 409632 | tf_op jit(solution)/shard_map/ppermute | solution.py:47
  61.2 0.0 collective-permute-start.7
  61.3 2.2 %copy-done.1 = f32[8192,80]{1,0:T(8,128)S(1)} copy-done((f32[8192,80]{1,0:T(8,128)S(1)}, f32[8192,80]{1,0:T(8,128)}, u32[]{:S(2)}) %copy-start.1) | copy-done | bytes 2621464
  63.4 2.2 %copy-done.9 = f32[8192,80]{1,0:T(8,128)S(1)} copy-done((f32[8192,80]{1,0:T(8,128)S(1)}, f32[8192,80]{1,0:T(8,128)}, u32[]{:S(2)}) %copy-start.9) | copy-done | bytes 2621464
  65.6 6.1 %gather_first.2 = (f32[8192,80]{1,0:T(8,128)S(1)}, bf16[80,2048]{1,0:T(8,128)(2,1)S(1)}) custom-call(s32[4]{0:T(128)S(1)} %get-tuple-element.95.bases, s32[4,20]{1,0:T(4,128)S(1)} %bitcast.12, s32[8192]{0:T(1024)S(1)} %copy-done.10, f32[8192,80]{1,0:T(8,128)S(1)} %copy-done.9, f32[8192,80]{1,0:T(8,128)S(1)} %copy-done.1, bf16[80,128,128]{2,1,0:T(8,128)(2,1)S(1)} %bitcast.7, ...), custom_call_target="tpu_custom_call" | custom-call | bytes 4194304 | tf_op jit(solution)/shard_map/gather_first/pallas_call | solution.py:32
  71.7 3.1 %gather_next.8 = bf16[80,2048]{1,0:T(8,128)(2,1)S(1)} custom-call(s32[4]{0:T(128)S(1)} %get-tuple-element.95.bases, s32[8192]{0:T(1024)S(1)} %copy-done.10, f32[8192,80]{1,0:T(8,128)S(1)} %get-tuple-element.76.total), custom_call_target="tpu_custom_call" | custom-call | bytes 65536 | tf_op jit(solution)/shard_map/gather_next/pallas_call | solution.py:32
  74.9 3.1 %gather_next.7 = bf16[80,2048]{1,0:T(8,128)(2,1)S(1)} custom-call(s32[4]{0:T(128)S(1)} %get-tuple-element.95.bases, s32[8192]{0:T(1024)S(1)} %copy-done.10, f32[8192,80]{1,0:T(8,128)S(1)} %get-tuple-element.76.total), custom_call_target="tpu_custom_call" | custom-call | bytes 65536 | tf_op jit(solution)/shard_map/gather_next/pallas_call | solution.py:32
  78.0 1.5 %collective-permute-start.10 = (bf16[80,2048]{1,0:T(8,128)(2,1)S(1)}, bf16[80,2048]{1,0:T(8,128)(2,1)S(1)}, u32[]{:S(2)}, u32[]{:S(2)}) collective-permute-start(bf16[80,2048]{1,0:T(8,128)(2,1)S(1)} %gather_next.8), channel_id=1, source_target_pairs={{0,2},{1,3},{2,0},{3,1},{4,6},{5,7},{6,4},{7,5},{8,10},{9,11},{10,... | collective-permute-start | bytes 983048 | tf_op jit(solution)/shard_map/ppermute | solution.py:51
  79.6 0.0 collective-permute-start.9
  79.6 0.0 collective-permute-done.6.refs_0_
  79.6 0.7 collective-permute-start.11
  80.2 3.1 %gather_next.6.refs_0_ = bf16[80,2048]{1,0:T(8,128)(2,1)S(1)} custom-call(s32[4]{0:T(128)S(1)} %get-tuple-element.95.bases, s32[8192]{0:T(1024)S(1)} %copy-done.10, f32[8192,80]{1,0:T(8,128)S(1)} %get-tuple-element.76.total), custom_call_target="tpu_custom_call" | custom-call | bytes 65536 | tf_op jit(solution)/shard_map/gather_next/pallas_call | solution.py:32
  83.4 0.0 collective-permute-done.7.refs_1_
  83.4 5.7 %gather_first.3 = (f32[8192,48]{1,0:T(8,128)S(1)}, bf16[48,2048]{1,0:T(8,128)(2,1)S(1)}) custom-call(s32[4]{0:T(128)S(1)} %get-tuple-element.95.bases, s32[4,20]{1,0:T(4,128)S(1)} %bitcast.13, s32[8192]{0:T(1024)S(1)} %copy-done.10, f32[8192,48]{1,0:T(8,128)S(1)} %copy-done.7, f32[8192,80]{1,0:T(8,128)S(1)} %copy-done.2, bf16[80,128,128]{2,1,0:T(8,128)(2,1)S(1)} %bitcast.8, ...), custom_call_target="tpu_custom_call" | custom-call | bytes 4194304 | tf_op jit(solution)/shard_map/gather_first/pallas_call | solution.py:32
  89.1 1.1 %collective-permute-start.12 = (bf16[48,2048]{1,0:T(8,128)(2,1)S(1)}, bf16[48,2048]{1,0:T(8,128)(2,1)S(1)}, u32[]{:S(2)}, u32[]{:S(2)}) collective-permute-start(bf16[48,2048]{1,0:T(8,128)(2,1)S(1)} %get-tuple-element.89), channel_id=1, source_target_pairs={{0,3},{1,2},{2,1},{3,0},{4,7},{5,6},{6,5},{7,4},{8,11},{9,10},{10,... | collective-permute-start | bytes 589832 | tf_op jit(solution)/shard_map/ppermute | solution.py:51
  90.3 3.1 %gather_next.9 = (bf16[48,1536]{1,0:T(8,128)(2,1)S(1)}, bf16[48,512]{1,0:T(8,128)(2,1)S(1)}) custom-call(s32[4]{0:T(128)S(1)} %get-tuple-element.95.bases, s32[8192]{0:T(1024)S(1)} %copy-done.10, f32[8192,48]{1,0:T(8,128)S(1)} %get-tuple-element.92.total), custom_call_target="tpu_custom_call" | custom-call | bytes 65536 | tf_op jit(solution)/shard_map/gather_next/pallas_call | solution.py:32
  93.4 0.6 collective-permute-start.13
  94.0 0.0 collective-permute-done.10.refs_2_
  94.0 0.0 collective-permute-done.9.refs_1_
  94.0 3.1 %gather_next.10 = (bf16[48,1024]{1,0:T(8,128)(2,1)S(1)}, bf16[48,1024]{1,0:T(8,128)(2,1)S(1)}) custom-call(s32[4]{0:T(128)S(1)} %get-tuple-element.95.bases, s32[8192]{0:T(1024)S(1)} %copy-done.10, f32[8192,48]{1,0:T(8,128)S(1)} %get-tuple-element.92.total), custom_call_target="tpu_custom_call" | custom-call | bytes 65536 | tf_op jit(solution)/shard_map/gather_next/pallas_call | solution.py:32
  97.2 1.2 %collective-permute-start.15 = (bf16[48,1024]{1,0:T(8,128)(2,1)S(1)}, bf16[48,1024]{1,0:T(8,128)(2,1)S(1)}, u32[]{:S(2)}, u32[]{:S(2)}) collective-permute-start(bf16[48,1024]{1,0:T(8,128)(2,1)S(1)} %get-tuple-element.93), channel_id=1, source_target_pairs={{0,1},{1,0},{2,3},{3,2},{4,5},{5,4},{6,7},{7,6},{8,9},{9,8},{10,11... | collective-permute-start | bytes 294920 | tf_op jit(solution)/shard_map/ppermute | solution.py:51
  98.3 0.1 collective-permute-start.16
  98.4 1.5 %collective-permute-start.14 = (bf16[48,512]{1,0:T(8,128)(2,1)S(1)}, bf16[48,512]{1,0:T(8,128)(2,1)S(1)}, u32[]{:S(2)}, u32[]{:S(2)}) collective-permute-start(bf16[48,512]{1,0:T(8,128)(2,1)S(1)} %get-tuple-element.91), channel_id=1, source_target_pairs={{0,2},{1,3},{2,0},{3,1},{4,6},{5,7},{6,4},{7,5},{8,10},{9,11},{10,... | collective-permute-start | bytes 147464 | tf_op jit(solution)/shard_map/ppermute | solution.py:51
  99.9 3.1 %gather_next.11.refs_9_ = bf16[48,2048]{1,0:T(8,128)(2,1)S(1)} custom-call(s32[4]{0:T(128)S(1)} %get-tuple-element.95.bases, s32[8192]{0:T(1024)S(1)} %copy-done.10, f32[8192,48]{1,0:T(8,128)S(1)} %get-tuple-element.92.total), custom_call_target="tpu_custom_call" | custom-call | bytes 65536 | tf_op jit(solution)/shard_map/gather_next/pallas_call | solution.py:32
  103.1 2.8 %mix.1 = bf16[512,2048]{1,0:T(8,128)(2,1)} custom-call(s32[4]{0:T(128)S(1)} %get-tuple-element.96.starts, bf16[512,512]{1,0:T(8,128)(2,1)S(1)} %bitcast.9, f32[512,128]{1,0:T(8,128)S(1)} %get-tuple-element.56.bias, bf16[80,2048]{1,0:T(8,128)(2,1)S(1)} %gather_next.6.refs_0_, bf16[80,2048]{1,0:T(8,128)(2,1)S(1)} %collective-permute-done.9.refs_1_, ...), custom_call_target="tpu_custom_call" | custom-call | flops 1073741824 | bytes 5242880 | tf_op jit(solution)/shard_map/mix/pallas_call | solution.py:291
  (38 shorter events, 0.1 us)
Async XLA Ops:
  0.0 18.0 %copy-start.3 = (bf16[1,4,20,128,128]{4,3,2,1,0:T(8,128)(2,1)S(1)}, bf16[1,4,20,128,128]{4,3,2,1,0:T(8,128)(2,1)}, u32[]{:S(2)}) copy-start(bf16[1,4,20,128,128]{4,3,2,1,0:T(8,128)(2,1)} %param.11) | copy-start | bytes 7864324
  0.0 9.4 %collective-permute-start.2 = (s32[4,20]{1,0:T(4,128)}, s32[4,20]{1,0:T(4,128)S(1)}, u32[]{:S(2)}, u32[]{:S(2)}) collective-permute-start(s32[4,20]{1,0:T(4,128)} %bitcast.15), channel_id=1, source_target_pairs={{0,4},{4,8},{8,12},{12,0},{1,5},{5,9},{9,13},{13,1},{2,6},{6,10},{... | collective-permute-start | bytes 968 | tf_op jit(solution)/shard_map/ppermute | solution.py:47
  3.0 6.4 %collective-permute-start.1 = (s32[4,20]{1,0:T(4,128)}, s32[4,20]{1,0:T(4,128)S(1)}, u32[]{:S(2)}, u32[]{:S(2)}) collective-permute-start(s32[4,20]{1,0:T(4,128)} %bitcast.16), channel_id=1, source_target_pairs={{0,8},{4,12},{8,0},{12,4},{1,9},{5,13},{9,1},{13,5},{2,10},{6,14},... | collective-permute-start | bytes 968 | tf_op jit(solution)/shard_map/ppermute | solution.py:47
  5.6 3.8 %collective-permute-start = (s32[4,20]{1,0:T(4,128)}, s32[4,20]{1,0:T(4,128)S(1)}, u32[]{:S(2)}, u32[]{:S(2)}) collective-permute-start(s32[4,20]{1,0:T(4,128)} %bitcast.17), channel_id=1, source_target_pairs={{0,12},{4,0},{8,4},{12,8},{1,13},{5,1},{9,5},{13,9},{2,14},{6,2},{... | collective-permute-start | bytes 968 | tf_op jit(solution)/shard_map/ppermute | solution.py:47
  7.0 1.6 %copy-start.11 = (bf16[128,8192]{1,0:T(8,128)(2,1)S(1)}, bf16[128,8192]{1,0:T(8,128)(2,1)}, u32[]{:S(2)}) copy-start(bf16[128,8192]{1,0:T(8,128)(2,1)} %panel.1) | copy-start | bytes 6291460
  8.6 0.7 copy-start.13
  9.2 8.7 %copy-start.12 = (s32[1,4,20]{2,1,0:T(4,128)S(1)}, s32[1,4,20]{2,1,0:T(4,128)}, u32[]{:S(2)}) copy-start(s32[1,4,20]{2,1,0:T(4,128)} %param.9) | copy-start | bytes 964
  11.6 1.3 %copy-start.4 = (bf16[128,8192]{1,0:T(8,128)(2,1)}, bf16[128,8192]{1,0:T(8,128)(2,1)S(1)}, u32[]{:S(2)}) copy-start(bf16[128,8192]{1,0:T(8,128)(2,1)S(1)} %get-tuple-element.52.panel.refs_3_) | copy-start | bytes 6291460
  12.9 23.1 %collective-permute-start.3 = (bf16[20,80,128]{2,1,0:T(8,128)(2,1)}, bf16[20,80,128]{2,1,0:T(8,128)(2,1)}, u32[]{:S(2)}, u32[]{:S(2)}) collective-permute-start(bf16[20,80,128]{2,1,0:T(8,128)(2,1)} %get-tuple-element.68), channel_id=1, source_target_pairs={{0,4},{4,8},{8,12},{12,0},{1,5},{5,9},{9,13},{13,1},{2,6},{6,10},{... | collective-permute-start | bytes 1228808 | tf_op jit(solution)/shard_map/ppermute | solution.py:47
  13.6 27.3 %collective-permute-start.5 = (bf16[20,80,128]{2,1,0:T(8,128)(2,1)}, bf16[20,80,128]{2,1,0:T(8,128)(2,1)}, u32[]{:S(2)}, u32[]{:S(2)}) collective-permute-start(bf16[20,80,128]{2,1,0:T(8,128)(2,1)} %get-tuple-element.74), channel_id=1, source_target_pairs={{0,12},{4,0},{8,4},{12,8},{1,13},{5,1},{9,5},{13,9},{2,14},{6,2},{... | collective-permute-start | bytes 1228808 | tf_op jit(solution)/shard_map/ppermute | solution.py:47
  16.7 44.5 %collective-permute-start.4 = (bf16[20,80,128]{2,1,0:T(8,128)(2,1)}, bf16[20,80,128]{2,1,0:T(8,128)(2,1)}, u32[]{:S(2)}, u32[]{:S(2)}) collective-permute-start(bf16[20,80,128]{2,1,0:T(8,128)(2,1)} %get-tuple-element.71), channel_id=1, source_target_pairs={{0,8},{4,12},{8,0},{12,4},{1,9},{5,13},{9,1},{13,5},{2,10},{6,14},... | collective-permute-start | bytes 1228808 | tf_op jit(solution)/shard_map/ppermute | solution.py:47
  18.0 4.6 %copy-start.5 = (bf16[128,8192]{1,0:T(8,128)(2,1)S(1)}, bf16[128,8192]{1,0:T(8,128)(2,1)}, u32[]{:S(2)}) copy-start(bf16[128,8192]{1,0:T(8,128)(2,1)} %copy-done.4) | copy-start | bytes 6291460
  18.0 8.0 %copy-start.14 = (s32[1,4,20]{2,1,0:T(4,128)S(1)}, s32[1,4,20]{2,1,0:T(4,128)}, u32[]{:S(2)}) copy-start(s32[1,4,20]{2,1,0:T(4,128)} %param.10) | copy-start | bytes 964
  22.5 9.3 %copy-start = (f32[8192,80]{1,0:T(8,128)}, f32[8192,80]{1,0:T(8,128)S(1)}, u32[]{:S(2)}) copy-start(f32[8192,80]{1,0:T(8,128)S(1)} %degrees.1.inverse) | copy-start | bytes 7864324
  24.6 0.7 copy-start.15
  25.3 0.7 copy-start.16
  26.0 35.2 %copy-start.17 = (s32[4]{0:T(128)S(1)}, s32[4]{0:T(128)}, u32[]{:S(2)}) copy-start(s32[4]{0:T(128)} %constant.10.clone) | copy-start | bytes 52
  26.0 35.2 %copy-start.10 = (s32[8192]{0:T(1024)S(1)}, s32[8192]{0:T(1024)}, u32[]{:S(2)}) copy-start(s32[8192]{0:T(1024)} %order.15) | copy-start | bytes 98308
  31.9 2.0 %copy-start.6 = (f32[8192,48]{1,0:T(8,128)}, f32[8192,48]{1,0:T(8,128)S(1)}, u32[]{:S(2)}) copy-start(f32[8192,48]{1,0:T(8,128)S(1)} %get-tuple-element.78.acc) | copy-start | bytes 4718596
  33.9 2.0 %copy-start.8 = (f32[8192,80]{1,0:T(8,128)}, f32[8192,80]{1,0:T(8,128)S(1)}, u32[]{:S(2)}) copy-start(f32[8192,80]{1,0:T(8,128)S(1)} %get-tuple-element.58.acc) | copy-start | bytes 7864324
  36.0 43.6 %collective-permute-start.6 = (bf16[20,48,128]{2,1,0:T(8,128)(2,1)}, bf16[20,48,128]{2,1,0:T(8,128)(2,1)}, u32[]{:S(2)}, u32[]{:S(2)}) collective-permute-start(bf16[20,48,128]{2,1,0:T(8,128)(2,1)} %get-tuple-element.79), channel_id=1, source_target_pairs={{0,4},{4,8},{8,12},{12,0},{1,5},{5,9},{9,13},{13,1},{2,6},{6,10},{... | collective-permute-start | bytes 737288 | tf_op jit(solution)/shard_map/ppermute | solution.py:47
  61.2 22.1 %collective-permute-start.7 = (bf16[20,48,128]{2,1,0:T(8,128)(2,1)}, bf16[20,48,128]{2,1,0:T(8,128)(2,1)S(1)}, u32[]{:S(2)}, u32[]{:S(2)}) collective-permute-start(bf16[20,48,128]{2,1,0:T(8,128)(2,1)} %copy-done.16), channel_id=1, source_target_pairs={{0,8},{4,12},{8,0},{12,4},{1,9},{5,13},{9,1},{13,5},{2,10},{6,14},... | collective-permute-start | bytes 737288 | tf_op jit(solution)/shard_map/ppermute | solution.py:47
  61.2 22.1 %collective-permute-start.8 = (bf16[20,48,128]{2,1,0:T(8,128)(2,1)}, bf16[20,48,128]{2,1,0:T(8,128)(2,1)S(1)}, u32[]{:S(2)}, u32[]{:S(2)}) collective-permute-start(bf16[20,48,128]{2,1,0:T(8,128)(2,1)} %copy-done.15), channel_id=1, source_target_pairs={{0,12},{4,0},{8,4},{12,8},{1,13},{5,1},{9,5},{13,9},{2,14},{6,2},{... | collective-permute-start | bytes 737288 | tf_op jit(solution)/shard_map/ppermute | solution.py:47
  61.2 2.2 %copy-start.1 = (f32[8192,80]{1,0:T(8,128)S(1)}, f32[8192,80]{1,0:T(8,128)}, u32[]{:S(2)}) copy-start(f32[8192,80]{1,0:T(8,128)} %copy-done) | copy-start | bytes 7864324
  63.4 2.2 %copy-start.9 = (f32[8192,80]{1,0:T(8,128)S(1)}, f32[8192,80]{1,0:T(8,128)}, u32[]{:S(2)}) copy-start(f32[8192,80]{1,0:T(8,128)} %copy-done.8) | copy-start | bytes 7864324
  74.9 8.5 %copy-start.2 = (f32[8192,80]{1,0:T(8,128)S(1)}, f32[8192,80]{1,0:T(8,128)}, u32[]{:S(2)}) copy-start(f32[8192,80]{1,0:T(8,128)} %copy-done) | copy-start | bytes 7864324
  74.9 8.5 %copy-start.7 = (f32[8192,48]{1,0:T(8,128)S(1)}, f32[8192,48]{1,0:T(8,128)}, u32[]{:S(2)}) copy-start(f32[8192,48]{1,0:T(8,128)} %copy-done.6) | copy-start | bytes 4718596
  78.0 16.0 %collective-permute-start.10 = (bf16[80,2048]{1,0:T(8,128)(2,1)S(1)}, bf16[80,2048]{1,0:T(8,128)(2,1)S(1)}, u32[]{:S(2)}, u32[]{:S(2)}) collective-permute-start(bf16[80,2048]{1,0:T(8,128)(2,1)S(1)} %gather_next.8), channel_id=1, source_target_pairs={{0,2},{1,3},{2,0},{3,1},{4,6},{5,7},{6,4},{7,5},{8,10},{9,11},{10,... | collective-permute-start | bytes 983048 | tf_op jit(solution)/shard_map/ppermute | solution.py:51
  79.6 14.5 %collective-permute-start.9 = (bf16[80,2048]{1,0:T(8,128)(2,1)S(1)}, bf16[80,2048]{1,0:T(8,128)(2,1)S(1)}, u32[]{:S(2)}, u32[]{:S(2)}) collective-permute-start(bf16[80,2048]{1,0:T(8,128)(2,1)S(1)} %get-tuple-element.84), channel_id=1, source_target_pairs={{0,3},{1,2},{2,1},{3,0},{4,7},{5,6},{6,5},{7,4},{8,11},{9,10},{10,... | collective-permute-start | bytes 983048 | tf_op jit(solution)/shard_map/ppermute | solution.py:51
  79.6 14.5 %collective-permute-start.11 = (bf16[80,2048]{1,0:T(8,128)(2,1)S(1)}, bf16[80,2048]{1,0:T(8,128)(2,1)S(1)}, u32[]{:S(2)}, u32[]{:S(2)}) collective-permute-start(bf16[80,2048]{1,0:T(8,128)(2,1)S(1)} %gather_next.7), channel_id=1, source_target_pairs={{0,1},{1,0},{2,3},{3,2},{4,5},{5,4},{6,7},{7,6},{8,9},{9,8},{10,11... | collective-permute-start | bytes 983048 | tf_op jit(solution)/shard_map/ppermute | solution.py:51
  89.1 13.9 %collective-permute-start.12 = (bf16[48,2048]{1,0:T(8,128)(2,1)S(1)}, bf16[48,2048]{1,0:T(8,128)(2,1)S(1)}, u32[]{:S(2)}, u32[]{:S(2)}) collective-permute-start(bf16[48,2048]{1,0:T(8,128)(2,1)S(1)} %get-tuple-element.89), channel_id=1, source_target_pairs={{0,3},{1,2},{2,1},{3,0},{4,7},{5,6},{6,5},{7,4},{8,11},{9,10},{10,... | collective-permute-start | bytes 589832 | tf_op jit(solution)/shard_map/ppermute | solution.py:51
  93.4 9.6 %collective-permute-start.13 = (bf16[48,1536]{1,0:T(8,128)(2,1)S(1)}, bf16[48,1536]{1,0:T(8,128)(2,1)S(1)}, u32[]{:S(2)}, u32[]{:S(2)}) collective-permute-start(bf16[48,1536]{1,0:T(8,128)(2,1)S(1)} %get-tuple-element.90), channel_id=1, source_target_pairs={{0,2},{1,3},{2,0},{3,1},{4,6},{5,7},{6,4},{7,5},{8,10},{9,11},{10,... | collective-permute-start | bytes 442376 | tf_op jit(solution)/shard_map/ppermute | solution.py:51
  97.2 5.9 %collective-permute-start.15 = (bf16[48,1024]{1,0:T(8,128)(2,1)S(1)}, bf16[48,1024]{1,0:T(8,128)(2,1)S(1)}, u32[]{:S(2)}, u32[]{:S(2)}) collective-permute-start(bf16[48,1024]{1,0:T(8,128)(2,1)S(1)} %get-tuple-element.93), channel_id=1, source_target_pairs={{0,1},{1,0},{2,3},{3,2},{4,5},{5,4},{6,7},{7,6},{8,9},{9,8},{10,11... | collective-permute-start | bytes 294920 | tf_op jit(solution)/shard_map/ppermute | solution.py:51
  98.3 4.7 %collective-permute-start.16 = (bf16[48,1024]{1,0:T(8,128)(2,1)S(1)}, bf16[48,1024]{1,0:T(8,128)(2,1)S(1)}, u32[]{:S(2)}, u32[]{:S(2)}) collective-permute-start(bf16[48,1024]{1,0:T(8,128)(2,1)S(1)} %get-tuple-element.94), channel_id=1, source_target_pairs={{0,1},{1,0},{2,3},{3,2},{4,5},{5,4},{6,7},{7,6},{8,9},{9,8},{10,11... | collective-permute-start | bytes 294920 | tf_op jit(solution)/shard_map/ppermute | solution.py:51
  98.4 4.6 %collective-permute-start.14 = (bf16[48,512]{1,0:T(8,128)(2,1)S(1)}, bf16[48,512]{1,0:T(8,128)(2,1)S(1)}, u32[]{:S(2)}, u32[]{:S(2)}) collective-permute-start(bf16[48,512]{1,0:T(8,128)(2,1)S(1)} %get-tuple-element.91), channel_id=1, source_target_pairs={{0,2},{1,3},{2,0},{3,1},{4,6},{5,7},{6,4},{7,5},{8,10},{9,11},{10,... | collective-permute-start | bytes 147464 | tf_op jit(solution)/shard_map/ppermute | solution.py:51

commit v5 on v4

v5 whole, which is shorter than its diff:
```python
import functools

import jax
import jax.numpy as jnp
from jax import lax
from jax.experimental import pallas as pl
from jax.experimental.pallas import tpu as pltpu
from jax.sharding import PartitionSpec as P

NN = (((1,), (0,)), ((), ()))
NT = (((1,), (1,)), ((), ()))
VMEM = pl.BlockSpec(memory_space=pltpu.VMEM)
SMEM = pl.BlockSpec(memory_space=pltpu.SMEM)
ANY = pl.BlockSpec(memory_space=pl.ANY)
CHUNK = 256
UNROLL = 64


def dot(a, b, dims):
    return lax.dot_general(a, b, dims, preferred_element_type=jnp.float32)


def padded(shape, dtype):
    rows = 1
    for extent in shape[:-1]:
        rows *= extent
    return rows * -(-shape[-1] // 128) * 128 * jnp.dtype(dtype).itemsize


def call(kernel, name, scalars, arrays, outs, scratch=(), moved=2**16):
    held = sum(padded(a.shape, a.dtype) for a in list(arrays) + list(outs))
    held += sum(padded(shape, dtype) for shape, dtype in scratch)
    return pl.pallas_call(
        kernel,
        out_shape=list(outs),
        in_specs=[SMEM] * len(scalars) + [VMEM] * len(arrays),
        out_specs=[VMEM] * len(outs),
        scratch_shapes=[pltpu.VMEM(shape, dtype) for shape, dtype in scratch],
        compiler_params=pltpu.CompilerParams(vmem_limit_bytes=held + 2**20),
        cost_estimate=pl.CostEstimate(flops=0, bytes_accessed=moved, transcendentals=0),
        name=name,
    )(*scalars, *arrays)


def shifted(value, axis, steps):
    count = lax.axis_size(axis)
    pairs = [(source, (source + steps) % count) for source in range(count)]
    return lax.ppermute(value, axis, pairs)


def traded(value, axis, k):
    return lax.ppermute(value, axis, [(i, i ^ k) for i in range(lax.axis_size(axis))])


def cuts(width):
    first = width * 5 // 8 // 16 * 16
    return ((0, first), (first, width - first))


def identity(size):
    row = lax.broadcasted_iota(jnp.int32, (size, size), 0)
    col = lax.broadcasted_iota(jnp.int32, (size, size), 1)
    return (row == col).astype(jnp.float32).astype(jnp.bfloat16)


def stage_kernel(panel, out):
    out[...] = panel[...]


def staged(panel):
    shape = jax.ShapeDtypeStruct(panel.shape, panel.dtype)
    return call(stage_kernel, "stage", [], [panel], [shape])[0]


def pack_kernel(low, size, offsets, slots, tile, *refs):
    asked, panel = refs[:offsets], refs[offsets]
    outs, sems = refs[offsets + 1 : -1], refs[-1]
    for s in range(offsets):

        def body(t, carry, s=s):
            at = pl.multiple_of(asked[s][s + 1, t] * tile, tile)
            pltpu.make_async_copy(
                panel.at[pl.ds(low, size), pl.ds(at, tile)], outs[s].at[t], sems.at[s]
            ).start()
            return carry

        lax.fori_loop(0, slots, body, 0, unroll=4)
    for s in range(offsets):
        pltpu.make_async_copy(outs[s], outs[s], sems.at[s]).wait()


def pack(panel, asked, low, size, tile):
    offsets, slots = len(asked), asked[0].shape[1]
    return pl.pallas_call(
        functools.partial(pack_kernel, low, size, offsets, slots, tile),
        out_shape=[jax.ShapeDtypeStruct((slots, size, tile), panel.dtype)] * offsets,
        in_specs=[SMEM] * offsets + [ANY],
        out_specs=[ANY] * offsets,
        scratch_shapes=[pltpu.SemaphoreType.DMA((offsets,))],
        compiler_params=pltpu.CompilerParams(vmem_limit_bytes=2**20),
        cost_estimate=pl.CostEstimate(flops=0, bytes_accessed=2**16, transcendentals=0),
        name="pack",
    )(*asked, panel)


def own_kernel(ranges, blocks, slots, tile, rows, cols, panel, counts, bias, *refs):
    accs, (column, inverse, product) = refs[:-3], refs[-3:]
    lanes = inverse.shape[1]
    row_tiles = panel.shape[1] // tile
    eye = identity(tile)
    ones = jnp.ones((tile, lanes), jnp.bfloat16)
    column[...] = jnp.broadcast_to(bias[...], column.shape[::-1]).T
    inverse[...] = jnp.ones(inverse.shape, jnp.float32)

    def block(s, carry):
        def multiply(t, inner):
            product[t] = dot(counts[s * slots + t], ones, NN)
            return inner

        def add(t, inner):
            at = pl.multiple_of(rows[s, t] * tile, tile)
            inverse[pl.ds(at, tile), :] += product[t]
            return inner

        lax.fori_loop(0, slots, multiply, 0, unroll=10)
        lax.fori_loop(0, slots, add, 0)
        return carry

    lax.fori_loop(0, blocks, block, 0)

    def start(r, carry):
        at = pl.multiple_of(r * tile, tile)
        scale = 1.0 / inverse[pl.ds(at, tile), :]
        inverse[pl.ds(at, tile), :] = scale
        for acc, (low, size) in zip(accs, ranges):
            here = dot(eye, panel[pl.ds(low, size), pl.ds(at, tile)], NT)
            acc[pl.ds(at, tile), pl.ds(0, size)] = here * scale[:, :size]
            acc[pl.ds(at, tile), pl.ds(size, 1)] = scale[:, :1]
        return carry

    lax.fori_loop(0, row_tiles, start, 0, unroll=4)

    for acc, (low, size) in zip(accs, ranges):

        def multiply(t, carry, low=low, size=size):
            col = pl.multiple_of(cols[0, t] * tile, tile)
            product[t, :, :size] = dot(counts[t], panel[pl.ds(low, size), pl.ds(col, tile)], NT)
            return carry

        def add(t, carry, acc=acc, size=size):
            at = pl.multiple_of(rows[0, t] * tile, tile)
            acc[pl.ds(at, tile), pl.ds(0, size)] += (
                product[t, :, :size] * inverse[pl.ds(at, tile), :size]
            )
            return carry

        lax.fori_loop(0, slots, multiply, 0, unroll=10)
        lax.fori_loop(0, slots, add, 0)


def own(panel, rows, cols, counts, bias, ranges):
    blocks, slots = rows.shape
    nodes, tile = panel.shape[1], counts.shape[-1]
    lanes = max(size for _, size in ranges)
    shapes = [jax.ShapeDtypeStruct((nodes, size + 1), jnp.float32) for _, size in ranges]
    shapes.append(jax.ShapeDtypeStruct((bias.shape[0], 128), bias.dtype))
    outs = call(
        functools.partial(own_kernel, ranges, blocks, slots, tile),
        "own",
        [rows, cols],
        [panel, counts, bias[None, :]],
        shapes,
        [((nodes, lanes), jnp.float32), ((slots, tile, lanes), jnp.float32)],
    )
    return outs[:-1], outs[-1]


def pick(order, nodes, stage, outs):
    count, size = stage.shape
    eye = identity(size)

    def group(i, carry):
        at = pl.multiple_of(i * UNROLL, UNROLL)
        for u in range(UNROLL):
            source = order[at + u]
            stage[pl.ds(at + u, 1), :] = nodes[pl.ds(source, 1), :]
        return carry

    lax.fori_loop(0, count // UNROLL, group, 0)
    first = 0
    for out in outs:
        columns = out.shape[1]
        for at in range(0, columns, CHUNK):
            chunk = stage[pl.ds(first + at, CHUNK), :].astype(jnp.bfloat16)
            out[:, pl.ds(at, CHUNK)] = dot(eye, chunk, NT).astype(out.dtype)
        first += columns


def far_kernel(offsets, slots, tile, far, rows, *refs):
    orders, acc, counts = refs[:far], refs[far], refs[far + 1]
    got, total = refs[far + 2 : far + 2 + offsets], refs[far + 2 + offsets]
    outs, (product, stage) = refs[far + 3 + offsets : -2], refs[-2:]
    size = total.shape[1]
    total[...] = acc[:, :size]
    for s in range(offsets):

        def multiply(t, carry, s=s):
            product[t] = dot(counts[(s + 1) * slots + t], got[s][t], NT)
            return carry

        def add(t, carry, s=s):
            at = pl.multiple_of(rows[s + 1, t] * tile, tile)
            total[pl.ds(at, tile), :] += product[t] * acc[pl.ds(at, tile), pl.ds(size, 1)]
            return carry

        lax.fori_loop(0, slots, multiply, 0, unroll=10)
        lax.fori_loop(0, slots, add, 0)
    for order, out in zip(orders, outs):
        pick(order, total, stage, [out])


def gather_far(acc, rows, orders, counts, got):
    nodes, size = acc.shape[0], acc.shape[1] - 1
    slots, tile = rows.shape[1], counts.shape[-1]
    share, far = orders[0].shape[0], len(orders)
    outs = call(
        functools.partial(far_kernel, len(got), slots, tile, far),
        "gather_far",
        [rows, *orders],
        [acc, counts, *got],
        [jax.ShapeDtypeStruct((nodes, size), jnp.float32)]
        + [jax.ShapeDtypeStruct((size, share), jnp.bfloat16)] * far,
        [((slots, tile, size), jnp.float32), ((share, size), jnp.float32)],
        2**22,
    )
    return outs[0], outs[1:]


def next_kernel(order, total, *refs):
    pick(order, total, refs[-1], refs[:-1])


def gather_next(total, order, widths):
    size = total.shape[1]
    return call(
        next_kernel,
        "gather_next",
        [order],
        [total],
        [jax.ShapeDtypeStruct((size, width), jnp.bfloat16) for width in widths],
        [((sum(widths), size), jnp.float32)],
    )


def mix_kernel(places, starts, weight, bias, *refs):
    pieces, (out, nodes, ready, sems) = refs[:-4], refs[-4:]
    for piece, (i, low, first) in zip(pieces, places):
        height, columns = piece.shape
        at = pl.multiple_of(starts[i] + low, 16)
        nodes[pl.ds(at, height), pl.ds(first, columns)] = piece[...]
    copies = []
    for c in range(ready.shape[0]):
        step = ready.shape[2]
        mixed = dot(weight[...], nodes[:, pl.ds(c * step, step)], NN)
        ready[c] = jnp.maximum(mixed + bias[:, :1], 0.0).astype(out.dtype)
        copies.append(
            pltpu.make_async_copy(ready.at[c], out.at[:, pl.ds(c * step, step)], sems.at[c])
        )
        copies[-1].start()
    for copy in copies:
        copy.wait()


def mix(starts, weight, bias, placed, nodes):
    places, pieces = tuple(placed), list(placed.values())
    hidden, width = weight.shape
    step = min(512, nodes)
    return pl.pallas_call(
        functools.partial(mix_kernel, places),
        out_shape=jax.ShapeDtypeStruct((hidden, nodes), jnp.bfloat16),
        in_specs=[SMEM] + [VMEM] * (2 + len(pieces)),
        out_specs=ANY,
        scratch_shapes=[
            pltpu.VMEM((width, nodes), jnp.bfloat16),
            pltpu.VMEM((nodes // step, hidden, step), jnp.bfloat16),
            pltpu.SemaphoreType.DMA((nodes // step,)),
        ],
        compiler_params=pltpu.CompilerParams(vmem_limit_bytes=16 * 2**20),
        cost_estimate=pl.CostEstimate(
            flops=2 * hidden * width * nodes, bytes_accessed=5 * 2**20, transcendentals=0
        ),
        name="mix",
    )(starts, weight, bias, *pieces)


def on_device(features, tile_rows, tile_cols, tile_weights, order, weight, bias):
    width, nodes = features.shape
    _, blocks, slots, tile, _ = tile_weights.shape
    groups = lax.axis_size("grp")
    me = lax.axis_index("grp")
    share = nodes // groups
    ranges = cuts(width)
    rows = tile_rows.reshape(blocks, slots)
    cols = tile_cols.reshape(blocks, slots)
    counts = tile_weights.reshape(blocks * slots, tile, tile)

    ranks = list(range(groups - 1, -1, -1))
    whose = me ^ jnp.asarray(ranks, jnp.int32)
    far = groups - 2
    picks = [lax.dynamic_slice(order, ((me ^ k) * share,), (share,)) for k in ranks]

    asked = [shifted(cols, "blk", -s) for s in range(1, blocks)]
    *asked, panel = lax.optimization_barrier((*asked, staged(features)))
    sent = []
    for low, size in ranges:
        source = features if sent else panel
        sent.append(list(pack(source, asked, low, size, tile)))
        *asked, sent[-1][0] = lax.optimization_barrier((*asked, sent[-1][0]))
    accs, column = own(features, rows, cols, counts, bias, ranges)
    accs, across, picks, starts = lax.optimization_barrier(
        (accs, weight.T, picks, whose * width)
    )

    got = [[shifted(value, "blk", s + 1) for s, value in enumerate(sent[0])]]
    for later in sent[1:]:
        later, got[-1], accs = lax.optimization_barrier((later, got[-1], accs))
        got.append([shifted(value, "blk", s + 1) for s, value in enumerate(later)])

    pieces, waits, kept = {}, {}, {}
    for p, (low, size) in enumerate(ranges):
        last = p == len(ranges) - 1
        acc, kept = lax.optimization_barrier((accs[p], kept))
        pieces.update(kept)
        total, out_far = gather_far(acc, rows, picks[:far], counts, got[p])
        now = {(i, low, 0): traded(piece, "grp", ranks[i]) for i, piece in enumerate(out_far)}
        widths = (share,)
        if not last:
            kept = gather_next(total, picks[-1], (share,))[0]
            total, kept = lax.optimization_barrier((total, kept))
        else:
            total, waits = lax.optimization_barrier((total, waits))
            pieces.update(waits)
            widths = (share // 2, share // 2)
        first = 0
        for piece in gather_next(total, picks[far], widths):
            if not last:
                piece, got[p + 1] = lax.optimization_barrier((piece, got[p + 1]))
            now[far, low, first] = traded(piece, "grp", ranks[far])
            first += piece.shape[1]
        if last:
            kept = gather_next(total, picks[-1], (share,))[0]
        kept = {(groups - 1, low, 0): kept}
        waits = now
    pieces.update(waits)
    pieces.update(kept)
    return mix(starts, across, column, pieces, share)


def solution(mesh):
    in_specs = (
        P("grp", ("parts", "blk")),
        P(("parts", "blk"), None, None),
        P(("parts", "blk"), None, None),
        P(("parts", "blk"), None, None, None, None),
        P(("parts", "blk")),
        P(),
        P(),
    )
    out_specs = P(None, ("parts", "blk", "grp"))
    return jax.shard_map(
        on_device, mesh=mesh, in_specs=in_specs, out_specs=out_specs, check_vma=False
    )
```

time: 106 us -> 104 us (0.981)
  starting transfers between devices: 22.4 us -> 31.7 us
  local copies, waits for them, and re-layouts: 14.7 us -> 6.53 us
  waiting for transfers between devices: 20.4 us -> 14 us
  Pallas kernels: 48.1 us -> 50.8 us
    ppermute x9, starting transfers between devices: 15.7 us -> 27.2 us  [shifted(): return lax.ppermute(value, axis, pairs)]
    ppermute x9, waiting for transfers between devices: 20.4 us -> 10.5 us  [shifted(): return lax.ppermute(value, axis, pairs)]
    unnamed x37 -> x29, local copies, waits for them, and re-layouts: 14.7 us -> 6.51 us
    ppermute x8 -> x7, waiting for transfers between devices: 0.02 us -> 3.53 us  [traded(): lax.ppermute(value, axis, [(i, i ^ k) for i in range(lax.axis_size(axis))])]
    pallas_call x0 -> x2, Pallas kernels: none -> 3.06 us  [pack(): pl.pallas_call(functools.partial(pack_kernel, low, size, offsets, slots,...]
    ppermute x8 -> x7, starting transfers between devices: 6.7 us -> 4.48 us  [traded(): lax.ppermute(value, axis, [(i, i ^ k) for i in range(lax.axis_size(axis))])]
    pallas_call x13 -> x8, Pallas kernels: 45.3 us -> 44.9 us  [call(): pl.pallas_call(kernel, out_shape=list(outs), in_specs=[SMEM] * len(scalar...]
  transfers between devices with their start and end apart: 17 -> 16, of which waited for: 1 -> 3; matrix products, arithmetic and copies ran while one was open for 1% -> 1% of each run, Pallas kernels for 41% -> 45%
where the time goes in v5:
time: 104 us; the launch traced here: 103 us
  Pallas kernels  50.8 us (49%)
  starting transfers between devices  31.7 us (30%)
  waiting for transfers between devices  14 us (13%)
  local copies, waits for them, and re-layouts  6.53 us (6%)
    pallas_call x8, Pallas kernels, call(): pl.pallas_call(kernel, out_shape=list(outs), in_specs=[SMEM] * len(scalar...  44.9 us
    ppermute x9, starting transfers between devices, shifted(): return lax.ppermute(value, axis, pairs)  27.2 us
    ppermute x9, waiting for transfers between devices, shifted(): return lax.ppermute(value, axis, pairs)  10.5 us
    unnamed x29, local copies, waits for them, and re-layouts  6.51 us
    ppermute x7, starting transfers between devices, traded(): lax.ppermute(value, axis, [(i, i ^ k) for i in range(lax.axis_size(axis))])  4.48 us
    ppermute x7, waiting for transfers between devices, traded(): lax.ppermute(value, axis, [(i, i ^ k) for i in range(lax.axis_size(axis))])  3.53 us
    pallas_call x2, Pallas kernels, pack(): pl.pallas_call(functools.partial(pack_kernel, low, size, offsets, slots,...  3.06 us
    pallas_call x1, Pallas kernels, mix(): pl.pallas_call(functools.partial(mix_kernel, places), out_shape=jax.Shape...  2.79 us
  transfers between devices with their start and end apart: 16, of which 3 were waited for; matrix products, arithmetic and copies ran while one was open for 1% of the time, Pallas kernels for 45%

profile of v5, /device:TPU:0, one launch (start us, length us, event | category | flops | bytes accessed | tf_op | source)
XLA Modules:
  0.0 103.3 jit_solution(3078106628541120668)
XLA Ops:
  0.0 3.0 %collective-permute-start.2 = (s32[4,20]{1,0:T(4,128)}, s32[4,20]{1,0:T(4,128)S(1)}, u32[]{:S(2)}, u32[]{:S(2)}) collective-permute-start(s32[4,20]{1,0:T(4,128)} %bitcast.12), channel_id=1, source_target_pairs={{0,4},{4,8},{8,12},{12,0},{1,5},{5,9},{9,13},{13,1},{2,6},{6,10},{... | collective-permute-start | bytes 968 | tf_op jit(solution)/shard_map/ppermute | solution.py:48
  3.0 2.6 %collective-permute-start.1 = (s32[4,20]{1,0:T(4,128)}, s32[4,20]{1,0:T(4,128)S(1)}, u32[]{:S(2)}, u32[]{:S(2)}) collective-permute-start(s32[4,20]{1,0:T(4,128)} %bitcast.13), channel_id=1, source_target_pairs={{0,8},{4,12},{8,0},{12,4},{1,9},{5,13},{9,1},{13,5},{2,10},{6,14},... | collective-permute-start | bytes 968 | tf_op jit(solution)/shard_map/ppermute | solution.py:48
  5.6 1.3 %collective-permute-start = (s32[4,20]{1,0:T(4,128)}, s32[4,20]{1,0:T(4,128)S(1)}, u32[]{:S(2)}, u32[]{:S(2)}) collective-permute-start(s32[4,20]{1,0:T(4,128)} %bitcast.14), channel_id=1, source_target_pairs={{0,12},{4,0},{8,4},{12,8},{1,13},{5,1},{9,5},{13,9},{2,14},{6,2},{... | collective-permute-start | bytes 968 | tf_op jit(solution)/shard_map/ppermute | solution.py:48
  7.0 1.6 %copy-done.1 = bf16[128,8192]{1,0:T(8,128)(2,1)S(1)} copy-done((bf16[128,8192]{1,0:T(8,128)(2,1)S(1)}, bf16[128,8192]{1,0:T(8,128)(2,1)}, u32[]{:S(2)}) %copy-start.1) | copy-done | bytes 2097176
  8.6 0.1 stage.1.refs_3_
  8.7 0.0 collective-permute-done.2.refs_2_
  8.7 0.0 collective-permute-done.1.refs_1_
  8.7 0.7 collective-permute-done.refs_0_
  9.4 1.6 %pack.2 = (bf16[20,80,128]{2,1,0:T(8,128)(2,1)}, bf16[20,80,128]{2,1,0:T(8,128)(2,1)}, bf16[20,80,128]{2,1,0:T(8,128)(2,1)}) custom-call(s32[4,20]{1,0:T(4,128)S(1)} %collective-permute-done.refs_0_, s32[4,20]{1,0:T(4,128)S(1)} %collective-permute-done.1.refs_1_, s32[4,20]{1,0:T(4,128)S(1)} %collective-permute-done.2.refs_2_, bf16[128,8192]{1,0:T(8,128)(2,1)S(1)} %stage.1.refs_3_), custom_call_target="tpu_custom_call" | custom-call | bytes 65536 | tf_op jit(solution)/shard_map/pack/pallas_call | solution.py:94
  11.1 0.1 collective-permute-start.3
  11.2 3.6 %collective-permute-start.4 = (bf16[20,80,128]{2,1,0:T(8,128)(2,1)}, bf16[20,80,128]{2,1,0:T(8,128)(2,1)}, u32[]{:S(2)}, u32[]{:S(2)}) collective-permute-start(bf16[20,80,128]{2,1,0:T(8,128)(2,1)} %get-tuple-element.77), channel_id=1, source_target_pairs={{0,8},{4,12},{8,0},{12,4},{1,9},{5,13},{9,1},{13,5},{2,10},{6,14},... | collective-permute-start | bytes 1228808 | tf_op jit(solution)/shard_map/ppermute | solution.py:48
  14.8 0.1 collective-permute-start.5
  15.0 1.3 %copy.9 = bf16[512,512]{0,1:T(8,128)(2,1)S(1)} copy(bf16[512,512]{1,0:T(8,128)(2,1)} %param.13) | data formatting | bytes 1048576 | tf_op args[5]
  16.2 0.0 copy-start.13
  16.3 0.0 copy-start.2
  16.3 1.6 %copy-done.2 = bf16[128,8192]{1,0:T(8,128)(2,1)S(1)} copy-done((bf16[128,8192]{1,0:T(8,128)(2,1)S(1)}, bf16[128,8192]{1,0:T(8,128)(2,1)}, u32[]{:S(2)}) %copy-start.2) | copy-done | bytes 2097176
  17.9 0.7 copy-done.3
  18.6 0.7 copy-done.10
  19.2 0.7 copy-done.11
  19.9 9.5 %own.1 = (f32[8192,81]{1,0:T(8,128)S(1)}, f32[8192,49]{1,0:T(8,128)S(1)}, f32[512,128]{1,0:T(8,128)S(1)}) custom-call(s32[4,20]{1,0:T(4,128)S(1)} %bitcast.9, s32[4,20]{1,0:T(4,128)S(1)} %bitcast.15, bf16[128,8192]{1,0:T(8,128)(2,1)S(1)} %copy-done.2, bf16[80,128,128]{2,1,0:T(8,128)(2,1)S(1)} %bitcast.5, f32[1,512]{1,0:T(1,128)S(1)} %bitcast.16), custom_call_target="tpu_custom_call" | custom-call | bytes 65536 | tf_op jit(solution)/shard_map/own/pallas_call | solution.py:33
  29.5 1.4 %pack.3 = (bf16[20,48,128]{2,1,0:T(8,128)(2,1)S(1)}, bf16[20,48,128]{2,1,0:T(8,128)(2,1)S(1)}, bf16[20,48,128]{2,1,0:T(8,128)(2,1)S(1)}) custom-call(s32[4,20]{1,0:T(4,128)S(1)} %copy-done.9, s32[4,20]{1,0:T(4,128)S(1)} %copy-done.7, s32[4,20]{1,0:T(4,128)S(1)} %copy-done.5, bf16[128,8192]{1,0:T(8,128)(2,1)S(1)} %copy-done.2), custom_call_target="tpu_custom_call" | custom-call | bytes 65536 | tf_op jit(solution)/shard_map/pack/pallas_call | solution.py:94
  31.0 0.0 collective-permute-done.3.refs_4_
  31.0 9.8 %collective-permute-done.4.refs_5_ = bf16[20,80,128]{2,1,0:T(8,128)(2,1)} collective-permute-done((bf16[20,80,128]{2,1,0:T(8,128)(2,1)}, bf16[20,80,128]{2,1,0:T(8,128)(2,1)}, u32[]{:S(2)}, u32[]{:S(2)}) %collective-permute-start.4) | collective-permute-done | bytes 409632 | tf_op jit(solution)/shard_map/ppermute | solution.py:48
  40.8 0.0 collective-permute-done.5.refs_6_
  40.8 14.0 %collective-permute-start.6 = (bf16[20,48,128]{2,1,0:T(8,128)(2,1)S(1)}, bf16[20,48,128]{2,1,0:T(8,128)(2,1)S(1)}, u32[]{:S(2)}, u32[]{:S(2)}) collective-permute-start(bf16[20,48,128]{2,1,0:T(8,128)(2,1)S(1)} %get-tuple-element.95), channel_id=1, source_target_pairs={{0,4},{4,8},{8,12},{12,0},{1,5},{5,9},{9,13},{13,1},{2,6},{6,10},{... | collective-permute-start | bytes 737288 | tf_op jit(solution)/shard_map/ppermute | solution.py:48
  54.8 0.0 collective-permute-start.7
  54.8 2.4 %collective-permute-start.8 = (bf16[20,48,128]{2,1,0:T(8,128)(2,1)S(1)}, bf16[20,48,128]{2,1,0:T(8,128)(2,1)S(1)}, u32[]{:S(2)}, u32[]{:S(2)}) collective-permute-start(bf16[20,48,128]{2,1,0:T(8,128)(2,1)S(1)} %get-tuple-element.97), channel_id=1, source_target_pairs={{0,12},{4,0},{8,4},{12,8},{1,13},{5,1},{9,5},{13,9},{2,14},{6,2},{... | collective-permute-start | bytes 737288 | tf_op jit(solution)/shard_map/ppermute | solution.py:48
  57.2 12.4 %gather_far.2 = (f32[8192,80]{1,0:T(8,128)S(1)}, bf16[80,2048]{1,0:T(8,128)(2,1)S(1)}, bf16[80,2048]{1,0:T(8,128)(2,1)S(1)}) custom-call(s32[4,20]{1,0:T(4,128)S(1)} %bitcast.10, s32[2048]{0:T(1024)S(1)} %get-tuple-element.82.refs_0_, s32[2048]{0:T(1024)S(1)} %get-tuple-element.83.refs_1_, f32[8192,81]{1,0:T(8,128)S(1)} %get-tuple-element.84.refs_2_, ...), custom_call_target="tpu_custom_call" | custom-call | bytes 4194304 | tf_op jit(solution)/shard_map/gather_far/pallas_call | solution.py:33
  69.6 2.7 %gather_next.4.refs_0_ = bf16[80,2048]{1,0:T(8,128)(2,1)S(1)} custom-call(s32[2048]{0:T(1024)S(1)} %get-tuple-element.89.order, f32[8192,80]{1,0:T(8,128)S(1)} %get-tuple-element.94.total), custom_call_target="tpu_custom_call" | custom-call | bytes 65536 | tf_op jit(solution)/shard_map/gather_next/pallas_call | solution.py:33
  72.4 0.1 collective-permute-start.9
  72.4 1.6 %collective-permute-start.10 = (bf16[80,2048]{1,0:T(8,128)(2,1)S(1)}, bf16[80,2048]{1,0:T(8,128)(2,1)S(1)}, u32[]{:S(2)}, u32[]{:S(2)}) collective-permute-start(bf16[80,2048]{1,0:T(8,128)(2,1)S(1)} %get-tuple-element.103), channel_id=1, source_target_pairs={{0,2},{1,3},{2,0},{3,1},{4,6},{5,7},{6,4},{7,5},{8,10},{9,11},{10,... | collective-permute-start | bytes 983048 | tf_op jit(solution)/shard_map/ppermute | solution.py:52
  74.0 2.7 %gather_next.5 = bf16[80,2048]{1,0:T(8,128)(2,1)S(1)} custom-call(s32[2048]{0:T(1024)S(1)} %get-tuple-element.93.order, f32[8192,80]{1,0:T(8,128)S(1)} %get-tuple-element.94.total), custom_call_target="tpu_custom_call" | custom-call | bytes 65536 | tf_op jit(solution)/shard_map/gather_next/pallas_call | solution.py:33
  76.7 0.0 collective-permute-done.6.refs_4_
  76.7 0.0 collective-permute-done.7.refs_5_
  76.8 0.0 collective-permute-done.8.refs_6_
  76.8 0.3 collective-permute-start.11
  77.1 11.9 %gather_far.3 = (f32[8192,48]{1,0:T(8,128)S(1)}, bf16[48,2048]{1,0:T(8,128)(2,1)S(1)}, bf16[48,2048]{1,0:T(8,128)(2,1)S(1)}) custom-call(s32[4,20]{1,0:T(4,128)S(1)} %bitcast.11, s32[2048]{0:T(1024)S(1)} %get-tuple-element.82.refs_0_, s32[2048]{0:T(1024)S(1)} %get-tuple-element.83.refs_1_, f32[8192,49]{1,0:T(8,128)S(1)} %get-tuple-element.92.refs_2_, ...), custom_call_target="tpu_custom_call" | custom-call | bytes 4194304 | tf_op jit(solution)/shard_map/gather_far/pallas_call | solution.py:33
  89.0 1.2 %collective-permute-start.12 = (bf16[48,2048]{1,0:T(8,128)(2,1)S(1)}, bf16[48,2048]{1,0:T(8,128)(2,1)S(1)}, u32[]{:S(2)}, u32[]{:S(2)}) collective-permute-start(bf16[48,2048]{1,0:T(8,128)(2,1)S(1)} %get-tuple-element.108), channel_id=1, source_target_pairs={{0,3},{1,2},{2,1},{3,0},{4,7},{5,6},{6,5},{7,4},{8,11},{9,10},{10,... | collective-permute-start | bytes 589832 | tf_op jit(solution)/shard_map/ppermute | solution.py:52
  90.3 0.7 collective-permute-start.13
  91.0 0.0 collective-permute-done.9.refs_1_
  91.0 2.7 %gather_next.6 = (bf16[48,1024]{1,0:T(8,128)(2,1)S(1)}, bf16[48,1024]{1,0:T(8,128)(2,1)S(1)}) custom-call(s32[2048]{0:T(1024)S(1)} %get-tuple-element.93.order, f32[8192,48]{1,0:T(8,128)S(1)} %get-tuple-element.110.total), custom_call_target="tpu_custom_call" | custom-call | bytes 65536 | tf_op jit(solution)/shard_map/gather_next/pallas_call | solution.py:33
  93.7 0.1 collective-permute-start.14
  93.8 0.5 collective-permute-start.15
  94.3 2.7 %gather_next.7.refs_8_ = bf16[48,2048]{1,0:T(8,128)(2,1)S(1)} custom-call(s32[2048]{0:T(1024)S(1)} %get-tuple-element.89.order, f32[8192,48]{1,0:T(8,128)S(1)} %get-tuple-element.110.total), custom_call_target="tpu_custom_call" | custom-call | bytes 65536 | tf_op jit(solution)/shard_map/gather_next/pallas_call | solution.py:33
  97.0 3.5 %collective-permute-done.13.refs_5_ = bf16[48,2048]{1,0:T(8,128)(2,1)S(1)} collective-permute-done((bf16[48,2048]{1,0:T(8,128)(2,1)S(1)}, bf16[48,2048]{1,0:T(8,128)(2,1)S(1)}, u32[]{:S(2)}, u32[]{:S(2)}) %collective-permute-start.13) | collective-permute-done | bytes 196640 | tf_op jit(solution)/shard_map/ppermute | solution.py:52
  100.5 0.0 collective-permute-done.14.refs_6_
  100.5 0.0 collective-permute-done.15.refs_7_
  100.5 2.8 %mix.1 = bf16[512,2048]{1,0:T(8,128)(2,1)} custom-call(s32[4]{0:T(128)S(1)} %xor_multiply_fusion.starts, bf16[512,512]{1,0:T(8,128)(2,1)S(1)} %bitcast.8, f32[512,128]{1,0:T(8,128)S(1)} %get-tuple-element.63.bias, bf16[80,2048]{1,0:T(8,128)(2,1)S(1)} %gather_next.4.refs_0_, bf16[80,2048]{1,0:T(8,128)(2,1)S(1)} %collective-permute-done.9.refs_1_, ...), custom_call_target="tpu_custom_call" | custom-call | flops 1073741824 | bytes 5242880 | tf_op jit(solution)/shard_map/mix/pallas_call | solution.py:278
  (26 shorter events, 0.1 us)
Async XLA Ops:
  0.0 16.3 %copy-start = (bf16[1,4,20,128,128]{4,3,2,1,0:T(8,128)(2,1)S(1)}, bf16[1,4,20,128,128]{4,3,2,1,0:T(8,128)(2,1)}, u32[]{:S(2)}) copy-start(bf16[1,4,20,128,128]{4,3,2,1,0:T(8,128)(2,1)} %param.11) | copy-start | bytes 7864324
  0.0 8.7 %collective-permute-start.2 = (s32[4,20]{1,0:T(4,128)}, s32[4,20]{1,0:T(4,128)S(1)}, u32[]{:S(2)}, u32[]{:S(2)}) collective-permute-start(s32[4,20]{1,0:T(4,128)} %bitcast.12), channel_id=1, source_target_pairs={{0,4},{4,8},{8,12},{12,0},{1,5},{5,9},{9,13},{13,1},{2,6},{6,10},{... | collective-permute-start | bytes 968 | tf_op jit(solution)/shard_map/ppermute | solution.py:48
  3.0 5.7 %collective-permute-start.1 = (s32[4,20]{1,0:T(4,128)}, s32[4,20]{1,0:T(4,128)S(1)}, u32[]{:S(2)}, u32[]{:S(2)}) collective-permute-start(s32[4,20]{1,0:T(4,128)} %bitcast.13), channel_id=1, source_target_pairs={{0,8},{4,12},{8,0},{12,4},{1,9},{5,13},{9,1},{13,5},{2,10},{6,14},... | collective-permute-start | bytes 968 | tf_op jit(solution)/shard_map/ppermute | solution.py:48
  5.6 3.8 %collective-permute-start = (s32[4,20]{1,0:T(4,128)}, s32[4,20]{1,0:T(4,128)S(1)}, u32[]{:S(2)}, u32[]{:S(2)}) collective-permute-start(s32[4,20]{1,0:T(4,128)} %bitcast.14), channel_id=1, source_target_pairs={{0,12},{4,0},{8,4},{12,8},{1,13},{5,1},{9,5},{13,9},{2,14},{6,2},{... | collective-permute-start | bytes 968 | tf_op jit(solution)/shard_map/ppermute | solution.py:48
  7.0 1.6 %copy-start.1 = (bf16[128,8192]{1,0:T(8,128)(2,1)S(1)}, bf16[128,8192]{1,0:T(8,128)(2,1)}, u32[]{:S(2)}) copy-start(bf16[128,8192]{1,0:T(8,128)(2,1)} %refs_3_.1) | copy-start | bytes 6291460
  8.7 2.4 %copy-start.4 = (s32[4,20]{1,0:T(4,128)}, s32[4,20]{1,0:T(4,128)S(1)}, u32[]{:S(2)}) copy-start(s32[4,20]{1,0:T(4,128)S(1)} %collective-permute-done.2.refs_2_) | copy-start | bytes 964
  8.7 2.3 %copy-start.6 = (s32[4,20]{1,0:T(4,128)}, s32[4,20]{1,0:T(4,128)S(1)}, u32[]{:S(2)}) copy-start(s32[4,20]{1,0:T(4,128)S(1)} %collective-permute-done.1.refs_1_) | copy-start | bytes 964
  9.4 1.8 %copy-start.8 = (s32[4,20]{1,0:T(4,128)}, s32[4,20]{1,0:T(4,128)S(1)}, u32[]{:S(2)}) copy-start(s32[4,20]{1,0:T(4,128)S(1)} %collective-permute-done.refs_0_) | copy-start | bytes 964
  11.1 19.9 %collective-permute-start.3 = (bf16[20,80,128]{2,1,0:T(8,128)(2,1)}, bf16[20,80,128]{2,1,0:T(8,128)(2,1)S(1)}, u32[]{:S(2)}, u32[]{:S(2)}) collective-permute-start(bf16[20,80,128]{2,1,0:T(8,128)(2,1)} %get-tuple-element.76), channel_id=1, source_target_pairs={{0,4},{4,8},{8,12},{12,0},{1,5},{5,9},{9,13},{13,1},{2,6},{6,10},{... | collective-permute-start | bytes 1228808 | tf_op jit(solution)/shard_map/ppermute | solution.py:48
  11.2 29.6 %collective-permute-start.4 = (bf16[20,80,128]{2,1,0:T(8,128)(2,1)}, bf16[20,80,128]{2,1,0:T(8,128)(2,1)}, u32[]{:S(2)}, u32[]{:S(2)}) collective-permute-start(bf16[20,80,128]{2,1,0:T(8,128)(2,1)} %get-tuple-element.77), channel_id=1, source_target_pairs={{0,8},{4,12},{8,0},{12,4},{1,9},{5,13},{9,1},{13,5},{2,10},{6,14},... | collective-permute-start | bytes 1228808 | tf_op jit(solution)/shard_map/ppermute | solution.py:48
  14.8 26.0 %collective-permute-start.5 = (bf16[20,80,128]{2,1,0:T(8,128)(2,1)}, bf16[20,80,128]{2,1,0:T(8,128)(2,1)}, u32[]{:S(2)}, u32[]{:S(2)}) collective-permute-start(bf16[20,80,128]{2,1,0:T(8,128)(2,1)} %get-tuple-element.78), channel_id=1, source_target_pairs={{0,12},{4,0},{8,4},{12,8},{1,13},{5,1},{9,5},{13,9},{2,14},{6,2},{... | collective-permute-start | bytes 1228808 | tf_op jit(solution)/shard_map/ppermute | solution.py:48
  16.2 13.3 %copy-start.13 = (s32[4]{0:T(128)S(1)}, s32[4]{0:T(128)}, u32[]{:S(2)}) copy-start(s32[4]{0:T(128)} %constant.20.clone) | copy-start | bytes 52
  16.2 13.3 %copy-start.5 = (s32[4,20]{1,0:T(4,128)S(1)}, s32[4,20]{1,0:T(4,128)}, u32[]{:S(2)}) copy-start(s32[4,20]{1,0:T(4,128)} %copy-done.4) | copy-start | bytes 964
  16.3 13.3 %copy-start.7 = (s32[4,20]{1,0:T(4,128)S(1)}, s32[4,20]{1,0:T(4,128)}, u32[]{:S(2)}) copy-start(s32[4,20]{1,0:T(4,128)} %copy-done.6) | copy-start | bytes 964
  16.3 1.6 %copy-start.2 = (bf16[128,8192]{1,0:T(8,128)(2,1)S(1)}, bf16[128,8192]{1,0:T(8,128)(2,1)}, u32[]{:S(2)}) copy-start(bf16[128,8192]{1,0:T(8,128)(2,1)} %refs_3_.1) | copy-start | bytes 6291460
  17.9 0.7 copy-start.3
  18.6 0.7 copy-start.10
  19.2 0.7 copy-start.11
  19.9 9.5 %copy-start.12 = (s32[8192]{0:T(1024)S(1)}, s32[8192]{0:T(1024)}, u32[]{:S(2)}) copy-start(s32[8192]{0:T(1024)} %param.12) | copy-start | bytes 98308
  19.9 9.6 %copy-start.9 = (s32[4,20]{1,0:T(4,128)S(1)}, s32[4,20]{1,0:T(4,128)}, u32[]{:S(2)}) copy-start(s32[4,20]{1,0:T(4,128)} %copy-done.8) | copy-start | bytes 964
  40.8 35.9 %collective-permute-start.6 = (bf16[20,48,128]{2,1,0:T(8,128)(2,1)S(1)}, bf16[20,48,128]{2,1,0:T(8,128)(2,1)S(1)}, u32[]{:S(2)}, u32[]{:S(2)}) collective-permute-start(bf16[20,48,128]{2,1,0:T(8,128)(2,1)S(1)} %get-tuple-element.95), channel_id=1, source_target_pairs={{0,4},{4,8},{8,12},{12,0},{1,5},{5,9},{9,13},{13,1},{2,6},{6,10},{... | collective-permute-start | bytes 737288 | tf_op jit(solution)/shard_map/ppermute | solution.py:48
  54.8 21.9 %collective-permute-start.7 = (bf16[20,48,128]{2,1,0:T(8,128)(2,1)S(1)}, bf16[20,48,128]{2,1,0:T(8,128)(2,1)S(1)}, u32[]{:S(2)}, u32[]{:S(2)}) collective-permute-start(bf16[20,48,128]{2,1,0:T(8,128)(2,1)S(1)} %get-tuple-element.96), channel_id=1, source_target_pairs={{0,8},{4,12},{8,0},{12,4},{1,9},{5,13},{9,1},{13,5},{2,10},{6,14},... | collective-permute-start | bytes 737288 | tf_op jit(solution)/shard_map/ppermute | solution.py:48
  54.8 21.9 %collective-permute-start.8 = (bf16[20,48,128]{2,1,0:T(8,128)(2,1)S(1)}, bf16[20,48,128]{2,1,0:T(8,128)(2,1)S(1)}, u32[]{:S(2)}, u32[]{:S(2)}) collective-permute-start(bf16[20,48,128]{2,1,0:T(8,128)(2,1)S(1)} %get-tuple-element.97), channel_id=1, source_target_pairs={{0,12},{4,0},{8,4},{12,8},{1,13},{5,1},{9,5},{13,9},{2,14},{6,2},{... | collective-permute-start | bytes 737288 | tf_op jit(solution)/shard_map/ppermute | solution.py:48
  72.4 18.6 %collective-permute-start.9 = (bf16[80,2048]{1,0:T(8,128)(2,1)S(1)}, bf16[80,2048]{1,0:T(8,128)(2,1)S(1)}, u32[]{:S(2)}, u32[]{:S(2)}) collective-permute-start(bf16[80,2048]{1,0:T(8,128)(2,1)S(1)} %get-tuple-element.102), channel_id=1, source_target_pairs={{0,3},{1,2},{2,1},{3,0},{4,7},{5,6},{6,5},{7,4},{8,11},{9,10},{10,... | collective-permute-start | bytes 983048 | tf_op jit(solution)/shard_map/ppermute | solution.py:52
  72.4 18.5 %collective-permute-start.10 = (bf16[80,2048]{1,0:T(8,128)(2,1)S(1)}, bf16[80,2048]{1,0:T(8,128)(2,1)S(1)}, u32[]{:S(2)}, u32[]{:S(2)}) collective-permute-start(bf16[80,2048]{1,0:T(8,128)(2,1)S(1)} %get-tuple-element.103), channel_id=1, source_target_pairs={{0,2},{1,3},{2,0},{3,1},{4,6},{5,7},{6,4},{7,5},{8,10},{9,11},{10,... | collective-permute-start | bytes 983048 | tf_op jit(solution)/shard_map/ppermute | solution.py:52
  76.8 14.2 %collective-permute-start.11 = (bf16[80,2048]{1,0:T(8,128)(2,1)S(1)}, bf16[80,2048]{1,0:T(8,128)(2,1)S(1)}, u32[]{:S(2)}, u32[]{:S(2)}) collective-permute-start(bf16[80,2048]{1,0:T(8,128)(2,1)S(1)} %gather_next.5), channel_id=1, source_target_pairs={{0,1},{1,0},{2,3},{3,2},{4,5},{5,4},{6,7},{7,6},{8,9},{9,8},{10,11... | collective-permute-start | bytes 983048 | tf_op jit(solution)/shard_map/ppermute | solution.py:52
  89.0 8.0 %collective-permute-start.12 = (bf16[48,2048]{1,0:T(8,128)(2,1)S(1)}, bf16[48,2048]{1,0:T(8,128)(2,1)S(1)}, u32[]{:S(2)}, u32[]{:S(2)}) collective-permute-start(bf16[48,2048]{1,0:T(8,128)(2,1)S(1)} %get-tuple-element.108), channel_id=1, source_target_pairs={{0,3},{1,2},{2,1},{3,0},{4,7},{5,6},{6,5},{7,4},{8,11},{9,10},{10,... | collective-permute-start | bytes 589832 | tf_op jit(solution)/shard_map/ppermute | solution.py:52
  90.3 10.3 %collective-permute-start.13 = (bf16[48,2048]{1,0:T(8,128)(2,1)S(1)}, bf16[48,2048]{1,0:T(8,128)(2,1)S(1)}, u32[]{:S(2)}, u32[]{:S(2)}) collective-permute-start(bf16[48,2048]{1,0:T(8,128)(2,1)S(1)} %get-tuple-element.109), channel_id=1, source_target_pairs={{0,2},{1,3},{2,0},{3,1},{4,6},{5,7},{6,4},{7,5},{8,10},{9,11},{10,... | collective-permute-start | bytes 589832 | tf_op jit(solution)/shard_map/ppermute | solution.py:52
  93.7 6.8 %collective-permute-start.14 = (bf16[48,1024]{1,0:T(8,128)(2,1)S(1)}, bf16[48,1024]{1,0:T(8,128)(2,1)S(1)}, u32[]{:S(2)}, u32[]{:S(2)}) collective-permute-start(bf16[48,1024]{1,0:T(8,128)(2,1)S(1)} %get-tuple-element.111), channel_id=1, source_target_pairs={{0,1},{1,0},{2,3},{3,2},{4,5},{5,4},{6,7},{7,6},{8,9},{9,8},{10,11... | collective-permute-start | bytes 294920 | tf_op jit(solution)/shard_map/ppermute | solution.py:52
  93.8 6.7 %collective-permute-start.15 = (bf16[48,1024]{1,0:T(8,128)(2,1)S(1)}, bf16[48,1024]{1,0:T(8,128)(2,1)S(1)}, u32[]{:S(2)}, u32[]{:S(2)}) collective-permute-start(bf16[48,1024]{1,0:T(8,128)(2,1)S(1)} %get-tuple-element.112), channel_id=1, source_target_pairs={{0,1},{1,0},{2,3},{3,2},{4,5},{5,4},{6,7},{7,6},{8,9},{9,8},{10,11... | collective-permute-start | bytes 294920 | tf_op jit(solution)/shard_map/ppermute | solution.py:52

commit v6 on v5

--- a/solution.py
+++ b/solution.py
@@ -53,7 +53,7 @@
 
 
 def cuts(width):
-    first = width * 5 // 8 // 16 * 16
+    first = width * 3 // 4
     return ((0, first), (first, width - first))
 
 
@@ -104,7 +104,7 @@
 
 
 def own_kernel(ranges, blocks, slots, tile, rows, cols, panel, counts, bias, *refs):
-    accs, (column, inverse, product) = refs[:-3], refs[-3:]
+    accs, (inverse, column, product) = refs[:-3], refs[-3:]
     lanes = inverse.shape[1]
     row_tiles = panel.shape[1] // tile
     eye = identity(tile)
@@ -134,8 +134,7 @@
         inverse[pl.ds(at, tile), :] = scale
         for acc, (low, size) in zip(accs, ranges):
             here = dot(eye, panel[pl.ds(low, size), pl.ds(at, tile)], NT)
-            acc[pl.ds(at, tile), pl.ds(0, size)] = here * scale[:, :size]
-            acc[pl.ds(at, tile), pl.ds(size, 1)] = scale[:, :1]
+            acc[pl.ds(at, tile), :] = here * scale[:, :size]
         return carry
 
     lax.fori_loop(0, row_tiles, start, 0, unroll=4)
@@ -149,9 +148,7 @@
 
         def add(t, carry, acc=acc, size=size):
             at = pl.multiple_of(rows[0, t] * tile, tile)
-            acc[pl.ds(at, tile), pl.ds(0, size)] += (
-                product[t, :, :size] * inverse[pl.ds(at, tile), :size]
-            )
+            acc[pl.ds(at, tile), :] += product[t, :, :size] * inverse[pl.ds(at, tile), :size]
             return carry
 
         lax.fori_loop(0, slots, multiply, 0, unroll=10)
@@ -162,7 +159,8 @@
     blocks, slots = rows.shape
     nodes, tile = panel.shape[1], counts.shape[-1]
     lanes = max(size for _, size in ranges)
-    shapes = [jax.ShapeDtypeStruct((nodes, size + 1), jnp.float32) for _, size in ranges]
+    shapes = [jax.ShapeDtypeStruct((nodes, size), jnp.float32) for _, size in ranges]
+    shapes.append(jax.ShapeDtypeStruct((nodes, lanes), jnp.float32))
     shapes.append(jax.ShapeDtypeStruct((bias.shape[0], 128), bias.dtype))
     outs = call(
         functools.partial(own_kernel, ranges, blocks, slots, tile),
@@ -170,9 +168,9 @@
         [rows, cols],
         [panel, counts, bias[None, :]],
         shapes,
-        [((nodes, lanes), jnp.float32), ((slots, tile, lanes), jnp.float32)],
-    )
-    return outs[:-1], outs[-1]
+        [((slots, tile, lanes), jnp.float32)],
+    )
+    return outs[:-2], outs[-2], outs[-1]
 
 
 def pick(order, nodes, stage, outs):
@@ -196,38 +194,58 @@
         first += columns
 
 
-def far_kernel(offsets, slots, tile, far, rows, *refs):
-    orders, acc, counts = refs[:far], refs[far], refs[far + 1]
-    got, total = refs[far + 2 : far + 2 + offsets], refs[far + 2 + offsets]
-    outs, (product, stage) = refs[far + 3 + offsets : -2], refs[-2:]
-    size = total.shape[1]
-    total[...] = acc[:, :size]
-    for s in range(offsets):
-
-        def multiply(t, carry, s=s):
-            product[t] = dot(counts[(s + 1) * slots + t], got[s][t], NT)
+def add_tiles(first, rows, acc, inverse, counts, got, total, product):
+    slots, tile, size = product.shape
+    total[...] = acc[...]
+    for s, tiles in enumerate(got, first):
+
+        def multiply(t, carry, s=s, tiles=tiles):
+            product[t] = dot(counts[s * slots + t], tiles[t], NT)
             return carry
 
         def add(t, carry, s=s):
-            at = pl.multiple_of(rows[s + 1, t] * tile, tile)
-            total[pl.ds(at, tile), :] += product[t] * acc[pl.ds(at, tile), pl.ds(size, 1)]
+            at = pl.multiple_of(rows[s, t] * tile, tile)
+            total[pl.ds(at, tile), :] += product[t] * inverse[pl.ds(at, tile), :size]
             return carry
 
         lax.fori_loop(0, slots, multiply, 0, unroll=10)
-        lax.fori_loop(0, slots, add, 0)
+        lax.fori_loop(0, slots, add, 0, unroll=2)
+
+
+def early_kernel(first, offsets, rows, acc, inverse, counts, *refs):
+    add_tiles(first, rows, acc, inverse, counts, refs[:offsets], *refs[offsets:])
+
+
+def add_early(acc, inverse, rows, counts, got, first):
+    slots, tile = rows.shape[1], counts.shape[-1]
+    return call(
+        functools.partial(early_kernel, first, len(got)),
+        "add_early",
+        [rows],
+        [acc, inverse, counts, *got],
+        [jax.ShapeDtypeStruct(acc.shape, jnp.float32)],
+        [((slots, tile, acc.shape[1]), jnp.float32)],
+    )[0]
+
+
+def far_kernel(first, offsets, far, rows, *refs):
+    orders, (acc, inverse, counts) = refs[:far], refs[far : far + 3]
+    got, total = refs[far + 3 : far + 3 + offsets], refs[far + 3 + offsets]
+    outs, (product, stage) = refs[far + 4 + offsets : -2], refs[-2:]
+    add_tiles(first, rows, acc, inverse, counts, got, total, product)
     for order, out in zip(orders, outs):
         pick(order, total, stage, [out])
 
 
-def gather_far(acc, rows, orders, counts, got):
-    nodes, size = acc.shape[0], acc.shape[1] - 1
+def gather_far(acc, inverse, rows, orders, counts, got, first):
+    nodes, size = acc.shape
     slots, tile = rows.shape[1], counts.shape[-1]
     share, far = orders[0].shape[0], len(orders)
     outs = call(
-        functools.partial(far_kernel, len(got), slots, tile, far),
+        functools.partial(far_kernel, first, len(got), far),
         "gather_far",
         [rows, *orders],
-        [acc, counts, *got],
+        [acc, inverse, counts, *got],
         [jax.ShapeDtypeStruct((nodes, size), jnp.float32)]
         + [jax.ShapeDtypeStruct((size, share), jnp.bfloat16)] * far,
         [((slots, tile, size), jnp.float32), ((share, size), jnp.float32)],
@@ -316,22 +334,28 @@
         source = features if sent else panel
         sent.append(list(pack(source, asked, low, size, tile)))
         *asked, sent[-1][0] = lax.optimization_barrier((*asked, sent[-1][0]))
-    accs, column = own(features, rows, cols, counts, bias, ranges)
+    accs, inverse, column = own(features, rows, cols, counts, bias, ranges)
     accs, across, picks, starts = lax.optimization_barrier(
         (accs, weight.T, picks, whose * width)
     )
 
-    got = [[shifted(value, "blk", s + 1) for s, value in enumerate(sent[0])]]
-    for later in sent[1:]:
-        later, got[-1], accs = lax.optimization_barrier((later, got[-1], accs))
-        got.append([shifted(value, "blk", s + 1) for s, value in enumerate(later)])
+    got, early = [], []
+    for p, leaving in enumerate(sent):
+        if p:
+            leaving, got[-1], early[-1], accs = lax.optimization_barrier(
+                (leaving, got[-1], early[-1], accs)
+            )
+        got.append([shifted(value, "blk", s + 1) for s, value in enumerate(leaving)])
+        early.append(add_early(accs[p], inverse, rows, counts, got[p][:-1], 1))
 
     pieces, waits, kept = {}, {}, {}
     for p, (low, size) in enumerate(ranges):
         last = p == len(ranges) - 1
-        acc, kept = lax.optimization_barrier((accs[p], kept))
+        acc, kept = lax.optimization_barrier((early[p], kept))
         pieces.update(kept)
-        total, out_far = gather_far(acc, rows, picks[:far], counts, got[p])
+        total, out_far = gather_far(
+            acc, inverse, rows, picks[:far], counts, got[p][-1:], blocks - 1
+        )
         now = {(i, low, 0): traded(piece, "grp", ranks[i]) for i, piece in enumerate(out_far)}
         widths = (share,)
         if not last:
@@ -344,7 +368,9 @@
         first = 0
         for piece in gather_next(total, picks[far], widths):
             if not last:
-                piece, got[p + 1] = lax.optimization_barrier((piece, got[p + 1]))
+                piece, got[p + 1], early[p + 1] = lax.optimization_barrier(
+                    (piece, got[p + 1], early[p + 1])
+                )
             now[far, low, first] = traded(piece, "grp", ranks[far])
             first += piece.shape[1]
         if last:

time: 104 us -> 98.3 us (0.945)
  waiting for transfers between devices: 14 us -> 23.4 us
  Pallas kernels: 50.8 us -> 43.6 us
  starting transfers between devices: 31.7 us -> 26.2 us
  local copies, waits for them, and re-layouts: 6.53 us -> 4.48 us
    ppermute x9, waiting for transfers between devices: 10.5 us -> 18.2 us  [shifted(): return lax.ppermute(value, axis, pairs)]
    pallas_call x8 -> x10, Pallas kernels: 44.9 us -> 37.7 us  [call(): pl.pallas_call(kernel, out_shape=list(outs), in_specs=[SMEM] * len(scalar...]
    ppermute x9, starting transfers between devices: 27.2 us -> 21.8 us  [shifted(): return lax.ppermute(value, axis, pairs)]
    unnamed x29 -> x17, local copies, waits for them, and re-layouts: 6.51 us -> 4.46 us
    ppermute x7, waiting for transfers between devices: 3.53 us -> 5.2 us  [traded(): lax.ppermute(value, axis, [(i, i ^ k) for i in range(lax.axis_size(axis))])]
  transfers between devices with their start and end apart: 16 -> 16, of which waited for: 3 -> 3; matrix products, arithmetic and copies ran while one was open for 1% -> 1% of each run, Pallas kernels for 45% -> 40%
where the time goes in v6:
time: 98.3 us; the launch traced here: 98 us
  Pallas kernels  43.6 us (44%)
  starting transfers between devices  26.2 us (27%)
  waiting for transfers between devices  23.4 us (24%)
  local copies, waits for them, and re-layouts  4.48 us (5%)
    pallas_call x10, Pallas kernels, call(): pl.pallas_call(kernel, out_shape=list(outs), in_specs=[SMEM] * len(scalar...  37.7 us
    ppermute x9, starting transfers between devices, shifted(): return lax.ppermute(value, axis, pairs)  21.8 us
    ppermute x9, waiting for transfers between devices, shifted(): return lax.ppermute(value, axis, pairs)  18.2 us
    ppermute x7, waiting for transfers between devices, traded(): lax.ppermute(value, axis, [(i, i ^ k) for i in range(lax.axis_size(axis))])  5.2 us
    ppermute x7, starting transfers between devices, traded(): lax.ppermute(value, axis, [(i, i ^ k) for i in range(lax.axis_size(axis))])  4.46 us
    unnamed x17, local copies, waits for them, and re-layouts  4.46 us
    pallas_call x2, Pallas kernels, pack(): pl.pallas_call(functools.partial(pack_kernel, low, size, offsets, slots,...  3.09 us
    pallas_call x1, Pallas kernels, mix(): pl.pallas_call(functools.partial(mix_kernel, places), out_shape=jax.Shape...  2.82 us
  transfers between devices with their start and end apart: 16, of which 3 were waited for; matrix products, arithmetic and copies ran while one was open for 1% of the time, Pallas kernels for 40%

profile of v6, /device:TPU:0, one launch (start us, length us, event | category | flops | bytes accessed | tf_op | source)
XLA Modules:
  0.0 98.0 jit_solution(3404910435894480909)
XLA Ops:
  0.0 3.0 %collective-permute-start.2 = (s32[4,20]{1,0:T(4,128)}, s32[4,20]{1,0:T(4,128)S(1)}, u32[]{:S(2)}, u32[]{:S(2)}) collective-permute-start(s32[4,20]{1,0:T(4,128)} %bitcast.16), channel_id=1, source_target_pairs={{0,4},{4,8},{8,12},{12,0},{1,5},{5,9},{9,13},{13,1},{2,6},{6,10},{... | collective-permute-start | bytes 968 | tf_op jit(solution)/shard_map/ppermute | solution.py:48
  3.0 2.6 %collective-permute-start.1 = (s32[4,20]{1,0:T(4,128)}, s32[4,20]{1,0:T(4,128)S(1)}, u32[]{:S(2)}, u32[]{:S(2)}) collective-permute-start(s32[4,20]{1,0:T(4,128)} %bitcast.17), channel_id=1, source_target_pairs={{0,8},{4,12},{8,0},{12,4},{1,9},{5,13},{9,1},{13,5},{2,10},{6,14},... | collective-permute-start | bytes 968 | tf_op jit(solution)/shard_map/ppermute | solution.py:48
  5.6 1.3 %collective-permute-start = (s32[4,20]{1,0:T(4,128)}, s32[4,20]{1,0:T(4,128)S(1)}, u32[]{:S(2)}, u32[]{:S(2)}) collective-permute-start(s32[4,20]{1,0:T(4,128)} %bitcast.18), channel_id=1, source_target_pairs={{0,12},{4,0},{8,4},{12,8},{1,13},{5,1},{9,5},{13,9},{2,14},{6,2},{... | collective-permute-start | bytes 968 | tf_op jit(solution)/shard_map/ppermute | solution.py:48
  7.0 1.6 %copy-done.1 = bf16[128,8192]{1,0:T(8,128)(2,1)S(1)} copy-done((bf16[128,8192]{1,0:T(8,128)(2,1)S(1)}, bf16[128,8192]{1,0:T(8,128)(2,1)}, u32[]{:S(2)}) %copy-start.1) | copy-done | bytes 2097176
  8.6 0.1 stage.1.refs_3_
  8.7 0.0 copy-start.6
  8.7 0.0 copy-start.7
  8.7 0.0 collective-permute-done.2.refs_2_
  8.7 0.0 collective-permute-done.1.refs_1_
  8.7 0.7 collective-permute-done.refs_0_
  9.4 1.7 %pack.2 = (bf16[20,96,128]{2,1,0:T(8,128)(2,1)}, bf16[20,96,128]{2,1,0:T(8,128)(2,1)}, bf16[20,96,128]{2,1,0:T(8,128)(2,1)}) custom-call(s32[4,20]{1,0:T(4,128)S(1)} %collective-permute-done.refs_0_, s32[4,20]{1,0:T(4,128)S(1)} %collective-permute-done.1.refs_1_, s32[4,20]{1,0:T(4,128)S(1)} %collective-permute-done.2.refs_2_, bf16[128,8192]{1,0:T(8,128)(2,1)S(1)} %stage.1.refs_3_), custom_call_target="tpu_custom_call" | custom-call | bytes 65536 | tf_op jit(solution)/shard_map/pack/pallas_call | solution.py:94
  11.2 0.1 collective-permute-start.3
  11.3 3.6 %collective-permute-start.4 = (bf16[20,96,128]{2,1,0:T(8,128)(2,1)}, bf16[20,96,128]{2,1,0:T(8,128)(2,1)}, u32[]{:S(2)}, u32[]{:S(2)}) collective-permute-start(bf16[20,96,128]{2,1,0:T(8,128)(2,1)} %get-tuple-element.78), channel_id=1, source_target_pairs={{0,8},{4,12},{8,0},{12,4},{1,9},{5,13},{9,1},{13,5},{2,10},{6,14},... | collective-permute-start | bytes 1474568 | tf_op jit(solution)/shard_map/ppermute | solution.py:48
  14.9 0.1 collective-permute-start.5
  15.0 1.3 %copy.9 = bf16[512,512]{0,1:T(8,128)(2,1)S(1)} copy(bf16[512,512]{1,0:T(8,128)(2,1)} %param.13) | data formatting | bytes 1048576 | tf_op args[5]
  16.3 0.0 copy-start.2
  16.4 1.6 %copy-done.2 = bf16[128,8192]{1,0:T(8,128)(2,1)S(1)} copy-done((bf16[128,8192]{1,0:T(8,128)(2,1)S(1)}, bf16[128,8192]{1,0:T(8,128)(2,1)}, u32[]{:S(2)}) %copy-start.2) | copy-done | bytes 2097176
  17.9 9.2 %own.1 = (f32[8192,96]{1,0:T(8,128)S(1)}, f32[8192,32]{1,0:T(8,128)S(1)}, f32[8192,96]{1,0:T(8,128)S(1)}, f32[512,128]{1,0:T(8,128)S(1)}) custom-call(s32[4,20]{1,0:T(4,128)S(1)} %bitcast.11, s32[4,20]{1,0:T(4,128)S(1)} %bitcast.19, bf16[128,8192]{1,0:T(8,128)(2,1)S(1)} %copy-done.2, bf16[80,128,128]{2,1,0:T(8,128)(2,1)S(1)} %bitcast.5, f32[1,512]{1,0:T(1,128)S(1)} %bitcast.20), custom_call_target="tpu_custom_call" | custom-call | bytes 65536 | tf_op jit(solution)/shard_map/own/pallas_call | solution.py:33
  27.2 1.4 %pack.3 = (bf16[20,32,128]{2,1,0:T(8,128)(2,1)S(1)}, bf16[20,32,128]{2,1,0:T(8,128)(2,1)S(1)}, bf16[20,32,128]{2,1,0:T(8,128)(2,1)S(1)}) custom-call(s32[4,20]{1,0:T(4,128)S(1)} %collective-permute-done.refs_0_, s32[4,20]{1,0:T(4,128)S(1)} %collective-permute-done.1.refs_1_, s32[4,20]{1,0:T(4,128)S(1)} %collective-permute-done.2.refs_2_, ...), custom_call_target="tpu_custom_call" | custom-call | bytes 65536 | tf_op jit(solution)/shard_map/pack/pallas_call | solution.py:94
  28.6 0.0 collective-permute-done.3.refs_0_
  28.6 17.5 %collective-permute-done.4.refs_1_ = bf16[20,96,128]{2,1,0:T(8,128)(2,1)} collective-permute-done((bf16[20,96,128]{2,1,0:T(8,128)(2,1)}, bf16[20,96,128]{2,1,0:T(8,128)(2,1)}, u32[]{:S(2)}, u32[]{:S(2)}) %collective-permute-start.4) | collective-permute-done | bytes 491552 | tf_op jit(solution)/shard_map/ppermute | solution.py:48
  46.1 3.1 %add_early.2.refs_2_ = f32[8192,96]{1,0:T(8,128)S(1)} custom-call(s32[4,20]{1,0:T(4,128)S(1)} %bitcast.12, f32[8192,96]{1,0:T(8,128)S(1)} %get-tuple-element.80.acc, f32[8192,96]{1,0:T(8,128)S(1)} %get-tuple-element.81.inverse.refs_3_, bf16[80,128,128]{2,1,0:T(8,128)(2,1)S(1)} %bitcast.6, bf16[20,96,128]{2,1,0:T(8,128)(2,1)} %collective-permute-done.3.refs_0_, ...), custom_call_target="tpu_custom_call" | custom-call | bytes 65536 | tf_op jit(solution)/shard_map/add_early/pallas_call | solution.py:33
  49.3 0.0 collective-permute-done.5.refs_5_
  49.3 7.5 %collective-permute-start.6 = (bf16[20,32,128]{2,1,0:T(8,128)(2,1)S(1)}, bf16[20,32,128]{2,1,0:T(8,128)(2,1)S(1)}, u32[]{:S(2)}, u32[]{:S(2)}) collective-permute-start(bf16[20,32,128]{2,1,0:T(8,128)(2,1)S(1)} %get-tuple-element.88), channel_id=1, source_target_pairs={{0,4},{4,8},{8,12},{12,0},{1,5},{5,9},{9,13},{13,1},{2,6},{6,10},{... | collective-permute-start | bytes 491528 | tf_op jit(solution)/shard_map/ppermute | solution.py:48
  56.8 3.4 %collective-permute-start.7 = (bf16[20,32,128]{2,1,0:T(8,128)(2,1)S(1)}, bf16[20,32,128]{2,1,0:T(8,128)(2,1)S(1)}, u32[]{:S(2)}, u32[]{:S(2)}) collective-permute-start(bf16[20,32,128]{2,1,0:T(8,128)(2,1)S(1)} %get-tuple-element.89), channel_id=1, source_target_pairs={{0,8},{4,12},{8,0},{12,4},{1,9},{5,13},{9,1},{13,5},{2,10},{6,14},... | collective-permute-start | bytes 491528 | tf_op jit(solution)/shard_map/ppermute | solution.py:48
  60.2 0.0 collective-permute-start.8
  60.2 6.3 %gather_far.2 = (f32[8192,96]{1,0:T(8,128)S(1)}, bf16[96,2048]{1,0:T(8,128)(2,1)S(1)}, bf16[96,2048]{1,0:T(8,128)(2,1)S(1)}) custom-call(s32[4,20]{1,0:T(4,128)S(1)} %bitcast.13, s32[2048]{0:T(1024)S(1)} %get-tuple-element.63.refs_0_, s32[2048]{0:T(1024)S(1)} %get-tuple-element.64.refs_1_, f32[8192,96]{1,0:T(8,128)S(1)} %add_early.2.refs_2_, ...), custom_call_target="tpu_custom_call" | custom-call | bytes 4194304 | tf_op jit(solution)/shard_map/gather_far/pallas_call | solution.py:33
  66.5 2.7 %gather_next.4.refs_0_ = bf16[96,2048]{1,0:T(8,128)(2,1)S(1)} custom-call(s32[2048]{0:T(1024)S(1)} %get-tuple-element.86.order, f32[8192,96]{1,0:T(8,128)S(1)} %get-tuple-element.87.total), custom_call_target="tpu_custom_call" | custom-call | bytes 65536 | tf_op jit(solution)/shard_map/gather_next/pallas_call | solution.py:33
  69.2 0.1 collective-permute-start.9
  69.3 1.6 %collective-permute-start.10 = (bf16[96,2048]{1,0:T(8,128)(2,1)S(1)}, bf16[96,2048]{1,0:T(8,128)(2,1)S(1)}, u32[]{:S(2)}, u32[]{:S(2)}) collective-permute-start(bf16[96,2048]{1,0:T(8,128)(2,1)S(1)} %get-tuple-element.99), channel_id=1, source_target_pairs={{0,2},{1,3},{2,0},{3,1},{4,6},{5,7},{6,4},{7,5},{8,10},{9,11},{10,... | collective-permute-start | bytes 1179656 | tf_op jit(solution)/shard_map/ppermute | solution.py:52
  70.9 2.7 %gather_next.5 = bf16[96,2048]{1,0:T(8,128)(2,1)S(1)} custom-call(s32[2048]{0:T(1024)S(1)} %get-tuple-element.62.order, f32[8192,96]{1,0:T(8,128)S(1)} %get-tuple-element.87.total), custom_call_target="tpu_custom_call" | custom-call | bytes 65536 | tf_op jit(solution)/shard_map/gather_next/pallas_call | solution.py:33
  73.6 0.0 collective-permute-done.6.refs_0_
  73.6 0.0 collective-permute-done.7.refs_1_
  73.6 2.2 %add_early.3.refs_2_ = f32[8192,32]{1,0:T(8,128)S(1)} custom-call(s32[4,20]{1,0:T(4,128)S(1)} %bitcast.14, f32[8192,32]{1,0:T(8,128)S(1)} %get-tuple-element.91.acc, f32[8192,96]{1,0:T(8,128)S(1)} %get-tuple-element.81.inverse.refs_3_, bf16[80,128,128]{2,1,0:T(8,128)(2,1)S(1)} %bitcast.8, bf16[20,32,128]{2,1,0:T(8,128)(2,1)S(1)} %collective-permute-done.6.refs_0_, ...), custom_call_target="tpu_custom_call" | custom-call | bytes 65536 | tf_op jit(solution)/shard_map/add_early/pallas_call | solution.py:33
  75.8 0.0 collective-permute-done.8.refs_5_
  75.9 0.4 collective-permute-start.11
  76.2 5.9 %gather_far.3 = (f32[8192,32]{1,0:T(8,128)S(1)}, bf16[32,2048]{1,0:T(8,128)(2,1)S(1)}, bf16[32,2048]{1,0:T(8,128)(2,1)S(1)}) custom-call(s32[4,20]{1,0:T(4,128)S(1)} %bitcast.15, s32[2048]{0:T(1024)S(1)} %get-tuple-element.63.refs_0_, s32[2048]{0:T(1024)S(1)} %get-tuple-element.64.refs_1_, f32[8192,32]{1,0:T(8,128)S(1)} %add_early.3.refs_2_, ...), custom_call_target="tpu_custom_call" | custom-call | bytes 4194304 | tf_op jit(solution)/shard_map/gather_far/pallas_call | solution.py:33
  82.1 1.2 %collective-permute-start.12 = (bf16[32,2048]{1,0:T(8,128)(2,1)S(1)}, bf16[32,2048]{1,0:T(8,128)(2,1)S(1)}, u32[]{:S(2)}, u32[]{:S(2)}) collective-permute-start(bf16[32,2048]{1,0:T(8,128)(2,1)S(1)} %get-tuple-element.104), channel_id=1, source_target_pairs={{0,3},{1,2},{2,1},{3,0},{4,7},{5,6},{6,5},{7,4},{8,11},{9,10},{10,... | collective-permute-start | bytes 393224 | tf_op jit(solution)/shard_map/ppermute | solution.py:52
  83.3 0.7 collective-permute-start.13
  84.0 0.0 collective-permute-done.9.refs_1_
  84.0 5.2 %collective-permute-done.10.refs_2_ = bf16[96,2048]{1,0:T(8,128)(2,1)S(1)} collective-permute-done((bf16[96,2048]{1,0:T(8,128)(2,1)S(1)}, bf16[96,2048]{1,0:T(8,128)(2,1)S(1)}, u32[]{:S(2)}, u32[]{:S(2)}) %collective-permute-start.10) | collective-permute-done | bytes 393248 | tf_op jit(solution)/shard_map/ppermute | solution.py:52
  89.2 2.7 %gather_next.6 = (bf16[32,1024]{1,0:T(8,128)(2,1)S(1)}, bf16[32,1024]{1,0:T(8,128)(2,1)S(1)}) custom-call(s32[2048]{0:T(1024)S(1)} %get-tuple-element.62.order, f32[8192,32]{1,0:T(8,128)S(1)} %get-tuple-element.106.total), custom_call_target="tpu_custom_call" | custom-call | bytes 65536 | tf_op jit(solution)/shard_map/gather_next/pallas_call | solution.py:33
  91.9 0.1 collective-permute-start.14
  92.0 0.5 collective-permute-start.15
  92.5 2.7 %gather_next.7.refs_8_ = bf16[32,2048]{1,0:T(8,128)(2,1)S(1)} custom-call(s32[2048]{0:T(1024)S(1)} %get-tuple-element.86.order, f32[8192,32]{1,0:T(8,128)S(1)} %get-tuple-element.106.total), custom_call_target="tpu_custom_call" | custom-call | bytes 65536 | tf_op jit(solution)/shard_map/gather_next/pallas_call | solution.py:33
  95.2 0.0 collective-permute-done.12.refs_4_
  95.2 0.0 collective-permute-done.15.refs_7_
  95.2 2.8 %mix.1 = bf16[512,2048]{1,0:T(8,128)(2,1)} custom-call(s32[4]{0:T(128)S(1)} %xor_multiply_fusion.starts, bf16[512,512]{1,0:T(8,128)(2,1)S(1)} %bitcast.10, f32[512,128]{1,0:T(8,128)S(1)} %get-tuple-element.61.bias, bf16[96,2048]{1,0:T(8,128)(2,1)S(1)} %gather_next.4.refs_0_, bf16[96,2048]{1,0:T(8,128)(2,1)S(1)} %collective-permute-done.9.refs_1_, ...), custom_call_target="tpu_custom_call" | custom-call | flops 1073741824 | bytes 5242880 | tf_op jit(solution)/shard_map/mix/pallas_call | solution.py:296
  (16 shorter events, 0.1 us)
Async XLA Ops:
  0.0 16.3 %copy-start = (bf16[1,4,20,128,128]{4,3,2,1,0:T(8,128)(2,1)S(1)}, bf16[1,4,20,128,128]{4,3,2,1,0:T(8,128)(2,1)}, u32[]{:S(2)}) copy-start(bf16[1,4,20,128,128]{4,3,2,1,0:T(8,128)(2,1)} %param.11) | copy-start | bytes 7864324
  0.0 8.7 %collective-permute-start.2 = (s32[4,20]{1,0:T(4,128)}, s32[4,20]{1,0:T(4,128)S(1)}, u32[]{:S(2)}, u32[]{:S(2)}) collective-permute-start(s32[4,20]{1,0:T(4,128)} %bitcast.16), channel_id=1, source_target_pairs={{0,4},{4,8},{8,12},{12,0},{1,5},{5,9},{9,13},{13,1},{2,6},{6,10},{... | collective-permute-start | bytes 968 | tf_op jit(solution)/shard_map/ppermute | solution.py:48
  3.0 5.7 %collective-permute-start.1 = (s32[4,20]{1,0:T(4,128)}, s32[4,20]{1,0:T(4,128)S(1)}, u32[]{:S(2)}, u32[]{:S(2)}) collective-permute-start(s32[4,20]{1,0:T(4,128)} %bitcast.17), channel_id=1, source_target_pairs={{0,8},{4,12},{8,0},{12,4},{1,9},{5,13},{9,1},{13,5},{2,10},{6,14},... | collective-permute-start | bytes 968 | tf_op jit(solution)/shard_map/ppermute | solution.py:48
  5.6 3.8 %collective-permute-start = (s32[4,20]{1,0:T(4,128)}, s32[4,20]{1,0:T(4,128)S(1)}, u32[]{:S(2)}, u32[]{:S(2)}) collective-permute-start(s32[4,20]{1,0:T(4,128)} %bitcast.18), channel_id=1, source_target_pairs={{0,12},{4,0},{8,4},{12,8},{1,13},{5,1},{9,5},{13,9},{2,14},{6,2},{... | collective-permute-start | bytes 968 | tf_op jit(solution)/shard_map/ppermute | solution.py:48
  7.0 1.6 %copy-start.1 = (bf16[128,8192]{1,0:T(8,128)(2,1)S(1)}, bf16[128,8192]{1,0:T(8,128)(2,1)}, u32[]{:S(2)}) copy-start(bf16[128,8192]{1,0:T(8,128)(2,1)} %refs_3_.1) | copy-start | bytes 6291460
  8.6 7.8 %copy-start.3 = (s32[1,4,20]{2,1,0:T(4,128)S(1)}, s32[1,4,20]{2,1,0:T(4,128)}, u32[]{:S(2)}) copy-start(s32[1,4,20]{2,1,0:T(4,128)} %param.9) | copy-start | bytes 964
  8.6 7.8 %copy-start.4 = (s32[1,4,20]{2,1,0:T(4,128)S(1)}, s32[1,4,20]{2,1,0:T(4,128)}, u32[]{:S(2)}) copy-start(s32[1,4,20]{2,1,0:T(4,128)} %param.10) | copy-start | bytes 964
  8.6 7.8 %copy-start.5 = (f32[512]{0:T(512)S(1)}, f32[512]{0:T(512)}, u32[]{:S(2)}) copy-start(f32[512]{0:T(512)} %param.14) | copy-start | bytes 6148
  8.7 18.5 %copy-start.6 = (s32[8192]{0:T(1024)S(1)}, s32[8192]{0:T(1024)}, u32[]{:S(2)}) copy-start(s32[8192]{0:T(1024)} %param.12) | copy-start | bytes 98308
  8.7 18.5 %copy-start.7 = (s32[4]{0:T(128)S(1)}, s32[4]{0:T(128)}, u32[]{:S(2)}) copy-start(s32[4]{0:T(128)} %constant.20.clone) | copy-start | bytes 52
  11.2 17.5 %collective-permute-start.3 = (bf16[20,96,128]{2,1,0:T(8,128)(2,1)}, bf16[20,96,128]{2,1,0:T(8,128)(2,1)}, u32[]{:S(2)}, u32[]{:S(2)}) collective-permute-start(bf16[20,96,128]{2,1,0:T(8,128)(2,1)} %get-tuple-element.77), channel_id=1, source_target_pairs={{0,4},{4,8},{8,12},{12,0},{1,5},{5,9},{9,13},{13,1},{2,6},{6,10},{... | collective-permute-start | bytes 1474568 | tf_op jit(solution)/shard_map/ppermute | solution.py:48
  11.3 34.9 %collective-permute-start.4 = (bf16[20,96,128]{2,1,0:T(8,128)(2,1)}, bf16[20,96,128]{2,1,0:T(8,128)(2,1)}, u32[]{:S(2)}, u32[]{:S(2)}) collective-permute-start(bf16[20,96,128]{2,1,0:T(8,128)(2,1)} %get-tuple-element.78), channel_id=1, source_target_pairs={{0,8},{4,12},{8,0},{12,4},{1,9},{5,13},{9,1},{13,5},{2,10},{6,14},... | collective-permute-start | bytes 1474568 | tf_op jit(solution)/shard_map/ppermute | solution.py:48
  14.9 34.4 %collective-permute-start.5 = (bf16[20,96,128]{2,1,0:T(8,128)(2,1)}, bf16[20,96,128]{2,1,0:T(8,128)(2,1)}, u32[]{:S(2)}, u32[]{:S(2)}) collective-permute-start(bf16[20,96,128]{2,1,0:T(8,128)(2,1)} %get-tuple-element.79), channel_id=1, source_target_pairs={{0,12},{4,0},{8,4},{12,8},{1,13},{5,1},{9,5},{13,9},{2,14},{6,2},{... | collective-permute-start | bytes 1474568 | tf_op jit(solution)/shard_map/ppermute | solution.py:48
  16.3 1.6 %copy-start.2 = (bf16[128,8192]{1,0:T(8,128)(2,1)S(1)}, bf16[128,8192]{1,0:T(8,128)(2,1)}, u32[]{:S(2)}) copy-start(bf16[128,8192]{1,0:T(8,128)(2,1)} %refs_3_.1) | copy-start | bytes 6291460
  49.3 24.3 %collective-permute-start.6 = (bf16[20,32,128]{2,1,0:T(8,128)(2,1)S(1)}, bf16[20,32,128]{2,1,0:T(8,128)(2,1)S(1)}, u32[]{:S(2)}, u32[]{:S(2)}) collective-permute-start(bf16[20,32,128]{2,1,0:T(8,128)(2,1)S(1)} %get-tuple-element.88), channel_id=1, source_target_pairs={{0,4},{4,8},{8,12},{12,0},{1,5},{5,9},{9,13},{13,1},{2,6},{6,10},{... | collective-permute-start | bytes 491528 | tf_op jit(solution)/shard_map/ppermute | solution.py:48
  56.8 16.8 %collective-permute-start.7 = (bf16[20,32,128]{2,1,0:T(8,128)(2,1)S(1)}, bf16[20,32,128]{2,1,0:T(8,128)(2,1)S(1)}, u32[]{:S(2)}, u32[]{:S(2)}) collective-permute-start(bf16[20,32,128]{2,1,0:T(8,128)(2,1)S(1)} %get-tuple-element.89), channel_id=1, source_target_pairs={{0,8},{4,12},{8,0},{12,4},{1,9},{5,13},{9,1},{13,5},{2,10},{6,14},... | collective-permute-start | bytes 491528 | tf_op jit(solution)/shard_map/ppermute | solution.py:48
  60.2 15.6 %collective-permute-start.8 = (bf16[20,32,128]{2,1,0:T(8,128)(2,1)S(1)}, bf16[20,32,128]{2,1,0:T(8,128)(2,1)S(1)}, u32[]{:S(2)}, u32[]{:S(2)}) collective-permute-start(bf16[20,32,128]{2,1,0:T(8,128)(2,1)S(1)} %get-tuple-element.90), channel_id=1, source_target_pairs={{0,12},{4,0},{8,4},{12,8},{1,13},{5,1},{9,5},{13,9},{2,14},{6,2},{... | collective-permute-start | bytes 491528 | tf_op jit(solution)/shard_map/ppermute | solution.py:48
  69.2 14.8 %collective-permute-start.9 = (bf16[96,2048]{1,0:T(8,128)(2,1)S(1)}, bf16[96,2048]{1,0:T(8,128)(2,1)S(1)}, u32[]{:S(2)}, u32[]{:S(2)}) collective-permute-start(bf16[96,2048]{1,0:T(8,128)(2,1)S(1)} %get-tuple-element.98), channel_id=1, source_target_pairs={{0,3},{1,2},{2,1},{3,0},{4,7},{5,6},{6,5},{7,4},{8,11},{9,10},{10,... | collective-permute-start | bytes 1179656 | tf_op jit(solution)/shard_map/ppermute | solution.py:52
  69.3 19.9 %collective-permute-start.10 = (bf16[96,2048]{1,0:T(8,128)(2,1)S(1)}, bf16[96,2048]{1,0:T(8,128)(2,1)S(1)}, u32[]{:S(2)}, u32[]{:S(2)}) collective-permute-start(bf16[96,2048]{1,0:T(8,128)(2,1)S(1)} %get-tuple-element.99), channel_id=1, source_target_pairs={{0,2},{1,3},{2,0},{3,1},{4,6},{5,7},{6,4},{7,5},{8,10},{9,11},{10,... | collective-permute-start | bytes 1179656 | tf_op jit(solution)/shard_map/ppermute | solution.py:52
  75.9 13.3 %collective-permute-start.11 = (bf16[96,2048]{1,0:T(8,128)(2,1)S(1)}, bf16[96,2048]{1,0:T(8,128)(2,1)S(1)}, u32[]{:S(2)}, u32[]{:S(2)}) collective-permute-start(bf16[96,2048]{1,0:T(8,128)(2,1)S(1)} %gather_next.5), channel_id=1, source_target_pairs={{0,1},{1,0},{2,3},{3,2},{4,5},{5,4},{6,7},{7,6},{8,9},{9,8},{10,11... | collective-permute-start | bytes 1179656 | tf_op jit(solution)/shard_map/ppermute | solution.py:52
  82.1 13.1 %collective-permute-start.12 = (bf16[32,2048]{1,0:T(8,128)(2,1)S(1)}, bf16[32,2048]{1,0:T(8,128)(2,1)S(1)}, u32[]{:S(2)}, u32[]{:S(2)}) collective-permute-start(bf16[32,2048]{1,0:T(8,128)(2,1)S(1)} %get-tuple-element.104), channel_id=1, source_target_pairs={{0,3},{1,2},{2,1},{3,0},{4,7},{5,6},{6,5},{7,4},{8,11},{9,10},{10,... | collective-permute-start | bytes 393224 | tf_op jit(solution)/shard_map/ppermute | solution.py:52
  83.3 11.9 %collective-permute-start.13 = (bf16[32,2048]{1,0:T(8,128)(2,1)S(1)}, bf16[32,2048]{1,0:T(8,128)(2,1)S(1)}, u32[]{:S(2)}, u32[]{:S(2)}) collective-permute-start(bf16[32,2048]{1,0:T(8,128)(2,1)S(1)} %get-tuple-element.105), channel_id=1, source_target_pairs={{0,2},{1,3},{2,0},{3,1},{4,6},{5,7},{6,4},{7,5},{8,10},{9,11},{10,... | collective-permute-start | bytes 393224 | tf_op jit(solution)/shard_map/ppermute | solution.py:52
  91.9 3.3 %collective-permute-start.14 = (bf16[32,1024]{1,0:T(8,128)(2,1)S(1)}, bf16[32,1024]{1,0:T(8,128)(2,1)S(1)}, u32[]{:S(2)}, u32[]{:S(2)}) collective-permute-start(bf16[32,1024]{1,0:T(8,128)(2,1)S(1)} %get-tuple-element.107), channel_id=1, source_target_pairs={{0,1},{1,0},{2,3},{3,2},{4,5},{5,4},{6,7},{7,6},{8,9},{9,8},{10,11... | collective-permute-start | bytes 196616 | tf_op jit(solution)/shard_map/ppermute | solution.py:52
  92.0 3.2 %collective-permute-start.15 = (bf16[32,1024]{1,0:T(8,128)(2,1)S(1)}, bf16[32,1024]{1,0:T(8,128)(2,1)S(1)}, u32[]{:S(2)}, u32[]{:S(2)}) collective-permute-start(bf16[32,1024]{1,0:T(8,128)(2,1)S(1)} %get-tuple-element.108), channel_id=1, source_target_pairs={{0,1},{1,0},{2,3},{3,2},{4,5},{5,4},{6,7},{7,6},{8,9},{9,8},{10,11... | collective-permute-start | bytes 196616 | tf_op jit(solution)/shard_map/ppermute | solution.py:52

commit v7 on v6

--- a/solution.py
+++ b/solution.py
@@ -53,7 +53,7 @@
 
 
 def cuts(width):
-    first = width * 3 // 4
+    first = width * 5 // 8 // 16 * 16
     return ((0, first), (first, width - first))
 
 
@@ -254,19 +254,23 @@
     return outs[0], outs[1:]
 
 
-def next_kernel(order, total, *refs):
-    pick(order, total, refs[-1], refs[:-1])
-
-
-def gather_next(total, order, widths):
+def next_kernel(orders, cuts_of, *refs):
+    order, total, outs, stage = refs[:orders], refs[orders], refs[orders + 1 : -1], refs[-1]
+    first = 0
+    for indices, count in zip(order, cuts_of):
+        pick(indices, total, stage, outs[first : first + count])
+        first += count
+
+
+def gather_next(total, orders, widths):
     size = total.shape[1]
     return call(
-        next_kernel,
+        functools.partial(next_kernel, len(orders), tuple(len(w) for w in widths)),
         "gather_next",
-        [order],
+        orders,
         [total],
-        [jax.ShapeDtypeStruct((size, width), jnp.bfloat16) for width in widths],
-        [((sum(widths), size), jnp.float32)],
+        [jax.ShapeDtypeStruct((size, width), jnp.bfloat16) for w in widths for width in w],
+        [((orders[0].shape[0], size), jnp.float32)],
     )
 
 
@@ -339,46 +343,43 @@
         (accs, weight.T, picks, whose * width)
     )
 
-    got, early = [], []
+    got = []
     for p, leaving in enumerate(sent):
         if p:
-            leaving, got[-1], early[-1], accs = lax.optimization_barrier(
-                (leaving, got[-1], early[-1], accs)
-            )
+            leaving, got[-1], accs = lax.optimization_barrier((leaving, got[-1], accs))
         got.append([shifted(value, "blk", s + 1) for s, value in enumerate(leaving)])
-        early.append(add_early(accs[p], inverse, rows, counts, got[p][:-1], 1))
 
     pieces, waits, kept = {}, {}, {}
-    for p, (low, size) in enumerate(ranges):
-        last = p == len(ranges) - 1
-        acc, kept = lax.optimization_barrier((early[p], kept))
-        pieces.update(kept)
-        total, out_far = gather_far(
-            acc, inverse, rows, picks[:far], counts, got[p][-1:], blocks - 1
+    acc, late = accs[0], 1
+    for p, (low, size) in enumerate(ranges[:-1]):
+        total, out_far = gather_far(acc, inverse, rows, picks[:far], counts, got[p], 1)
+        for i, piece in enumerate(out_far):
+            waits[i, low, 0] = traded(piece, "grp", ranks[i])
+        beside, kept = gather_next(total, picks[far:], [(share,), (share,)])
+        early, late = got[p + 1][:-1], blocks - 1
+        acc = add_early(accs[p + 1], inverse, rows, counts, early, 1)
+        beside, kept, acc, got[p + 1] = lax.optimization_barrier(
+            (beside, kept, acc, got[p + 1])
         )
-        now = {(i, low, 0): traded(piece, "grp", ranks[i]) for i, piece in enumerate(out_far)}
+        waits[far, low, 0] = traded(beside, "grp", 1)
+        pieces[far + 1, low, 0] = kept
+
+    low, size = ranges[-1]
+    total, out_far = gather_far(acc, inverse, rows, picks[:1], counts, got[-1][late - 1 :], late)
+    pieces[0, low, 0] = traded(out_far[0], "grp", ranks[0])
+    for i in range(1, groups):
         widths = (share,)
-        if not last:
-            kept = gather_next(total, picks[-1], (share,))[0]
-            total, kept = lax.optimization_barrier((total, kept))
-        else:
+        if i < far:
             total, waits = lax.optimization_barrier((total, waits))
             pieces.update(waits)
+            widths = (share // 4 * 3, share // 4)
+        elif i == far:
             widths = (share // 2, share // 2)
         first = 0
-        for piece in gather_next(total, picks[far], widths):
-            if not last:
-                piece, got[p + 1], early[p + 1] = lax.optimization_barrier(
-                    (piece, got[p + 1], early[p + 1])
-                )
-            now[far, low, first] = traded(piece, "grp", ranks[far])
+        for piece in gather_next(total, [picks[i]], [widths]):
+            pieces[i, low, first] = traded(piece, "grp", ranks[i]) if ranks[i] else piece
             first += piece.shape[1]
-        if last:
-            kept = gather_next(total, picks[-1], (share,))[0]
-        kept = {(groups - 1, low, 0): kept}
-        waits = now
     pieces.update(waits)
-    pieces.update(kept)
     return mix(starts, across, column, pieces, share)
 
 

time: 98.3 us -> 96.2 us (0.979)
  waiting for transfers between devices: 23.4 us -> 13.8 us
  starting transfers between devices: 26.2 us -> 33.1 us
  local copies, waits for them, and re-layouts: 4.48 us -> 6.54 us
  Pallas kernels: 43.6 us -> 42.1 us
    ppermute x9, waiting for transfers between devices: 18.2 us -> 10.8 us  [shifted(): return lax.ppermute(value, axis, pairs)]
    ppermute x9, starting transfers between devices: 21.8 us -> 27.2 us  [shifted(): return lax.ppermute(value, axis, pairs)]
    ppermute x7 -> x8, waiting for transfers between devices: 5.2 us -> 3.01 us  [traded(): lax.ppermute(value, axis, [(i, i ^ k) for i in range(lax.axis_size(axis))])]
    unnamed x17 -> x31, local copies, waits for them, and re-layouts: 4.46 us -> 6.52 us
    pallas_call x10 -> x9, Pallas kernels: 37.7 us -> 36.2 us  [call(): pl.pallas_call(kernel, out_shape=list(outs), in_specs=[SMEM] * len(scalar...]
    ppermute x7 -> x8, starting transfers between devices: 4.46 us -> 5.83 us  [traded(): lax.ppermute(value, axis, [(i, i ^ k) for i in range(lax.axis_size(axis))])]
  transfers between devices with their start and end apart: 16 -> 17, of which waited for: 3 -> 3; matrix products, arithmetic and copies ran while one was open for 1% -> 1% of each run, Pallas kernels for 40% -> 39%
where the time goes in v7:
time: 96.2 us; the launch traced here: 95.9 us
  Pallas kernels  42.1 us (44%)
  starting transfers between devices  33.1 us (34%)
  waiting for transfers between devices  13.8 us (14%)
  local copies, waits for them, and re-layouts  6.54 us (7%)
    pallas_call x9, Pallas kernels, call(): pl.pallas_call(kernel, out_shape=list(outs), in_specs=[SMEM] * len(scalar...  36.2 us
    ppermute x9, starting transfers between devices, shifted(): return lax.ppermute(value, axis, pairs)  27.2 us
    ppermute x9, waiting for transfers between devices, shifted(): return lax.ppermute(value, axis, pairs)  10.8 us
    unnamed x31, local copies, waits for them, and re-layouts  6.52 us
    ppermute x8, starting transfers between devices, traded(): lax.ppermute(value, axis, [(i, i ^ k) for i in range(lax.axis_size(axis))])  5.83 us
    pallas_call x2, Pallas kernels, pack(): pl.pallas_call(functools.partial(pack_kernel, low, size, offsets, slots,...  3.06 us
    ppermute x8, waiting for transfers between devices, traded(): lax.ppermute(value, axis, [(i, i ^ k) for i in range(lax.axis_size(axis))])  3.01 us
    pallas_call x1, Pallas kernels, mix(): pl.pallas_call(functools.partial(mix_kernel, places), out_shape=jax.Shape...  2.79 us
  transfers between devices with their start and end apart: 17, of which 3 were waited for; matrix products, arithmetic and copies ran while one was open for 1% of the time, Pallas kernels for 39%

profile of v7, /device:TPU:0, one launch (start us, length us, event | category | flops | bytes accessed | tf_op | source)
XLA Modules:
  0.0 95.9 jit_solution(8176036247699842903)
XLA Ops:
  0.0 3.0 %collective-permute-start.2 = (s32[4,20]{1,0:T(4,128)}, s32[4,20]{1,0:T(4,128)S(1)}, u32[]{:S(2)}, u32[]{:S(2)}) collective-permute-start(s32[4,20]{1,0:T(4,128)} %bitcast.14), channel_id=1, source_target_pairs={{0,4},{4,8},{8,12},{12,0},{1,5},{5,9},{9,13},{13,1},{2,6},{6,10},{... | collective-permute-start | bytes 968 | tf_op jit(solution)/shard_map/ppermute | solution.py:48
  3.0 2.6 %collective-permute-start.1 = (s32[4,20]{1,0:T(4,128)}, s32[4,20]{1,0:T(4,128)S(1)}, u32[]{:S(2)}, u32[]{:S(2)}) collective-permute-start(s32[4,20]{1,0:T(4,128)} %bitcast.15), channel_id=1, source_target_pairs={{0,8},{4,12},{8,0},{12,4},{1,9},{5,13},{9,1},{13,5},{2,10},{6,14},... | collective-permute-start | bytes 968 | tf_op jit(solution)/shard_map/ppermute | solution.py:48
  5.6 1.3 %collective-permute-start = (s32[4,20]{1,0:T(4,128)}, s32[4,20]{1,0:T(4,128)S(1)}, u32[]{:S(2)}, u32[]{:S(2)}) collective-permute-start(s32[4,20]{1,0:T(4,128)} %bitcast.16), channel_id=1, source_target_pairs={{0,12},{4,0},{8,4},{12,8},{1,13},{5,1},{9,5},{13,9},{2,14},{6,2},{... | collective-permute-start | bytes 968 | tf_op jit(solution)/shard_map/ppermute | solution.py:48
  7.0 1.6 %copy-done.1 = bf16[128,8192]{1,0:T(8,128)(2,1)S(1)} copy-done((bf16[128,8192]{1,0:T(8,128)(2,1)S(1)}, bf16[128,8192]{1,0:T(8,128)(2,1)}, u32[]{:S(2)}) %copy-start.1) | copy-done | bytes 2097176
  8.6 0.1 stage.1.refs_3_
  8.7 0.0 collective-permute-done.2.refs_2_
  8.7 0.7 collective-permute-done.refs_0_
  9.4 1.6 %pack.2 = (bf16[20,80,128]{2,1,0:T(8,128)(2,1)}, bf16[20,80,128]{2,1,0:T(8,128)(2,1)}, bf16[20,80,128]{2,1,0:T(8,128)(2,1)}) custom-call(s32[4,20]{1,0:T(4,128)S(1)} %collective-permute-done.refs_0_, s32[4,20]{1,0:T(4,128)S(1)} %collective-permute-done.1.refs_1_, s32[4,20]{1,0:T(4,128)S(1)} %collective-permute-done.2.refs_2_, bf16[128,8192]{1,0:T(8,128)(2,1)S(1)} %stage.1.refs_3_), custom_call_target="tpu_custom_call" | custom-call | bytes 65536 | tf_op jit(solution)/shard_map/pack/pallas_call | solution.py:94
  11.1 0.1 collective-permute-start.3
  11.2 3.6 %collective-permute-start.4 = (bf16[20,80,128]{2,1,0:T(8,128)(2,1)}, bf16[20,80,128]{2,1,0:T(8,128)(2,1)}, u32[]{:S(2)}, u32[]{:S(2)}) collective-permute-start(bf16[20,80,128]{2,1,0:T(8,128)(2,1)} %get-tuple-element.81), channel_id=1, source_target_pairs={{0,8},{4,12},{8,0},{12,4},{1,9},{5,13},{9,1},{13,5},{2,10},{6,14},... | collective-permute-start | bytes 1228808 | tf_op jit(solution)/shard_map/ppermute | solution.py:48
  14.8 0.1 collective-permute-start.5
  15.0 1.3 %copy.9 = bf16[512,512]{0,1:T(8,128)(2,1)S(1)} copy(bf16[512,512]{1,0:T(8,128)(2,1)} %param.13) | data formatting | bytes 1048576 | tf_op args[5]
  16.2 0.0 copy-start.14
  16.3 0.0 copy-start.4
  16.3 0.0 copy-start.2
  16.3 1.6 %copy-done.2 = bf16[128,8192]{1,0:T(8,128)(2,1)S(1)} copy-done((bf16[128,8192]{1,0:T(8,128)(2,1)S(1)}, bf16[128,8192]{1,0:T(8,128)(2,1)}, u32[]{:S(2)}) %copy-start.2) | copy-done | bytes 2097176
  17.9 0.7 copy-done.3
  18.6 0.7 copy-done.11
  19.2 0.7 copy-done.12
  19.9 9.2 %own.1 = (f32[8192,80]{1,0:T(8,128)S(1)}, f32[8192,48]{1,0:T(8,128)S(1)}, f32[8192,80]{1,0:T(8,128)S(1)}, f32[512,128]{1,0:T(8,128)S(1)}) custom-call(s32[4,20]{1,0:T(4,128)S(1)} %bitcast.10, s32[4,20]{1,0:T(4,128)S(1)} %bitcast.17, bf16[128,8192]{1,0:T(8,128)(2,1)S(1)} %copy-done.2, bf16[80,128,128]{2,1,0:T(8,128)(2,1)S(1)} %bitcast.5, f32[1,512]{1,0:T(1,128)S(1)} %bitcast.18), custom_call_target="tpu_custom_call" | custom-call | bytes 65536 | tf_op jit(solution)/shard_map/own/pallas_call | solution.py:33
  29.2 1.4 %pack.3 = (bf16[20,48,128]{2,1,0:T(8,128)(2,1)S(1)}, bf16[20,48,128]{2,1,0:T(8,128)(2,1)S(1)}, bf16[20,48,128]{2,1,0:T(8,128)(2,1)S(1)}) custom-call(s32[4,20]{1,0:T(4,128)S(1)} %copy-done.10, s32[4,20]{1,0:T(4,128)S(1)} %copy-done.8, s32[4,20]{1,0:T(4,128)S(1)} %copy-done.6, bf16[128,8192]{1,0:T(8,128)(2,1)S(1)} %copy-done.2), custom_call_target="tpu_custom_call" | custom-call | bytes 65536 | tf_op jit(solution)/shard_map/pack/pallas_call | solution.py:94
  30.7 10.1 %collective-permute-done.4.refs_6_ = bf16[20,80,128]{2,1,0:T(8,128)(2,1)} collective-permute-done((bf16[20,80,128]{2,1,0:T(8,128)(2,1)}, bf16[20,80,128]{2,1,0:T(8,128)(2,1)}, u32[]{:S(2)}, u32[]{:S(2)}) %collective-permute-start.4) | collective-permute-done | bytes 409632 | tf_op jit(solution)/shard_map/ppermute | solution.py:48
  40.8 14.0 %collective-permute-start.6 = (bf16[20,48,128]{2,1,0:T(8,128)(2,1)S(1)}, bf16[20,48,128]{2,1,0:T(8,128)(2,1)S(1)}, u32[]{:S(2)}, u32[]{:S(2)}) collective-permute-start(bf16[20,48,128]{2,1,0:T(8,128)(2,1)S(1)} %get-tuple-element.94), channel_id=1, source_target_pairs={{0,4},{4,8},{8,12},{12,0},{1,5},{5,9},{9,13},{13,1},{2,6},{6,10},{... | collective-permute-start | bytes 737288 | tf_op jit(solution)/shard_map/ppermute | solution.py:48
  54.8 2.4 %collective-permute-start.8 = (bf16[20,48,128]{2,1,0:T(8,128)(2,1)S(1)}, bf16[20,48,128]{2,1,0:T(8,128)(2,1)S(1)}, u32[]{:S(2)}, u32[]{:S(2)}) collective-permute-start(bf16[20,48,128]{2,1,0:T(8,128)(2,1)S(1)} %get-tuple-element.96), channel_id=1, source_target_pairs={{0,12},{4,0},{8,4},{12,8},{1,13},{5,1},{9,5},{13,9},{2,14},{6,2},{... | collective-permute-start | bytes 737288 | tf_op jit(solution)/shard_map/ppermute | solution.py:48
  57.2 7.8 %gather_far.2 = (f32[8192,80]{1,0:T(8,128)S(1)}, bf16[80,2048]{1,0:T(8,128)(2,1)S(1)}, bf16[80,2048]{1,0:T(8,128)(2,1)S(1)}) custom-call(s32[4,20]{1,0:T(4,128)S(1)} %bitcast.11, s32[2048]{0:T(1024)S(1)} %get-tuple-element.66.refs_0_, s32[2048]{0:T(1024)S(1)} %get-tuple-element.67.refs_1_.refs_0_, f32[8192,80]{1,0:T(8,128)S(1)} %get-tuple-element.85.refs_2_, ...), custom_call_target="tpu_custom_call" | custom-call | bytes 4194304 | tf_op jit(solution)/shard_map/gather_far/pallas_call | solution.py:33
  65.1 0.1 collective-permute-start.10
  65.1 1.6 %collective-permute-start.11 = (bf16[80,2048]{1,0:T(8,128)(2,1)S(1)}, bf16[80,2048]{1,0:T(8,128)(2,1)S(1)}, u32[]{:S(2)}, u32[]{:S(2)}) collective-permute-start(bf16[80,2048]{1,0:T(8,128)(2,1)S(1)} %get-tuple-element.103), channel_id=1, source_target_pairs={{0,2},{1,3},{2,0},{3,1},{4,6},{5,7},{6,4},{7,5},{8,10},{9,11},{10,... | collective-permute-start | bytes 983048 | tf_op jit(solution)/shard_map/ppermute | solution.py:52
  66.7 4.9 %gather_next.4 = (bf16[80,2048]{1,0:T(8,128)(2,1)S(1)}, bf16[80,2048]{1,0:T(8,128)(2,1)S(1)}) custom-call(s32[2048]{0:T(1024)S(1)} %get-tuple-element.64.refs_0_, s32[2048]{0:T(1024)S(1)} %get-tuple-element.65.refs_1_.refs_0_, f32[8192,80]{1,0:T(8,128)S(1)} %get-tuple-element.90.refs_2_), custom_call_target="tpu_custom_call" | custom-call | bytes 65536 | tf_op jit(solution)/shard_map/gather_next/pallas_call | solution.py:33
  71.6 0.0 collective-permute-done.6.refs_0_
  71.7 2.2 %add_early.1.refs_1_ = f32[8192,48]{1,0:T(8,128)S(1)} custom-call(s32[4,20]{1,0:T(4,128)S(1)} %bitcast.12, f32[8192,48]{1,0:T(8,128)S(1)} %get-tuple-element.93.acc, f32[8192,80]{1,0:T(8,128)S(1)} %get-tuple-element.86.refs_3_.inverse.refs_2_, bf16[80,128,128]{2,1,0:T(8,128)(2,1)S(1)} %bitcast.7, bf16[20,48,128]{2,1,0:T(8,128)(2,1)S(1)} %collective-permute-done.6.refs_0_, ...), custom_call_target="tpu_custom_call" | custom-call | bytes 65536 | tf_op jit(solution)/shard_map/add_early/pallas_call | solution.py:33
  73.9 0.0 collective-permute-done.8.refs_4_
  73.9 0.4 collective-permute-start.12
  74.3 3.7 %gather_far.3 = (f32[8192,48]{1,0:T(8,128)S(1)}, bf16[48,2048]{1,0:T(8,128)(2,1)S(1)}) custom-call(s32[4,20]{1,0:T(4,128)S(1)} %bitcast.13, s32[2048]{0:T(1024)S(1)} %get-tuple-element.66.refs_0_, f32[8192,48]{1,0:T(8,128)S(1)} %add_early.1.refs_1_, f32[8192,80]{1,0:T(8,128)S(1)} %get-tuple-element.86.refs_3_.inverse.refs_2_, ...), custom_call_target="tpu_custom_call" | custom-call | bytes 4194304 | tf_op jit(solution)/shard_map/gather_far/pallas_call | solution.py:33
  78.0 1.2 %collective-permute-start.9 = (bf16[48,2048]{1,0:T(8,128)(2,1)S(1)}, bf16[48,2048]{1,0:T(8,128)(2,1)S(1)}, u32[]{:S(2)}, u32[]{:S(2)}) collective-permute-start(bf16[48,2048]{1,0:T(8,128)(2,1)S(1)} %get-tuple-element.100), channel_id=1, source_target_pairs={{0,3},{1,2},{2,1},{3,0},{4,7},{5,6},{6,5},{7,4},{8,11},{9,10},{10,... | collective-permute-start | bytes 589832 | tf_op jit(solution)/shard_map/ppermute | solution.py:52
  79.2 3.0 %collective-permute-done.11.refs_3_ = bf16[80,2048]{1,0:T(8,128)(2,1)S(1)} collective-permute-done((bf16[80,2048]{1,0:T(8,128)(2,1)S(1)}, bf16[80,2048]{1,0:T(8,128)(2,1)S(1)}, u32[]{:S(2)}, u32[]{:S(2)}) %collective-permute-start.11) | collective-permute-done | bytes 327712 | tf_op jit(solution)/shard_map/ppermute | solution.py:52
  82.2 0.0 collective-permute-done.12.refs_4_
  82.2 2.7 %gather_next.5 = (bf16[48,1536]{1,0:T(8,128)(2,1)S(1)}, bf16[48,512]{1,0:T(8,128)(2,1)S(1)}) custom-call(s32[2048]{0:T(1024)S(1)} %get-tuple-element.67.refs_1_.refs_0_, f32[8192,48]{1,0:T(8,128)S(1)} %get-tuple-element.108.refs_1_), custom_call_target="tpu_custom_call" | custom-call | bytes 65536 | tf_op jit(solution)/shard_map/gather_next/pallas_call | solution.py:33
  84.9 0.1 collective-permute-start.13
  85.0 2.7 %gather_next.6 = (bf16[48,1024]{1,0:T(8,128)(2,1)S(1)}, bf16[48,1024]{1,0:T(8,128)(2,1)S(1)}) custom-call(s32[2048]{0:T(1024)S(1)} %get-tuple-element.64.refs_0_, f32[8192,48]{1,0:T(8,128)S(1)} %get-tuple-element.108.refs_1_), custom_call_target="tpu_custom_call" | custom-call | bytes 65536 | tf_op jit(solution)/shard_map/gather_next/pallas_call | solution.py:33
  87.7 0.1 collective-permute-start.15
  87.8 0.5 collective-permute-start.16
  88.3 2.0 %collective-permute-start.14 = (bf16[48,512]{1,0:T(8,128)(2,1)S(1)}, bf16[48,512]{1,0:T(8,128)(2,1)S(1)}, u32[]{:S(2)}, u32[]{:S(2)}) collective-permute-start(bf16[48,512]{1,0:T(8,128)(2,1)S(1)} %get-tuple-element.110), channel_id=1, source_target_pairs={{0,2},{1,3},{2,0},{3,1},{4,6},{5,7},{6,4},{7,5},{8,10},{9,11},{10,... | collective-permute-start | bytes 147464 | tf_op jit(solution)/shard_map/ppermute | solution.py:52
  90.3 2.7 %gather_next.7.refs_9_ = bf16[48,2048]{1,0:T(8,128)(2,1)S(1)} custom-call(s32[2048]{0:T(1024)S(1)} %get-tuple-element.65.refs_1_.refs_0_, f32[8192,48]{1,0:T(8,128)S(1)} %get-tuple-element.108.refs_1_), custom_call_target="tpu_custom_call" | custom-call | bytes 65536 | tf_op jit(solution)/shard_map/gather_next/pallas_call | solution.py:33
  93.0 0.0 collective-permute-done.9.refs_1_
  93.0 0.0 collective-permute-done.14.refs_6_
  93.1 0.0 collective-permute-done.16.refs_8_
  93.1 0.0 collective-permute-done.13.refs_5_
  93.1 2.8 %mix.1 = bf16[512,2048]{1,0:T(8,128)(2,1)} custom-call(s32[4]{0:T(128)S(1)} %xor_multiply_fusion.starts, bf16[512,512]{1,0:T(8,128)(2,1)S(1)} %bitcast.9, f32[512,128]{1,0:T(8,128)S(1)} %get-tuple-element.63.bias, bf16[80,2048]{1,0:T(8,128)(2,1)S(1)} %get-tuple-element.97.refs_0_, bf16[48,2048]{1,0:T(8,128)(2,1)S(1)} %collective-permute-done.9.refs_1_, ...), custom_call_target="tpu_custom_call" | custom-call | flops 1073741824 | bytes 5242880 | tf_op jit(solution)/shard_map/mix/pallas_call | solution.py:300
  (31 shorter events, 0.1 us)
Async XLA Ops:
  0.0 16.3 %copy-start = (bf16[1,4,20,128,128]{4,3,2,1,0:T(8,128)(2,1)S(1)}, bf16[1,4,20,128,128]{4,3,2,1,0:T(8,128)(2,1)}, u32[]{:S(2)}) copy-start(bf16[1,4,20,128,128]{4,3,2,1,0:T(8,128)(2,1)} %param.11) | copy-start | bytes 7864324
  0.0 8.7 %collective-permute-start.2 = (s32[4,20]{1,0:T(4,128)}, s32[4,20]{1,0:T(4,128)S(1)}, u32[]{:S(2)}, u32[]{:S(2)}) collective-permute-start(s32[4,20]{1,0:T(4,128)} %bitcast.14), channel_id=1, source_target_pairs={{0,4},{4,8},{8,12},{12,0},{1,5},{5,9},{9,13},{13,1},{2,6},{6,10},{... | collective-permute-start | bytes 968 | tf_op jit(solution)/shard_map/ppermute | solution.py:48
  3.0 5.7 %collective-permute-start.1 = (s32[4,20]{1,0:T(4,128)}, s32[4,20]{1,0:T(4,128)S(1)}, u32[]{:S(2)}, u32[]{:S(2)}) collective-permute-start(s32[4,20]{1,0:T(4,128)} %bitcast.15), channel_id=1, source_target_pairs={{0,8},{4,12},{8,0},{12,4},{1,9},{5,13},{9,1},{13,5},{2,10},{6,14},... | collective-permute-start | bytes 968 | tf_op jit(solution)/shard_map/ppermute | solution.py:48
  5.6 3.8 %collective-permute-start = (s32[4,20]{1,0:T(4,128)}, s32[4,20]{1,0:T(4,128)S(1)}, u32[]{:S(2)}, u32[]{:S(2)}) collective-permute-start(s32[4,20]{1,0:T(4,128)} %bitcast.16), channel_id=1, source_target_pairs={{0,12},{4,0},{8,4},{12,8},{1,13},{5,1},{9,5},{13,9},{2,14},{6,2},{... | collective-permute-start | bytes 968 | tf_op jit(solution)/shard_map/ppermute | solution.py:48
  7.0 1.6 %copy-start.1 = (bf16[128,8192]{1,0:T(8,128)(2,1)S(1)}, bf16[128,8192]{1,0:T(8,128)(2,1)}, u32[]{:S(2)}) copy-start(bf16[128,8192]{1,0:T(8,128)(2,1)} %refs_3_.1) | copy-start | bytes 6291460
  8.7 2.4 %copy-start.5 = (s32[4,20]{1,0:T(4,128)}, s32[4,20]{1,0:T(4,128)S(1)}, u32[]{:S(2)}) copy-start(s32[4,20]{1,0:T(4,128)S(1)} %collective-permute-done.2.refs_2_) | copy-start | bytes 964
  8.7 2.3 %copy-start.7 = (s32[4,20]{1,0:T(4,128)}, s32[4,20]{1,0:T(4,128)S(1)}, u32[]{:S(2)}) copy-start(s32[4,20]{1,0:T(4,128)S(1)} %collective-permute-done.1.refs_1_) | copy-start | bytes 964
  9.4 1.8 %copy-start.9 = (s32[4,20]{1,0:T(4,128)}, s32[4,20]{1,0:T(4,128)S(1)}, u32[]{:S(2)}) copy-start(s32[4,20]{1,0:T(4,128)S(1)} %collective-permute-done.refs_0_) | copy-start | bytes 964
  11.1 19.6 %collective-permute-start.3 = (bf16[20,80,128]{2,1,0:T(8,128)(2,1)}, bf16[20,80,128]{2,1,0:T(8,128)(2,1)S(1)}, u32[]{:S(2)}, u32[]{:S(2)}) collective-permute-start(bf16[20,80,128]{2,1,0:T(8,128)(2,1)} %get-tuple-element.80), channel_id=1, source_target_pairs={{0,4},{4,8},{8,12},{12,0},{1,5},{5,9},{9,13},{13,1},{2,6},{6,10},{... | collective-permute-start | bytes 1228808 | tf_op jit(solution)/shard_map/ppermute | solution.py:48
  11.2 29.6 %collective-permute-start.4 = (bf16[20,80,128]{2,1,0:T(8,128)(2,1)}, bf16[20,80,128]{2,1,0:T(8,128)(2,1)}, u32[]{:S(2)}, u32[]{:S(2)}) collective-permute-start(bf16[20,80,128]{2,1,0:T(8,128)(2,1)} %get-tuple-element.81), channel_id=1, source_target_pairs={{0,8},{4,12},{8,0},{12,4},{1,9},{5,13},{9,1},{13,5},{2,10},{6,14},... | collective-permute-start | bytes 1228808 | tf_op jit(solution)/shard_map/ppermute | solution.py:48
  14.8 26.0 %collective-permute-start.5 = (bf16[20,80,128]{2,1,0:T(8,128)(2,1)}, bf16[20,80,128]{2,1,0:T(8,128)(2,1)}, u32[]{:S(2)}, u32[]{:S(2)}) collective-permute-start(bf16[20,80,128]{2,1,0:T(8,128)(2,1)} %get-tuple-element.82), channel_id=1, source_target_pairs={{0,12},{4,0},{8,4},{12,8},{1,13},{5,1},{9,5},{13,9},{2,14},{6,2},{... | collective-permute-start | bytes 1228808 | tf_op jit(solution)/shard_map/ppermute | solution.py:48
  16.2 12.9 %copy-start.14 = (s32[4]{0:T(128)S(1)}, s32[4]{0:T(128)}, u32[]{:S(2)}) copy-start(s32[4]{0:T(128)} %constant.20.clone) | copy-start | bytes 52
  16.3 13.0 %copy-start.6 = (s32[4,20]{1,0:T(4,128)S(1)}, s32[4,20]{1,0:T(4,128)}, u32[]{:S(2)}) copy-start(s32[4,20]{1,0:T(4,128)} %copy-done.5) | copy-start | bytes 964
  16.3 40.9 %copy-start.4 = (s32[1,4,20]{2,1,0:T(4,128)S(1)}, s32[1,4,20]{2,1,0:T(4,128)}, u32[]{:S(2)}) copy-start(s32[1,4,20]{2,1,0:T(4,128)} %param.9) | copy-start | bytes 964
  16.3 1.6 %copy-start.2 = (bf16[128,8192]{1,0:T(8,128)(2,1)S(1)}, bf16[128,8192]{1,0:T(8,128)(2,1)}, u32[]{:S(2)}) copy-start(bf16[128,8192]{1,0:T(8,128)(2,1)} %refs_3_.1) | copy-start | bytes 6291460
  17.9 0.7 copy-start.3
  18.6 0.7 copy-start.11
  19.2 0.7 copy-start.12
  19.9 9.2 %copy-start.13 = (s32[8192]{0:T(1024)S(1)}, s32[8192]{0:T(1024)}, u32[]{:S(2)}) copy-start(s32[8192]{0:T(1024)} %param.12) | copy-start | bytes 98308
  19.9 9.3 %copy-start.8 = (s32[4,20]{1,0:T(4,128)S(1)}, s32[4,20]{1,0:T(4,128)}, u32[]{:S(2)}) copy-start(s32[4,20]{1,0:T(4,128)} %copy-done.7) | copy-start | bytes 964
  19.9 9.3 %copy-start.10 = (s32[4,20]{1,0:T(4,128)S(1)}, s32[4,20]{1,0:T(4,128)}, u32[]{:S(2)}) copy-start(s32[4,20]{1,0:T(4,128)} %copy-done.9) | copy-start | bytes 964
  40.8 30.8 %collective-permute-start.6 = (bf16[20,48,128]{2,1,0:T(8,128)(2,1)S(1)}, bf16[20,48,128]{2,1,0:T(8,128)(2,1)S(1)}, u32[]{:S(2)}, u32[]{:S(2)}) collective-permute-start(bf16[20,48,128]{2,1,0:T(8,128)(2,1)S(1)} %get-tuple-element.94), channel_id=1, source_target_pairs={{0,4},{4,8},{8,12},{12,0},{1,5},{5,9},{9,13},{13,1},{2,6},{6,10},{... | collective-permute-start | bytes 737288 | tf_op jit(solution)/shard_map/ppermute | solution.py:48
  54.8 16.8 %collective-permute-start.7 = (bf16[20,48,128]{2,1,0:T(8,128)(2,1)S(1)}, bf16[20,48,128]{2,1,0:T(8,128)(2,1)S(1)}, u32[]{:S(2)}, u32[]{:S(2)}) collective-permute-start(bf16[20,48,128]{2,1,0:T(8,128)(2,1)S(1)} %get-tuple-element.95), channel_id=1, source_target_pairs={{0,8},{4,12},{8,0},{12,4},{1,9},{5,13},{9,1},{13,5},{2,10},{6,14},... | collective-permute-start | bytes 737288 | tf_op jit(solution)/shard_map/ppermute | solution.py:48
  54.8 19.1 %collective-permute-start.8 = (bf16[20,48,128]{2,1,0:T(8,128)(2,1)S(1)}, bf16[20,48,128]{2,1,0:T(8,128)(2,1)S(1)}, u32[]{:S(2)}, u32[]{:S(2)}) collective-permute-start(bf16[20,48,128]{2,1,0:T(8,128)(2,1)S(1)} %get-tuple-element.96), channel_id=1, source_target_pairs={{0,12},{4,0},{8,4},{12,8},{1,13},{5,1},{9,5},{13,9},{2,14},{6,2},{... | collective-permute-start | bytes 737288 | tf_op jit(solution)/shard_map/ppermute | solution.py:48
  65.1 14.2 %collective-permute-start.10 = (bf16[80,2048]{1,0:T(8,128)(2,1)S(1)}, bf16[80,2048]{1,0:T(8,128)(2,1)S(1)}, u32[]{:S(2)}, u32[]{:S(2)}) collective-permute-start(bf16[80,2048]{1,0:T(8,128)(2,1)S(1)} %get-tuple-element.102), channel_id=1, source_target_pairs={{0,3},{1,2},{2,1},{3,0},{4,7},{5,6},{6,5},{7,4},{8,11},{9,10},{10,... | collective-permute-start | bytes 983048 | tf_op jit(solution)/shard_map/ppermute | solution.py:52
  65.1 17.1 %collective-permute-start.11 = (bf16[80,2048]{1,0:T(8,128)(2,1)S(1)}, bf16[80,2048]{1,0:T(8,128)(2,1)S(1)}, u32[]{:S(2)}, u32[]{:S(2)}) collective-permute-start(bf16[80,2048]{1,0:T(8,128)(2,1)S(1)} %get-tuple-element.103), channel_id=1, source_target_pairs={{0,2},{1,3},{2,0},{3,1},{4,6},{5,7},{6,4},{7,5},{8,10},{9,11},{10,... | collective-permute-start | bytes 983048 | tf_op jit(solution)/shard_map/ppermute | solution.py:52
  73.9 8.3 %collective-permute-start.12 = (bf16[80,2048]{1,0:T(8,128)(2,1)S(1)}, bf16[80,2048]{1,0:T(8,128)(2,1)S(1)}, u32[]{:S(2)}, u32[]{:S(2)}) collective-permute-start(bf16[80,2048]{1,0:T(8,128)(2,1)S(1)} %get-tuple-element.104), channel_id=1, source_target_pairs={{0,1},{1,0},{2,3},{3,2},{4,5},{5,4},{6,7},{7,6},{8,9},{9,8},{10,11... | collective-permute-start | bytes 983048 | tf_op jit(solution)/shard_map/ppermute | solution.py:52
  78.0 15.0 %collective-permute-start.9 = (bf16[48,2048]{1,0:T(8,128)(2,1)S(1)}, bf16[48,2048]{1,0:T(8,128)(2,1)S(1)}, u32[]{:S(2)}, u32[]{:S(2)}) collective-permute-start(bf16[48,2048]{1,0:T(8,128)(2,1)S(1)} %get-tuple-element.100), channel_id=1, source_target_pairs={{0,3},{1,2},{2,1},{3,0},{4,7},{5,6},{6,5},{7,4},{8,11},{9,10},{10,... | collective-permute-start | bytes 589832 | tf_op jit(solution)/shard_map/ppermute | solution.py:52
  84.9 8.1 %collective-permute-start.13 = (bf16[48,1536]{1,0:T(8,128)(2,1)S(1)}, bf16[48,1536]{1,0:T(8,128)(2,1)S(1)}, u32[]{:S(2)}, u32[]{:S(2)}) collective-permute-start(bf16[48,1536]{1,0:T(8,128)(2,1)S(1)} %get-tuple-element.109), channel_id=1, source_target_pairs={{0,2},{1,3},{2,0},{3,1},{4,6},{5,7},{6,4},{7,5},{8,10},{9,11},{10,... | collective-permute-start | bytes 442376 | tf_op jit(solution)/shard_map/ppermute | solution.py:52
  87.7 5.3 %collective-permute-start.15 = (bf16[48,1024]{1,0:T(8,128)(2,1)S(1)}, bf16[48,1024]{1,0:T(8,128)(2,1)S(1)}, u32[]{:S(2)}, u32[]{:S(2)}) collective-permute-start(bf16[48,1024]{1,0:T(8,128)(2,1)S(1)} %get-tuple-element.111), channel_id=1, source_target_pairs={{0,1},{1,0},{2,3},{3,2},{4,5},{5,4},{6,7},{7,6},{8,9},{9,8},{10,11... | collective-permute-start | bytes 294920 | tf_op jit(solution)/shard_map/ppermute | solution.py:52
  87.8 5.2 %collective-permute-start.16 = (bf16[48,1024]{1,0:T(8,128)(2,1)S(1)}, bf16[48,1024]{1,0:T(8,128)(2,1)S(1)}, u32[]{:S(2)}, u32[]{:S(2)}) collective-permute-start(bf16[48,1024]{1,0:T(8,128)(2,1)S(1)} %get-tuple-element.112), channel_id=1, source_target_pairs={{0,1},{1,0},{2,3},{3,2},{4,5},{5,4},{6,7},{7,6},{8,9},{9,8},{10,11... | collective-permute-start | bytes 294920 | tf_op jit(solution)/shard_map/ppermute | solution.py:52
  88.3 4.7 %collective-permute-start.14 = (bf16[48,512]{1,0:T(8,128)(2,1)S(1)}, bf16[48,512]{1,0:T(8,128)(2,1)S(1)}, u32[]{:S(2)}, u32[]{:S(2)}) collective-permute-start(bf16[48,512]{1,0:T(8,128)(2,1)S(1)} %get-tuple-element.110), channel_id=1, source_target_pairs={{0,2},{1,3},{2,0},{3,1},{4,6},{5,7},{6,4},{7,5},{8,10},{9,11},{10,... | collective-permute-start | bytes 147464 | tf_op jit(solution)/shard_map/ppermute | solution.py:52

commit v8 on v7

--- a/solution.py
+++ b/solution.py
@@ -249,7 +249,7 @@
         [jax.ShapeDtypeStruct((nodes, size), jnp.float32)]
         + [jax.ShapeDtypeStruct((size, share), jnp.bfloat16)] * far,
         [((slots, tile, size), jnp.float32), ((share, size), jnp.float32)],
-        2**22,
+        2**20,
     )
     return outs[0], outs[1:]
 
@@ -343,43 +343,50 @@
         (accs, weight.T, picks, whose * width)
     )
 
-    got = []
+    got, early = [], []
     for p, leaving in enumerate(sent):
         if p:
-            leaving, got[-1], accs = lax.optimization_barrier((leaving, got[-1], accs))
+            leaving, got[-1], early[-1], accs = lax.optimization_barrier(
+                (leaving, got[-1], early[-1], accs)
+            )
         got.append([shifted(value, "blk", s + 1) for s, value in enumerate(leaving)])
-
-    pieces, waits, kept = {}, {}, {}
-    acc, late = accs[0], 1
+        early.append(add_early(accs[p], inverse, rows, counts, got[p][:-1], 1))
+
+    pieces, across_x, beside = {}, {}, {}
     for p, (low, size) in enumerate(ranges[:-1]):
-        total, out_far = gather_far(acc, inverse, rows, picks[:far], counts, got[p], 1)
+        total, out_far = gather_far(
+            early[p], inverse, rows, picks[:far], counts, got[p][-1:], blocks - 1
+        )
         for i, piece in enumerate(out_far):
-            waits[i, low, 0] = traded(piece, "grp", ranks[i])
-        beside, kept = gather_next(total, picks[far:], [(share,), (share,)])
-        early, late = got[p + 1][:-1], blocks - 1
-        acc = add_early(accs[p + 1], inverse, rows, counts, early, 1)
-        beside, kept, acc, got[p + 1] = lax.optimization_barrier(
-            (beside, kept, acc, got[p + 1])
+            across_x[i, low, 0] = traded(piece, "grp", ranks[i])
+        halves = (share // 2, share // 2)
+        near = gather_next(total, picks[far:], [halves, (share,)])
+        near, early[p + 1], got[p + 1] = lax.optimization_barrier(
+            (near, early[p + 1], got[p + 1])
         )
-        waits[far, low, 0] = traded(beside, "grp", 1)
-        pieces[far + 1, low, 0] = kept
+        beside[far, low, 0] = traded(near[0], "grp", 1)
+        beside[far, low, share // 2] = traded(near[1], "grp", 1)
+        pieces[far + 1, low, 0] = near[2]
 
     low, size = ranges[-1]
-    total, out_far = gather_far(acc, inverse, rows, picks[:1], counts, got[-1][late - 1 :], late)
+    total, out_far = gather_far(
+        early[-1], inverse, rows, picks[:1], counts, got[-1][-1:], blocks - 1
+    )
     pieces[0, low, 0] = traded(out_far[0], "grp", ranks[0])
     for i in range(1, groups):
         widths = (share,)
         if i < far:
-            total, waits = lax.optimization_barrier((total, waits))
-            pieces.update(waits)
+            total, beside = lax.optimization_barrier((total, beside))
             widths = (share // 4 * 3, share // 4)
         elif i == far:
+            total, across_x = lax.optimization_barrier((total, across_x))
             widths = (share // 2, share // 2)
         first = 0
         for piece in gather_next(total, [picks[i]], [widths]):
             pieces[i, low, first] = traded(piece, "grp", ranks[i]) if ranks[i] else piece
             first += piece.shape[1]
-    pieces.update(waits)
+    pieces.update(beside)
+    pieces.update(across_x)
     return mix(starts, across, column, pieces, share)
 
 

time: 96.2 us -> 90.1 us (0.937)
  the two profiles are of different devices: /device:TPU:0 before, /device:TPU:25 now
where the time goes in v8:
time: 90.1 us; the launch traced here: 89.7 us
  Pallas kernels  43.2 us (48%)
  waiting for transfers between devices  24.6 us (27%)
  starting transfers between devices  15.2 us (17%)
  local copies, waits for them, and re-layouts  6.53 us (7%)
    pallas_call x10, Pallas kernels, call(): pl.pallas_call(kernel, out_shape=list(outs), in_specs=[SMEM] * len(scalar...  37.3 us
    ppermute x9, waiting for transfers between devices, shifted(): return lax.ppermute(value, axis, pairs)  24.6 us
    ppermute x9, starting transfers between devices, traded(): lax.ppermute(value, axis, [(i, i ^ k) for i in range(lax.axis_size(axis))])  9.31 us
    unnamed x29, local copies, waits for them, and re-layouts  6.51 us
    ppermute x9, starting transfers between devices, shifted(): return lax.ppermute(value, axis, pairs)  5.85 us
    pallas_call x2, Pallas kernels, pack(): pl.pallas_call(functools.partial(pack_kernel, low, size, offsets, slots,...  3.06 us
    pallas_call x1, Pallas kernels, mix(): pl.pallas_call(functools.partial(mix_kernel, places), out_shape=jax.Shape...  2.78 us
  transfers between devices with their start and end apart: 18, of which 4 were waited for; matrix products, arithmetic and copies ran while one was open for 1% of the time, Pallas kernels for 43%

profile of v8, /device:TPU:25, one launch (start us, length us, event | category | flops | bytes accessed | tf_op | source)
XLA Modules:
  0.0 89.7 jit_solution(12215248499143805178)
XLA Ops:
  0.0 1.3 %collective-permute-start.1 = (s32[4,20]{1,0:T(4,128)}, s32[4,20]{1,0:T(4,128)S(1)}, u32[]{:S(2)}, u32[]{:S(2)}) collective-permute-start(s32[4,20]{1,0:T(4,128)} %bitcast.17), channel_id=1, source_target_pairs={{0,8},{4,12},{8,0},{12,4},{1,9},{5,13},{9,1},{13,5},{2,10},{6,14},... | collective-permute-start | bytes 968 | tf_op jit(solution)/shard_map/ppermute | solution.py:48
  1.4 0.2 collective-permute-start
  1.5 1.6 %copy-done.1 = bf16[128,8192]{1,0:T(8,128)(2,1)S(1)} copy-done((bf16[128,8192]{1,0:T(8,128)(2,1)S(1)}, bf16[128,8192]{1,0:T(8,128)(2,1)}, u32[]{:S(2)}) %copy-start.1) | copy-done | bytes 2097176
  3.1 0.1 stage.1.refs_3_
  3.3 0.0 collective-permute-done.2.refs_2_
  3.3 0.3 collective-permute-done.1.refs_1_
  3.6 2.2 %collective-permute-done.refs_0_ = s32[4,20]{1,0:T(4,128)S(1)} collective-permute-done((s32[4,20]{1,0:T(4,128)}, s32[4,20]{1,0:T(4,128)S(1)}, u32[]{:S(2)}, u32[]{:S(2)}) %collective-permute-start) | collective-permute-done | bytes 352 | tf_op jit(solution)/shard_map/ppermute | solution.py:48
  5.8 1.6 %pack.2 = (bf16[20,80,128]{2,1,0:T(8,128)(2,1)}, bf16[20,80,128]{2,1,0:T(8,128)(2,1)}, bf16[20,80,128]{2,1,0:T(8,128)(2,1)}) custom-call(s32[4,20]{1,0:T(4,128)S(1)} %collective-permute-done.refs_0_, s32[4,20]{1,0:T(4,128)S(1)} %collective-permute-done.1.refs_1_, s32[4,20]{1,0:T(4,128)S(1)} %collective-permute-done.2.refs_2_, bf16[128,8192]{1,0:T(8,128)(2,1)S(1)} %stage.1.refs_3_), custom_call_target="tpu_custom_call" | custom-call | bytes 65536 | tf_op jit(solution)/shard_map/pack/pallas_call | solution.py:94
  7.4 0.7 collective-permute-start.3
  8.2 0.8 collective-permute-start.5
  9.0 1.3 %copy.9 = bf16[512,512]{0,1:T(8,128)(2,1)S(1)} copy(bf16[512,512]{1,0:T(8,128)(2,1)} %param.13) | data formatting | bytes 1048576 | tf_op args[5]
  10.3 0.0 copy-start.13
  10.3 0.0 copy-start.2
  10.4 1.6 %copy-done.2 = bf16[128,8192]{1,0:T(8,128)(2,1)S(1)} copy-done((bf16[128,8192]{1,0:T(8,128)(2,1)S(1)}, bf16[128,8192]{1,0:T(8,128)(2,1)}, u32[]{:S(2)}) %copy-start.2) | copy-done | bytes 2097176
  11.9 0.7 copy-done.3
  12.6 0.7 copy-done.10
  13.3 0.7 copy-done.11
  14.0 9.2 %own.1 = (f32[8192,80]{1,0:T(8,128)S(1)}, f32[8192,48]{1,0:T(8,128)S(1)}, f32[8192,80]{1,0:T(8,128)S(1)}, f32[512,128]{1,0:T(8,128)S(1)}) custom-call(s32[4,20]{1,0:T(4,128)S(1)} %bitcast.11, s32[4,20]{1,0:T(4,128)S(1)} %bitcast.19, bf16[128,8192]{1,0:T(8,128)(2,1)S(1)} %copy-done.2, bf16[80,128,128]{2,1,0:T(8,128)(2,1)S(1)} %bitcast.5, f32[1,512]{1,0:T(1,128)S(1)} %bitcast.20), custom_call_target="tpu_custom_call" | custom-call | bytes 65536 | tf_op jit(solution)/shard_map/own/pallas_call | solution.py:33
  23.3 1.4 %pack.3 = (bf16[20,48,128]{2,1,0:T(8,128)(2,1)S(1)}, bf16[20,48,128]{2,1,0:T(8,128)(2,1)S(1)}, bf16[20,48,128]{2,1,0:T(8,128)(2,1)S(1)}) custom-call(s32[4,20]{1,0:T(4,128)S(1)} %copy-done.9, s32[4,20]{1,0:T(4,128)S(1)} %copy-done.7, s32[4,20]{1,0:T(4,128)S(1)} %copy-done.5, bf16[128,8192]{1,0:T(8,128)(2,1)S(1)} %copy-done.2), custom_call_target="tpu_custom_call" | custom-call | bytes 65536 | tf_op jit(solution)/shard_map/pack/pallas_call | solution.py:94
  24.7 17.2 %collective-permute-done.4.refs_1_ = bf16[20,80,128]{2,1,0:T(8,128)(2,1)} collective-permute-done((bf16[20,80,128]{2,1,0:T(8,128)(2,1)}, bf16[20,80,128]{2,1,0:T(8,128)(2,1)}, u32[]{:S(2)}, u32[]{:S(2)}) %collective-permute-start.4) | collective-permute-done | bytes 409632 | tf_op jit(solution)/shard_map/ppermute | solution.py:48
  41.9 2.9 %add_early.2.refs_2_ = f32[8192,80]{1,0:T(8,128)S(1)} custom-call(s32[4,20]{1,0:T(4,128)S(1)} %bitcast.12, f32[8192,80]{1,0:T(8,128)S(1)} %get-tuple-element.85.acc, f32[8192,80]{1,0:T(8,128)S(1)} %get-tuple-element.86.inverse.refs_3_.refs_2_, bf16[80,128,128]{2,1,0:T(8,128)(2,1)S(1)} %bitcast.6, bf16[20,80,128]{2,1,0:T(8,128)(2,1)} %collective-permute-done.3.refs_0_, ...), custom_call_target="tpu_custom_call" | custom-call | bytes 65536 | tf_op jit(solution)/shard_map/add_early/pallas_call | solution.py:33
  44.9 0.1 collective-permute-start.6
  45.0 1.2 %collective-permute-start.7 = (bf16[20,48,128]{2,1,0:T(8,128)(2,1)S(1)}, bf16[20,48,128]{2,1,0:T(8,128)(2,1)S(1)}, u32[]{:S(2)}, u32[]{:S(2)}) collective-permute-start(bf16[20,48,128]{2,1,0:T(8,128)(2,1)S(1)} %get-tuple-element.96), channel_id=1, source_target_pairs={{0,8},{4,12},{8,0},{12,4},{1,9},{5,13},{9,1},{13,5},{2,10},{6,14},... | collective-permute-start | bytes 737288 | tf_op jit(solution)/shard_map/ppermute | solution.py:48
  46.2 1.5 %collective-permute-start.8 = (bf16[20,48,128]{2,1,0:T(8,128)(2,1)S(1)}, bf16[20,48,128]{2,1,0:T(8,128)(2,1)S(1)}, u32[]{:S(2)}, u32[]{:S(2)}) collective-permute-start(bf16[20,48,128]{2,1,0:T(8,128)(2,1)S(1)} %get-tuple-element.97), channel_id=1, source_target_pairs={{0,12},{4,0},{8,4},{12,8},{1,13},{5,1},{9,5},{13,9},{2,14},{6,2},{... | collective-permute-start | bytes 737288 | tf_op jit(solution)/shard_map/ppermute | solution.py:48
  47.6 6.0 %gather_far.2 = (f32[8192,80]{1,0:T(8,128)S(1)}, bf16[80,2048]{1,0:T(8,128)(2,1)S(1)}, bf16[80,2048]{1,0:T(8,128)(2,1)S(1)}) custom-call(s32[4,20]{1,0:T(4,128)S(1)} %bitcast.13, s32[2048]{0:T(1024)S(1)} %get-tuple-element.68.refs_0_, s32[2048]{0:T(1024)S(1)} %get-tuple-element.69.refs_1_.refs_0_, f32[8192,80]{1,0:T(8,128)S(1)} %add_early.2.refs_2_, ...), custom_call_target="tpu_custom_call" | custom-call | bytes 1048576 | tf_op jit(solution)/shard_map/gather_far/pallas_call | solution.py:33
  53.7 3.5 %collective-permute-start.14 = (bf16[80,2048]{1,0:T(8,128)(2,1)S(1)}, bf16[80,2048]{1,0:T(8,128)(2,1)S(1)}, u32[]{:S(2)}, u32[]{:S(2)}) collective-permute-start(bf16[80,2048]{1,0:T(8,128)(2,1)S(1)} %get-tuple-element.108), channel_id=1, source_target_pairs={{0,3},{1,2},{2,1},{3,0},{4,7},{5,6},{6,5},{7,4},{8,11},{9,10},{10,... | collective-permute-start | bytes 983048 | tf_op jit(solution)/shard_map/ppermute | solution.py:52
  57.2 0.2 collective-permute-start.15
  57.4 4.9 %gather_next.4 = (bf16[80,1024]{1,0:T(8,128)(2,1)S(1)}, bf16[80,1024]{1,0:T(8,128)(2,1)S(1)}, bf16[80,2048]{1,0:T(8,128)(2,1)S(1)}) custom-call(s32[2048]{0:T(1024)S(1)} %get-tuple-element.66.refs_0_, s32[2048]{0:T(1024)S(1)} %get-tuple-element.67.refs_1_.refs_0_, f32[8192,80]{1,0:T(8,128)S(1)} %get-tuple-element.90.refs_2_), custom_call_target="tpu_custom_call" | custom-call | bytes 65536 | tf_op jit(solution)/shard_map/gather_next/pallas_call | solution.py:33
  62.4 0.0 collective-permute-done.6.refs_0_
  62.4 4.9 %collective-permute-done.7.refs_1_ = bf16[20,48,128]{2,1,0:T(8,128)(2,1)S(1)} collective-permute-done((bf16[20,48,128]{2,1,0:T(8,128)(2,1)S(1)}, bf16[20,48,128]{2,1,0:T(8,128)(2,1)S(1)}, u32[]{:S(2)}, u32[]{:S(2)}) %collective-permute-start.7) | collective-permute-done | bytes 245792 | tf_op jit(solution)/shard_map/ppermute | solution.py:48
  67.2 2.2 %add_early.3.refs_1_ = f32[8192,48]{1,0:T(8,128)S(1)} custom-call(s32[4,20]{1,0:T(4,128)S(1)} %bitcast.14, f32[8192,48]{1,0:T(8,128)S(1)} %get-tuple-element.94.acc, f32[8192,80]{1,0:T(8,128)S(1)} %get-tuple-element.86.inverse.refs_3_.refs_2_, bf16[80,128,128]{2,1,0:T(8,128)(2,1)S(1)} %bitcast.8, bf16[20,48,128]{2,1,0:T(8,128)(2,1)S(1)} %collective-permute-done.6.refs_0_, ...), custom_call_target="tpu_custom_call" | custom-call | bytes 65536 | tf_op jit(solution)/shard_map/add_early/pallas_call | solution.py:33
  69.4 0.0 collective-permute-done.8.refs_4_
  69.5 1.8 %collective-permute-start.10 = (bf16[80,1024]{1,0:T(8,128)(2,1)S(1)}, bf16[80,1024]{1,0:T(8,128)(2,1)S(1)}, u32[]{:S(2)}, u32[]{:S(2)}) collective-permute-start(bf16[80,1024]{1,0:T(8,128)(2,1)S(1)} %get-tuple-element.103), channel_id=1, source_target_pairs={{0,1},{1,0},{2,3},{3,2},{4,5},{5,4},{6,7},{7,6},{8,9},{9,8},{10,11... | collective-permute-start | bytes 491528 | tf_op jit(solution)/shard_map/ppermute | solution.py:52
  71.2 0.1 collective-permute-start.11
  71.3 3.7 %gather_far.3 = (f32[8192,48]{1,0:T(8,128)S(1)}, bf16[48,2048]{1,0:T(8,128)(2,1)S(1)}) custom-call(s32[4,20]{1,0:T(4,128)S(1)} %bitcast.15, s32[2048]{0:T(1024)S(1)} %get-tuple-element.68.refs_0_, f32[8192,48]{1,0:T(8,128)S(1)} %add_early.3.refs_1_, f32[8192,80]{1,0:T(8,128)S(1)} %get-tuple-element.86.inverse.refs_3_.refs_2_, ...), custom_call_target="tpu_custom_call" | custom-call | bytes 1048576 | tf_op jit(solution)/shard_map/gather_far/pallas_call | solution.py:33
  75.0 1.6 %collective-permute-start.9 = (bf16[48,2048]{1,0:T(8,128)(2,1)S(1)}, bf16[48,2048]{1,0:T(8,128)(2,1)S(1)}, u32[]{:S(2)}, u32[]{:S(2)}) collective-permute-start(bf16[48,2048]{1,0:T(8,128)(2,1)S(1)} %get-tuple-element.101), channel_id=1, source_target_pairs={{0,3},{1,2},{2,1},{3,0},{4,7},{5,6},{6,5},{7,4},{8,11},{9,10},{10,... | collective-permute-start | bytes 589832 | tf_op jit(solution)/shard_map/ppermute | solution.py:52
  76.6 2.7 %gather_next.5 = (bf16[48,1536]{1,0:T(8,128)(2,1)S(1)}, bf16[48,512]{1,0:T(8,128)(2,1)S(1)}) custom-call(s32[2048]{0:T(1024)S(1)} %get-tuple-element.69.refs_1_.refs_0_, f32[8192,48]{1,0:T(8,128)S(1)} %get-tuple-element.110.refs_1_), custom_call_target="tpu_custom_call" | custom-call | bytes 65536 | tf_op jit(solution)/shard_map/gather_next/pallas_call | solution.py:33
  79.4 0.3 collective-permute-start.12
  79.7 0.0 collective-permute-done.14.refs_9_
  79.7 0.0 collective-permute-done.15.refs_10_
  79.7 2.7 %gather_next.6 = (bf16[48,1024]{1,0:T(8,128)(2,1)S(1)}, bf16[48,1024]{1,0:T(8,128)(2,1)S(1)}) custom-call(s32[2048]{0:T(1024)S(1)} %get-tuple-element.66.refs_0_, f32[8192,48]{1,0:T(8,128)S(1)} %get-tuple-element.110.refs_1_), custom_call_target="tpu_custom_call" | custom-call | bytes 65536 | tf_op jit(solution)/shard_map/gather_next/pallas_call | solution.py:33
  82.4 0.4 collective-permute-start.16
  82.8 0.2 collective-permute-start.17
  83.0 1.2 %collective-permute-start.13 = (bf16[48,512]{1,0:T(8,128)(2,1)S(1)}, bf16[48,512]{1,0:T(8,128)(2,1)S(1)}, u32[]{:S(2)}, u32[]{:S(2)}) collective-permute-start(bf16[48,512]{1,0:T(8,128)(2,1)S(1)} %get-tuple-element.107), channel_id=1, source_target_pairs={{0,2},{1,3},{2,0},{3,1},{4,6},{5,7},{6,4},{7,5},{8,10},{9,11},{10,... | collective-permute-start | bytes 147464 | tf_op jit(solution)/shard_map/ppermute | solution.py:52
  84.2 2.7 %gather_next.7.refs_6_ = bf16[48,2048]{1,0:T(8,128)(2,1)S(1)} custom-call(s32[2048]{0:T(1024)S(1)} %get-tuple-element.67.refs_1_.refs_0_, f32[8192,48]{1,0:T(8,128)S(1)} %get-tuple-element.110.refs_1_), custom_call_target="tpu_custom_call" | custom-call | bytes 65536 | tf_op jit(solution)/shard_map/gather_next/pallas_call | solution.py:33
  86.9 0.0 collective-permute-done.13.refs_3_
  86.9 0.0 collective-permute-done.16.refs_4_
  87.0 2.8 %mix.1 = bf16[512,2048]{1,0:T(8,128)(2,1)} custom-call(s32[4]{0:T(128)S(1)} %xor_multiply_fusion.starts, bf16[512,512]{1,0:T(8,128)(2,1)S(1)} %bitcast.10, f32[512,128]{1,0:T(8,128)S(1)} %get-tuple-element.65.bias, bf16[80,2048]{1,0:T(8,128)(2,1)S(1)} %get-tuple-element.98.refs_0_, bf16[48,2048]{1,0:T(8,128)(2,1)S(1)} %collective-permute-done.9.refs_1_, ...), custom_call_target="tpu_custom_call" | custom-call | flops 1073741824 | bytes 5242880 | tf_op jit(solution)/shard_map/mix/pallas_call | solution.py:300
  (32 shorter events, 0.1 us)
Async XLA Ops:
  0.0 10.3 %copy-start = (bf16[1,4,20,128,128]{4,3,2,1,0:T(8,128)(2,1)S(1)}, bf16[1,4,20,128,128]{4,3,2,1,0:T(8,128)(2,1)}, u32[]{:S(2)}) copy-start(bf16[1,4,20,128,128]{4,3,2,1,0:T(8,128)(2,1)} %param.11) | copy-start | bytes 7864324
  0.0 3.3 %collective-permute-start.2 = (s32[4,20]{1,0:T(4,128)}, s32[4,20]{1,0:T(4,128)S(1)}, u32[]{:S(2)}, u32[]{:S(2)}) collective-permute-start(s32[4,20]{1,0:T(4,128)} %bitcast.16), channel_id=1, source_target_pairs={{0,4},{4,8},{8,12},{12,0},{1,5},{5,9},{9,13},{13,1},{2,6},{6,10},{... | collective-permute-start | bytes 968 | tf_op jit(solution)/shard_map/ppermute | solution.py:48
  0.0 3.6 %collective-permute-start.1 = (s32[4,20]{1,0:T(4,128)}, s32[4,20]{1,0:T(4,128)S(1)}, u32[]{:S(2)}, u32[]{:S(2)}) collective-permute-start(s32[4,20]{1,0:T(4,128)} %bitcast.17), channel_id=1, source_target_pairs={{0,8},{4,12},{8,0},{12,4},{1,9},{5,13},{9,1},{13,5},{2,10},{6,14},... | collective-permute-start | bytes 968 | tf_op jit(solution)/shard_map/ppermute | solution.py:48
  1.4 4.4 %collective-permute-start = (s32[4,20]{1,0:T(4,128)}, s32[4,20]{1,0:T(4,128)S(1)}, u32[]{:S(2)}, u32[]{:S(2)}) collective-permute-start(s32[4,20]{1,0:T(4,128)} %bitcast.18), channel_id=1, source_target_pairs={{0,12},{4,0},{8,4},{12,8},{1,13},{5,1},{9,5},{13,9},{2,14},{6,2},{... | collective-permute-start | bytes 968 | tf_op jit(solution)/shard_map/ppermute | solution.py:48
  1.5 1.6 %copy-start.1 = (bf16[128,8192]{1,0:T(8,128)(2,1)S(1)}, bf16[128,8192]{1,0:T(8,128)(2,1)}, u32[]{:S(2)}) copy-start(bf16[128,8192]{1,0:T(8,128)(2,1)} %refs_3_.1) | copy-start | bytes 6291460
  3.3 4.9 %copy-start.4 = (s32[4,20]{1,0:T(4,128)}, s32[4,20]{1,0:T(4,128)S(1)}, u32[]{:S(2)}) copy-start(s32[4,20]{1,0:T(4,128)S(1)} %collective-permute-done.2.refs_2_) | copy-start | bytes 964
  3.6 4.6 %copy-start.6 = (s32[4,20]{1,0:T(4,128)}, s32[4,20]{1,0:T(4,128)S(1)}, u32[]{:S(2)}) copy-start(s32[4,20]{1,0:T(4,128)S(1)} %collective-permute-done.1.refs_1_) | copy-start | bytes 964
  5.8 3.2 %copy-start.8 = (s32[4,20]{1,0:T(4,128)}, s32[4,20]{1,0:T(4,128)S(1)}, u32[]{:S(2)}) copy-start(s32[4,20]{1,0:T(4,128)S(1)} %collective-permute-done.refs_0_) | copy-start | bytes 964
  7.4 17.3 %collective-permute-start.3 = (bf16[20,80,128]{2,1,0:T(8,128)(2,1)}, bf16[20,80,128]{2,1,0:T(8,128)(2,1)}, u32[]{:S(2)}, u32[]{:S(2)}) collective-permute-start(bf16[20,80,128]{2,1,0:T(8,128)(2,1)} %get-tuple-element.82), channel_id=1, source_target_pairs={{0,4},{4,8},{8,12},{12,0},{1,5},{5,9},{9,13},{13,1},{2,6},{6,10},{... | collective-permute-start | bytes 1228808 | tf_op jit(solution)/shard_map/ppermute | solution.py:48
  8.2 33.7 %collective-permute-start.4 = (bf16[20,80,128]{2,1,0:T(8,128)(2,1)}, bf16[20,80,128]{2,1,0:T(8,128)(2,1)}, u32[]{:S(2)}, u32[]{:S(2)}) collective-permute-start(bf16[20,80,128]{2,1,0:T(8,128)(2,1)} %get-tuple-element.83), channel_id=1, source_target_pairs={{0,8},{4,12},{8,0},{12,4},{1,9},{5,13},{9,1},{13,5},{2,10},{6,14},... | collective-permute-start | bytes 1228808 | tf_op jit(solution)/shard_map/ppermute | solution.py:48
  8.2 36.7 %collective-permute-start.5 = (bf16[20,80,128]{2,1,0:T(8,128)(2,1)}, bf16[20,80,128]{2,1,0:T(8,128)(2,1)S(1)}, u32[]{:S(2)}, u32[]{:S(2)}) collective-permute-start(bf16[20,80,128]{2,1,0:T(8,128)(2,1)} %get-tuple-element.84), channel_id=1, source_target_pairs={{0,12},{4,0},{8,4},{12,8},{1,13},{5,1},{9,5},{13,9},{2,14},{6,2},{... | collective-permute-start | bytes 1228808 | tf_op jit(solution)/shard_map/ppermute | solution.py:48
  10.3 12.9 %copy-start.13 = (s32[4]{0:T(128)S(1)}, s32[4]{0:T(128)}, u32[]{:S(2)}) copy-start(s32[4]{0:T(128)} %constant.20.clone) | copy-start | bytes 52
  10.3 13.0 %copy-start.5 = (s32[4,20]{1,0:T(4,128)S(1)}, s32[4,20]{1,0:T(4,128)}, u32[]{:S(2)}) copy-start(s32[4,20]{1,0:T(4,128)} %copy-done.4) | copy-start | bytes 964
  10.3 13.0 %copy-start.7 = (s32[4,20]{1,0:T(4,128)S(1)}, s32[4,20]{1,0:T(4,128)}, u32[]{:S(2)}) copy-start(s32[4,20]{1,0:T(4,128)} %copy-done.6) | copy-start | bytes 964
  10.3 1.6 %copy-start.2 = (bf16[128,8192]{1,0:T(8,128)(2,1)S(1)}, bf16[128,8192]{1,0:T(8,128)(2,1)}, u32[]{:S(2)}) copy-start(bf16[128,8192]{1,0:T(8,128)(2,1)} %refs_3_.1) | copy-start | bytes 6291460
  11.9 0.7 copy-start.3
  12.6 0.7 copy-start.10
  13.3 0.7 copy-start.11
  14.0 9.2 %copy-start.12 = (s32[8192]{0:T(1024)S(1)}, s32[8192]{0:T(1024)}, u32[]{:S(2)}) copy-start(s32[8192]{0:T(1024)} %param.12) | copy-start | bytes 98308
  14.0 9.3 %copy-start.9 = (s32[4,20]{1,0:T(4,128)S(1)}, s32[4,20]{1,0:T(4,128)}, u32[]{:S(2)}) copy-start(s32[4,20]{1,0:T(4,128)} %copy-done.8) | copy-start | bytes 964
  44.9 17.5 %collective-permute-start.6 = (bf16[20,48,128]{2,1,0:T(8,128)(2,1)S(1)}, bf16[20,48,128]{2,1,0:T(8,128)(2,1)S(1)}, u32[]{:S(2)}, u32[]{:S(2)}) collective-permute-start(bf16[20,48,128]{2,1,0:T(8,128)(2,1)S(1)} %get-tuple-element.95), channel_id=1, source_target_pairs={{0,4},{4,8},{8,12},{12,0},{1,5},{5,9},{9,13},{13,1},{2,6},{6,10},{... | collective-permute-start | bytes 737288 | tf_op jit(solution)/shard_map/ppermute | solution.py:48
  45.0 22.3 %collective-permute-start.7 = (bf16[20,48,128]{2,1,0:T(8,128)(2,1)S(1)}, bf16[20,48,128]{2,1,0:T(8,128)(2,1)S(1)}, u32[]{:S(2)}, u32[]{:S(2)}) collective-permute-start(bf16[20,48,128]{2,1,0:T(8,128)(2,1)S(1)} %get-tuple-element.96), channel_id=1, source_target_pairs={{0,8},{4,12},{8,0},{12,4},{1,9},{5,13},{9,1},{13,5},{2,10},{6,14},... | collective-permute-start | bytes 737288 | tf_op jit(solution)/shard_map/ppermute | solution.py:48
  46.2 23.3 %collective-permute-start.8 = (bf16[20,48,128]{2,1,0:T(8,128)(2,1)S(1)}, bf16[20,48,128]{2,1,0:T(8,128)(2,1)S(1)}, u32[]{:S(2)}, u32[]{:S(2)}) collective-permute-start(bf16[20,48,128]{2,1,0:T(8,128)(2,1)S(1)} %get-tuple-element.97), channel_id=1, source_target_pairs={{0,12},{4,0},{8,4},{12,8},{1,13},{5,1},{9,5},{13,9},{2,14},{6,2},{... | collective-permute-start | bytes 737288 | tf_op jit(solution)/shard_map/ppermute | solution.py:48
  53.7 26.0 %collective-permute-start.14 = (bf16[80,2048]{1,0:T(8,128)(2,1)S(1)}, bf16[80,2048]{1,0:T(8,128)(2,1)S(1)}, u32[]{:S(2)}, u32[]{:S(2)}) collective-permute-start(bf16[80,2048]{1,0:T(8,128)(2,1)S(1)} %get-tuple-element.108), channel_id=1, source_target_pairs={{0,3},{1,2},{2,1},{3,0},{4,7},{5,6},{6,5},{7,4},{8,11},{9,10},{10,... | collective-permute-start | bytes 983048 | tf_op jit(solution)/shard_map/ppermute | solution.py:52
  57.2 22.5 %collective-permute-start.15 = (bf16[80,2048]{1,0:T(8,128)(2,1)S(1)}, bf16[80,2048]{1,0:T(8,128)(2,1)S(1)}, u32[]{:S(2)}, u32[]{:S(2)}) collective-permute-start(bf16[80,2048]{1,0:T(8,128)(2,1)S(1)} %get-tuple-element.109), channel_id=1, source_target_pairs={{0,2},{1,3},{2,0},{3,1},{4,6},{5,7},{6,4},{7,5},{8,10},{9,11},{10,... | collective-permute-start | bytes 983048 | tf_op jit(solution)/shard_map/ppermute | solution.py:52
  69.5 7.2 %collective-permute-start.10 = (bf16[80,1024]{1,0:T(8,128)(2,1)S(1)}, bf16[80,1024]{1,0:T(8,128)(2,1)S(1)}, u32[]{:S(2)}, u32[]{:S(2)}) collective-permute-start(bf16[80,1024]{1,0:T(8,128)(2,1)S(1)} %get-tuple-element.103), channel_id=1, source_target_pairs={{0,1},{1,0},{2,3},{3,2},{4,5},{5,4},{6,7},{7,6},{8,9},{9,8},{10,11... | collective-permute-start | bytes 491528 | tf_op jit(solution)/shard_map/ppermute | solution.py:52
  71.2 5.4 %collective-permute-start.11 = (bf16[80,1024]{1,0:T(8,128)(2,1)S(1)}, bf16[80,1024]{1,0:T(8,128)(2,1)S(1)}, u32[]{:S(2)}, u32[]{:S(2)}) collective-permute-start(bf16[80,1024]{1,0:T(8,128)(2,1)S(1)} %get-tuple-element.104), channel_id=1, source_target_pairs={{0,1},{1,0},{2,3},{3,2},{4,5},{5,4},{6,7},{7,6},{8,9},{9,8},{10,11... | collective-permute-start | bytes 491528 | tf_op jit(solution)/shard_map/ppermute | solution.py:52
  75.0 11.9 %collective-permute-start.9 = (bf16[48,2048]{1,0:T(8,128)(2,1)S(1)}, bf16[48,2048]{1,0:T(8,128)(2,1)S(1)}, u32[]{:S(2)}, u32[]{:S(2)}) collective-permute-start(bf16[48,2048]{1,0:T(8,128)(2,1)S(1)} %get-tuple-element.101), channel_id=1, source_target_pairs={{0,3},{1,2},{2,1},{3,0},{4,7},{5,6},{6,5},{7,4},{8,11},{9,10},{10,... | collective-permute-start | bytes 589832 | tf_op jit(solution)/shard_map/ppermute | solution.py:52
  79.4 7.6 %collective-permute-start.12 = (bf16[48,1536]{1,0:T(8,128)(2,1)S(1)}, bf16[48,1536]{1,0:T(8,128)(2,1)S(1)}, u32[]{:S(2)}, u32[]{:S(2)}) collective-permute-start(bf16[48,1536]{1,0:T(8,128)(2,1)S(1)} %get-tuple-element.106), channel_id=1, source_target_pairs={{0,2},{1,3},{2,0},{3,1},{4,6},{5,7},{6,4},{7,5},{8,10},{9,11},{10,... | collective-permute-start | bytes 442376 | tf_op jit(solution)/shard_map/ppermute | solution.py:52
  82.4 4.5 %collective-permute-start.16 = (bf16[48,1024]{1,0:T(8,128)(2,1)S(1)}, bf16[48,1024]{1,0:T(8,128)(2,1)S(1)}, u32[]{:S(2)}, u32[]{:S(2)}) collective-permute-start(bf16[48,1024]{1,0:T(8,128)(2,1)S(1)} %get-tuple-element.111), channel_id=1, source_target_pairs={{0,1},{1,0},{2,3},{3,2},{4,5},{5,4},{6,7},{7,6},{8,9},{9,8},{10,11... | collective-permute-start | bytes 294920 | tf_op jit(solution)/shard_map/ppermute | solution.py:52
  82.8 4.1 %collective-permute-start.17 = (bf16[48,1024]{1,0:T(8,128)(2,1)S(1)}, bf16[48,1024]{1,0:T(8,128)(2,1)S(1)}, u32[]{:S(2)}, u32[]{:S(2)}) collective-permute-start(bf16[48,1024]{1,0:T(8,128)(2,1)S(1)} %get-tuple-element.112), channel_id=1, source_target_pairs={{0,1},{1,0},{2,3},{3,2},{4,5},{5,4},{6,7},{7,6},{8,9},{9,8},{10,11... | collective-permute-start | bytes 294920 | tf_op jit(solution)/shard_map/ppermute | solution.py:52
  83.0 3.9 %collective-permute-start.13 = (bf16[48,512]{1,0:T(8,128)(2,1)S(1)}, bf16[48,512]{1,0:T(8,128)(2,1)S(1)}, u32[]{:S(2)}, u32[]{:S(2)}) collective-permute-start(bf16[48,512]{1,0:T(8,128)(2,1)S(1)} %get-tuple-element.107), channel_id=1, source_target_pairs={{0,2},{1,3},{2,0},{3,1},{4,6},{5,7},{6,4},{7,5},{8,10},{9,11},{10,... | collective-permute-start | bytes 147464 | tf_op jit(solution)/shard_map/ppermute | solution.py:52

commit v9 on v8

--- a/solution.py
+++ b/solution.py
@@ -103,13 +103,21 @@
     )(*asked, panel)
 
 
-def own_kernel(ranges, blocks, slots, tile, rows, cols, panel, counts, bias, *refs):
-    accs, (inverse, column, product) = refs[:-3], refs[-3:]
+def own_kernel(
+    ranges, blocks, slots, tile, rows, cols, starts, panel, counts, bias, weight, *refs
+):
+    accs, (inverse, column, across, product, sorted_rows) = refs[:-5], refs[-5:]
     lanes = inverse.shape[1]
     row_tiles = panel.shape[1] // tile
     eye = identity(tile)
     ones = jnp.ones((tile, lanes), jnp.bfloat16)
     column[...] = jnp.broadcast_to(bias[...], column.shape[::-1]).T
+    groups = starts.shape[0]
+    for low, size in ranges:
+        for i in range(groups):
+            source = pl.multiple_of(starts[i] + low, 16)
+            sorted_rows[pl.ds(groups * low + i * size, size), :] = weight[pl.ds(source, size), :]
+    across[...] = dot(identity(across.shape[0]), sorted_rows[...], NT).astype(across.dtype)
     inverse[...] = jnp.ones(inverse.shape, jnp.float32)
 
     def block(s, carry):
@@ -155,22 +163,23 @@
         lax.fori_loop(0, slots, add, 0)
 
 
-def own(panel, rows, cols, counts, bias, ranges):
+def own(panel, rows, cols, starts, counts, bias, weight, ranges):
     blocks, slots = rows.shape
     nodes, tile = panel.shape[1], counts.shape[-1]
     lanes = max(size for _, size in ranges)
     shapes = [jax.ShapeDtypeStruct((nodes, size), jnp.float32) for _, size in ranges]
     shapes.append(jax.ShapeDtypeStruct((nodes, lanes), jnp.float32))
     shapes.append(jax.ShapeDtypeStruct((bias.shape[0], 128), bias.dtype))
+    shapes.append(jax.ShapeDtypeStruct(weight.shape[::-1], weight.dtype))
     outs = call(
         functools.partial(own_kernel, ranges, blocks, slots, tile),
         "own",
-        [rows, cols],
-        [panel, counts, bias[None, :]],
+        [rows, cols, starts],
+        [panel, counts, bias[None, :], weight],
         shapes,
-        [((slots, tile, lanes), jnp.float32)],
-    )
-    return outs[:-2], outs[-2], outs[-1]
+        [((slots, tile, lanes), jnp.float32), (weight.shape, weight.dtype)],
+    )
+    return outs[:-3], *outs[-3:]
 
 
 def pick(order, nodes, stage, outs):
@@ -262,7 +271,7 @@
         first += count
 
 
-def gather_next(total, orders, widths):
+def gather_next(total, orders, widths, moved=2**16):
     size = total.shape[1]
     return call(
         functools.partial(next_kernel, len(orders), tuple(len(w) for w in widths)),
@@ -271,36 +280,41 @@
         [total],
         [jax.ShapeDtypeStruct((size, width), jnp.bfloat16) for w in widths for width in w],
         [((orders[0].shape[0], size), jnp.float32)],
-    )
-
-
-def mix_kernel(places, starts, weight, bias, *refs):
+        moved,
+    )
+
+
+def mix_kernel(places, weight, bias, *refs):
     pieces, (out, nodes, ready, sems) = refs[:-4], refs[-4:]
-    for piece, (i, low, first) in zip(pieces, places):
-        height, columns = piece.shape
-        at = pl.multiple_of(starts[i] + low, 16)
-        nodes[pl.ds(at, height), pl.ds(first, columns)] = piece[...]
     copies = []
     for c in range(ready.shape[0]):
         step = ready.shape[2]
-        mixed = dot(weight[...], nodes[:, pl.ds(c * step, step)], NN)
+        low, high = c * step, (c + 1) * step
+        for piece, (row, first) in zip(pieces, places):
+            height, columns = piece.shape
+            start, stop = max(low, first), min(high, first + columns)
+            if start < stop:
+                nodes[pl.ds(row, height), pl.ds(start, stop - start)] = piece[
+                    :, pl.ds(start - first, stop - start)
+                ]
+        mixed = dot(weight[...], nodes[:, pl.ds(low, step)], NN)
         ready[c] = jnp.maximum(mixed + bias[:, :1], 0.0).astype(out.dtype)
         copies.append(
-            pltpu.make_async_copy(ready.at[c], out.at[:, pl.ds(c * step, step)], sems.at[c])
+            pltpu.make_async_copy(ready.at[c], out.at[:, pl.ds(low, step)], sems.at[c])
         )
         copies[-1].start()
     for copy in copies:
         copy.wait()
 
 
-def mix(starts, weight, bias, placed, nodes):
+def mix(weight, bias, placed, nodes):
     places, pieces = tuple(placed), list(placed.values())
     hidden, width = weight.shape
     step = min(512, nodes)
     return pl.pallas_call(
         functools.partial(mix_kernel, places),
         out_shape=jax.ShapeDtypeStruct((hidden, nodes), jnp.bfloat16),
-        in_specs=[SMEM] + [VMEM] * (2 + len(pieces)),
+        in_specs=[VMEM] * (2 + len(pieces)),
         out_specs=ANY,
         scratch_shapes=[
             pltpu.VMEM((width, nodes), jnp.bfloat16),
@@ -312,7 +326,7 @@
             flops=2 * hidden * width * nodes, bytes_accessed=5 * 2**20, transcendentals=0
         ),
         name="mix",
-    )(starts, weight, bias, *pieces)
+    )(weight, bias, *pieces)
 
 
 def on_device(features, tile_rows, tile_cols, tile_weights, order, weight, bias):
@@ -338,10 +352,10 @@
         source = features if sent else panel
         sent.append(list(pack(source, asked, low, size, tile)))
         *asked, sent[-1][0] = lax.optimization_barrier((*asked, sent[-1][0]))
-    accs, inverse, column = own(features, rows, cols, counts, bias, ranges)
-    accs, across, picks, starts = lax.optimization_barrier(
-        (accs, weight.T, picks, whose * width)
-    )
+    accs, inverse, column, across = own(
+        features, rows, cols, whose * width, counts, bias, weight, ranges
+    )
+    accs, picks = lax.optimization_barrier((accs, picks))
 
     got, early = [], []
     for p, leaving in enumerate(sent):
@@ -354,40 +368,45 @@
 
     pieces, across_x, beside = {}, {}, {}
     for p, (low, size) in enumerate(ranges[:-1]):
+        at = [groups * low + i * size for i in range(groups)]
         total, out_far = gather_far(
             early[p], inverse, rows, picks[:far], counts, got[p][-1:], blocks - 1
         )
         for i, piece in enumerate(out_far):
-            across_x[i, low, 0] = traded(piece, "grp", ranks[i])
+            across_x[at[i], 0] = traded(piece, "grp", ranks[i])
         halves = (share // 2, share // 2)
         near = gather_next(total, picks[far:], [halves, (share,)])
         near, early[p + 1], got[p + 1] = lax.optimization_barrier(
             (near, early[p + 1], got[p + 1])
         )
-        beside[far, low, 0] = traded(near[0], "grp", 1)
-        beside[far, low, share // 2] = traded(near[1], "grp", 1)
-        pieces[far + 1, low, 0] = near[2]
+        beside[at[far], 0] = traded(near[0], "grp", 1)
+        beside[at[far], share // 2] = traded(near[1], "grp", 1)
+        pieces[at[far + 1], 0] = near[2]
 
     low, size = ranges[-1]
-    total, out_far = gather_far(
+    at = [groups * low + i * size for i in range(groups)]
+    total, (piece,) = gather_far(
         early[-1], inverse, rows, picks[:1], counts, got[-1][-1:], blocks - 1
     )
-    pieces[0, low, 0] = traded(out_far[0], "grp", ranks[0])
+    first = traded(piece, "grp", ranks[0])
     for i in range(1, groups):
-        widths = (share,)
+        widths, moved = (share,), 2**16
         if i < far:
             total, beside = lax.optimization_barrier((total, beside))
-            widths = (share // 4 * 3, share // 4)
         elif i == far:
             total, across_x = lax.optimization_barrier((total, across_x))
             widths = (share // 2, share // 2)
-        first = 0
-        for piece in gather_next(total, [picks[i]], [widths]):
-            pieces[i, low, first] = traded(piece, "grp", ranks[i]) if ranks[i] else piece
-            first += piece.shape[1]
+        else:
+            total, first = lax.optimization_barrier((total, first))
+            moved = 2**22
+        column_at = 0
+        for piece in gather_next(total, [picks[i]], [widths], moved):
+            pieces[at[i], column_at] = traded(piece, "grp", ranks[i]) if ranks[i] else piece
+            column_at += piece.shape[1]
+    pieces[at[0], 0] = first
     pieces.update(beside)
     pieces.update(across_x)
-    return mix(starts, across, column, pieces, share)
+    return mix(across, column, pieces, share)
 
 
 def solution(mesh):

time: 90.1 us -> 88.7 us (0.984)
  the two profiles are of different devices: /device:TPU:25 before, /device:TPU:27 now
where the time goes in v9:
time: 88.7 us; the launch traced here: 88.4 us
  Pallas kernels  42.8 us (48%)
  waiting for transfers between devices  25.5 us (29%)
  starting transfers between devices  13.9 us (16%)
  local copies, waits for them, and re-layouts  5.28 us (6%)
    pallas_call x10, Pallas kernels, call(): pl.pallas_call(kernel, out_shape=list(outs), in_specs=[SMEM] * len(scalar...  37.7 us
    ppermute x9, waiting for transfers between devices, shifted(): return lax.ppermute(value, axis, pairs)  24.9 us
    ppermute x8, starting transfers between devices, traded(): lax.ppermute(value, axis, [(i, i ^ k) for i in range(lax.axis_size(axis))])  8.07 us
    ppermute x9, starting transfers between devices, shifted(): return lax.ppermute(value, axis, pairs)  5.85 us
    unnamed x28, local copies, waits for them, and re-layouts  5.26 us
    pallas_call x2, Pallas kernels, pack(): pl.pallas_call(functools.partial(pack_kernel, low, size, offsets, slots,...  3.06 us
    pallas_call x1, Pallas kernels, mix(): pl.pallas_call(functools.partial(mix_kernel, places), out_shape=jax.Shape...  2.11 us
  transfers between devices with their start and end apart: 17, of which 5 were waited for; matrix products, arithmetic and copies ran while one was open for 1% of the time, Pallas kernels for 44%

profile of v9, /device:TPU:27, one launch (start us, length us, event | category | flops | bytes accessed | tf_op | source)
XLA Modules:
  0.0 88.4 jit_solution(3414804226753017718)
XLA Ops:
  0.0 0.0 collective-permute-start.2
  0.0 1.3 %collective-permute-start.1 = (s32[4,20]{1,0:T(4,128)}, s32[4,20]{1,0:T(4,128)S(1)}, u32[]{:S(2)}, u32[]{:S(2)}) collective-permute-start(s32[4,20]{1,0:T(4,128)} %bitcast.15), channel_id=1, source_target_pairs={{0,8},{4,12},{8,0},{12,4},{1,9},{5,13},{9,1},{13,5},{2,10},{6,14},... | collective-permute-start | bytes 968 | tf_op jit(solution)/shard_map/ppermute | solution.py:48
  1.4 0.2 collective-permute-start
  1.5 1.6 %copy-done.1 = bf16[128,8192]{1,0:T(8,128)(2,1)S(1)} copy-done((bf16[128,8192]{1,0:T(8,128)(2,1)S(1)}, bf16[128,8192]{1,0:T(8,128)(2,1)}, u32[]{:S(2)}) %copy-start.1) | copy-done | bytes 2097176
  3.1 0.1 stage.1.refs_3_
  3.3 0.0 collective-permute-done.2.refs_2_
  3.3 0.3 collective-permute-done.1.refs_1_
  3.6 2.2 %collective-permute-done.refs_0_ = s32[4,20]{1,0:T(4,128)S(1)} collective-permute-done((s32[4,20]{1,0:T(4,128)}, s32[4,20]{1,0:T(4,128)S(1)}, u32[]{:S(2)}, u32[]{:S(2)}) %collective-permute-start) | collective-permute-done | bytes 352 | tf_op jit(solution)/shard_map/ppermute | solution.py:48
  5.8 1.6 %pack.2 = (bf16[20,80,128]{2,1,0:T(8,128)(2,1)}, bf16[20,80,128]{2,1,0:T(8,128)(2,1)}, bf16[20,80,128]{2,1,0:T(8,128)(2,1)}) custom-call(s32[4,20]{1,0:T(4,128)S(1)} %collective-permute-done.refs_0_, s32[4,20]{1,0:T(4,128)S(1)} %collective-permute-done.1.refs_1_, s32[4,20]{1,0:T(4,128)S(1)} %collective-permute-done.2.refs_2_, bf16[128,8192]{1,0:T(8,128)(2,1)S(1)} %stage.1.refs_3_), custom_call_target="tpu_custom_call" | custom-call | bytes 65536 | tf_op jit(solution)/shard_map/pack/pallas_call | solution.py:94
  7.4 0.7 collective-permute-start.3
  8.2 0.0 collective-permute-start.4
  8.2 0.8 collective-permute-start.5
  9.0 0.7 xor_multiply_fusion.starts
  9.7 1.6 %copy-done.2 = bf16[128,8192]{1,0:T(8,128)(2,1)S(1)} copy-done((bf16[128,8192]{1,0:T(8,128)(2,1)S(1)}, bf16[128,8192]{1,0:T(8,128)(2,1)}, u32[]{:S(2)}) %copy-start.2) | copy-done | bytes 2097176
  11.3 0.7 copy-done.4
  12.0 0.7 copy-done.11
  12.7 0.7 copy-done.12
  13.4 9.5 %own.1 = (f32[8192,80]{1,0:T(8,128)S(1)}, f32[8192,48]{1,0:T(8,128)S(1)}, f32[8192,80]{1,0:T(8,128)S(1)}, f32[512,128]{1,0:T(8,128)S(1)}, bf16[512,512]{1,0:T(8,128)(2,1)S(1)}) custom-call(s32[4,20]{1,0:T(4,128)S(1)} %bitcast.9, s32[4,20]{1,0:T(4,128)S(1)} %bitcast.17, s32[4]{0:T(128)S(1)} %xor_multiply_fusion.starts, bf16[128,8192]{1,0:T(8,128)(2,1)S(1)} %copy-done.2, ...), custom_call_target="tpu_custom_call" | custom-call | bytes 65536 | tf_op jit(solution)/shard_map/own/pallas_call | solution.py:33
  23.0 1.4 %pack.3 = (bf16[20,48,128]{2,1,0:T(8,128)(2,1)S(1)}, bf16[20,48,128]{2,1,0:T(8,128)(2,1)S(1)}, bf16[20,48,128]{2,1,0:T(8,128)(2,1)S(1)}) custom-call(s32[4,20]{1,0:T(4,128)S(1)} %copy-done.10, s32[4,20]{1,0:T(4,128)S(1)} %copy-done.8, s32[4,20]{1,0:T(4,128)S(1)} %copy-done.6, bf16[128,8192]{1,0:T(8,128)(2,1)S(1)} %copy-done.2), custom_call_target="tpu_custom_call" | custom-call | bytes 65536 | tf_op jit(solution)/shard_map/pack/pallas_call | solution.py:94
  24.4 0.0 collective-permute-done.3.refs_0_
  24.4 17.5 %collective-permute-done.4.refs_1_ = bf16[20,80,128]{2,1,0:T(8,128)(2,1)} collective-permute-done((bf16[20,80,128]{2,1,0:T(8,128)(2,1)}, bf16[20,80,128]{2,1,0:T(8,128)(2,1)}, u32[]{:S(2)}, u32[]{:S(2)}) %collective-permute-start.4) | collective-permute-done | bytes 409632 | tf_op jit(solution)/shard_map/ppermute | solution.py:48
  41.9 2.9 %add_early.2.refs_2_ = f32[8192,80]{1,0:T(8,128)S(1)} custom-call(s32[4,20]{1,0:T(4,128)S(1)} %bitcast.10, f32[8192,80]{1,0:T(8,128)S(1)} %get-tuple-element.83.acc, f32[8192,80]{1,0:T(8,128)S(1)} %get-tuple-element.84.inverse.refs_3_.refs_2_, bf16[80,128,128]{2,1,0:T(8,128)(2,1)S(1)} %bitcast.5, bf16[20,80,128]{2,1,0:T(8,128)(2,1)} %collective-permute-done.3.refs_0_, ...), custom_call_target="tpu_custom_call" | custom-call | bytes 65536 | tf_op jit(solution)/shard_map/add_early/pallas_call | solution.py:33
  44.9 0.0 collective-permute-done.5.refs_5_
  44.9 0.1 collective-permute-start.6
  45.0 1.2 %collective-permute-start.7 = (bf16[20,48,128]{2,1,0:T(8,128)(2,1)S(1)}, bf16[20,48,128]{2,1,0:T(8,128)(2,1)S(1)}, u32[]{:S(2)}, u32[]{:S(2)}) collective-permute-start(bf16[20,48,128]{2,1,0:T(8,128)(2,1)S(1)} %get-tuple-element.94), channel_id=1, source_target_pairs={{0,8},{4,12},{8,0},{12,4},{1,9},{5,13},{9,1},{13,5},{2,10},{6,14},... | collective-permute-start | bytes 737288 | tf_op jit(solution)/shard_map/ppermute | solution.py:48
  46.2 1.5 %collective-permute-start.8 = (bf16[20,48,128]{2,1,0:T(8,128)(2,1)S(1)}, bf16[20,48,128]{2,1,0:T(8,128)(2,1)S(1)}, u32[]{:S(2)}, u32[]{:S(2)}) collective-permute-start(bf16[20,48,128]{2,1,0:T(8,128)(2,1)S(1)} %get-tuple-element.95), channel_id=1, source_target_pairs={{0,12},{4,0},{8,4},{12,8},{1,13},{5,1},{9,5},{13,9},{2,14},{6,2},{... | collective-permute-start | bytes 737288 | tf_op jit(solution)/shard_map/ppermute | solution.py:48
  47.7 6.0 %gather_far.2 = (f32[8192,80]{1,0:T(8,128)S(1)}, bf16[80,2048]{1,0:T(8,128)(2,1)S(1)}, bf16[80,2048]{1,0:T(8,128)(2,1)S(1)}) custom-call(s32[4,20]{1,0:T(4,128)S(1)} %bitcast.11, s32[2048]{0:T(1024)S(1)} %get-tuple-element.66.refs_0_, s32[2048]{0:T(1024)S(1)} %get-tuple-element.67.refs_1_.refs_0_, f32[8192,80]{1,0:T(8,128)S(1)} %add_early.2.refs_2_, ...), custom_call_target="tpu_custom_call" | custom-call | bytes 1048576 | tf_op jit(solution)/shard_map/gather_far/pallas_call | solution.py:33
  53.7 2.5 %collective-permute-start.12 = (bf16[80,2048]{1,0:T(8,128)(2,1)S(1)}, bf16[80,2048]{1,0:T(8,128)(2,1)S(1)}, u32[]{:S(2)}, u32[]{:S(2)}) collective-permute-start(bf16[80,2048]{1,0:T(8,128)(2,1)S(1)} %get-tuple-element.103), channel_id=1, source_target_pairs={{0,3},{1,2},{2,1},{3,0},{4,7},{5,6},{6,5},{7,4},{8,11},{9,10},{10,... | collective-permute-start | bytes 983048 | tf_op jit(solution)/shard_map/ppermute | solution.py:52
  56.2 1.2 %collective-permute-start.13 = (bf16[80,2048]{1,0:T(8,128)(2,1)S(1)}, bf16[80,2048]{1,0:T(8,128)(2,1)S(1)}, u32[]{:S(2)}, u32[]{:S(2)}) collective-permute-start(bf16[80,2048]{1,0:T(8,128)(2,1)S(1)} %get-tuple-element.104), channel_id=1, source_target_pairs={{0,2},{1,3},{2,0},{3,1},{4,6},{5,7},{6,4},{7,5},{8,10},{9,11},{10,... | collective-permute-start | bytes 983048 | tf_op jit(solution)/shard_map/ppermute | solution.py:52
  57.4 4.9 %gather_next.4 = (bf16[80,1024]{1,0:T(8,128)(2,1)S(1)}, bf16[80,1024]{1,0:T(8,128)(2,1)S(1)}, bf16[80,2048]{1,0:T(8,128)(2,1)S(1)}) custom-call(s32[2048]{0:T(1024)S(1)} %get-tuple-element.64.refs_0_, s32[2048]{0:T(1024)S(1)} %get-tuple-element.65.refs_1_.refs_0_, f32[8192,80]{1,0:T(8,128)S(1)} %get-tuple-element.88.refs_2_), custom_call_target="tpu_custom_call" | custom-call | bytes 65536 | tf_op jit(solution)/shard_map/gather_next/pallas_call | solution.py:33
  62.4 0.0 collective-permute-done.6.refs_0_
  62.4 4.9 %collective-permute-done.7.refs_1_ = bf16[20,48,128]{2,1,0:T(8,128)(2,1)S(1)} collective-permute-done((bf16[20,48,128]{2,1,0:T(8,128)(2,1)S(1)}, bf16[20,48,128]{2,1,0:T(8,128)(2,1)S(1)}, u32[]{:S(2)}, u32[]{:S(2)}) %collective-permute-start.7) | collective-permute-done | bytes 245792 | tf_op jit(solution)/shard_map/ppermute | solution.py:48
  67.2 2.2 %add_early.3.refs_1_ = f32[8192,48]{1,0:T(8,128)S(1)} custom-call(s32[4,20]{1,0:T(4,128)S(1)} %bitcast.12, f32[8192,48]{1,0:T(8,128)S(1)} %get-tuple-element.92.acc, f32[8192,80]{1,0:T(8,128)S(1)} %get-tuple-element.84.inverse.refs_3_.refs_2_, bf16[80,128,128]{2,1,0:T(8,128)(2,1)S(1)} %bitcast.7, bf16[20,48,128]{2,1,0:T(8,128)(2,1)S(1)} %collective-permute-done.6.refs_0_, ...), custom_call_target="tpu_custom_call" | custom-call | bytes 65536 | tf_op jit(solution)/shard_map/add_early/pallas_call | solution.py:33
  69.5 1.7 %collective-permute-start.9 = (bf16[80,1024]{1,0:T(8,128)(2,1)S(1)}, bf16[80,1024]{1,0:T(8,128)(2,1)S(1)}, u32[]{:S(2)}, u32[]{:S(2)}) collective-permute-start(bf16[80,1024]{1,0:T(8,128)(2,1)S(1)} %get-tuple-element.100), channel_id=1, source_target_pairs={{0,1},{1,0},{2,3},{3,2},{4,5},{5,4},{6,7},{7,6},{8,9},{9,8},{10,11... | collective-permute-start | bytes 491528 | tf_op jit(solution)/shard_map/ppermute | solution.py:52
  71.2 0.1 collective-permute-start.10
  71.3 3.7 %gather_far.3 = (f32[8192,48]{1,0:T(8,128)S(1)}, bf16[48,2048]{1,0:T(8,128)(2,1)S(1)}) custom-call(s32[4,20]{1,0:T(4,128)S(1)} %bitcast.13, s32[2048]{0:T(1024)S(1)} %get-tuple-element.66.refs_0_, f32[8192,48]{1,0:T(8,128)S(1)} %add_early.3.refs_1_, f32[8192,80]{1,0:T(8,128)S(1)} %get-tuple-element.84.inverse.refs_3_.refs_2_, ...), custom_call_target="tpu_custom_call" | custom-call | bytes 1048576 | tf_op jit(solution)/shard_map/gather_far/pallas_call | solution.py:33
  75.1 0.6 collective-permute-start.16
  75.7 2.7 %gather_next.5 = bf16[48,2048]{1,0:T(8,128)(2,1)S(1)} custom-call(s32[2048]{0:T(1024)S(1)} %get-tuple-element.67.refs_1_.refs_0_, f32[8192,48]{1,0:T(8,128)S(1)} %get-tuple-element.109.refs_1_), custom_call_target="tpu_custom_call" | custom-call | bytes 65536 | tf_op jit(solution)/shard_map/gather_next/pallas_call | solution.py:33
  78.4 1.3 %collective-permute-start.11 = (bf16[48,2048]{1,0:T(8,128)(2,1)S(1)}, bf16[48,2048]{1,0:T(8,128)(2,1)S(1)}, u32[]{:S(2)}, u32[]{:S(2)}) collective-permute-start(bf16[48,2048]{1,0:T(8,128)(2,1)S(1)} %gather_next.5), channel_id=1, source_target_pairs={{0,2},{1,3},{2,0},{3,1},{4,6},{5,7},{6,4},{7,5},{8,10},{9,11},{10,... | collective-permute-start | bytes 589832 | tf_op jit(solution)/shard_map/ppermute | solution.py:52
  79.7 2.7 %gather_next.6 = (bf16[48,1024]{1,0:T(8,128)(2,1)S(1)}, bf16[48,1024]{1,0:T(8,128)(2,1)S(1)}) custom-call(s32[2048]{0:T(1024)S(1)} %get-tuple-element.64.refs_0_, f32[8192,48]{1,0:T(8,128)S(1)} %get-tuple-element.109.refs_1_), custom_call_target="tpu_custom_call" | custom-call | bytes 65536 | tf_op jit(solution)/shard_map/gather_next/pallas_call | solution.py:33
  82.4 0.4 collective-permute-start.14
  82.8 0.2 collective-permute-start.15
  83.0 0.0 collective-permute-done.16.refs_5_
  83.0 2.7 %gather_next.7.refs_4_ = bf16[48,2048]{1,0:T(8,128)(2,1)S(1)} custom-call(s32[2048]{0:T(1024)S(1)} %get-tuple-element.65.refs_1_.refs_0_, f32[8192,48]{1,0:T(8,128)S(1)} %get-tuple-element.109.refs_1_), custom_call_target="tpu_custom_call" | custom-call | bytes 4194304 | tf_op jit(solution)/shard_map/gather_next/pallas_call | solution.py:33
  85.7 0.0 collective-permute-done.14.refs_2_
  85.7 0.0 collective-permute-done.15.refs_3_
  85.8 0.5 collective-permute-done.11.refs_1_
  86.3 2.1 %mix.1 = bf16[512,2048]{1,0:T(8,128)(2,1)} custom-call(bf16[512,512]{1,0:T(8,128)(2,1)S(1)} %get-tuple-element.60.weight, f32[512,128]{1,0:T(8,128)S(1)} %get-tuple-element.61.bias, bf16[80,2048]{1,0:T(8,128)(2,1)S(1)} %get-tuple-element.96.refs_0_, bf16[48,2048]{1,0:T(8,128)(2,1)S(1)} %collective-permute-done.11.refs_1_, ...), custom_call_target="tpu_custom_call" | custom-call | flops 1073741824 | bytes 5242880 | tf_op jit(solution)/shard_map/mix/pallas_call | solution.py:314
  (29 shorter events, 0.1 us)
Async XLA Ops:
  0.0 9.7 %copy-start = (bf16[1,4,20,128,128]{4,3,2,1,0:T(8,128)(2,1)S(1)}, bf16[1,4,20,128,128]{4,3,2,1,0:T(8,128)(2,1)}, u32[]{:S(2)}) copy-start(bf16[1,4,20,128,128]{4,3,2,1,0:T(8,128)(2,1)} %param.11) | copy-start | bytes 7864324
  0.0 3.3 %collective-permute-start.2 = (s32[4,20]{1,0:T(4,128)}, s32[4,20]{1,0:T(4,128)S(1)}, u32[]{:S(2)}, u32[]{:S(2)}) collective-permute-start(s32[4,20]{1,0:T(4,128)} %bitcast.14), channel_id=1, source_target_pairs={{0,4},{4,8},{8,12},{12,0},{1,5},{5,9},{9,13},{13,1},{2,6},{6,10},{... | collective-permute-start | bytes 968 | tf_op jit(solution)/shard_map/ppermute | solution.py:48
  0.0 3.6 %collective-permute-start.1 = (s32[4,20]{1,0:T(4,128)}, s32[4,20]{1,0:T(4,128)S(1)}, u32[]{:S(2)}, u32[]{:S(2)}) collective-permute-start(s32[4,20]{1,0:T(4,128)} %bitcast.15), channel_id=1, source_target_pairs={{0,8},{4,12},{8,0},{12,4},{1,9},{5,13},{9,1},{13,5},{2,10},{6,14},... | collective-permute-start | bytes 968 | tf_op jit(solution)/shard_map/ppermute | solution.py:48
  1.4 4.4 %collective-permute-start = (s32[4,20]{1,0:T(4,128)}, s32[4,20]{1,0:T(4,128)S(1)}, u32[]{:S(2)}, u32[]{:S(2)}) collective-permute-start(s32[4,20]{1,0:T(4,128)} %bitcast.16), channel_id=1, source_target_pairs={{0,12},{4,0},{8,4},{12,8},{1,13},{5,1},{9,5},{13,9},{2,14},{6,2},{... | collective-permute-start | bytes 968 | tf_op jit(solution)/shard_map/ppermute | solution.py:48
  1.5 1.6 %copy-start.1 = (bf16[128,8192]{1,0:T(8,128)(2,1)S(1)}, bf16[128,8192]{1,0:T(8,128)(2,1)}, u32[]{:S(2)}) copy-start(bf16[128,8192]{1,0:T(8,128)(2,1)} %refs_3_.1) | copy-start | bytes 6291460
  3.1 6.6 %copy-start.3 = (bf16[512,512]{1,0:T(8,128)(2,1)S(1)}, bf16[512,512]{1,0:T(8,128)(2,1)}, u32[]{:S(2)}) copy-start(bf16[512,512]{1,0:T(8,128)(2,1)} %weight.1) | copy-start | bytes 1572868
  3.3 4.9 %copy-start.5 = (s32[4,20]{1,0:T(4,128)}, s32[4,20]{1,0:T(4,128)S(1)}, u32[]{:S(2)}) copy-start(s32[4,20]{1,0:T(4,128)S(1)} %collective-permute-done.2.refs_2_) | copy-start | bytes 964
  3.6 4.6 %copy-start.7 = (s32[4,20]{1,0:T(4,128)}, s32[4,20]{1,0:T(4,128)S(1)}, u32[]{:S(2)}) copy-start(s32[4,20]{1,0:T(4,128)S(1)} %collective-permute-done.1.refs_1_) | copy-start | bytes 964
  5.8 3.2 %copy-start.9 = (s32[4,20]{1,0:T(4,128)}, s32[4,20]{1,0:T(4,128)S(1)}, u32[]{:S(2)}) copy-start(s32[4,20]{1,0:T(4,128)S(1)} %collective-permute-done.refs_0_) | copy-start | bytes 964
  7.4 17.0 %collective-permute-start.3 = (bf16[20,80,128]{2,1,0:T(8,128)(2,1)}, bf16[20,80,128]{2,1,0:T(8,128)(2,1)}, u32[]{:S(2)}, u32[]{:S(2)}) collective-permute-start(bf16[20,80,128]{2,1,0:T(8,128)(2,1)} %get-tuple-element.80), channel_id=1, source_target_pairs={{0,4},{4,8},{8,12},{12,0},{1,5},{5,9},{9,13},{13,1},{2,6},{6,10},{... | collective-permute-start | bytes 1228808 | tf_op jit(solution)/shard_map/ppermute | solution.py:48
  8.2 33.7 %collective-permute-start.4 = (bf16[20,80,128]{2,1,0:T(8,128)(2,1)}, bf16[20,80,128]{2,1,0:T(8,128)(2,1)}, u32[]{:S(2)}, u32[]{:S(2)}) collective-permute-start(bf16[20,80,128]{2,1,0:T(8,128)(2,1)} %get-tuple-element.81), channel_id=1, source_target_pairs={{0,8},{4,12},{8,0},{12,4},{1,9},{5,13},{9,1},{13,5},{2,10},{6,14},... | collective-permute-start | bytes 1228808 | tf_op jit(solution)/shard_map/ppermute | solution.py:48
  8.2 36.7 %collective-permute-start.5 = (bf16[20,80,128]{2,1,0:T(8,128)(2,1)}, bf16[20,80,128]{2,1,0:T(8,128)(2,1)S(1)}, u32[]{:S(2)}, u32[]{:S(2)}) collective-permute-start(bf16[20,80,128]{2,1,0:T(8,128)(2,1)} %get-tuple-element.82), channel_id=1, source_target_pairs={{0,12},{4,0},{8,4},{12,8},{1,13},{5,1},{9,5},{13,9},{2,14},{6,2},{... | collective-permute-start | bytes 1228808 | tf_op jit(solution)/shard_map/ppermute | solution.py:48
  9.0 13.9 %copy-start.6 = (s32[4,20]{1,0:T(4,128)S(1)}, s32[4,20]{1,0:T(4,128)}, u32[]{:S(2)}) copy-start(s32[4,20]{1,0:T(4,128)} %copy-done.5) | copy-start | bytes 964
  9.0 13.9 %copy-start.8 = (s32[4,20]{1,0:T(4,128)S(1)}, s32[4,20]{1,0:T(4,128)}, u32[]{:S(2)}) copy-start(s32[4,20]{1,0:T(4,128)} %copy-done.7) | copy-start | bytes 964
  9.0 13.9 %copy-start.10 = (s32[4,20]{1,0:T(4,128)S(1)}, s32[4,20]{1,0:T(4,128)}, u32[]{:S(2)}) copy-start(s32[4,20]{1,0:T(4,128)} %copy-done.9) | copy-start | bytes 964
  9.7 1.6 %copy-start.2 = (bf16[128,8192]{1,0:T(8,128)(2,1)S(1)}, bf16[128,8192]{1,0:T(8,128)(2,1)}, u32[]{:S(2)}) copy-start(bf16[128,8192]{1,0:T(8,128)(2,1)} %refs_3_.1) | copy-start | bytes 6291460
  11.3 0.7 copy-start.4
  12.0 0.7 copy-start.11
  12.7 0.7 copy-start.12
  13.4 9.6 %copy-start.13 = (s32[8192]{0:T(1024)S(1)}, s32[8192]{0:T(1024)}, u32[]{:S(2)}) copy-start(s32[8192]{0:T(1024)} %param.12) | copy-start | bytes 98308
  44.9 17.5 %collective-permute-start.6 = (bf16[20,48,128]{2,1,0:T(8,128)(2,1)S(1)}, bf16[20,48,128]{2,1,0:T(8,128)(2,1)S(1)}, u32[]{:S(2)}, u32[]{:S(2)}) collective-permute-start(bf16[20,48,128]{2,1,0:T(8,128)(2,1)S(1)} %get-tuple-element.93), channel_id=1, source_target_pairs={{0,4},{4,8},{8,12},{12,0},{1,5},{5,9},{9,13},{13,1},{2,6},{6,10},{... | collective-permute-start | bytes 737288 | tf_op jit(solution)/shard_map/ppermute | solution.py:48
  45.0 22.3 %collective-permute-start.7 = (bf16[20,48,128]{2,1,0:T(8,128)(2,1)S(1)}, bf16[20,48,128]{2,1,0:T(8,128)(2,1)S(1)}, u32[]{:S(2)}, u32[]{:S(2)}) collective-permute-start(bf16[20,48,128]{2,1,0:T(8,128)(2,1)S(1)} %get-tuple-element.94), channel_id=1, source_target_pairs={{0,8},{4,12},{8,0},{12,4},{1,9},{5,13},{9,1},{13,5},{2,10},{6,14},... | collective-permute-start | bytes 737288 | tf_op jit(solution)/shard_map/ppermute | solution.py:48
  46.2 23.3 %collective-permute-start.8 = (bf16[20,48,128]{2,1,0:T(8,128)(2,1)S(1)}, bf16[20,48,128]{2,1,0:T(8,128)(2,1)S(1)}, u32[]{:S(2)}, u32[]{:S(2)}) collective-permute-start(bf16[20,48,128]{2,1,0:T(8,128)(2,1)S(1)} %get-tuple-element.95), channel_id=1, source_target_pairs={{0,12},{4,0},{8,4},{12,8},{1,13},{5,1},{9,5},{13,9},{2,14},{6,2},{... | collective-permute-start | bytes 737288 | tf_op jit(solution)/shard_map/ppermute | solution.py:48
  53.7 26.1 %collective-permute-start.12 = (bf16[80,2048]{1,0:T(8,128)(2,1)S(1)}, bf16[80,2048]{1,0:T(8,128)(2,1)S(1)}, u32[]{:S(2)}, u32[]{:S(2)}) collective-permute-start(bf16[80,2048]{1,0:T(8,128)(2,1)S(1)} %get-tuple-element.103), channel_id=1, source_target_pairs={{0,3},{1,2},{2,1},{3,0},{4,7},{5,6},{6,5},{7,4},{8,11},{9,10},{10,... | collective-permute-start | bytes 983048 | tf_op jit(solution)/shard_map/ppermute | solution.py:52
  56.2 23.5 %collective-permute-start.13 = (bf16[80,2048]{1,0:T(8,128)(2,1)S(1)}, bf16[80,2048]{1,0:T(8,128)(2,1)S(1)}, u32[]{:S(2)}, u32[]{:S(2)}) collective-permute-start(bf16[80,2048]{1,0:T(8,128)(2,1)S(1)} %get-tuple-element.104), channel_id=1, source_target_pairs={{0,2},{1,3},{2,0},{3,1},{4,6},{5,7},{6,4},{7,5},{8,10},{9,11},{10,... | collective-permute-start | bytes 983048 | tf_op jit(solution)/shard_map/ppermute | solution.py:52
  69.5 6.2 %collective-permute-start.9 = (bf16[80,1024]{1,0:T(8,128)(2,1)S(1)}, bf16[80,1024]{1,0:T(8,128)(2,1)S(1)}, u32[]{:S(2)}, u32[]{:S(2)}) collective-permute-start(bf16[80,1024]{1,0:T(8,128)(2,1)S(1)} %get-tuple-element.100), channel_id=1, source_target_pairs={{0,1},{1,0},{2,3},{3,2},{4,5},{5,4},{6,7},{7,6},{8,9},{9,8},{10,11... | collective-permute-start | bytes 491528 | tf_op jit(solution)/shard_map/ppermute | solution.py:52
  71.2 4.4 %collective-permute-start.10 = (bf16[80,1024]{1,0:T(8,128)(2,1)S(1)}, bf16[80,1024]{1,0:T(8,128)(2,1)S(1)}, u32[]{:S(2)}, u32[]{:S(2)}) collective-permute-start(bf16[80,1024]{1,0:T(8,128)(2,1)S(1)} %get-tuple-element.101), channel_id=1, source_target_pairs={{0,1},{1,0},{2,3},{3,2},{4,5},{5,4},{6,7},{7,6},{8,9},{9,8},{10,11... | collective-permute-start | bytes 491528 | tf_op jit(solution)/shard_map/ppermute | solution.py:52
  75.1 8.0 %collective-permute-start.16 = (bf16[48,2048]{1,0:T(8,128)(2,1)S(1)}, bf16[48,2048]{1,0:T(8,128)(2,1)S(1)}, u32[]{:S(2)}, u32[]{:S(2)}) collective-permute-start(bf16[48,2048]{1,0:T(8,128)(2,1)S(1)} %get-tuple-element.108), channel_id=1, source_target_pairs={{0,3},{1,2},{2,1},{3,0},{4,7},{5,6},{6,5},{7,4},{8,11},{9,10},{10,... | collective-permute-start | bytes 589832 | tf_op jit(solution)/shard_map/ppermute | solution.py:52
  78.4 7.9 %collective-permute-start.11 = (bf16[48,2048]{1,0:T(8,128)(2,1)S(1)}, bf16[48,2048]{1,0:T(8,128)(2,1)S(1)}, u32[]{:S(2)}, u32[]{:S(2)}) collective-permute-start(bf16[48,2048]{1,0:T(8,128)(2,1)S(1)} %gather_next.5), channel_id=1, source_target_pairs={{0,2},{1,3},{2,0},{3,1},{4,6},{5,7},{6,4},{7,5},{8,10},{9,11},{10,... | collective-permute-start | bytes 589832 | tf_op jit(solution)/shard_map/ppermute | solution.py:52
  82.4 3.3 %collective-permute-start.14 = (bf16[48,1024]{1,0:T(8,128)(2,1)S(1)}, bf16[48,1024]{1,0:T(8,128)(2,1)S(1)}, u32[]{:S(2)}, u32[]{:S(2)}) collective-permute-start(bf16[48,1024]{1,0:T(8,128)(2,1)S(1)} %get-tuple-element.106), channel_id=1, source_target_pairs={{0,1},{1,0},{2,3},{3,2},{4,5},{5,4},{6,7},{7,6},{8,9},{9,8},{10,11... | collective-permute-start | bytes 294920 | tf_op jit(solution)/shard_map/ppermute | solution.py:52
  82.8 2.9 %collective-permute-start.15 = (bf16[48,1024]{1,0:T(8,128)(2,1)S(1)}, bf16[48,1024]{1,0:T(8,128)(2,1)S(1)}, u32[]{:S(2)}, u32[]{:S(2)}) collective-permute-start(bf16[48,1024]{1,0:T(8,128)(2,1)S(1)} %get-tuple-element.107), channel_id=1, source_target_pairs={{0,1},{1,0},{2,3},{3,2},{4,5},{5,4},{6,7},{7,6},{8,9},{9,8},{10,11... | collective-permute-start | bytes 294920 | tf_op jit(solution)/shard_map/ppermute | solution.py:52

commit v10 on v9

--- a/solution.py
+++ b/solution.py
@@ -190,7 +190,8 @@
         at = pl.multiple_of(i * UNROLL, UNROLL)
         for u in range(UNROLL):
             source = order[at + u]
-            stage[pl.ds(at + u, 1), :] = nodes[pl.ds(source, 1), :]
+            row = nodes[pl.ds(source, 1), :] if len(nodes.shape) == 2 else nodes[source]
+            stage[pl.ds(at + u, 1), :] = row
         return carry
 
     lax.fori_loop(0, count // UNROLL, group, 0)
@@ -272,7 +273,8 @@
 
 
 def gather_next(total, orders, widths, moved=2**16):
-    size = total.shape[1]
+    nodes, size = total.shape
+    total = total.reshape(nodes, 1, size)
     return call(
         functools.partial(next_kernel, len(orders), tuple(len(w) for w in widths)),
         "gather_next",

time: 88.7 us -> 88.7 us (level)
  the two profiles are of different devices: /device:TPU:27 before, /device:TPU:31 now
where the time goes in v10:
time: 88.7 us; the launch traced here: 88.4 us
  Pallas kernels  42.8 us (48%)
  waiting for transfers between devices  25.5 us (29%)
  starting transfers between devices  13.9 us (16%)
  local copies, waits for them, and re-layouts  5.28 us (6%)
    pallas_call x10, Pallas kernels, call(): pl.pallas_call(kernel, out_shape=list(outs), in_specs=[SMEM] * len(scalar...  37.7 us
    ppermute x9, waiting for transfers between devices, shifted(): return lax.ppermute(value, axis, pairs)  24.9 us
    ppermute x8, starting transfers between devices, traded(): lax.ppermute(value, axis, [(i, i ^ k) for i in range(lax.axis_size(axis))])  8.09 us
    ppermute x9, starting transfers between devices, shifted(): return lax.ppermute(value, axis, pairs)  5.85 us
    unnamed x28, local copies, waits for them, and re-layouts  5.26 us
    pallas_call x2, Pallas kernels, pack(): pl.pallas_call(functools.partial(pack_kernel, low, size, offsets, slots,...  3.06 us
    pallas_call x1, Pallas kernels, mix(): pl.pallas_call(functools.partial(mix_kernel, places), out_shape=jax.Shape...  2.11 us
  transfers between devices with their start and end apart: 17, of which 5 were waited for; matrix products, arithmetic and copies ran while one was open for 1% of the time, Pallas kernels for 44%

profile of v10, /device:TPU:31, one launch (start us, length us, event | category | flops | bytes accessed | tf_op | source)
XLA Modules:
  0.0 88.4 jit_solution(5915047917738063335)
XLA Ops:
  0.0 0.0 collective-permute-start.2
  0.0 1.3 %collective-permute-start.1 = (s32[4,20]{1,0:T(4,128)}, s32[4,20]{1,0:T(4,128)S(1)}, u32[]{:S(2)}, u32[]{:S(2)}) collective-permute-start(s32[4,20]{1,0:T(4,128)} %bitcast.23), channel_id=1, source_target_pairs={{0,8},{4,12},{8,0},{12,4},{1,9},{5,13},{9,1},{13,5},{2,10},{6,14},... | collective-permute-start | bytes 968 | tf_op jit(solution)/shard_map/ppermute | solution.py:48
  1.4 0.2 collective-permute-start
  1.5 1.6 %copy-done.1 = bf16[128,8192]{1,0:T(8,128)(2,1)S(1)} copy-done((bf16[128,8192]{1,0:T(8,128)(2,1)S(1)}, bf16[128,8192]{1,0:T(8,128)(2,1)}, u32[]{:S(2)}) %copy-start.1) | copy-done | bytes 2097176
  3.1 0.1 stage.1.refs_3_
  3.3 0.0 collective-permute-done.2.refs_2_
  3.3 0.3 collective-permute-done.1.refs_1_
  3.6 2.2 %collective-permute-done.refs_0_ = s32[4,20]{1,0:T(4,128)S(1)} collective-permute-done((s32[4,20]{1,0:T(4,128)}, s32[4,20]{1,0:T(4,128)S(1)}, u32[]{:S(2)}, u32[]{:S(2)}) %collective-permute-start) | collective-permute-done | bytes 352 | tf_op jit(solution)/shard_map/ppermute | solution.py:48
  5.8 1.6 %pack.2 = (bf16[20,80,128]{2,1,0:T(8,128)(2,1)}, bf16[20,80,128]{2,1,0:T(8,128)(2,1)}, bf16[20,80,128]{2,1,0:T(8,128)(2,1)}) custom-call(s32[4,20]{1,0:T(4,128)S(1)} %collective-permute-done.refs_0_, s32[4,20]{1,0:T(4,128)S(1)} %collective-permute-done.1.refs_1_, s32[4,20]{1,0:T(4,128)S(1)} %collective-permute-done.2.refs_2_, bf16[128,8192]{1,0:T(8,128)(2,1)S(1)} %stage.1.refs_3_), custom_call_target="tpu_custom_call" | custom-call | bytes 65536 | tf_op jit(solution)/shard_map/pack/pallas_call | solution.py:94
  7.4 0.7 collective-permute-start.3
  8.2 0.0 collective-permute-start.4
  8.2 0.8 collective-permute-start.5
  9.0 0.7 xor_multiply_fusion.starts
  9.7 1.6 %copy-done.2 = bf16[128,8192]{1,0:T(8,128)(2,1)S(1)} copy-done((bf16[128,8192]{1,0:T(8,128)(2,1)S(1)}, bf16[128,8192]{1,0:T(8,128)(2,1)}, u32[]{:S(2)}) %copy-start.2) | copy-done | bytes 2097176
  11.3 0.7 copy-done.4
  12.0 0.7 copy-done.11
  12.7 0.7 copy-done.12
  13.4 9.6 %own.1 = (f32[8192,80]{1,0:T(8,128)S(1)}, f32[8192,48]{1,0:T(8,128)S(1)}, f32[8192,80]{1,0:T(8,128)S(1)}, f32[512,128]{1,0:T(8,128)S(1)}, bf16[512,512]{1,0:T(8,128)(2,1)S(1)}) custom-call(s32[4,20]{1,0:T(4,128)S(1)} %bitcast.17, s32[4,20]{1,0:T(4,128)S(1)} %bitcast.25, s32[4]{0:T(128)S(1)} %xor_multiply_fusion.starts, bf16[128,8192]{1,0:T(8,128)(2,1)S(1)} %copy-done.2, ...), custom_call_target="tpu_custom_call" | custom-call | bytes 65536 | tf_op jit(solution)/shard_map/own/pallas_call | solution.py:33
  23.0 1.4 %pack.3 = (bf16[20,48,128]{2,1,0:T(8,128)(2,1)S(1)}, bf16[20,48,128]{2,1,0:T(8,128)(2,1)S(1)}, bf16[20,48,128]{2,1,0:T(8,128)(2,1)S(1)}) custom-call(s32[4,20]{1,0:T(4,128)S(1)} %copy-done.10, s32[4,20]{1,0:T(4,128)S(1)} %copy-done.8, s32[4,20]{1,0:T(4,128)S(1)} %copy-done.6, bf16[128,8192]{1,0:T(8,128)(2,1)S(1)} %copy-done.2), custom_call_target="tpu_custom_call" | custom-call | bytes 65536 | tf_op jit(solution)/shard_map/pack/pallas_call | solution.py:94
  24.4 17.5 %collective-permute-done.4.refs_1_ = bf16[20,80,128]{2,1,0:T(8,128)(2,1)} collective-permute-done((bf16[20,80,128]{2,1,0:T(8,128)(2,1)}, bf16[20,80,128]{2,1,0:T(8,128)(2,1)}, u32[]{:S(2)}, u32[]{:S(2)}) %collective-permute-start.4) | collective-permute-done | bytes 409632 | tf_op jit(solution)/shard_map/ppermute | solution.py:48
  41.9 2.9 %add_early.2.refs_2_ = f32[8192,80]{1,0:T(8,128)S(1)} custom-call(s32[4,20]{1,0:T(4,128)S(1)} %bitcast.18, f32[8192,80]{1,0:T(8,128)S(1)} %get-tuple-element.83.acc, f32[8192,80]{1,0:T(8,128)S(1)} %get-tuple-element.84.inverse.refs_3_.refs_2_, bf16[80,128,128]{2,1,0:T(8,128)(2,1)S(1)} %bitcast.9, bf16[20,80,128]{2,1,0:T(8,128)(2,1)} %collective-permute-done.3.refs_0_, ...), custom_call_target="tpu_custom_call" | custom-call | bytes 65536 | tf_op jit(solution)/shard_map/add_early/pallas_call | solution.py:33
  44.9 0.0 collective-permute-done.5.refs_5_
  44.9 0.1 collective-permute-start.6
  45.0 1.2 %collective-permute-start.7 = (bf16[20,48,128]{2,1,0:T(8,128)(2,1)S(1)}, bf16[20,48,128]{2,1,0:T(8,128)(2,1)S(1)}, u32[]{:S(2)}, u32[]{:S(2)}) collective-permute-start(bf16[20,48,128]{2,1,0:T(8,128)(2,1)S(1)} %get-tuple-element.94), channel_id=1, source_target_pairs={{0,8},{4,12},{8,0},{12,4},{1,9},{5,13},{9,1},{13,5},{2,10},{6,14},... | collective-permute-start | bytes 737288 | tf_op jit(solution)/shard_map/ppermute | solution.py:48
  46.2 1.5 %collective-permute-start.8 = (bf16[20,48,128]{2,1,0:T(8,128)(2,1)S(1)}, bf16[20,48,128]{2,1,0:T(8,128)(2,1)S(1)}, u32[]{:S(2)}, u32[]{:S(2)}) collective-permute-start(bf16[20,48,128]{2,1,0:T(8,128)(2,1)S(1)} %get-tuple-element.95), channel_id=1, source_target_pairs={{0,12},{4,0},{8,4},{12,8},{1,13},{5,1},{9,5},{13,9},{2,14},{6,2},{... | collective-permute-start | bytes 737288 | tf_op jit(solution)/shard_map/ppermute | solution.py:48
  47.7 6.0 %gather_far.2 = (f32[8192,80]{1,0:T(8,128)S(1)}, bf16[80,2048]{1,0:T(8,128)(2,1)S(1)}, bf16[80,2048]{1,0:T(8,128)(2,1)S(1)}) custom-call(s32[4,20]{1,0:T(4,128)S(1)} %bitcast.19, s32[2048]{0:T(1024)S(1)} %get-tuple-element.66.refs_0_, s32[2048]{0:T(1024)S(1)} %get-tuple-element.67.refs_1_.refs_0_, f32[8192,80]{1,0:T(8,128)S(1)} %add_early.2.refs_2_, ...), custom_call_target="tpu_custom_call" | custom-call | bytes 1048576 | tf_op jit(solution)/shard_map/gather_far/pallas_call | solution.py:33
  53.7 2.5 %collective-permute-start.12 = (bf16[80,2048]{1,0:T(8,128)(2,1)S(1)}, bf16[80,2048]{1,0:T(8,128)(2,1)S(1)}, u32[]{:S(2)}, u32[]{:S(2)}) collective-permute-start(bf16[80,2048]{1,0:T(8,128)(2,1)S(1)} %get-tuple-element.103), channel_id=1, source_target_pairs={{0,3},{1,2},{2,1},{3,0},{4,7},{5,6},{6,5},{7,4},{8,11},{9,10},{10,... | collective-permute-start | bytes 983048 | tf_op jit(solution)/shard_map/ppermute | solution.py:52
  56.2 1.2 %collective-permute-start.13 = (bf16[80,2048]{1,0:T(8,128)(2,1)S(1)}, bf16[80,2048]{1,0:T(8,128)(2,1)S(1)}, u32[]{:S(2)}, u32[]{:S(2)}) collective-permute-start(bf16[80,2048]{1,0:T(8,128)(2,1)S(1)} %get-tuple-element.104), channel_id=1, source_target_pairs={{0,2},{1,3},{2,0},{3,1},{4,6},{5,7},{6,4},{7,5},{8,10},{9,11},{10,... | collective-permute-start | bytes 983048 | tf_op jit(solution)/shard_map/ppermute | solution.py:52
  57.4 4.9 %gather_next.4 = (bf16[80,1024]{1,0:T(8,128)(2,1)S(1)}, bf16[80,1024]{1,0:T(8,128)(2,1)S(1)}, bf16[80,2048]{1,0:T(8,128)(2,1)S(1)}) custom-call(s32[2048]{0:T(1024)S(1)} %get-tuple-element.64.refs_0_, s32[2048]{0:T(1024)S(1)} %get-tuple-element.65.refs_1_.refs_0_, f32[8192,1,80]{2,1,0:T(1,128)S(1)} %bitcast.16), custom_call_target="tpu_custom_call" | custom-call | bytes 65536 | tf_op jit(solution)/shard_map/gather_next/pallas_call | solution.py:33
  62.4 0.0 collective-permute-done.6.refs_0_
  62.4 4.9 %collective-permute-done.7.refs_1_ = bf16[20,48,128]{2,1,0:T(8,128)(2,1)S(1)} collective-permute-done((bf16[20,48,128]{2,1,0:T(8,128)(2,1)S(1)}, bf16[20,48,128]{2,1,0:T(8,128)(2,1)S(1)}, u32[]{:S(2)}, u32[]{:S(2)}) %collective-permute-start.7) | collective-permute-done | bytes 245792 | tf_op jit(solution)/shard_map/ppermute | solution.py:48
  67.2 2.2 %add_early.3.refs_1_ = f32[8192,48]{1,0:T(8,128)S(1)} custom-call(s32[4,20]{1,0:T(4,128)S(1)} %bitcast.20, f32[8192,48]{1,0:T(8,128)S(1)} %get-tuple-element.92.acc, f32[8192,80]{1,0:T(8,128)S(1)} %get-tuple-element.84.inverse.refs_3_.refs_2_, bf16[80,128,128]{2,1,0:T(8,128)(2,1)S(1)} %bitcast.11, bf16[20,48,128]{2,1,0:T(8,128)(2,1)S(1)} %collective-permute-done.6.refs_0_, ...), custom_call_target="tpu_custom_call" | custom-call | bytes 65536 | tf_op jit(solution)/shard_map/add_early/pallas_call | solution.py:33
  69.5 0.0 collective-permute-done.8.refs_4_
  69.5 1.8 %collective-permute-start.9 = (bf16[80,1024]{1,0:T(8,128)(2,1)S(1)}, bf16[80,1024]{1,0:T(8,128)(2,1)S(1)}, u32[]{:S(2)}, u32[]{:S(2)}) collective-permute-start(bf16[80,1024]{1,0:T(8,128)(2,1)S(1)} %get-tuple-element.100), channel_id=1, source_target_pairs={{0,1},{1,0},{2,3},{3,2},{4,5},{5,4},{6,7},{7,6},{8,9},{9,8},{10,11... | collective-permute-start | bytes 491528 | tf_op jit(solution)/shard_map/ppermute | solution.py:52
  71.2 0.1 collective-permute-start.10
  71.3 3.7 %gather_far.3 = (f32[8192,48]{1,0:T(8,128)S(1)}, bf16[48,2048]{1,0:T(8,128)(2,1)S(1)}) custom-call(s32[4,20]{1,0:T(4,128)S(1)} %bitcast.21, s32[2048]{0:T(1024)S(1)} %get-tuple-element.66.refs_0_, f32[8192,48]{1,0:T(8,128)S(1)} %add_early.3.refs_1_, f32[8192,80]{1,0:T(8,128)S(1)} %get-tuple-element.84.inverse.refs_3_.refs_2_, ...), custom_call_target="tpu_custom_call" | custom-call | bytes 1048576 | tf_op jit(solution)/shard_map/gather_far/pallas_call | solution.py:33
  75.0 0.6 collective-permute-start.16
  75.7 2.7 %gather_next.5 = bf16[48,2048]{1,0:T(8,128)(2,1)S(1)} custom-call(s32[2048]{0:T(1024)S(1)} %get-tuple-element.67.refs_1_.refs_0_, f32[8192,1,48]{2,1,0:T(1,128)S(1)} %bitcast.13), custom_call_target="tpu_custom_call" | custom-call | bytes 65536 | tf_op jit(solution)/shard_map/gather_next/pallas_call | solution.py:33
  78.4 1.3 %collective-permute-start.11 = (bf16[48,2048]{1,0:T(8,128)(2,1)S(1)}, bf16[48,2048]{1,0:T(8,128)(2,1)S(1)}, u32[]{:S(2)}, u32[]{:S(2)}) collective-permute-start(bf16[48,2048]{1,0:T(8,128)(2,1)S(1)} %gather_next.5), channel_id=1, source_target_pairs={{0,2},{1,3},{2,0},{3,1},{4,6},{5,7},{6,4},{7,5},{8,10},{9,11},{10,... | collective-permute-start | bytes 589832 | tf_op jit(solution)/shard_map/ppermute | solution.py:52
  79.7 0.0 collective-permute-done.12.refs_8_
  79.7 0.0 collective-permute-done.13.refs_9_
  79.7 2.7 %gather_next.6 = (bf16[48,1024]{1,0:T(8,128)(2,1)S(1)}, bf16[48,1024]{1,0:T(8,128)(2,1)S(1)}) custom-call(s32[2048]{0:T(1024)S(1)} %get-tuple-element.64.refs_0_, f32[8192,1,48]{2,1,0:T(1,128)S(1)} %bitcast.14), custom_call_target="tpu_custom_call" | custom-call | bytes 65536 | tf_op jit(solution)/shard_map/gather_next/pallas_call | solution.py:33
  82.4 0.4 collective-permute-start.14
  82.8 0.2 collective-permute-start.15
  83.0 2.7 %gather_next.7.refs_4_ = bf16[48,2048]{1,0:T(8,128)(2,1)S(1)} custom-call(s32[2048]{0:T(1024)S(1)} %get-tuple-element.65.refs_1_.refs_0_, f32[8192,1,48]{2,1,0:T(1,128)S(1)} %bitcast.15), custom_call_target="tpu_custom_call" | custom-call | bytes 4194304 | tf_op jit(solution)/shard_map/gather_next/pallas_call | solution.py:33
  85.7 0.0 collective-permute-done.14.refs_2_
  85.7 0.6 collective-permute-done.11.refs_1_
  86.3 2.1 %mix.1 = bf16[512,2048]{1,0:T(8,128)(2,1)} custom-call(bf16[512,512]{1,0:T(8,128)(2,1)S(1)} %get-tuple-element.60.weight, f32[512,128]{1,0:T(8,128)S(1)} %get-tuple-element.61.bias, bf16[80,2048]{1,0:T(8,128)(2,1)S(1)} %get-tuple-element.96.refs_0_, bf16[48,2048]{1,0:T(8,128)(2,1)S(1)} %collective-permute-done.11.refs_1_, ...), custom_call_target="tpu_custom_call" | custom-call | flops 1073741824 | bytes 5242880 | tf_op jit(solution)/shard_map/mix/pallas_call | solution.py:316
  (29 shorter events, 0.1 us)
Async XLA Ops:
  0.0 9.7 %copy-start = (bf16[1,4,20,128,128]{4,3,2,1,0:T(8,128)(2,1)S(1)}, bf16[1,4,20,128,128]{4,3,2,1,0:T(8,128)(2,1)}, u32[]{:S(2)}) copy-start(bf16[1,4,20,128,128]{4,3,2,1,0:T(8,128)(2,1)} %param.11) | copy-start | bytes 7864324
  0.0 3.3 %collective-permute-start.2 = (s32[4,20]{1,0:T(4,128)}, s32[4,20]{1,0:T(4,128)S(1)}, u32[]{:S(2)}, u32[]{:S(2)}) collective-permute-start(s32[4,20]{1,0:T(4,128)} %bitcast.22), channel_id=1, source_target_pairs={{0,4},{4,8},{8,12},{12,0},{1,5},{5,9},{9,13},{13,1},{2,6},{6,10},{... | collective-permute-start | bytes 968 | tf_op jit(solution)/shard_map/ppermute | solution.py:48
  0.0 3.6 %collective-permute-start.1 = (s32[4,20]{1,0:T(4,128)}, s32[4,20]{1,0:T(4,128)S(1)}, u32[]{:S(2)}, u32[]{:S(2)}) collective-permute-start(s32[4,20]{1,0:T(4,128)} %bitcast.23), channel_id=1, source_target_pairs={{0,8},{4,12},{8,0},{12,4},{1,9},{5,13},{9,1},{13,5},{2,10},{6,14},... | collective-permute-start | bytes 968 | tf_op jit(solution)/shard_map/ppermute | solution.py:48
  1.4 4.4 %collective-permute-start = (s32[4,20]{1,0:T(4,128)}, s32[4,20]{1,0:T(4,128)S(1)}, u32[]{:S(2)}, u32[]{:S(2)}) collective-permute-start(s32[4,20]{1,0:T(4,128)} %bitcast.24), channel_id=1, source_target_pairs={{0,12},{4,0},{8,4},{12,8},{1,13},{5,1},{9,5},{13,9},{2,14},{6,2},{... | collective-permute-start | bytes 968 | tf_op jit(solution)/shard_map/ppermute | solution.py:48
  1.5 1.6 %copy-start.1 = (bf16[128,8192]{1,0:T(8,128)(2,1)S(1)}, bf16[128,8192]{1,0:T(8,128)(2,1)}, u32[]{:S(2)}) copy-start(bf16[128,8192]{1,0:T(8,128)(2,1)} %refs_3_.1) | copy-start | bytes 6291460
  3.1 6.6 %copy-start.3 = (bf16[512,512]{1,0:T(8,128)(2,1)S(1)}, bf16[512,512]{1,0:T(8,128)(2,1)}, u32[]{:S(2)}) copy-start(bf16[512,512]{1,0:T(8,128)(2,1)} %weight.1) | copy-start | bytes 1572868
  3.3 4.9 %copy-start.5 = (s32[4,20]{1,0:T(4,128)}, s32[4,20]{1,0:T(4,128)S(1)}, u32[]{:S(2)}) copy-start(s32[4,20]{1,0:T(4,128)S(1)} %collective-permute-done.2.refs_2_) | copy-start | bytes 964
  3.6 4.6 %copy-start.7 = (s32[4,20]{1,0:T(4,128)}, s32[4,20]{1,0:T(4,128)S(1)}, u32[]{:S(2)}) copy-start(s32[4,20]{1,0:T(4,128)S(1)} %collective-permute-done.1.refs_1_) | copy-start | bytes 964
  5.8 3.2 %copy-start.9 = (s32[4,20]{1,0:T(4,128)}, s32[4,20]{1,0:T(4,128)S(1)}, u32[]{:S(2)}) copy-start(s32[4,20]{1,0:T(4,128)S(1)} %collective-permute-done.refs_0_) | copy-start | bytes 964
  7.4 17.0 %collective-permute-start.3 = (bf16[20,80,128]{2,1,0:T(8,128)(2,1)}, bf16[20,80,128]{2,1,0:T(8,128)(2,1)}, u32[]{:S(2)}, u32[]{:S(2)}) collective-permute-start(bf16[20,80,128]{2,1,0:T(8,128)(2,1)} %get-tuple-element.80), channel_id=1, source_target_pairs={{0,4},{4,8},{8,12},{12,0},{1,5},{5,9},{9,13},{13,1},{2,6},{6,10},{... | collective-permute-start | bytes 1228808 | tf_op jit(solution)/shard_map/ppermute | solution.py:48
  8.2 33.7 %collective-permute-start.4 = (bf16[20,80,128]{2,1,0:T(8,128)(2,1)}, bf16[20,80,128]{2,1,0:T(8,128)(2,1)}, u32[]{:S(2)}, u32[]{:S(2)}) collective-permute-start(bf16[20,80,128]{2,1,0:T(8,128)(2,1)} %get-tuple-element.81), channel_id=1, source_target_pairs={{0,8},{4,12},{8,0},{12,4},{1,9},{5,13},{9,1},{13,5},{2,10},{6,14},... | collective-permute-start | bytes 1228808 | tf_op jit(solution)/shard_map/ppermute | solution.py:48
  8.2 36.7 %collective-permute-start.5 = (bf16[20,80,128]{2,1,0:T(8,128)(2,1)}, bf16[20,80,128]{2,1,0:T(8,128)(2,1)S(1)}, u32[]{:S(2)}, u32[]{:S(2)}) collective-permute-start(bf16[20,80,128]{2,1,0:T(8,128)(2,1)} %get-tuple-element.82), channel_id=1, source_target_pairs={{0,12},{4,0},{8,4},{12,8},{1,13},{5,1},{9,5},{13,9},{2,14},{6,2},{... | collective-permute-start | bytes 1228808 | tf_op jit(solution)/shard_map/ppermute | solution.py:48
  9.0 13.9 %copy-start.6 = (s32[4,20]{1,0:T(4,128)S(1)}, s32[4,20]{1,0:T(4,128)}, u32[]{:S(2)}) copy-start(s32[4,20]{1,0:T(4,128)} %copy-done.5) | copy-start | bytes 964
  9.0 13.9 %copy-start.8 = (s32[4,20]{1,0:T(4,128)S(1)}, s32[4,20]{1,0:T(4,128)}, u32[]{:S(2)}) copy-start(s32[4,20]{1,0:T(4,128)} %copy-done.7) | copy-start | bytes 964
  9.0 13.9 %copy-start.10 = (s32[4,20]{1,0:T(4,128)S(1)}, s32[4,20]{1,0:T(4,128)}, u32[]{:S(2)}) copy-start(s32[4,20]{1,0:T(4,128)} %copy-done.9) | copy-start | bytes 964
  9.7 1.6 %copy-start.2 = (bf16[128,8192]{1,0:T(8,128)(2,1)S(1)}, bf16[128,8192]{1,0:T(8,128)(2,1)}, u32[]{:S(2)}) copy-start(bf16[128,8192]{1,0:T(8,128)(2,1)} %refs_3_.1) | copy-start | bytes 6291460
  11.3 0.7 copy-start.4
  12.0 0.7 copy-start.11
  12.7 0.7 copy-start.12
  13.4 9.6 %copy-start.13 = (s32[8192]{0:T(1024)S(1)}, s32[8192]{0:T(1024)}, u32[]{:S(2)}) copy-start(s32[8192]{0:T(1024)} %param.12) | copy-start | bytes 98308
  44.9 17.5 %collective-permute-start.6 = (bf16[20,48,128]{2,1,0:T(8,128)(2,1)S(1)}, bf16[20,48,128]{2,1,0:T(8,128)(2,1)S(1)}, u32[]{:S(2)}, u32[]{:S(2)}) collective-permute-start(bf16[20,48,128]{2,1,0:T(8,128)(2,1)S(1)} %get-tuple-element.93), channel_id=1, source_target_pairs={{0,4},{4,8},{8,12},{12,0},{1,5},{5,9},{9,13},{13,1},{2,6},{6,10},{... | collective-permute-start | bytes 737288 | tf_op jit(solution)/shard_map/ppermute | solution.py:48
  45.0 22.3 %collective-permute-start.7 = (bf16[20,48,128]{2,1,0:T(8,128)(2,1)S(1)}, bf16[20,48,128]{2,1,0:T(8,128)(2,1)S(1)}, u32[]{:S(2)}, u32[]{:S(2)}) collective-permute-start(bf16[20,48,128]{2,1,0:T(8,128)(2,1)S(1)} %get-tuple-element.94), channel_id=1, source_target_pairs={{0,8},{4,12},{8,0},{12,4},{1,9},{5,13},{9,1},{13,5},{2,10},{6,14},... | collective-permute-start | bytes 737288 | tf_op jit(solution)/shard_map/ppermute | solution.py:48
  46.2 23.3 %collective-permute-start.8 = (bf16[20,48,128]{2,1,0:T(8,128)(2,1)S(1)}, bf16[20,48,128]{2,1,0:T(8,128)(2,1)S(1)}, u32[]{:S(2)}, u32[]{:S(2)}) collective-permute-start(bf16[20,48,128]{2,1,0:T(8,128)(2,1)S(1)} %get-tuple-element.95), channel_id=1, source_target_pairs={{0,12},{4,0},{8,4},{12,8},{1,13},{5,1},{9,5},{13,9},{2,14},{6,2},{... | collective-permute-start | bytes 737288 | tf_op jit(solution)/shard_map/ppermute | solution.py:48
  53.7 26.0 %collective-permute-start.12 = (bf16[80,2048]{1,0:T(8,128)(2,1)S(1)}, bf16[80,2048]{1,0:T(8,128)(2,1)S(1)}, u32[]{:S(2)}, u32[]{:S(2)}) collective-permute-start(bf16[80,2048]{1,0:T(8,128)(2,1)S(1)} %get-tuple-element.103), channel_id=1, source_target_pairs={{0,3},{1,2},{2,1},{3,0},{4,7},{5,6},{6,5},{7,4},{8,11},{9,10},{10,... | collective-permute-start | bytes 983048 | tf_op jit(solution)/shard_map/ppermute | solution.py:52
  56.2 23.5 %collective-permute-start.13 = (bf16[80,2048]{1,0:T(8,128)(2,1)S(1)}, bf16[80,2048]{1,0:T(8,128)(2,1)S(1)}, u32[]{:S(2)}, u32[]{:S(2)}) collective-permute-start(bf16[80,2048]{1,0:T(8,128)(2,1)S(1)} %get-tuple-element.104), channel_id=1, source_target_pairs={{0,2},{1,3},{2,0},{3,1},{4,6},{5,7},{6,4},{7,5},{8,10},{9,11},{10,... | collective-permute-start | bytes 983048 | tf_op jit(solution)/shard_map/ppermute | solution.py:52
  69.5 6.2 %collective-permute-start.9 = (bf16[80,1024]{1,0:T(8,128)(2,1)S(1)}, bf16[80,1024]{1,0:T(8,128)(2,1)S(1)}, u32[]{:S(2)}, u32[]{:S(2)}) collective-permute-start(bf16[80,1024]{1,0:T(8,128)(2,1)S(1)} %get-tuple-element.100), channel_id=1, source_target_pairs={{0,1},{1,0},{2,3},{3,2},{4,5},{5,4},{6,7},{7,6},{8,9},{9,8},{10,11... | collective-permute-start | bytes 491528 | tf_op jit(solution)/shard_map/ppermute | solution.py:52
  71.2 4.5 %collective-permute-start.10 = (bf16[80,1024]{1,0:T(8,128)(2,1)S(1)}, bf16[80,1024]{1,0:T(8,128)(2,1)S(1)}, u32[]{:S(2)}, u32[]{:S(2)}) collective-permute-start(bf16[80,1024]{1,0:T(8,128)(2,1)S(1)} %get-tuple-element.101), channel_id=1, source_target_pairs={{0,1},{1,0},{2,3},{3,2},{4,5},{5,4},{6,7},{7,6},{8,9},{9,8},{10,11... | collective-permute-start | bytes 491528 | tf_op jit(solution)/shard_map/ppermute | solution.py:52
  75.0 8.0 %collective-permute-start.16 = (bf16[48,2048]{1,0:T(8,128)(2,1)S(1)}, bf16[48,2048]{1,0:T(8,128)(2,1)S(1)}, u32[]{:S(2)}, u32[]{:S(2)}) collective-permute-start(bf16[48,2048]{1,0:T(8,128)(2,1)S(1)} %get-tuple-element.108), channel_id=1, source_target_pairs={{0,3},{1,2},{2,1},{3,0},{4,7},{5,6},{6,5},{7,4},{8,11},{9,10},{10,... | collective-permute-start | bytes 589832 | tf_op jit(solution)/shard_map/ppermute | solution.py:52
  78.4 7.9 %collective-permute-start.11 = (bf16[48,2048]{1,0:T(8,128)(2,1)S(1)}, bf16[48,2048]{1,0:T(8,128)(2,1)S(1)}, u32[]{:S(2)}, u32[]{:S(2)}) collective-permute-start(bf16[48,2048]{1,0:T(8,128)(2,1)S(1)} %gather_next.5), channel_id=1, source_target_pairs={{0,2},{1,3},{2,0},{3,1},{4,6},{5,7},{6,4},{7,5},{8,10},{9,11},{10,... | collective-permute-start | bytes 589832 | tf_op jit(solution)/shard_map/ppermute | solution.py:52
  82.4 3.3 %collective-permute-start.14 = (bf16[48,1024]{1,0:T(8,128)(2,1)S(1)}, bf16[48,1024]{1,0:T(8,128)(2,1)S(1)}, u32[]{:S(2)}, u32[]{:S(2)}) collective-permute-start(bf16[48,1024]{1,0:T(8,128)(2,1)S(1)} %get-tuple-element.106), channel_id=1, source_target_pairs={{0,1},{1,0},{2,3},{3,2},{4,5},{5,4},{6,7},{7,6},{8,9},{9,8},{10,11... | collective-permute-start | bytes 294920 | tf_op jit(solution)/shard_map/ppermute | solution.py:52
  82.8 2.9 %collective-permute-start.15 = (bf16[48,1024]{1,0:T(8,128)(2,1)S(1)}, bf16[48,1024]{1,0:T(8,128)(2,1)S(1)}, u32[]{:S(2)}, u32[]{:S(2)}) collective-permute-start(bf16[48,1024]{1,0:T(8,128)(2,1)S(1)} %get-tuple-element.107), channel_id=1, source_target_pairs={{0,1},{1,0},{2,3},{3,2},{4,5},{5,4},{6,7},{7,6},{8,9},{9,8},{10,11... | collective-permute-start | bytes 294920 | tf_op jit(solution)/shard_map/ppermute | solution.py:52

commit v11 on v9

--- a/solution.py
+++ b/solution.py
@@ -185,12 +185,19 @@
 def pick(order, nodes, stage, outs):
     count, size = stage.shape
     eye = identity(size)
+    place = lax.broadcasted_iota(jnp.int32, (8, size), 0)
+    odd = [(place >> bit) & 1 == 1 for bit in range(3)]
 
     def group(i, carry):
         at = pl.multiple_of(i * UNROLL, UNROLL)
-        for u in range(UNROLL):
-            source = order[at + u]
-            stage[pl.ds(at + u, 1), :] = nodes[pl.ds(source, 1), :]
+        for first in range(0, UNROLL, 8):
+            rows = [
+                jnp.broadcast_to(nodes[pl.ds(order[at + first + u], 1), :], (8, size))
+                for u in range(8)
+            ]
+            for mask in odd:
+                rows = [jnp.where(mask, b, a) for a, b in zip(rows[::2], rows[1::2])]
+            stage[pl.ds(at + first, 8), :] = rows[0]
         return carry
 
     lax.fori_loop(0, count // UNROLL, group, 0)

time: 88.7 us -> 88.7 us (level)
  transfers between devices with their start and end apart: 17 -> 17, of which waited for: 5 -> 5; matrix products, arithmetic and copies ran while one was open for 1% -> 1% of each run, Pallas kernels for 44% -> 45%
where the time goes in v11:
time: 88.7 us; the launch traced here: 88.5 us
  Pallas kernels  43.2 us (49%)
  waiting for transfers between devices  25.2 us (28%)
  starting transfers between devices  13.9 us (16%)
  local copies, waits for them, and re-layouts  5.28 us (6%)
    pallas_call x10, Pallas kernels, call(): pl.pallas_call(kernel, out_shape=list(outs), in_specs=[SMEM] * len(scalar...  38 us
    ppermute x9, waiting for transfers between devices, shifted(): return lax.ppermute(value, axis, pairs)  24.8 us
    ppermute x8, starting transfers between devices, traded(): lax.ppermute(value, axis, [(i, i ^ k) for i in range(lax.axis_size(axis))])  8.07 us
    ppermute x9, starting transfers between devices, shifted(): return lax.ppermute(value, axis, pairs)  5.85 us
    unnamed x28, local copies, waits for them, and re-layouts  5.26 us
    pallas_call x2, Pallas kernels, pack(): pl.pallas_call(functools.partial(pack_kernel, low, size, offsets, slots,...  3.06 us
    pallas_call x1, Pallas kernels, mix(): pl.pallas_call(functools.partial(mix_kernel, places), out_shape=jax.Shape...  2.12 us
  transfers between devices with their start and end apart: 17, of which 5 were waited for; matrix products, arithmetic and copies ran while one was open for 1% of the time, Pallas kernels for 45%

profile of v11, /device:TPU:27, one launch (start us, length us, event | category | flops | bytes accessed | tf_op | source)
XLA Modules:
  0.0 88.5 jit_solution(12835333795163794237)
XLA Ops:
  0.0 0.0 collective-permute-start.2
  0.0 1.3 %collective-permute-start.1 = (s32[4,20]{1,0:T(4,128)}, s32[4,20]{1,0:T(4,128)S(1)}, u32[]{:S(2)}, u32[]{:S(2)}) collective-permute-start(s32[4,20]{1,0:T(4,128)} %bitcast.15), channel_id=1, source_target_pairs={{0,8},{4,12},{8,0},{12,4},{1,9},{5,13},{9,1},{13,5},{2,10},{6,14},... | collective-permute-start | bytes 968 | tf_op jit(solution)/shard_map/ppermute | solution.py:48
  1.4 0.2 collective-permute-start
  1.5 1.6 %copy-done.1 = bf16[128,8192]{1,0:T(8,128)(2,1)S(1)} copy-done((bf16[128,8192]{1,0:T(8,128)(2,1)S(1)}, bf16[128,8192]{1,0:T(8,128)(2,1)}, u32[]{:S(2)}) %copy-start.1) | copy-done | bytes 2097176
  3.1 0.1 stage.1.refs_3_
  3.3 0.0 collective-permute-done.2.refs_2_
  3.3 0.3 collective-permute-done.1.refs_1_
  3.6 2.2 %collective-permute-done.refs_0_ = s32[4,20]{1,0:T(4,128)S(1)} collective-permute-done((s32[4,20]{1,0:T(4,128)}, s32[4,20]{1,0:T(4,128)S(1)}, u32[]{:S(2)}, u32[]{:S(2)}) %collective-permute-start) | collective-permute-done | bytes 352 | tf_op jit(solution)/shard_map/ppermute | solution.py:48
  5.8 1.6 %pack.2 = (bf16[20,80,128]{2,1,0:T(8,128)(2,1)}, bf16[20,80,128]{2,1,0:T(8,128)(2,1)}, bf16[20,80,128]{2,1,0:T(8,128)(2,1)}) custom-call(s32[4,20]{1,0:T(4,128)S(1)} %collective-permute-done.refs_0_, s32[4,20]{1,0:T(4,128)S(1)} %collective-permute-done.1.refs_1_, s32[4,20]{1,0:T(4,128)S(1)} %collective-permute-done.2.refs_2_, bf16[128,8192]{1,0:T(8,128)(2,1)S(1)} %stage.1.refs_3_), custom_call_target="tpu_custom_call" | custom-call | bytes 65536 | tf_op jit(solution)/shard_map/pack/pallas_call | solution.py:94
  7.4 0.7 collective-permute-start.3
  8.2 0.8 collective-permute-start.5
  9.0 0.7 xor_multiply_fusion.starts
  9.7 1.6 %copy-done.2 = bf16[128,8192]{1,0:T(8,128)(2,1)S(1)} copy-done((bf16[128,8192]{1,0:T(8,128)(2,1)S(1)}, bf16[128,8192]{1,0:T(8,128)(2,1)}, u32[]{:S(2)}) %copy-start.2) | copy-done | bytes 2097176
  11.3 0.7 copy-done.4
  12.0 0.7 copy-done.11
  12.7 0.7 copy-done.12
  13.4 9.5 %own.1 = (f32[8192,80]{1,0:T(8,128)S(1)}, f32[8192,48]{1,0:T(8,128)S(1)}, f32[8192,80]{1,0:T(8,128)S(1)}, f32[512,128]{1,0:T(8,128)S(1)}, bf16[512,512]{1,0:T(8,128)(2,1)S(1)}) custom-call(s32[4,20]{1,0:T(4,128)S(1)} %bitcast.9, s32[4,20]{1,0:T(4,128)S(1)} %bitcast.17, s32[4]{0:T(128)S(1)} %xor_multiply_fusion.starts, bf16[128,8192]{1,0:T(8,128)(2,1)S(1)} %copy-done.2, ...), custom_call_target="tpu_custom_call" | custom-call | bytes 65536 | tf_op jit(solution)/shard_map/own/pallas_call | solution.py:33
  23.0 1.4 %pack.3 = (bf16[20,48,128]{2,1,0:T(8,128)(2,1)S(1)}, bf16[20,48,128]{2,1,0:T(8,128)(2,1)S(1)}, bf16[20,48,128]{2,1,0:T(8,128)(2,1)S(1)}) custom-call(s32[4,20]{1,0:T(4,128)S(1)} %copy-done.10, s32[4,20]{1,0:T(4,128)S(1)} %copy-done.8, s32[4,20]{1,0:T(4,128)S(1)} %copy-done.6, bf16[128,8192]{1,0:T(8,128)(2,1)S(1)} %copy-done.2), custom_call_target="tpu_custom_call" | custom-call | bytes 65536 | tf_op jit(solution)/shard_map/pack/pallas_call | solution.py:94
  24.4 0.0 collective-permute-done.3.refs_0_
  24.4 17.5 %collective-permute-done.4.refs_1_ = bf16[20,80,128]{2,1,0:T(8,128)(2,1)} collective-permute-done((bf16[20,80,128]{2,1,0:T(8,128)(2,1)}, bf16[20,80,128]{2,1,0:T(8,128)(2,1)}, u32[]{:S(2)}, u32[]{:S(2)}) %collective-permute-start.4) | collective-permute-done | bytes 409632 | tf_op jit(solution)/shard_map/ppermute | solution.py:48
  41.9 2.9 %add_early.2.refs_2_ = f32[8192,80]{1,0:T(8,128)S(1)} custom-call(s32[4,20]{1,0:T(4,128)S(1)} %bitcast.10, f32[8192,80]{1,0:T(8,128)S(1)} %get-tuple-element.83.acc, f32[8192,80]{1,0:T(8,128)S(1)} %get-tuple-element.84.inverse.refs_3_.refs_2_, bf16[80,128,128]{2,1,0:T(8,128)(2,1)S(1)} %bitcast.5, bf16[20,80,128]{2,1,0:T(8,128)(2,1)} %collective-permute-done.3.refs_0_, ...), custom_call_target="tpu_custom_call" | custom-call | bytes 65536 | tf_op jit(solution)/shard_map/add_early/pallas_call | solution.py:33
  44.9 0.1 collective-permute-start.6
  45.0 1.2 %collective-permute-start.7 = (bf16[20,48,128]{2,1,0:T(8,128)(2,1)S(1)}, bf16[20,48,128]{2,1,0:T(8,128)(2,1)S(1)}, u32[]{:S(2)}, u32[]{:S(2)}) collective-permute-start(bf16[20,48,128]{2,1,0:T(8,128)(2,1)S(1)} %get-tuple-element.94), channel_id=1, source_target_pairs={{0,8},{4,12},{8,0},{12,4},{1,9},{5,13},{9,1},{13,5},{2,10},{6,14},... | collective-permute-start | bytes 737288 | tf_op jit(solution)/shard_map/ppermute | solution.py:48
  46.2 1.5 %collective-permute-start.8 = (bf16[20,48,128]{2,1,0:T(8,128)(2,1)S(1)}, bf16[20,48,128]{2,1,0:T(8,128)(2,1)S(1)}, u32[]{:S(2)}, u32[]{:S(2)}) collective-permute-start(bf16[20,48,128]{2,1,0:T(8,128)(2,1)S(1)} %get-tuple-element.95), channel_id=1, source_target_pairs={{0,12},{4,0},{8,4},{12,8},{1,13},{5,1},{9,5},{13,9},{2,14},{6,2},{... | collective-permute-start | bytes 737288 | tf_op jit(solution)/shard_map/ppermute | solution.py:48
  47.7 6.1 %gather_far.2 = (f32[8192,80]{1,0:T(8,128)S(1)}, bf16[80,2048]{1,0:T(8,128)(2,1)S(1)}, bf16[80,2048]{1,0:T(8,128)(2,1)S(1)}) custom-call(s32[4,20]{1,0:T(4,128)S(1)} %bitcast.11, s32[2048]{0:T(1024)S(1)} %get-tuple-element.66.refs_0_, s32[2048]{0:T(1024)S(1)} %get-tuple-element.67.refs_1_.refs_0_, f32[8192,80]{1,0:T(8,128)S(1)} %add_early.2.refs_2_, ...), custom_call_target="tpu_custom_call" | custom-call | bytes 1048576 | tf_op jit(solution)/shard_map/gather_far/pallas_call | solution.py:33
  53.7 2.5 %collective-permute-start.12 = (bf16[80,2048]{1,0:T(8,128)(2,1)S(1)}, bf16[80,2048]{1,0:T(8,128)(2,1)S(1)}, u32[]{:S(2)}, u32[]{:S(2)}) collective-permute-start(bf16[80,2048]{1,0:T(8,128)(2,1)S(1)} %get-tuple-element.103), channel_id=1, source_target_pairs={{0,3},{1,2},{2,1},{3,0},{4,7},{5,6},{6,5},{7,4},{8,11},{9,10},{10,... | collective-permute-start | bytes 983048 | tf_op jit(solution)/shard_map/ppermute | solution.py:52
  56.3 1.2 %collective-permute-start.13 = (bf16[80,2048]{1,0:T(8,128)(2,1)S(1)}, bf16[80,2048]{1,0:T(8,128)(2,1)S(1)}, u32[]{:S(2)}, u32[]{:S(2)}) collective-permute-start(bf16[80,2048]{1,0:T(8,128)(2,1)S(1)} %get-tuple-element.104), channel_id=1, source_target_pairs={{0,2},{1,3},{2,0},{3,1},{4,6},{5,7},{6,4},{7,5},{8,10},{9,11},{10,... | collective-permute-start | bytes 983048 | tf_op jit(solution)/shard_map/ppermute | solution.py:52
  57.5 5.0 %gather_next.4 = (bf16[80,1024]{1,0:T(8,128)(2,1)S(1)}, bf16[80,1024]{1,0:T(8,128)(2,1)S(1)}, bf16[80,2048]{1,0:T(8,128)(2,1)S(1)}) custom-call(s32[2048]{0:T(1024)S(1)} %get-tuple-element.64.refs_0_, s32[2048]{0:T(1024)S(1)} %get-tuple-element.65.refs_1_.refs_0_, f32[8192,80]{1,0:T(8,128)S(1)} %get-tuple-element.88.refs_2_), custom_call_target="tpu_custom_call" | custom-call | bytes 65536 | tf_op jit(solution)/shard_map/gather_next/pallas_call | solution.py:33
  62.5 0.0 collective-permute-done.6.refs_0_
  62.5 4.7 %collective-permute-done.7.refs_1_ = bf16[20,48,128]{2,1,0:T(8,128)(2,1)S(1)} collective-permute-done((bf16[20,48,128]{2,1,0:T(8,128)(2,1)S(1)}, bf16[20,48,128]{2,1,0:T(8,128)(2,1)S(1)}, u32[]{:S(2)}, u32[]{:S(2)}) %collective-permute-start.7) | collective-permute-done | bytes 245792 | tf_op jit(solution)/shard_map/ppermute | solution.py:48
  67.2 2.2 %add_early.3.refs_1_ = f32[8192,48]{1,0:T(8,128)S(1)} custom-call(s32[4,20]{1,0:T(4,128)S(1)} %bitcast.12, f32[8192,48]{1,0:T(8,128)S(1)} %get-tuple-element.92.acc, f32[8192,80]{1,0:T(8,128)S(1)} %get-tuple-element.84.inverse.refs_3_.refs_2_, bf16[80,128,128]{2,1,0:T(8,128)(2,1)S(1)} %bitcast.7, bf16[20,48,128]{2,1,0:T(8,128)(2,1)S(1)} %collective-permute-done.6.refs_0_, ...), custom_call_target="tpu_custom_call" | custom-call | bytes 65536 | tf_op jit(solution)/shard_map/add_early/pallas_call | solution.py:33
  69.5 0.0 collective-permute-done.8.refs_4_
  69.5 1.7 %collective-permute-start.9 = (bf16[80,1024]{1,0:T(8,128)(2,1)S(1)}, bf16[80,1024]{1,0:T(8,128)(2,1)S(1)}, u32[]{:S(2)}, u32[]{:S(2)}) collective-permute-start(bf16[80,1024]{1,0:T(8,128)(2,1)S(1)} %get-tuple-element.100), channel_id=1, source_target_pairs={{0,1},{1,0},{2,3},{3,2},{4,5},{5,4},{6,7},{7,6},{8,9},{9,8},{10,11... | collective-permute-start | bytes 491528 | tf_op jit(solution)/shard_map/ppermute | solution.py:52
  71.2 0.1 collective-permute-start.10
  71.3 3.8 %gather_far.3 = (f32[8192,48]{1,0:T(8,128)S(1)}, bf16[48,2048]{1,0:T(8,128)(2,1)S(1)}) custom-call(s32[4,20]{1,0:T(4,128)S(1)} %bitcast.13, s32[2048]{0:T(1024)S(1)} %get-tuple-element.66.refs_0_, f32[8192,48]{1,0:T(8,128)S(1)} %add_early.3.refs_1_, f32[8192,80]{1,0:T(8,128)S(1)} %get-tuple-element.84.inverse.refs_3_.refs_2_, ...), custom_call_target="tpu_custom_call" | custom-call | bytes 1048576 | tf_op jit(solution)/shard_map/gather_far/pallas_call | solution.py:33
  75.1 0.6 collective-permute-start.16
  75.7 0.0 collective-permute-done.9.refs_6_
  75.7 2.8 %gather_next.5 = bf16[48,2048]{1,0:T(8,128)(2,1)S(1)} custom-call(s32[2048]{0:T(1024)S(1)} %get-tuple-element.67.refs_1_.refs_0_, f32[8192,48]{1,0:T(8,128)S(1)} %get-tuple-element.109.refs_1_), custom_call_target="tpu_custom_call" | custom-call | bytes 65536 | tf_op jit(solution)/shard_map/gather_next/pallas_call | solution.py:33
  78.5 1.3 %collective-permute-start.11 = (bf16[48,2048]{1,0:T(8,128)(2,1)S(1)}, bf16[48,2048]{1,0:T(8,128)(2,1)S(1)}, u32[]{:S(2)}, u32[]{:S(2)}) collective-permute-start(bf16[48,2048]{1,0:T(8,128)(2,1)S(1)} %gather_next.5), channel_id=1, source_target_pairs={{0,2},{1,3},{2,0},{3,1},{4,6},{5,7},{6,4},{7,5},{8,10},{9,11},{10,... | collective-permute-start | bytes 589832 | tf_op jit(solution)/shard_map/ppermute | solution.py:52
  79.8 2.8 %gather_next.6 = (bf16[48,1024]{1,0:T(8,128)(2,1)S(1)}, bf16[48,1024]{1,0:T(8,128)(2,1)S(1)}) custom-call(s32[2048]{0:T(1024)S(1)} %get-tuple-element.64.refs_0_, f32[8192,48]{1,0:T(8,128)S(1)} %get-tuple-element.109.refs_1_), custom_call_target="tpu_custom_call" | custom-call | bytes 65536 | tf_op jit(solution)/shard_map/gather_next/pallas_call | solution.py:33
  82.6 0.4 collective-permute-start.14
  83.0 0.2 collective-permute-start.15
  83.1 0.0 collective-permute-done.16.refs_5_
  83.2 2.8 %gather_next.7.refs_4_ = bf16[48,2048]{1,0:T(8,128)(2,1)S(1)} custom-call(s32[2048]{0:T(1024)S(1)} %get-tuple-element.65.refs_1_.refs_0_, f32[8192,48]{1,0:T(8,128)S(1)} %get-tuple-element.109.refs_1_), custom_call_target="tpu_custom_call" | custom-call | bytes 4194304 | tf_op jit(solution)/shard_map/gather_next/pallas_call | solution.py:33
  85.9 0.0 collective-permute-done.14.refs_2_
  85.9 0.0 collective-permute-done.15.refs_3_
  85.9 0.4 collective-permute-done.11.refs_1_
  86.3 2.1 %mix.1 = bf16[512,2048]{1,0:T(8,128)(2,1)} custom-call(bf16[512,512]{1,0:T(8,128)(2,1)S(1)} %get-tuple-element.60.weight, f32[512,128]{1,0:T(8,128)S(1)} %get-tuple-element.61.bias, bf16[80,2048]{1,0:T(8,128)(2,1)S(1)} %get-tuple-element.96.refs_0_, bf16[48,2048]{1,0:T(8,128)(2,1)S(1)} %collective-permute-done.11.refs_1_, ...), custom_call_target="tpu_custom_call" | custom-call | flops 1073741824 | bytes 5242880 | tf_op jit(solution)/shard_map/mix/pallas_call | solution.py:321
  (29 shorter events, 0.1 us)
Async XLA Ops:
  0.0 9.7 %copy-start = (bf16[1,4,20,128,128]{4,3,2,1,0:T(8,128)(2,1)S(1)}, bf16[1,4,20,128,128]{4,3,2,1,0:T(8,128)(2,1)}, u32[]{:S(2)}) copy-start(bf16[1,4,20,128,128]{4,3,2,1,0:T(8,128)(2,1)} %param.11) | copy-start | bytes 7864324
  0.0 3.3 %collective-permute-start.2 = (s32[4,20]{1,0:T(4,128)}, s32[4,20]{1,0:T(4,128)S(1)}, u32[]{:S(2)}, u32[]{:S(2)}) collective-permute-start(s32[4,20]{1,0:T(4,128)} %bitcast.14), channel_id=1, source_target_pairs={{0,4},{4,8},{8,12},{12,0},{1,5},{5,9},{9,13},{13,1},{2,6},{6,10},{... | collective-permute-start | bytes 968 | tf_op jit(solution)/shard_map/ppermute | solution.py:48
  0.0 3.6 %collective-permute-start.1 = (s32[4,20]{1,0:T(4,128)}, s32[4,20]{1,0:T(4,128)S(1)}, u32[]{:S(2)}, u32[]{:S(2)}) collective-permute-start(s32[4,20]{1,0:T(4,128)} %bitcast.15), channel_id=1, source_target_pairs={{0,8},{4,12},{8,0},{12,4},{1,9},{5,13},{9,1},{13,5},{2,10},{6,14},... | collective-permute-start | bytes 968 | tf_op jit(solution)/shard_map/ppermute | solution.py:48
  1.4 4.4 %collective-permute-start = (s32[4,20]{1,0:T(4,128)}, s32[4,20]{1,0:T(4,128)S(1)}, u32[]{:S(2)}, u32[]{:S(2)}) collective-permute-start(s32[4,20]{1,0:T(4,128)} %bitcast.16), channel_id=1, source_target_pairs={{0,12},{4,0},{8,4},{12,8},{1,13},{5,1},{9,5},{13,9},{2,14},{6,2},{... | collective-permute-start | bytes 968 | tf_op jit(solution)/shard_map/ppermute | solution.py:48
  1.5 1.6 %copy-start.1 = (bf16[128,8192]{1,0:T(8,128)(2,1)S(1)}, bf16[128,8192]{1,0:T(8,128)(2,1)}, u32[]{:S(2)}) copy-start(bf16[128,8192]{1,0:T(8,128)(2,1)} %refs_3_.1) | copy-start | bytes 6291460
  3.1 6.6 %copy-start.3 = (bf16[512,512]{1,0:T(8,128)(2,1)S(1)}, bf16[512,512]{1,0:T(8,128)(2,1)}, u32[]{:S(2)}) copy-start(bf16[512,512]{1,0:T(8,128)(2,1)} %weight.1) | copy-start | bytes 1572868
  3.3 4.9 %copy-start.5 = (s32[4,20]{1,0:T(4,128)}, s32[4,20]{1,0:T(4,128)S(1)}, u32[]{:S(2)}) copy-start(s32[4,20]{1,0:T(4,128)S(1)} %collective-permute-done.2.refs_2_) | copy-start | bytes 964
  3.6 4.6 %copy-start.7 = (s32[4,20]{1,0:T(4,128)}, s32[4,20]{1,0:T(4,128)S(1)}, u32[]{:S(2)}) copy-start(s32[4,20]{1,0:T(4,128)S(1)} %collective-permute-done.1.refs_1_) | copy-start | bytes 964
  5.8 3.2 %copy-start.9 = (s32[4,20]{1,0:T(4,128)}, s32[4,20]{1,0:T(4,128)S(1)}, u32[]{:S(2)}) copy-start(s32[4,20]{1,0:T(4,128)S(1)} %collective-permute-done.refs_0_) | copy-start | bytes 964
  7.4 17.0 %collective-permute-start.3 = (bf16[20,80,128]{2,1,0:T(8,128)(2,1)}, bf16[20,80,128]{2,1,0:T(8,128)(2,1)}, u32[]{:S(2)}, u32[]{:S(2)}) collective-permute-start(bf16[20,80,128]{2,1,0:T(8,128)(2,1)} %get-tuple-element.80), channel_id=1, source_target_pairs={{0,4},{4,8},{8,12},{12,0},{1,5},{5,9},{9,13},{13,1},{2,6},{6,10},{... | collective-permute-start | bytes 1228808 | tf_op jit(solution)/shard_map/ppermute | solution.py:48
  8.2 33.7 %collective-permute-start.4 = (bf16[20,80,128]{2,1,0:T(8,128)(2,1)}, bf16[20,80,128]{2,1,0:T(8,128)(2,1)}, u32[]{:S(2)}, u32[]{:S(2)}) collective-permute-start(bf16[20,80,128]{2,1,0:T(8,128)(2,1)} %get-tuple-element.81), channel_id=1, source_target_pairs={{0,8},{4,12},{8,0},{12,4},{1,9},{5,13},{9,1},{13,5},{2,10},{6,14},... | collective-permute-start | bytes 1228808 | tf_op jit(solution)/shard_map/ppermute | solution.py:48
  8.2 36.7 %collective-permute-start.5 = (bf16[20,80,128]{2,1,0:T(8,128)(2,1)}, bf16[20,80,128]{2,1,0:T(8,128)(2,1)S(1)}, u32[]{:S(2)}, u32[]{:S(2)}) collective-permute-start(bf16[20,80,128]{2,1,0:T(8,128)(2,1)} %get-tuple-element.82), channel_id=1, source_target_pairs={{0,12},{4,0},{8,4},{12,8},{1,13},{5,1},{9,5},{13,9},{2,14},{6,2},{... | collective-permute-start | bytes 1228808 | tf_op jit(solution)/shard_map/ppermute | solution.py:48
  9.0 13.9 %copy-start.6 = (s32[4,20]{1,0:T(4,128)S(1)}, s32[4,20]{1,0:T(4,128)}, u32[]{:S(2)}) copy-start(s32[4,20]{1,0:T(4,128)} %copy-done.5) | copy-start | bytes 964
  9.0 13.9 %copy-start.8 = (s32[4,20]{1,0:T(4,128)S(1)}, s32[4,20]{1,0:T(4,128)}, u32[]{:S(2)}) copy-start(s32[4,20]{1,0:T(4,128)} %copy-done.7) | copy-start | bytes 964
  9.0 13.9 %copy-start.10 = (s32[4,20]{1,0:T(4,128)S(1)}, s32[4,20]{1,0:T(4,128)}, u32[]{:S(2)}) copy-start(s32[4,20]{1,0:T(4,128)} %copy-done.9) | copy-start | bytes 964
  9.7 1.6 %copy-start.2 = (bf16[128,8192]{1,0:T(8,128)(2,1)S(1)}, bf16[128,8192]{1,0:T(8,128)(2,1)}, u32[]{:S(2)}) copy-start(bf16[128,8192]{1,0:T(8,128)(2,1)} %refs_3_.1) | copy-start | bytes 6291460
  11.3 0.7 copy-start.4
  12.0 0.7 copy-start.11
  12.7 0.7 copy-start.12
  13.4 9.6 %copy-start.13 = (s32[8192]{0:T(1024)S(1)}, s32[8192]{0:T(1024)}, u32[]{:S(2)}) copy-start(s32[8192]{0:T(1024)} %param.12) | copy-start | bytes 98308
  44.9 17.6 %collective-permute-start.6 = (bf16[20,48,128]{2,1,0:T(8,128)(2,1)S(1)}, bf16[20,48,128]{2,1,0:T(8,128)(2,1)S(1)}, u32[]{:S(2)}, u32[]{:S(2)}) collective-permute-start(bf16[20,48,128]{2,1,0:T(8,128)(2,1)S(1)} %get-tuple-element.93), channel_id=1, source_target_pairs={{0,4},{4,8},{8,12},{12,0},{1,5},{5,9},{9,13},{13,1},{2,6},{6,10},{... | collective-permute-start | bytes 737288 | tf_op jit(solution)/shard_map/ppermute | solution.py:48
  45.0 22.3 %collective-permute-start.7 = (bf16[20,48,128]{2,1,0:T(8,128)(2,1)S(1)}, bf16[20,48,128]{2,1,0:T(8,128)(2,1)S(1)}, u32[]{:S(2)}, u32[]{:S(2)}) collective-permute-start(bf16[20,48,128]{2,1,0:T(8,128)(2,1)S(1)} %get-tuple-element.94), channel_id=1, source_target_pairs={{0,8},{4,12},{8,0},{12,4},{1,9},{5,13},{9,1},{13,5},{2,10},{6,14},... | collective-permute-start | bytes 737288 | tf_op jit(solution)/shard_map/ppermute | solution.py:48
  46.2 23.3 %collective-permute-start.8 = (bf16[20,48,128]{2,1,0:T(8,128)(2,1)S(1)}, bf16[20,48,128]{2,1,0:T(8,128)(2,1)S(1)}, u32[]{:S(2)}, u32[]{:S(2)}) collective-permute-start(bf16[20,48,128]{2,1,0:T(8,128)(2,1)S(1)} %get-tuple-element.95), channel_id=1, source_target_pairs={{0,12},{4,0},{8,4},{12,8},{1,13},{5,1},{9,5},{13,9},{2,14},{6,2},{... | collective-permute-start | bytes 737288 | tf_op jit(solution)/shard_map/ppermute | solution.py:48
  53.7 26.1 %collective-permute-start.12 = (bf16[80,2048]{1,0:T(8,128)(2,1)S(1)}, bf16[80,2048]{1,0:T(8,128)(2,1)S(1)}, u32[]{:S(2)}, u32[]{:S(2)}) collective-permute-start(bf16[80,2048]{1,0:T(8,128)(2,1)S(1)} %get-tuple-element.103), channel_id=1, source_target_pairs={{0,3},{1,2},{2,1},{3,0},{4,7},{5,6},{6,5},{7,4},{8,11},{9,10},{10,... | collective-permute-start | bytes 983048 | tf_op jit(solution)/shard_map/ppermute | solution.py:52
  56.3 23.5 %collective-permute-start.13 = (bf16[80,2048]{1,0:T(8,128)(2,1)S(1)}, bf16[80,2048]{1,0:T(8,128)(2,1)S(1)}, u32[]{:S(2)}, u32[]{:S(2)}) collective-permute-start(bf16[80,2048]{1,0:T(8,128)(2,1)S(1)} %get-tuple-element.104), channel_id=1, source_target_pairs={{0,2},{1,3},{2,0},{3,1},{4,6},{5,7},{6,4},{7,5},{8,10},{9,11},{10,... | collective-permute-start | bytes 983048 | tf_op jit(solution)/shard_map/ppermute | solution.py:52
  69.5 6.2 %collective-permute-start.9 = (bf16[80,1024]{1,0:T(8,128)(2,1)S(1)}, bf16[80,1024]{1,0:T(8,128)(2,1)S(1)}, u32[]{:S(2)}, u32[]{:S(2)}) collective-permute-start(bf16[80,1024]{1,0:T(8,128)(2,1)S(1)} %get-tuple-element.100), channel_id=1, source_target_pairs={{0,1},{1,0},{2,3},{3,2},{4,5},{5,4},{6,7},{7,6},{8,9},{9,8},{10,11... | collective-permute-start | bytes 491528 | tf_op jit(solution)/shard_map/ppermute | solution.py:52
  71.2 4.5 %collective-permute-start.10 = (bf16[80,1024]{1,0:T(8,128)(2,1)S(1)}, bf16[80,1024]{1,0:T(8,128)(2,1)S(1)}, u32[]{:S(2)}, u32[]{:S(2)}) collective-permute-start(bf16[80,1024]{1,0:T(8,128)(2,1)S(1)} %get-tuple-element.101), channel_id=1, source_target_pairs={{0,1},{1,0},{2,3},{3,2},{4,5},{5,4},{6,7},{7,6},{8,9},{9,8},{10,11... | collective-permute-start | bytes 491528 | tf_op jit(solution)/shard_map/ppermute | solution.py:52
  75.1 8.1 %collective-permute-start.16 = (bf16[48,2048]{1,0:T(8,128)(2,1)S(1)}, bf16[48,2048]{1,0:T(8,128)(2,1)S(1)}, u32[]{:S(2)}, u32[]{:S(2)}) collective-permute-start(bf16[48,2048]{1,0:T(8,128)(2,1)S(1)} %get-tuple-element.108), channel_id=1, source_target_pairs={{0,3},{1,2},{2,1},{3,0},{4,7},{5,6},{6,5},{7,4},{8,11},{9,10},{10,... | collective-permute-start | bytes 589832 | tf_op jit(solution)/shard_map/ppermute | solution.py:52
  78.5 7.9 %collective-permute-start.11 = (bf16[48,2048]{1,0:T(8,128)(2,1)S(1)}, bf16[48,2048]{1,0:T(8,128)(2,1)S(1)}, u32[]{:S(2)}, u32[]{:S(2)}) collective-permute-start(bf16[48,2048]{1,0:T(8,128)(2,1)S(1)} %gather_next.5), channel_id=1, source_target_pairs={{0,2},{1,3},{2,0},{3,1},{4,6},{5,7},{6,4},{7,5},{8,10},{9,11},{10,... | collective-permute-start | bytes 589832 | tf_op jit(solution)/shard_map/ppermute | solution.py:52
  82.6 3.4 %collective-permute-start.14 = (bf16[48,1024]{1,0:T(8,128)(2,1)S(1)}, bf16[48,1024]{1,0:T(8,128)(2,1)S(1)}, u32[]{:S(2)}, u32[]{:S(2)}) collective-permute-start(bf16[48,1024]{1,0:T(8,128)(2,1)S(1)} %get-tuple-element.106), channel_id=1, source_target_pairs={{0,1},{1,0},{2,3},{3,2},{4,5},{5,4},{6,7},{7,6},{8,9},{9,8},{10,11... | collective-permute-start | bytes 294920 | tf_op jit(solution)/shard_map/ppermute | solution.py:52
  83.0 2.9 %collective-permute-start.15 = (bf16[48,1024]{1,0:T(8,128)(2,1)S(1)}, bf16[48,1024]{1,0:T(8,128)(2,1)S(1)}, u32[]{:S(2)}, u32[]{:S(2)}) collective-permute-start(bf16[48,1024]{1,0:T(8,128)(2,1)S(1)} %get-tuple-element.107), channel_id=1, source_target_pairs={{0,1},{1,0},{2,3},{3,2},{4,5},{5,4},{6,7},{7,6},{8,9},{9,8},{10,11... | collective-permute-start | bytes 294920 | tf_op jit(solution)/shard_map/ppermute | solution.py:52

commit v12 on v9

--- a/solution.py
+++ b/solution.py
@@ -13,7 +13,7 @@
 SMEM = pl.BlockSpec(memory_space=pltpu.SMEM)
 ANY = pl.BlockSpec(memory_space=pl.ANY)
 CHUNK = 256
-UNROLL = 64
+UNROLL = 32
 
 
 def dot(a, b, dims):
@@ -182,18 +182,25 @@
     return outs[:-3], *outs[-3:]
 
 
+def paired(order):
+    half = order.shape[0] // 2
+    return order[:half] | (order[half:] << 16)
+
+
 def pick(order, nodes, stage, outs):
-    count, size = stage.shape
+    half, size = stage.shape[0] // 2, stage.shape[1]
     eye = identity(size)
 
     def group(i, carry):
         at = pl.multiple_of(i * UNROLL, UNROLL)
         for u in range(UNROLL):
-            source = order[at + u]
-            stage[pl.ds(at + u, 1), :] = nodes[pl.ds(source, 1), :]
+            pair = order[at + u]
+            lower, upper = pair & 0xFFFF, lax.shift_right_logical(pair, 16)
+            stage[pl.ds(at + u, 1), :] = nodes[pl.ds(lower, 1), :]
+            stage[pl.ds(half + at + u, 1), :] = nodes[pl.ds(upper, 1), :]
         return carry
 
-    lax.fori_loop(0, count // UNROLL, group, 0)
+    lax.fori_loop(0, half // UNROLL, group, 0)
     first = 0
     for out in outs:
         columns = out.shape[1]
@@ -249,7 +256,7 @@
 def gather_far(acc, inverse, rows, orders, counts, got, first):
     nodes, size = acc.shape
     slots, tile = rows.shape[1], counts.shape[-1]
-    share, far = orders[0].shape[0], len(orders)
+    share, far = 2 * orders[0].shape[0], len(orders)
     outs = call(
         functools.partial(far_kernel, first, len(got), far),
         "gather_far",
@@ -279,7 +286,7 @@
         orders,
         [total],
         [jax.ShapeDtypeStruct((size, width), jnp.bfloat16) for w in widths for width in w],
-        [((orders[0].shape[0], size), jnp.float32)],
+        [((2 * orders[0].shape[0], size), jnp.float32)],
         moved,
     )
 
@@ -343,7 +350,7 @@
     ranks = list(range(groups - 1, -1, -1))
     whose = me ^ jnp.asarray(ranks, jnp.int32)
     far = groups - 2
-    picks = [lax.dynamic_slice(order, ((me ^ k) * share,), (share,)) for k in ranks]
+    picks = [paired(lax.dynamic_slice(order, ((me ^ k) * share,), (share,))) for k in ranks]
 
     asked = [shifted(cols, "blk", -s) for s in range(1, blocks)]
     *asked, panel = lax.optimization_barrier((*asked, staged(features)))

time: 88.7 us -> 88.7 us (level)
  the two profiles are of different devices: /device:TPU:27 before, /device:TPU:31 now
where the time goes in v12:
time: 88.7 us; the launch traced here: 88.4 us
  Pallas kernels  42.7 us (48%)
  waiting for transfers between devices  25.6 us (29%)
  starting transfers between devices  13.9 us (16%)
  local copies, waits for them, and re-layouts  5.26 us (6%)
    pallas_call x10, Pallas kernels, call(): pl.pallas_call(kernel, out_shape=list(outs), in_specs=[SMEM] * len(scalar...  37.6 us
    ppermute x9, waiting for transfers between devices, shifted(): return lax.ppermute(value, axis, pairs)  25 us
    ppermute x8, starting transfers between devices, traded(): lax.ppermute(value, axis, [(i, i ^ k) for i in range(lax.axis_size(axis))])  8.09 us
    ppermute x9, starting transfers between devices, shifted(): return lax.ppermute(value, axis, pairs)  5.85 us
    unnamed x28, local copies, waits for them, and re-layouts  5.26 us
    pallas_call x2, Pallas kernels, pack(): pl.pallas_call(functools.partial(pack_kernel, low, size, offsets, slots,...  3.06 us
    pallas_call x1, Pallas kernels, mix(): pl.pallas_call(functools.partial(mix_kernel, places), out_shape=jax.Shape...  2.11 us
  transfers between devices with their start and end apart: 17, of which 5 were waited for; matrix products, arithmetic and copies ran while one was open for 1% of the time, Pallas kernels for 44%

profile of v12, /device:TPU:31, one launch (start us, length us, event | category | flops | bytes accessed | tf_op | source)
XLA Modules:
  0.0 88.4 jit_solution(7523727122867312448)
XLA Ops:
  0.0 0.0 collective-permute-start.2
  0.0 1.3 %collective-permute-start.1 = (s32[4,20]{1,0:T(4,128)}, s32[4,20]{1,0:T(4,128)S(1)}, u32[]{:S(2)}, u32[]{:S(2)}) collective-permute-start(s32[4,20]{1,0:T(4,128)} %bitcast.15), channel_id=1, source_target_pairs={{0,8},{4,12},{8,0},{12,4},{1,9},{5,13},{9,1},{13,5},{2,10},{6,14},... | collective-permute-start | bytes 968 | tf_op jit(solution)/shard_map/ppermute | solution.py:48
  1.4 0.2 collective-permute-start
  1.5 1.6 %copy-done.1 = bf16[128,8192]{1,0:T(8,128)(2,1)S(1)} copy-done((bf16[128,8192]{1,0:T(8,128)(2,1)S(1)}, bf16[128,8192]{1,0:T(8,128)(2,1)}, u32[]{:S(2)}) %copy-start.1) | copy-done | bytes 2097176
  3.1 0.1 stage.1.refs_3_
  3.3 0.0 collective-permute-done.2.refs_2_
  3.3 0.3 collective-permute-done.1.refs_1_
  3.6 2.2 %collective-permute-done.refs_0_ = s32[4,20]{1,0:T(4,128)S(1)} collective-permute-done((s32[4,20]{1,0:T(4,128)}, s32[4,20]{1,0:T(4,128)S(1)}, u32[]{:S(2)}, u32[]{:S(2)}) %collective-permute-start) | collective-permute-done | bytes 352 | tf_op jit(solution)/shard_map/ppermute | solution.py:48
  5.8 1.6 %pack.2 = (bf16[20,80,128]{2,1,0:T(8,128)(2,1)}, bf16[20,80,128]{2,1,0:T(8,128)(2,1)}, bf16[20,80,128]{2,1,0:T(8,128)(2,1)}) custom-call(s32[4,20]{1,0:T(4,128)S(1)} %collective-permute-done.refs_0_, s32[4,20]{1,0:T(4,128)S(1)} %collective-permute-done.1.refs_1_, s32[4,20]{1,0:T(4,128)S(1)} %collective-permute-done.2.refs_2_, bf16[128,8192]{1,0:T(8,128)(2,1)S(1)} %stage.1.refs_3_), custom_call_target="tpu_custom_call" | custom-call | bytes 65536 | tf_op jit(solution)/shard_map/pack/pallas_call | solution.py:94
  7.4 0.7 collective-permute-start.3
  8.2 0.0 collective-permute-start.4
  8.2 0.8 collective-permute-start.5
  9.0 0.7 xor_multiply_fusion.starts
  9.7 1.6 %copy-done.2 = bf16[128,8192]{1,0:T(8,128)(2,1)S(1)} copy-done((bf16[128,8192]{1,0:T(8,128)(2,1)S(1)}, bf16[128,8192]{1,0:T(8,128)(2,1)}, u32[]{:S(2)}) %copy-start.2) | copy-done | bytes 2097176
  11.3 0.7 copy-done.4
  12.0 0.7 copy-done.11
  12.7 0.7 copy-done.12
  13.4 9.6 %own.1 = (f32[8192,80]{1,0:T(8,128)S(1)}, f32[8192,48]{1,0:T(8,128)S(1)}, f32[8192,80]{1,0:T(8,128)S(1)}, f32[512,128]{1,0:T(8,128)S(1)}, bf16[512,512]{1,0:T(8,128)(2,1)S(1)}) custom-call(s32[4,20]{1,0:T(4,128)S(1)} %bitcast.9, s32[4,20]{1,0:T(4,128)S(1)} %bitcast.17, s32[4]{0:T(128)S(1)} %xor_multiply_fusion.starts, bf16[128,8192]{1,0:T(8,128)(2,1)S(1)} %copy-done.2, ...), custom_call_target="tpu_custom_call" | custom-call | bytes 65536 | tf_op jit(solution)/shard_map/own/pallas_call | solution.py:33
  23.0 1.4 %pack.3 = (bf16[20,48,128]{2,1,0:T(8,128)(2,1)S(1)}, bf16[20,48,128]{2,1,0:T(8,128)(2,1)S(1)}, bf16[20,48,128]{2,1,0:T(8,128)(2,1)S(1)}) custom-call(s32[4,20]{1,0:T(4,128)S(1)} %copy-done.10, s32[4,20]{1,0:T(4,128)S(1)} %copy-done.8, s32[4,20]{1,0:T(4,128)S(1)} %copy-done.6, bf16[128,8192]{1,0:T(8,128)(2,1)S(1)} %copy-done.2), custom_call_target="tpu_custom_call" | custom-call | bytes 65536 | tf_op jit(solution)/shard_map/pack/pallas_call | solution.py:94
  24.4 0.0 collective-permute-done.3.refs_0_
  24.4 17.5 %collective-permute-done.4.refs_1_ = bf16[20,80,128]{2,1,0:T(8,128)(2,1)} collective-permute-done((bf16[20,80,128]{2,1,0:T(8,128)(2,1)}, bf16[20,80,128]{2,1,0:T(8,128)(2,1)}, u32[]{:S(2)}, u32[]{:S(2)}) %collective-permute-start.4) | collective-permute-done | bytes 409632 | tf_op jit(solution)/shard_map/ppermute | solution.py:48
  41.9 2.9 %add_early.2.refs_2_ = f32[8192,80]{1,0:T(8,128)S(1)} custom-call(s32[4,20]{1,0:T(4,128)S(1)} %bitcast.10, f32[8192,80]{1,0:T(8,128)S(1)} %get-tuple-element.83.acc, f32[8192,80]{1,0:T(8,128)S(1)} %get-tuple-element.84.inverse.refs_3_.refs_2_, bf16[80,128,128]{2,1,0:T(8,128)(2,1)S(1)} %bitcast.5, bf16[20,80,128]{2,1,0:T(8,128)(2,1)} %collective-permute-done.3.refs_0_, ...), custom_call_target="tpu_custom_call" | custom-call | bytes 65536 | tf_op jit(solution)/shard_map/add_early/pallas_call | solution.py:33
  44.9 0.0 collective-permute-done.5.refs_5_
  44.9 0.1 collective-permute-start.6
  45.0 1.2 %collective-permute-start.7 = (bf16[20,48,128]{2,1,0:T(8,128)(2,1)S(1)}, bf16[20,48,128]{2,1,0:T(8,128)(2,1)S(1)}, u32[]{:S(2)}, u32[]{:S(2)}) collective-permute-start(bf16[20,48,128]{2,1,0:T(8,128)(2,1)S(1)} %get-tuple-element.94), channel_id=1, source_target_pairs={{0,8},{4,12},{8,0},{12,4},{1,9},{5,13},{9,1},{13,5},{2,10},{6,14},... | collective-permute-start | bytes 737288 | tf_op jit(solution)/shard_map/ppermute | solution.py:48
  46.2 1.5 %collective-permute-start.8 = (bf16[20,48,128]{2,1,0:T(8,128)(2,1)S(1)}, bf16[20,48,128]{2,1,0:T(8,128)(2,1)S(1)}, u32[]{:S(2)}, u32[]{:S(2)}) collective-permute-start(bf16[20,48,128]{2,1,0:T(8,128)(2,1)S(1)} %get-tuple-element.95), channel_id=1, source_target_pairs={{0,12},{4,0},{8,4},{12,8},{1,13},{5,1},{9,5},{13,9},{2,14},{6,2},{... | collective-permute-start | bytes 737288 | tf_op jit(solution)/shard_map/ppermute | solution.py:48
  47.7 6.0 %gather_far.2 = (f32[8192,80]{1,0:T(8,128)S(1)}, bf16[80,2048]{1,0:T(8,128)(2,1)S(1)}, bf16[80,2048]{1,0:T(8,128)(2,1)S(1)}) custom-call(s32[4,20]{1,0:T(4,128)S(1)} %bitcast.11, s32[1024]{0:T(1024)S(1)} %get-tuple-element.66.refs_0_, s32[1024]{0:T(1024)S(1)} %get-tuple-element.67.refs_1_.refs_0_, f32[8192,80]{1,0:T(8,128)S(1)} %add_early.2.refs_2_, ...), custom_call_target="tpu_custom_call" | custom-call | bytes 1048576 | tf_op jit(solution)/shard_map/gather_far/pallas_call | solution.py:33
  53.6 2.5 %collective-permute-start.12 = (bf16[80,2048]{1,0:T(8,128)(2,1)S(1)}, bf16[80,2048]{1,0:T(8,128)(2,1)S(1)}, u32[]{:S(2)}, u32[]{:S(2)}) collective-permute-start(bf16[80,2048]{1,0:T(8,128)(2,1)S(1)} %get-tuple-element.103), channel_id=1, source_target_pairs={{0,3},{1,2},{2,1},{3,0},{4,7},{5,6},{6,5},{7,4},{8,11},{9,10},{10,... | collective-permute-start | bytes 983048 | tf_op jit(solution)/shard_map/ppermute | solution.py:52
  56.2 1.2 %collective-permute-start.13 = (bf16[80,2048]{1,0:T(8,128)(2,1)S(1)}, bf16[80,2048]{1,0:T(8,128)(2,1)S(1)}, u32[]{:S(2)}, u32[]{:S(2)}) collective-permute-start(bf16[80,2048]{1,0:T(8,128)(2,1)S(1)} %get-tuple-element.104), channel_id=1, source_target_pairs={{0,2},{1,3},{2,0},{3,1},{4,6},{5,7},{6,4},{7,5},{8,10},{9,11},{10,... | collective-permute-start | bytes 983048 | tf_op jit(solution)/shard_map/ppermute | solution.py:52
  57.4 4.9 %gather_next.4 = (bf16[80,1024]{1,0:T(8,128)(2,1)S(1)}, bf16[80,1024]{1,0:T(8,128)(2,1)S(1)}, bf16[80,2048]{1,0:T(8,128)(2,1)S(1)}) custom-call(s32[1024]{0:T(1024)S(1)} %get-tuple-element.64.refs_0_, s32[1024]{0:T(1024)S(1)} %get-tuple-element.65.refs_1_.refs_0_, f32[8192,80]{1,0:T(8,128)S(1)} %get-tuple-element.88.refs_2_), custom_call_target="tpu_custom_call" | custom-call | bytes 65536 | tf_op jit(solution)/shard_map/gather_next/pallas_call | solution.py:33
  62.3 4.9 %collective-permute-done.7.refs_1_ = bf16[20,48,128]{2,1,0:T(8,128)(2,1)S(1)} collective-permute-done((bf16[20,48,128]{2,1,0:T(8,128)(2,1)S(1)}, bf16[20,48,128]{2,1,0:T(8,128)(2,1)S(1)}, u32[]{:S(2)}, u32[]{:S(2)}) %collective-permute-start.7) | collective-permute-done | bytes 245792 | tf_op jit(solution)/shard_map/ppermute | solution.py:48
  67.2 2.2 %add_early.3.refs_1_ = f32[8192,48]{1,0:T(8,128)S(1)} custom-call(s32[4,20]{1,0:T(4,128)S(1)} %bitcast.12, f32[8192,48]{1,0:T(8,128)S(1)} %get-tuple-element.92.acc, f32[8192,80]{1,0:T(8,128)S(1)} %get-tuple-element.84.inverse.refs_3_.refs_2_, bf16[80,128,128]{2,1,0:T(8,128)(2,1)S(1)} %bitcast.7, bf16[20,48,128]{2,1,0:T(8,128)(2,1)S(1)} %collective-permute-done.6.refs_0_, ...), custom_call_target="tpu_custom_call" | custom-call | bytes 65536 | tf_op jit(solution)/shard_map/add_early/pallas_call | solution.py:33
  69.5 1.8 %collective-permute-start.9 = (bf16[80,1024]{1,0:T(8,128)(2,1)S(1)}, bf16[80,1024]{1,0:T(8,128)(2,1)S(1)}, u32[]{:S(2)}, u32[]{:S(2)}) collective-permute-start(bf16[80,1024]{1,0:T(8,128)(2,1)S(1)} %get-tuple-element.100), channel_id=1, source_target_pairs={{0,1},{1,0},{2,3},{3,2},{4,5},{5,4},{6,7},{7,6},{8,9},{9,8},{10,11... | collective-permute-start | bytes 491528 | tf_op jit(solution)/shard_map/ppermute | solution.py:52
  71.2 0.1 collective-permute-start.10
  71.3 3.7 %gather_far.3 = (f32[8192,48]{1,0:T(8,128)S(1)}, bf16[48,2048]{1,0:T(8,128)(2,1)S(1)}) custom-call(s32[4,20]{1,0:T(4,128)S(1)} %bitcast.13, s32[1024]{0:T(1024)S(1)} %get-tuple-element.66.refs_0_, f32[8192,48]{1,0:T(8,128)S(1)} %add_early.3.refs_1_, f32[8192,80]{1,0:T(8,128)S(1)} %get-tuple-element.84.inverse.refs_3_.refs_2_, ...), custom_call_target="tpu_custom_call" | custom-call | bytes 1048576 | tf_op jit(solution)/shard_map/gather_far/pallas_call | solution.py:33
  75.0 0.6 collective-permute-start.16
  75.7 2.7 %gather_next.5 = bf16[48,2048]{1,0:T(8,128)(2,1)S(1)} custom-call(s32[1024]{0:T(1024)S(1)} %get-tuple-element.67.refs_1_.refs_0_, f32[8192,48]{1,0:T(8,128)S(1)} %get-tuple-element.109.refs_1_), custom_call_target="tpu_custom_call" | custom-call | bytes 65536 | tf_op jit(solution)/shard_map/gather_next/pallas_call | solution.py:33
  78.4 1.3 %collective-permute-start.11 = (bf16[48,2048]{1,0:T(8,128)(2,1)S(1)}, bf16[48,2048]{1,0:T(8,128)(2,1)S(1)}, u32[]{:S(2)}, u32[]{:S(2)}) collective-permute-start(bf16[48,2048]{1,0:T(8,128)(2,1)S(1)} %gather_next.5), channel_id=1, source_target_pairs={{0,2},{1,3},{2,0},{3,1},{4,6},{5,7},{6,4},{7,5},{8,10},{9,11},{10,... | collective-permute-start | bytes 589832 | tf_op jit(solution)/shard_map/ppermute | solution.py:52
  79.7 0.0 collective-permute-done.12.refs_8_
  79.7 0.0 collective-permute-done.13.refs_9_
  79.7 2.7 %gather_next.6 = (bf16[48,1024]{1,0:T(8,128)(2,1)S(1)}, bf16[48,1024]{1,0:T(8,128)(2,1)S(1)}) custom-call(s32[1024]{0:T(1024)S(1)} %get-tuple-element.64.refs_0_, f32[8192,48]{1,0:T(8,128)S(1)} %get-tuple-element.109.refs_1_), custom_call_target="tpu_custom_call" | custom-call | bytes 65536 | tf_op jit(solution)/shard_map/gather_next/pallas_call | solution.py:33
  82.4 0.4 collective-permute-start.14
  82.8 0.2 collective-permute-start.15
  83.0 0.0 collective-permute-done.16.refs_5_
  83.0 2.7 %gather_next.7.refs_4_ = bf16[48,2048]{1,0:T(8,128)(2,1)S(1)} custom-call(s32[1024]{0:T(1024)S(1)} %get-tuple-element.65.refs_1_.refs_0_, f32[8192,48]{1,0:T(8,128)S(1)} %get-tuple-element.109.refs_1_), custom_call_target="tpu_custom_call" | custom-call | bytes 4194304 | tf_op jit(solution)/shard_map/gather_next/pallas_call | solution.py:33
  85.7 0.0 collective-permute-done.15.refs_3_
  85.7 0.6 collective-permute-done.11.refs_1_
  86.3 2.1 %mix.1 = bf16[512,2048]{1,0:T(8,128)(2,1)} custom-call(bf16[512,512]{1,0:T(8,128)(2,1)S(1)} %get-tuple-element.60.weight, f32[512,128]{1,0:T(8,128)S(1)} %get-tuple-element.61.bias, bf16[80,2048]{1,0:T(8,128)(2,1)S(1)} %get-tuple-element.96.refs_0_, bf16[48,2048]{1,0:T(8,128)(2,1)S(1)} %collective-permute-done.11.refs_1_, ...), custom_call_target="tpu_custom_call" | custom-call | flops 1073741824 | bytes 5242880 | tf_op jit(solution)/shard_map/mix/pallas_call | solution.py:321
  (29 shorter events, 0.1 us)
Async XLA Ops:
  0.0 9.7 %copy-start = (bf16[1,4,20,128,128]{4,3,2,1,0:T(8,128)(2,1)S(1)}, bf16[1,4,20,128,128]{4,3,2,1,0:T(8,128)(2,1)}, u32[]{:S(2)}) copy-start(bf16[1,4,20,128,128]{4,3,2,1,0:T(8,128)(2,1)} %param.11) | copy-start | bytes 7864324
  0.0 3.3 %collective-permute-start.2 = (s32[4,20]{1,0:T(4,128)}, s32[4,20]{1,0:T(4,128)S(1)}, u32[]{:S(2)}, u32[]{:S(2)}) collective-permute-start(s32[4,20]{1,0:T(4,128)} %bitcast.14), channel_id=1, source_target_pairs={{0,4},{4,8},{8,12},{12,0},{1,5},{5,9},{9,13},{13,1},{2,6},{6,10},{... | collective-permute-start | bytes 968 | tf_op jit(solution)/shard_map/ppermute | solution.py:48
  0.0 3.6 %collective-permute-start.1 = (s32[4,20]{1,0:T(4,128)}, s32[4,20]{1,0:T(4,128)S(1)}, u32[]{:S(2)}, u32[]{:S(2)}) collective-permute-start(s32[4,20]{1,0:T(4,128)} %bitcast.15), channel_id=1, source_target_pairs={{0,8},{4,12},{8,0},{12,4},{1,9},{5,13},{9,1},{13,5},{2,10},{6,14},... | collective-permute-start | bytes 968 | tf_op jit(solution)/shard_map/ppermute | solution.py:48
  1.4 4.4 %collective-permute-start = (s32[4,20]{1,0:T(4,128)}, s32[4,20]{1,0:T(4,128)S(1)}, u32[]{:S(2)}, u32[]{:S(2)}) collective-permute-start(s32[4,20]{1,0:T(4,128)} %bitcast.16), channel_id=1, source_target_pairs={{0,12},{4,0},{8,4},{12,8},{1,13},{5,1},{9,5},{13,9},{2,14},{6,2},{... | collective-permute-start | bytes 968 | tf_op jit(solution)/shard_map/ppermute | solution.py:48
  1.5 1.6 %copy-start.1 = (bf16[128,8192]{1,0:T(8,128)(2,1)S(1)}, bf16[128,8192]{1,0:T(8,128)(2,1)}, u32[]{:S(2)}) copy-start(bf16[128,8192]{1,0:T(8,128)(2,1)} %refs_3_.1) | copy-start | bytes 6291460
  3.1 6.6 %copy-start.3 = (bf16[512,512]{1,0:T(8,128)(2,1)S(1)}, bf16[512,512]{1,0:T(8,128)(2,1)}, u32[]{:S(2)}) copy-start(bf16[512,512]{1,0:T(8,128)(2,1)} %weight.1) | copy-start | bytes 1572868
  3.3 4.9 %copy-start.5 = (s32[4,20]{1,0:T(4,128)}, s32[4,20]{1,0:T(4,128)S(1)}, u32[]{:S(2)}) copy-start(s32[4,20]{1,0:T(4,128)S(1)} %collective-permute-done.2.refs_2_) | copy-start | bytes 964
  3.6 4.6 %copy-start.7 = (s32[4,20]{1,0:T(4,128)}, s32[4,20]{1,0:T(4,128)S(1)}, u32[]{:S(2)}) copy-start(s32[4,20]{1,0:T(4,128)S(1)} %collective-permute-done.1.refs_1_) | copy-start | bytes 964
  5.8 3.2 %copy-start.9 = (s32[4,20]{1,0:T(4,128)}, s32[4,20]{1,0:T(4,128)S(1)}, u32[]{:S(2)}) copy-start(s32[4,20]{1,0:T(4,128)S(1)} %collective-permute-done.refs_0_) | copy-start | bytes 964
  7.4 17.0 %collective-permute-start.3 = (bf16[20,80,128]{2,1,0:T(8,128)(2,1)}, bf16[20,80,128]{2,1,0:T(8,128)(2,1)}, u32[]{:S(2)}, u32[]{:S(2)}) collective-permute-start(bf16[20,80,128]{2,1,0:T(8,128)(2,1)} %get-tuple-element.80), channel_id=1, source_target_pairs={{0,4},{4,8},{8,12},{12,0},{1,5},{5,9},{9,13},{13,1},{2,6},{6,10},{... | collective-permute-start | bytes 1228808 | tf_op jit(solution)/shard_map/ppermute | solution.py:48
  8.2 33.7 %collective-permute-start.4 = (bf16[20,80,128]{2,1,0:T(8,128)(2,1)}, bf16[20,80,128]{2,1,0:T(8,128)(2,1)}, u32[]{:S(2)}, u32[]{:S(2)}) collective-permute-start(bf16[20,80,128]{2,1,0:T(8,128)(2,1)} %get-tuple-element.81), channel_id=1, source_target_pairs={{0,8},{4,12},{8,0},{12,4},{1,9},{5,13},{9,1},{13,5},{2,10},{6,14},... | collective-permute-start | bytes 1228808 | tf_op jit(solution)/shard_map/ppermute | solution.py:48
  8.2 36.7 %collective-permute-start.5 = (bf16[20,80,128]{2,1,0:T(8,128)(2,1)}, bf16[20,80,128]{2,1,0:T(8,128)(2,1)S(1)}, u32[]{:S(2)}, u32[]{:S(2)}) collective-permute-start(bf16[20,80,128]{2,1,0:T(8,128)(2,1)} %get-tuple-element.82), channel_id=1, source_target_pairs={{0,12},{4,0},{8,4},{12,8},{1,13},{5,1},{9,5},{13,9},{2,14},{6,2},{... | collective-permute-start | bytes 1228808 | tf_op jit(solution)/shard_map/ppermute | solution.py:48
  9.0 13.9 %copy-start.6 = (s32[4,20]{1,0:T(4,128)S(1)}, s32[4,20]{1,0:T(4,128)}, u32[]{:S(2)}) copy-start(s32[4,20]{1,0:T(4,128)} %copy-done.5) | copy-start | bytes 964
  9.0 13.9 %copy-start.8 = (s32[4,20]{1,0:T(4,128)S(1)}, s32[4,20]{1,0:T(4,128)}, u32[]{:S(2)}) copy-start(s32[4,20]{1,0:T(4,128)} %copy-done.7) | copy-start | bytes 964
  9.0 13.9 %copy-start.10 = (s32[4,20]{1,0:T(4,128)S(1)}, s32[4,20]{1,0:T(4,128)}, u32[]{:S(2)}) copy-start(s32[4,20]{1,0:T(4,128)} %copy-done.9) | copy-start | bytes 964
  9.7 1.6 %copy-start.2 = (bf16[128,8192]{1,0:T(8,128)(2,1)S(1)}, bf16[128,8192]{1,0:T(8,128)(2,1)}, u32[]{:S(2)}) copy-start(bf16[128,8192]{1,0:T(8,128)(2,1)} %refs_3_.1) | copy-start | bytes 6291460
  11.3 0.7 copy-start.4
  12.0 0.7 copy-start.11
  12.7 0.7 copy-start.12
  13.4 9.6 %copy-start.13 = (s32[8192]{0:T(1024)S(1)}, s32[8192]{0:T(1024)}, u32[]{:S(2)}) copy-start(s32[8192]{0:T(1024)} %param.12) | copy-start | bytes 98308
  44.9 17.4 %collective-permute-start.6 = (bf16[20,48,128]{2,1,0:T(8,128)(2,1)S(1)}, bf16[20,48,128]{2,1,0:T(8,128)(2,1)S(1)}, u32[]{:S(2)}, u32[]{:S(2)}) collective-permute-start(bf16[20,48,128]{2,1,0:T(8,128)(2,1)S(1)} %get-tuple-element.93), channel_id=1, source_target_pairs={{0,4},{4,8},{8,12},{12,0},{1,5},{5,9},{9,13},{13,1},{2,6},{6,10},{... | collective-permute-start | bytes 737288 | tf_op jit(solution)/shard_map/ppermute | solution.py:48
  45.0 22.3 %collective-permute-start.7 = (bf16[20,48,128]{2,1,0:T(8,128)(2,1)S(1)}, bf16[20,48,128]{2,1,0:T(8,128)(2,1)S(1)}, u32[]{:S(2)}, u32[]{:S(2)}) collective-permute-start(bf16[20,48,128]{2,1,0:T(8,128)(2,1)S(1)} %get-tuple-element.94), channel_id=1, source_target_pairs={{0,8},{4,12},{8,0},{12,4},{1,9},{5,13},{9,1},{13,5},{2,10},{6,14},... | collective-permute-start | bytes 737288 | tf_op jit(solution)/shard_map/ppermute | solution.py:48
  46.2 23.3 %collective-permute-start.8 = (bf16[20,48,128]{2,1,0:T(8,128)(2,1)S(1)}, bf16[20,48,128]{2,1,0:T(8,128)(2,1)S(1)}, u32[]{:S(2)}, u32[]{:S(2)}) collective-permute-start(bf16[20,48,128]{2,1,0:T(8,128)(2,1)S(1)} %get-tuple-element.95), channel_id=1, source_target_pairs={{0,12},{4,0},{8,4},{12,8},{1,13},{5,1},{9,5},{13,9},{2,14},{6,2},{... | collective-permute-start | bytes 737288 | tf_op jit(solution)/shard_map/ppermute | solution.py:48
  53.6 26.0 %collective-permute-start.12 = (bf16[80,2048]{1,0:T(8,128)(2,1)S(1)}, bf16[80,2048]{1,0:T(8,128)(2,1)S(1)}, u32[]{:S(2)}, u32[]{:S(2)}) collective-permute-start(bf16[80,2048]{1,0:T(8,128)(2,1)S(1)} %get-tuple-element.103), channel_id=1, source_target_pairs={{0,3},{1,2},{2,1},{3,0},{4,7},{5,6},{6,5},{7,4},{8,11},{9,10},{10,... | collective-permute-start | bytes 983048 | tf_op jit(solution)/shard_map/ppermute | solution.py:52
  56.2 23.5 %collective-permute-start.13 = (bf16[80,2048]{1,0:T(8,128)(2,1)S(1)}, bf16[80,2048]{1,0:T(8,128)(2,1)S(1)}, u32[]{:S(2)}, u32[]{:S(2)}) collective-permute-start(bf16[80,2048]{1,0:T(8,128)(2,1)S(1)} %get-tuple-element.104), channel_id=1, source_target_pairs={{0,2},{1,3},{2,0},{3,1},{4,6},{5,7},{6,4},{7,5},{8,10},{9,11},{10,... | collective-permute-start | bytes 983048 | tf_op jit(solution)/shard_map/ppermute | solution.py:52
  69.5 6.2 %collective-permute-start.9 = (bf16[80,1024]{1,0:T(8,128)(2,1)S(1)}, bf16[80,1024]{1,0:T(8,128)(2,1)S(1)}, u32[]{:S(2)}, u32[]{:S(2)}) collective-permute-start(bf16[80,1024]{1,0:T(8,128)(2,1)S(1)} %get-tuple-element.100), channel_id=1, source_target_pairs={{0,1},{1,0},{2,3},{3,2},{4,5},{5,4},{6,7},{7,6},{8,9},{9,8},{10,11... | collective-permute-start | bytes 491528 | tf_op jit(solution)/shard_map/ppermute | solution.py:52
  71.2 4.4 %collective-permute-start.10 = (bf16[80,1024]{1,0:T(8,128)(2,1)S(1)}, bf16[80,1024]{1,0:T(8,128)(2,1)S(1)}, u32[]{:S(2)}, u32[]{:S(2)}) collective-permute-start(bf16[80,1024]{1,0:T(8,128)(2,1)S(1)} %get-tuple-element.101), channel_id=1, source_target_pairs={{0,1},{1,0},{2,3},{3,2},{4,5},{5,4},{6,7},{7,6},{8,9},{9,8},{10,11... | collective-permute-start | bytes 491528 | tf_op jit(solution)/shard_map/ppermute | solution.py:52
  75.0 8.0 %collective-permute-start.16 = (bf16[48,2048]{1,0:T(8,128)(2,1)S(1)}, bf16[48,2048]{1,0:T(8,128)(2,1)S(1)}, u32[]{:S(2)}, u32[]{:S(2)}) collective-permute-start(bf16[48,2048]{1,0:T(8,128)(2,1)S(1)} %get-tuple-element.108), channel_id=1, source_target_pairs={{0,3},{1,2},{2,1},{3,0},{4,7},{5,6},{6,5},{7,4},{8,11},{9,10},{10,... | collective-permute-start | bytes 589832 | tf_op jit(solution)/shard_map/ppermute | solution.py:52
  78.4 7.9 %collective-permute-start.11 = (bf16[48,2048]{1,0:T(8,128)(2,1)S(1)}, bf16[48,2048]{1,0:T(8,128)(2,1)S(1)}, u32[]{:S(2)}, u32[]{:S(2)}) collective-permute-start(bf16[48,2048]{1,0:T(8,128)(2,1)S(1)} %gather_next.5), channel_id=1, source_target_pairs={{0,2},{1,3},{2,0},{3,1},{4,6},{5,7},{6,4},{7,5},{8,10},{9,11},{10,... | collective-permute-start | bytes 589832 | tf_op jit(solution)/shard_map/ppermute | solution.py:52
  82.4 3.3 %collective-permute-start.14 = (bf16[48,1024]{1,0:T(8,128)(2,1)S(1)}, bf16[48,1024]{1,0:T(8,128)(2,1)S(1)}, u32[]{:S(2)}, u32[]{:S(2)}) collective-permute-start(bf16[48,1024]{1,0:T(8,128)(2,1)S(1)} %get-tuple-element.106), channel_id=1, source_target_pairs={{0,1},{1,0},{2,3},{3,2},{4,5},{5,4},{6,7},{7,6},{8,9},{9,8},{10,11... | collective-permute-start | bytes 294920 | tf_op jit(solution)/shard_map/ppermute | solution.py:52
  82.8 2.9 %collective-permute-start.15 = (bf16[48,1024]{1,0:T(8,128)(2,1)S(1)}, bf16[48,1024]{1,0:T(8,128)(2,1)S(1)}, u32[]{:S(2)}, u32[]{:S(2)}) collective-permute-start(bf16[48,1024]{1,0:T(8,128)(2,1)S(1)} %get-tuple-element.107), channel_id=1, source_target_pairs={{0,1},{1,0},{2,3},{3,2},{4,5},{5,4},{6,7},{7,6},{8,9},{9,8},{10,11... | collective-permute-start | bytes 294920 | tf_op jit(solution)/shard_map/ppermute | solution.py:52

commit v13 on v9

--- a/solution.py
+++ b/solution.py
@@ -72,13 +72,14 @@
     return call(stage_kernel, "stage", [], [panel], [shape])[0]
 
 
-def pack_kernel(low, size, offsets, slots, tile, *refs):
-    asked, panel = refs[:offsets], refs[offsets]
-    outs, sems = refs[offsets + 1 : -1], refs[-1]
+def pack_kernel(low, size, slots, tile, block, asked, panel, *refs):
+    outs, sems = refs[:-1], refs[-1]
+    offsets = len(outs)
     for s in range(offsets):
-
-        def body(t, carry, s=s):
-            at = pl.multiple_of(asked[s][s + 1, t] * tile, tile)
+        to = lax.rem(block[0] + s + 1, asked.shape[0])
+
+        def body(t, carry, s=s, to=to):
+            at = pl.multiple_of(asked[to, s + 1, t] * tile, tile)
             pltpu.make_async_copy(
                 panel.at[pl.ds(low, size), pl.ds(at, tile)], outs[s].at[t], sems.at[s]
             ).start()
@@ -89,18 +90,18 @@
         pltpu.make_async_copy(outs[s], outs[s], sems.at[s]).wait()
 
 
-def pack(panel, asked, low, size, tile):
-    offsets, slots = len(asked), asked[0].shape[1]
+def pack(panel, block, asked, low, size, tile):
+    offsets, slots = asked.shape[1] - 1, asked.shape[2]
     return pl.pallas_call(
-        functools.partial(pack_kernel, low, size, offsets, slots, tile),
+        functools.partial(pack_kernel, low, size, slots, tile),
         out_shape=[jax.ShapeDtypeStruct((slots, size, tile), panel.dtype)] * offsets,
-        in_specs=[SMEM] * offsets + [ANY],
+        in_specs=[SMEM, SMEM, ANY],
         out_specs=[ANY] * offsets,
         scratch_shapes=[pltpu.SemaphoreType.DMA((offsets,))],
         compiler_params=pltpu.CompilerParams(vmem_limit_bytes=2**20),
         cost_estimate=pl.CostEstimate(flops=0, bytes_accessed=2**16, transcendentals=0),
         name="pack",
-    )(*asked, panel)
+    )(block, asked, panel)
 
 
 def own_kernel(
@@ -345,13 +346,15 @@
     far = groups - 2
     picks = [lax.dynamic_slice(order, ((me ^ k) * share,), (share,)) for k in ranks]
 
-    asked = [shifted(cols, "blk", -s) for s in range(1, blocks)]
-    *asked, panel = lax.optimization_barrier((*asked, staged(features)))
+    block = lax.axis_index("blk").astype(jnp.int32)[None]
+    told = jnp.broadcast_to(cols[None], (blocks, *cols.shape))
+    told, panel, block = lax.optimization_barrier((told, staged(features), block))
+    asked = lax.all_to_all(told, "blk", 0, 0, tiled=True)
     sent = []
     for low, size in ranges:
         source = features if sent else panel
-        sent.append(list(pack(source, asked, low, size, tile)))
-        *asked, sent[-1][0] = lax.optimization_barrier((*asked, sent[-1][0]))
+        sent.append(list(pack(source, block, asked, low, size, tile)))
+        asked, sent[-1][0] = lax.optimization_barrier((asked, sent[-1][0]))
     accs, inverse, column, across = own(
         features, rows, cols, whose * width, counts, bias, weight, ranges
     )

time: 88.7 us -> 93.1 us (1.050)
  the two profiles are of different devices: /device:TPU:27 before, /device:TPU:0 now
where the time goes in v13:
time: 93.1 us; the launch traced here: 91.7 us
  Pallas kernels  43 us (46%)
  starting transfers between devices  17.7 us (19%)
  waiting for transfers between devices  12.6 us (14%)
  blocking collectives  11.7 us (13%)
  local copies, waits for them, and re-layouts  5.95 us (6%)
    pallas_call x10, Pallas kernels, call(): pl.pallas_call(kernel, out_shape=list(outs), in_specs=[SMEM] * len(scalar...  37.7 us
    ppermute x6, starting transfers between devices, shifted(): return lax.ppermute(value, axis, pairs)  13 us
    ppermute x6, waiting for transfers between devices, shifted(): return lax.ppermute(value, axis, pairs)  11.7 us
    all_to_all x1, blocking collectives, on_device(): asked = lax.all_to_all(told, 'blk', 0, 0, tiled=True)  11.7 us
    unnamed x22, local copies, waits for them, and re-layouts  5.93 us
    ppermute x8, starting transfers between devices, traded(): lax.ppermute(value, axis, [(i, i ^ k) for i in range(lax.axis_size(axis))])  4.62 us
    pallas_call x2, Pallas kernels, pack(): pl.pallas_call(functools.partial(pack_kernel, low, size, slots, tile), ou...  3.2 us
    pallas_call x1, Pallas kernels, mix(): pl.pallas_call(functools.partial(mix_kernel, places), out_shape=jax.Shape...  2.11 us
  transfers between devices with their start and end apart: 14, of which 3 were waited for; matrix products, arithmetic and copies ran while one was open for 1% of the time, Pallas kernels for 43%

profile of v13, /device:TPU:0, one launch (start us, length us, event | category | flops | bytes accessed | tf_op | source)
XLA Modules:
  0.0 91.7 jit_solution(2313318083953411050)
XLA Ops:
  0.0 1.7 %copy-done.1 = bf16[128,8192]{1,0:T(8,128)(2,1)S(1)} copy-done((bf16[128,8192]{1,0:T(8,128)(2,1)S(1)}, bf16[128,8192]{1,0:T(8,128)(2,1)}, u32[]{:S(2)}) %copy-start.1) | copy-done | bytes 2097176
  1.7 0.1 stage.1.panel
  1.9 0.5 copy-done.7
  2.4 11.7 %all_to_all.5.asked = s32[4,4,20]{2,1,0:T(4,128)S(1)} all-to-all(s32[4,4,20]{2,1,0:T(4,128)S(1)} %broadcast_in_dim.12), channel_id=1, replica_groups=mesh['parts'=2,'blk'=4,'grp'=4] {'blk'}, dimensions={0} | all-to-all | bytes 2560 | tf_op jit(solution)/shard_map/all_to_all | solution.py:352
  14.1 1.7 %pack.2 = (bf16[20,80,128]{2,1,0:T(8,128)(2,1)}, bf16[20,80,128]{2,1,0:T(8,128)(2,1)}, bf16[20,80,128]{2,1,0:T(8,128)(2,1)}) custom-call(s32[1]{0:T(128)} %bitcast.4.block, s32[4,4,20]{2,1,0:T(4,128)S(1)} %all_to_all.5.asked, bf16[128,8192]{1,0:T(8,128)(2,1)S(1)} %stage.1.panel), custom_call_target="tpu_custom_call" | custom-call | bytes 65536 | tf_op jit(solution)/shard_map/pack/pallas_call | solution.py:95
  15.8 0.7 collective-permute-start
  16.5 0.5 collective-permute-start.1
  17.0 2.7 %collective-permute-start.2 = (bf16[20,80,128]{2,1,0:T(8,128)(2,1)}, bf16[20,80,128]{2,1,0:T(8,128)(2,1)S(1)}, u32[]{:S(2)}, u32[]{:S(2)}) collective-permute-start(bf16[20,80,128]{2,1,0:T(8,128)(2,1)} %get-tuple-element.76), channel_id=1, source_target_pairs={{0,12},{4,0},{8,4},{12,8},{1,13},{5,1},{9,5},{13,9},{2,14},{6,2},{... | collective-permute-start | bytes 1228808 | tf_op jit(solution)/shard_map/ppermute | solution.py:48
  19.7 0.7 xor_multiply_fusion.starts
  20.4 1.6 %copy-done.2 = bf16[128,8192]{1,0:T(8,128)(2,1)S(1)} copy-done((bf16[128,8192]{1,0:T(8,128)(2,1)S(1)}, bf16[128,8192]{1,0:T(8,128)(2,1)}, u32[]{:S(2)}) %copy-start.2) | copy-done | bytes 2097176
  22.0 0.7 copy-done.6
  22.7 0.7 copy-done.8
  23.3 0.7 copy-done.9
  24.0 9.6 %own.1 = (f32[8192,80]{1,0:T(8,128)S(1)}, f32[8192,48]{1,0:T(8,128)S(1)}, f32[8192,80]{1,0:T(8,128)S(1)}, f32[512,128]{1,0:T(8,128)S(1)}, bf16[512,512]{1,0:T(8,128)(2,1)S(1)}) custom-call(s32[4,20]{1,0:T(4,128)S(1)} %bitcast.10, s32[4,20]{1,0:T(4,128)S(1)} %bitcast.16, s32[4]{0:T(128)S(1)} %xor_multiply_fusion.starts, bf16[128,8192]{1,0:T(8,128)(2,1)S(1)} %copy-done.2, ...), custom_call_target="tpu_custom_call" | custom-call | bytes 65536 | tf_op jit(solution)/shard_map/own/pallas_call | solution.py:33
  33.6 1.5 %pack.3 = (bf16[20,48,128]{2,1,0:T(8,128)(2,1)S(1)}, bf16[20,48,128]{2,1,0:T(8,128)(2,1)S(1)}, bf16[20,48,128]{2,1,0:T(8,128)(2,1)S(1)}) custom-call(s32[1]{0:T(128)} %bitcast.4.block, s32[4,4,20]{2,1,0:T(4,128)S(1)} %copy-done.5, bf16[128,8192]{1,0:T(8,128)(2,1)S(1)} %copy-done.2), custom_call_target="tpu_custom_call" | custom-call | bytes 65536 | tf_op jit(solution)/shard_map/pack/pallas_call | solution.py:95
  35.2 0.0 collective-permute-done.refs_0_
  35.2 10.3 %collective-permute-done.1.refs_1_ = bf16[20,80,128]{2,1,0:T(8,128)(2,1)} collective-permute-done((bf16[20,80,128]{2,1,0:T(8,128)(2,1)}, bf16[20,80,128]{2,1,0:T(8,128)(2,1)}, u32[]{:S(2)}, u32[]{:S(2)}) %collective-permute-start.1) | collective-permute-done | bytes 409632 | tf_op jit(solution)/shard_map/ppermute | solution.py:48
  45.5 2.9 %add_early.2.refs_2_ = f32[8192,80]{1,0:T(8,128)S(1)} custom-call(s32[4,20]{1,0:T(4,128)S(1)} %bitcast.11, f32[8192,80]{1,0:T(8,128)S(1)} %get-tuple-element.77.acc, f32[8192,80]{1,0:T(8,128)S(1)} %get-tuple-element.78.inverse.refs_3_.refs_2_, bf16[80,128,128]{2,1,0:T(8,128)(2,1)S(1)} %bitcast.6, bf16[20,80,128]{2,1,0:T(8,128)(2,1)} %collective-permute-done.refs_0_, ...), custom_call_target="tpu_custom_call" | custom-call | bytes 65536 | tf_op jit(solution)/shard_map/add_early/pallas_call | solution.py:33
  48.5 0.0 collective-permute-done.2.refs_5_
  48.5 5.8 %collective-permute-start.3 = (bf16[20,48,128]{2,1,0:T(8,128)(2,1)S(1)}, bf16[20,48,128]{2,1,0:T(8,128)(2,1)S(1)}, u32[]{:S(2)}, u32[]{:S(2)}) collective-permute-start(bf16[20,48,128]{2,1,0:T(8,128)(2,1)S(1)} %get-tuple-element.87), channel_id=1, source_target_pairs={{0,4},{4,8},{8,12},{12,0},{1,5},{5,9},{9,13},{13,1},{2,6},{6,10},{... | collective-permute-start | bytes 737288 | tf_op jit(solution)/shard_map/ppermute | solution.py:48
  54.2 3.4 %collective-permute-start.4 = (bf16[20,48,128]{2,1,0:T(8,128)(2,1)S(1)}, bf16[20,48,128]{2,1,0:T(8,128)(2,1)S(1)}, u32[]{:S(2)}, u32[]{:S(2)}) collective-permute-start(bf16[20,48,128]{2,1,0:T(8,128)(2,1)S(1)} %get-tuple-element.88), channel_id=1, source_target_pairs={{0,8},{4,12},{8,0},{12,4},{1,9},{5,13},{9,1},{13,5},{2,10},{6,14},... | collective-permute-start | bytes 737288 | tf_op jit(solution)/shard_map/ppermute | solution.py:48
  57.6 0.0 collective-permute-start.5
  57.6 6.0 %gather_far.2 = (f32[8192,80]{1,0:T(8,128)S(1)}, bf16[80,2048]{1,0:T(8,128)(2,1)S(1)}, bf16[80,2048]{1,0:T(8,128)(2,1)S(1)}) custom-call(s32[4,20]{1,0:T(4,128)S(1)} %bitcast.12, s32[2048]{0:T(1024)S(1)} %get-tuple-element.63.refs_0_, s32[2048]{0:T(1024)S(1)} %get-tuple-element.64.refs_1_.refs_0_, f32[8192,80]{1,0:T(8,128)S(1)} %add_early.2.refs_2_, ...), custom_call_target="tpu_custom_call" | custom-call | bytes 1048576 | tf_op jit(solution)/shard_map/gather_far/pallas_call | solution.py:33
  63.6 0.1 collective-permute-start.9
  63.7 1.6 %collective-permute-start.10 = (bf16[80,2048]{1,0:T(8,128)(2,1)S(1)}, bf16[80,2048]{1,0:T(8,128)(2,1)S(1)}, u32[]{:S(2)}, u32[]{:S(2)}) collective-permute-start(bf16[80,2048]{1,0:T(8,128)(2,1)S(1)} %get-tuple-element.98), channel_id=1, source_target_pairs={{0,2},{1,3},{2,0},{3,1},{4,6},{5,7},{6,4},{7,5},{8,10},{9,11},{10,... | collective-permute-start | bytes 983048 | tf_op jit(solution)/shard_map/ppermute | solution.py:52
  65.3 4.9 %gather_next.4 = (bf16[80,1024]{1,0:T(8,128)(2,1)S(1)}, bf16[80,1024]{1,0:T(8,128)(2,1)S(1)}, bf16[80,2048]{1,0:T(8,128)(2,1)S(1)}) custom-call(s32[2048]{0:T(1024)S(1)} %get-tuple-element.61.refs_0_, s32[2048]{0:T(1024)S(1)} %get-tuple-element.62.refs_1_.refs_0_, f32[8192,80]{1,0:T(8,128)S(1)} %get-tuple-element.82.refs_2_), custom_call_target="tpu_custom_call" | custom-call | bytes 65536 | tf_op jit(solution)/shard_map/gather_next/pallas_call | solution.py:33
  70.2 0.0 collective-permute-done.3.refs_0_
  70.2 1.3 %collective-permute-done.4.refs_1_ = bf16[20,48,128]{2,1,0:T(8,128)(2,1)S(1)} collective-permute-done((bf16[20,48,128]{2,1,0:T(8,128)(2,1)S(1)}, bf16[20,48,128]{2,1,0:T(8,128)(2,1)S(1)}, u32[]{:S(2)}, u32[]{:S(2)}) %collective-permute-start.4) | collective-permute-done | bytes 245792 | tf_op jit(solution)/shard_map/ppermute | solution.py:48
  71.6 2.3 %add_early.3.refs_1_ = f32[8192,48]{1,0:T(8,128)S(1)} custom-call(s32[4,20]{1,0:T(4,128)S(1)} %bitcast.13, f32[8192,48]{1,0:T(8,128)S(1)} %get-tuple-element.86.acc, f32[8192,80]{1,0:T(8,128)S(1)} %get-tuple-element.78.inverse.refs_3_.refs_2_, bf16[80,128,128]{2,1,0:T(8,128)(2,1)S(1)} %bitcast.8, bf16[20,48,128]{2,1,0:T(8,128)(2,1)S(1)} %collective-permute-done.3.refs_0_, ...), custom_call_target="tpu_custom_call" | custom-call | bytes 65536 | tf_op jit(solution)/shard_map/add_early/pallas_call | solution.py:33
  73.8 0.0 collective-permute-done.5.refs_4_
  73.8 0.1 collective-permute-start.6
  73.9 0.5 collective-permute-start.7
  74.4 3.7 %gather_far.3 = (f32[8192,48]{1,0:T(8,128)S(1)}, bf16[48,2048]{1,0:T(8,128)(2,1)S(1)}) custom-call(s32[4,20]{1,0:T(4,128)S(1)} %bitcast.14, s32[2048]{0:T(1024)S(1)} %get-tuple-element.63.refs_0_, f32[8192,48]{1,0:T(8,128)S(1)} %add_early.3.refs_1_, f32[8192,80]{1,0:T(8,128)S(1)} %get-tuple-element.78.inverse.refs_3_.refs_2_, ...), custom_call_target="tpu_custom_call" | custom-call | bytes 1048576 | tf_op jit(solution)/shard_map/gather_far/pallas_call | solution.py:33
  78.1 1.2 %collective-permute-start.13 = (bf16[48,2048]{1,0:T(8,128)(2,1)S(1)}, bf16[48,2048]{1,0:T(8,128)(2,1)S(1)}, u32[]{:S(2)}, u32[]{:S(2)}) collective-permute-start(bf16[48,2048]{1,0:T(8,128)(2,1)S(1)} %get-tuple-element.102), channel_id=1, source_target_pairs={{0,3},{1,2},{2,1},{3,0},{4,7},{5,6},{6,5},{7,4},{8,11},{9,10},{10,... | collective-permute-start | bytes 589832 | tf_op jit(solution)/shard_map/ppermute | solution.py:52
  79.4 0.0 collective-permute-done.6.refs_6_
  79.4 0.0 collective-permute-done.7.refs_7_
  79.4 2.7 %gather_next.5 = bf16[48,2048]{1,0:T(8,128)(2,1)S(1)} custom-call(s32[2048]{0:T(1024)S(1)} %get-tuple-element.64.refs_1_.refs_0_, f32[8192,48]{1,0:T(8,128)S(1)} %get-tuple-element.103.refs_1_), custom_call_target="tpu_custom_call" | custom-call | bytes 65536 | tf_op jit(solution)/shard_map/gather_next/pallas_call | solution.py:33
  82.1 0.6 collective-permute-start.8
  82.7 0.0 collective-permute-done.9.refs_8_
  82.7 2.7 %gather_next.6 = (bf16[48,1024]{1,0:T(8,128)(2,1)S(1)}, bf16[48,1024]{1,0:T(8,128)(2,1)S(1)}) custom-call(s32[2048]{0:T(1024)S(1)} %get-tuple-element.61.refs_0_, f32[8192,48]{1,0:T(8,128)S(1)} %get-tuple-element.103.refs_1_), custom_call_target="tpu_custom_call" | custom-call | bytes 65536 | tf_op jit(solution)/shard_map/gather_next/pallas_call | solution.py:33
  85.4 0.2 collective-permute-start.11
  85.7 0.3 collective-permute-start.12
  86.0 0.0 collective-permute-done.13.refs_5_
  86.0 2.7 %gather_next.7.refs_4_ = bf16[48,2048]{1,0:T(8,128)(2,1)S(1)} custom-call(s32[2048]{0:T(1024)S(1)} %get-tuple-element.62.refs_1_.refs_0_, f32[8192,48]{1,0:T(8,128)S(1)} %get-tuple-element.103.refs_1_), custom_call_target="tpu_custom_call" | custom-call | bytes 4194304 | tf_op jit(solution)/shard_map/gather_next/pallas_call | solution.py:33
  88.7 0.0 collective-permute-done.11.refs_2_
  88.8 0.0 collective-permute-done.12.refs_3_
  88.8 0.9 collective-permute-done.8.refs_1_
  89.6 2.1 %mix.1 = bf16[512,2048]{1,0:T(8,128)(2,1)} custom-call(bf16[512,512]{1,0:T(8,128)(2,1)S(1)} %get-tuple-element.57.weight, f32[512,128]{1,0:T(8,128)S(1)} %get-tuple-element.58.bias, bf16[80,2048]{1,0:T(8,128)(2,1)S(1)} %get-tuple-element.90.refs_0_, bf16[48,2048]{1,0:T(8,128)(2,1)S(1)} %collective-permute-done.8.refs_1_, ...), custom_call_target="tpu_custom_call" | custom-call | flops 1073741824 | bytes 5242880 | tf_op jit(solution)/shard_map/mix/pallas_call | solution.py:315
  (19 shorter events, 0.1 us)
Async XLA Ops:
  0.0 20.4 %copy-start = (bf16[1,4,20,128,128]{4,3,2,1,0:T(8,128)(2,1)S(1)}, bf16[1,4,20,128,128]{4,3,2,1,0:T(8,128)(2,1)}, u32[]{:S(2)}) copy-start(bf16[1,4,20,128,128]{4,3,2,1,0:T(8,128)(2,1)} %param.11) | copy-start | bytes 7864324
  0.0 1.7 %copy-start.1 = (bf16[128,8192]{1,0:T(8,128)(2,1)S(1)}, bf16[128,8192]{1,0:T(8,128)(2,1)}, u32[]{:S(2)}) copy-start(bf16[128,8192]{1,0:T(8,128)(2,1)} %panel.5) | copy-start | bytes 6291460
  1.7 0.7 copy-start.7
  1.7 18.6 %copy-start.3 = (bf16[512,512]{1,0:T(8,128)(2,1)S(1)}, bf16[512,512]{1,0:T(8,128)(2,1)}, u32[]{:S(2)}) copy-start(bf16[512,512]{1,0:T(8,128)(2,1)} %weight.1) | copy-start | bytes 1572868
  14.1 2.9 %copy-start.4 = (s32[4,4,20]{2,1,0:T(4,128)}, s32[4,4,20]{2,1,0:T(4,128)S(1)}, u32[]{:S(2)}) copy-start(s32[4,4,20]{2,1,0:T(4,128)S(1)} %all_to_all.5.asked) | copy-start | bytes 3844
  15.8 19.3 %collective-permute-start = (bf16[20,80,128]{2,1,0:T(8,128)(2,1)}, bf16[20,80,128]{2,1,0:T(8,128)(2,1)}, u32[]{:S(2)}, u32[]{:S(2)}) collective-permute-start(bf16[20,80,128]{2,1,0:T(8,128)(2,1)} %get-tuple-element.74), channel_id=1, source_target_pairs={{0,4},{4,8},{8,12},{12,0},{1,5},{5,9},{9,13},{13,1},{2,6},{6,10},{... | collective-permute-start | bytes 1228808 | tf_op jit(solution)/shard_map/ppermute | solution.py:48
  16.5 29.0 %collective-permute-start.1 = (bf16[20,80,128]{2,1,0:T(8,128)(2,1)}, bf16[20,80,128]{2,1,0:T(8,128)(2,1)}, u32[]{:S(2)}, u32[]{:S(2)}) collective-permute-start(bf16[20,80,128]{2,1,0:T(8,128)(2,1)} %get-tuple-element.75), channel_id=1, source_target_pairs={{0,8},{4,12},{8,0},{12,4},{1,9},{5,13},{9,1},{13,5},{2,10},{6,14},... | collective-permute-start | bytes 1228808 | tf_op jit(solution)/shard_map/ppermute | solution.py:48
  17.0 31.4 %collective-permute-start.2 = (bf16[20,80,128]{2,1,0:T(8,128)(2,1)}, bf16[20,80,128]{2,1,0:T(8,128)(2,1)S(1)}, u32[]{:S(2)}, u32[]{:S(2)}) collective-permute-start(bf16[20,80,128]{2,1,0:T(8,128)(2,1)} %get-tuple-element.76), channel_id=1, source_target_pairs={{0,12},{4,0},{8,4},{12,8},{1,13},{5,1},{9,5},{13,9},{2,14},{6,2},{... | collective-permute-start | bytes 1228808 | tf_op jit(solution)/shard_map/ppermute | solution.py:48
  20.4 1.6 %copy-start.2 = (bf16[128,8192]{1,0:T(8,128)(2,1)S(1)}, bf16[128,8192]{1,0:T(8,128)(2,1)}, u32[]{:S(2)}) copy-start(bf16[128,8192]{1,0:T(8,128)(2,1)} %panel.5) | copy-start | bytes 6291460
  22.0 0.7 copy-start.6
  22.6 0.7 copy-start.8
  23.3 0.7 copy-start.9
  24.0 9.6 %copy-start.10 = (s32[8192]{0:T(1024)S(1)}, s32[8192]{0:T(1024)}, u32[]{:S(2)}) copy-start(s32[8192]{0:T(1024)} %param.12) | copy-start | bytes 98308
  24.0 9.6 %copy-start.5 = (s32[4,4,20]{2,1,0:T(4,128)S(1)}, s32[4,4,20]{2,1,0:T(4,128)}, u32[]{:S(2)}) copy-start(s32[4,4,20]{2,1,0:T(4,128)} %copy-done.4) | copy-start | bytes 3844
  48.5 21.7 %collective-permute-start.3 = (bf16[20,48,128]{2,1,0:T(8,128)(2,1)S(1)}, bf16[20,48,128]{2,1,0:T(8,128)(2,1)S(1)}, u32[]{:S(2)}, u32[]{:S(2)}) collective-permute-start(bf16[20,48,128]{2,1,0:T(8,128)(2,1)S(1)} %get-tuple-element.87), channel_id=1, source_target_pairs={{0,4},{4,8},{8,12},{12,0},{1,5},{5,9},{9,13},{13,1},{2,6},{6,10},{... | collective-permute-start | bytes 737288 | tf_op jit(solution)/shard_map/ppermute | solution.py:48
  54.2 17.3 %collective-permute-start.4 = (bf16[20,48,128]{2,1,0:T(8,128)(2,1)S(1)}, bf16[20,48,128]{2,1,0:T(8,128)(2,1)S(1)}, u32[]{:S(2)}, u32[]{:S(2)}) collective-permute-start(bf16[20,48,128]{2,1,0:T(8,128)(2,1)S(1)} %get-tuple-element.88), channel_id=1, source_target_pairs={{0,8},{4,12},{8,0},{12,4},{1,9},{5,13},{9,1},{13,5},{2,10},{6,14},... | collective-permute-start | bytes 737288 | tf_op jit(solution)/shard_map/ppermute | solution.py:48
  57.6 16.2 %collective-permute-start.5 = (bf16[20,48,128]{2,1,0:T(8,128)(2,1)S(1)}, bf16[20,48,128]{2,1,0:T(8,128)(2,1)S(1)}, u32[]{:S(2)}, u32[]{:S(2)}) collective-permute-start(bf16[20,48,128]{2,1,0:T(8,128)(2,1)S(1)} %get-tuple-element.89), channel_id=1, source_target_pairs={{0,12},{4,0},{8,4},{12,8},{1,13},{5,1},{9,5},{13,9},{2,14},{6,2},{... | collective-permute-start | bytes 737288 | tf_op jit(solution)/shard_map/ppermute | solution.py:48
  63.6 19.1 %collective-permute-start.9 = (bf16[80,2048]{1,0:T(8,128)(2,1)S(1)}, bf16[80,2048]{1,0:T(8,128)(2,1)S(1)}, u32[]{:S(2)}, u32[]{:S(2)}) collective-permute-start(bf16[80,2048]{1,0:T(8,128)(2,1)S(1)} %get-tuple-element.97), channel_id=1, source_target_pairs={{0,3},{1,2},{2,1},{3,0},{4,7},{5,6},{6,5},{7,4},{8,11},{9,10},{10,... | collective-permute-start | bytes 983048 | tf_op jit(solution)/shard_map/ppermute | solution.py:52
  63.7 19.0 %collective-permute-start.10 = (bf16[80,2048]{1,0:T(8,128)(2,1)S(1)}, bf16[80,2048]{1,0:T(8,128)(2,1)S(1)}, u32[]{:S(2)}, u32[]{:S(2)}) collective-permute-start(bf16[80,2048]{1,0:T(8,128)(2,1)S(1)} %get-tuple-element.98), channel_id=1, source_target_pairs={{0,2},{1,3},{2,0},{3,1},{4,6},{5,7},{6,4},{7,5},{8,10},{9,11},{10,... | collective-permute-start | bytes 983048 | tf_op jit(solution)/shard_map/ppermute | solution.py:52
  73.8 5.6 %collective-permute-start.6 = (bf16[80,1024]{1,0:T(8,128)(2,1)S(1)}, bf16[80,1024]{1,0:T(8,128)(2,1)S(1)}, u32[]{:S(2)}, u32[]{:S(2)}) collective-permute-start(bf16[80,1024]{1,0:T(8,128)(2,1)S(1)} %get-tuple-element.94), channel_id=1, source_target_pairs={{0,1},{1,0},{2,3},{3,2},{4,5},{5,4},{6,7},{7,6},{8,9},{9,8},{10,11... | collective-permute-start | bytes 491528 | tf_op jit(solution)/shard_map/ppermute | solution.py:52
  73.9 5.5 %collective-permute-start.7 = (bf16[80,1024]{1,0:T(8,128)(2,1)S(1)}, bf16[80,1024]{1,0:T(8,128)(2,1)S(1)}, u32[]{:S(2)}, u32[]{:S(2)}) collective-permute-start(bf16[80,1024]{1,0:T(8,128)(2,1)S(1)} %get-tuple-element.95), channel_id=1, source_target_pairs={{0,1},{1,0},{2,3},{3,2},{4,5},{5,4},{6,7},{7,6},{8,9},{9,8},{10,11... | collective-permute-start | bytes 491528 | tf_op jit(solution)/shard_map/ppermute | solution.py:52
  78.1 7.9 %collective-permute-start.13 = (bf16[48,2048]{1,0:T(8,128)(2,1)S(1)}, bf16[48,2048]{1,0:T(8,128)(2,1)S(1)}, u32[]{:S(2)}, u32[]{:S(2)}) collective-permute-start(bf16[48,2048]{1,0:T(8,128)(2,1)S(1)} %get-tuple-element.102), channel_id=1, source_target_pairs={{0,3},{1,2},{2,1},{3,0},{4,7},{5,6},{6,5},{7,4},{8,11},{9,10},{10,... | collective-permute-start | bytes 589832 | tf_op jit(solution)/shard_map/ppermute | solution.py:52
  82.1 7.5 %collective-permute-start.8 = (bf16[48,2048]{1,0:T(8,128)(2,1)S(1)}, bf16[48,2048]{1,0:T(8,128)(2,1)S(1)}, u32[]{:S(2)}, u32[]{:S(2)}) collective-permute-start(bf16[48,2048]{1,0:T(8,128)(2,1)S(1)} %gather_next.5), channel_id=1, source_target_pairs={{0,2},{1,3},{2,0},{3,1},{4,6},{5,7},{6,4},{7,5},{8,10},{9,11},{10,... | collective-permute-start | bytes 589832 | tf_op jit(solution)/shard_map/ppermute | solution.py:52
  85.4 3.3 %collective-permute-start.11 = (bf16[48,1024]{1,0:T(8,128)(2,1)S(1)}, bf16[48,1024]{1,0:T(8,128)(2,1)S(1)}, u32[]{:S(2)}, u32[]{:S(2)}) collective-permute-start(bf16[48,1024]{1,0:T(8,128)(2,1)S(1)} %get-tuple-element.100), channel_id=1, source_target_pairs={{0,1},{1,0},{2,3},{3,2},{4,5},{5,4},{6,7},{7,6},{8,9},{9,8},{10,11... | collective-permute-start | bytes 294920 | tf_op jit(solution)/shard_map/ppermute | solution.py:52
  85.7 3.1 %collective-permute-start.12 = (bf16[48,1024]{1,0:T(8,128)(2,1)S(1)}, bf16[48,1024]{1,0:T(8,128)(2,1)S(1)}, u32[]{:S(2)}, u32[]{:S(2)}) collective-permute-start(bf16[48,1024]{1,0:T(8,128)(2,1)S(1)} %get-tuple-element.101), channel_id=1, source_target_pairs={{0,1},{1,0},{2,3},{3,2},{4,5},{5,4},{6,7},{7,6},{8,9},{9,8},{10,11... | collective-permute-start | bytes 294920 | tf_op jit(solution)/shard_map/ppermute | solution.py:52

commit v14 on v9

--- a/solution.py
+++ b/solution.py
@@ -364,13 +364,13 @@
                 (leaving, got[-1], early[-1], accs)
             )
         got.append([shifted(value, "blk", s + 1) for s, value in enumerate(leaving)])
-        early.append(add_early(accs[p], inverse, rows, counts, got[p][:-1], 1))
+        early.append(add_early(accs[p], inverse, rows, counts, got[p][:1], 1))
 
     pieces, across_x, beside = {}, {}, {}
     for p, (low, size) in enumerate(ranges[:-1]):
         at = [groups * low + i * size for i in range(groups)]
         total, out_far = gather_far(
-            early[p], inverse, rows, picks[:far], counts, got[p][-1:], blocks - 1
+            early[p], inverse, rows, picks[:far], counts, got[p][1:], 2
         )
         for i, piece in enumerate(out_far):
             across_x[at[i], 0] = traded(piece, "grp", ranks[i])
@@ -386,7 +386,7 @@
     low, size = ranges[-1]
     at = [groups * low + i * size for i in range(groups)]
     total, (piece,) = gather_far(
-        early[-1], inverse, rows, picks[:1], counts, got[-1][-1:], blocks - 1
+        early[-1], inverse, rows, picks[:1], counts, got[-1][1:], 2
     )
     first = traded(piece, "grp", ranks[0])
     for i in range(1, groups):

time: 88.7 us -> 92.2 us (1.039)
  the two profiles are of different devices: /device:TPU:27 before, /device:TPU:0 now
where the time goes in v14:
time: 92.2 us; the launch traced here: 91.9 us
  Pallas kernels  42.6 us (46%)
  starting transfers between devices  32.1 us (35%)
  waiting for transfers between devices  11.1 us (12%)
  local copies, waits for them, and re-layouts  5.28 us (6%)
    pallas_call x10, Pallas kernels, call(): pl.pallas_call(kernel, out_shape=list(outs), in_specs=[SMEM] * len(scalar...  37.4 us
    ppermute x9, starting transfers between devices, shifted(): return lax.ppermute(value, axis, pairs)  27.2 us
    ppermute x9, waiting for transfers between devices, shifted(): return lax.ppermute(value, axis, pairs)  9.55 us
    unnamed x28, local copies, waits for them, and re-layouts  5.26 us
    ppermute x8, starting transfers between devices, traded(): lax.ppermute(value, axis, [(i, i ^ k) for i in range(lax.axis_size(axis))])  4.82 us
    pallas_call x2, Pallas kernels, pack(): pl.pallas_call(functools.partial(pack_kernel, low, size, offsets, slots,...  3.06 us
    pallas_call x1, Pallas kernels, mix(): pl.pallas_call(functools.partial(mix_kernel, places), out_shape=jax.Shape...  2.11 us
  transfers between devices with their start and end apart: 17, of which 3 were waited for; matrix products, arithmetic and copies ran while one was open for 1% of the time, Pallas kernels for 42%

profile of v14, /device:TPU:0, one launch (start us, length us, event | category | flops | bytes accessed | tf_op | source)
XLA Modules:
  0.0 91.9 jit_solution(9619672458957155065)
XLA Ops:
  0.0 3.0 %collective-permute-start.2 = (s32[4,20]{1,0:T(4,128)}, s32[4,20]{1,0:T(4,128)S(1)}, u32[]{:S(2)}, u32[]{:S(2)}) collective-permute-start(s32[4,20]{1,0:T(4,128)} %bitcast.14), channel_id=1, source_target_pairs={{0,4},{4,8},{8,12},{12,0},{1,5},{5,9},{9,13},{13,1},{2,6},{6,10},{... | collective-permute-start | bytes 968 | tf_op jit(solution)/shard_map/ppermute | solution.py:48
  3.0 2.6 %collective-permute-start.1 = (s32[4,20]{1,0:T(4,128)}, s32[4,20]{1,0:T(4,128)S(1)}, u32[]{:S(2)}, u32[]{:S(2)}) collective-permute-start(s32[4,20]{1,0:T(4,128)} %bitcast.15), channel_id=1, source_target_pairs={{0,8},{4,12},{8,0},{12,4},{1,9},{5,13},{9,1},{13,5},{2,10},{6,14},... | collective-permute-start | bytes 968 | tf_op jit(solution)/shard_map/ppermute | solution.py:48
  5.6 1.3 %collective-permute-start = (s32[4,20]{1,0:T(4,128)}, s32[4,20]{1,0:T(4,128)S(1)}, u32[]{:S(2)}, u32[]{:S(2)}) collective-permute-start(s32[4,20]{1,0:T(4,128)} %bitcast.16), channel_id=1, source_target_pairs={{0,12},{4,0},{8,4},{12,8},{1,13},{5,1},{9,5},{13,9},{2,14},{6,2},{... | collective-permute-start | bytes 968 | tf_op jit(solution)/shard_map/ppermute | solution.py:48
  7.0 1.6 %copy-done.1 = bf16[128,8192]{1,0:T(8,128)(2,1)S(1)} copy-done((bf16[128,8192]{1,0:T(8,128)(2,1)S(1)}, bf16[128,8192]{1,0:T(8,128)(2,1)}, u32[]{:S(2)}) %copy-start.1) | copy-done | bytes 2097176
  8.6 0.1 stage.1.refs_3_
  8.7 0.0 collective-permute-done.2.refs_2_
  8.7 0.0 collective-permute-done.1.refs_1_
  8.7 0.7 collective-permute-done.refs_0_
  9.4 1.6 %pack.2 = (bf16[20,80,128]{2,1,0:T(8,128)(2,1)}, bf16[20,80,128]{2,1,0:T(8,128)(2,1)}, bf16[20,80,128]{2,1,0:T(8,128)(2,1)}) custom-call(s32[4,20]{1,0:T(4,128)S(1)} %collective-permute-done.refs_0_, s32[4,20]{1,0:T(4,128)S(1)} %collective-permute-done.1.refs_1_, s32[4,20]{1,0:T(4,128)S(1)} %collective-permute-done.2.refs_2_, bf16[128,8192]{1,0:T(8,128)(2,1)S(1)} %stage.1.refs_3_), custom_call_target="tpu_custom_call" | custom-call | bytes 65536 | tf_op jit(solution)/shard_map/pack/pallas_call | solution.py:94
  11.1 0.1 collective-permute-start.3
  11.2 3.6 %collective-permute-start.4 = (bf16[20,80,128]{2,1,0:T(8,128)(2,1)}, bf16[20,80,128]{2,1,0:T(8,128)(2,1)}, u32[]{:S(2)}, u32[]{:S(2)}) collective-permute-start(bf16[20,80,128]{2,1,0:T(8,128)(2,1)} %get-tuple-element.83), channel_id=1, source_target_pairs={{0,8},{4,12},{8,0},{12,4},{1,9},{5,13},{9,1},{13,5},{2,10},{6,14},... | collective-permute-start | bytes 1228808 | tf_op jit(solution)/shard_map/ppermute | solution.py:48
  14.8 0.1 collective-permute-start.5
  15.0 0.7 xor_multiply_fusion.starts
  15.6 1.6 %copy-done.2 = bf16[128,8192]{1,0:T(8,128)(2,1)S(1)} copy-done((bf16[128,8192]{1,0:T(8,128)(2,1)S(1)}, bf16[128,8192]{1,0:T(8,128)(2,1)}, u32[]{:S(2)}) %copy-start.2) | copy-done | bytes 2097176
  17.2 0.7 copy-done.4
  17.9 0.7 copy-done.11
  18.6 0.7 copy-done.12
  19.3 9.5 %own.1 = (f32[8192,80]{1,0:T(8,128)S(1)}, f32[8192,48]{1,0:T(8,128)S(1)}, f32[8192,80]{1,0:T(8,128)S(1)}, f32[512,128]{1,0:T(8,128)S(1)}, bf16[512,512]{1,0:T(8,128)(2,1)S(1)}) custom-call(s32[4,20]{1,0:T(4,128)S(1)} %bitcast.9, s32[4,20]{1,0:T(4,128)S(1)} %bitcast.17, s32[4]{0:T(128)S(1)} %xor_multiply_fusion.starts, bf16[128,8192]{1,0:T(8,128)(2,1)S(1)} %copy-done.2, ...), custom_call_target="tpu_custom_call" | custom-call | bytes 65536 | tf_op jit(solution)/shard_map/own/pallas_call | solution.py:33
  28.9 1.4 %pack.3 = (bf16[20,48,128]{2,1,0:T(8,128)(2,1)S(1)}, bf16[20,48,128]{2,1,0:T(8,128)(2,1)S(1)}, bf16[20,48,128]{2,1,0:T(8,128)(2,1)S(1)}) custom-call(s32[4,20]{1,0:T(4,128)S(1)} %copy-done.10, s32[4,20]{1,0:T(4,128)S(1)} %copy-done.8, s32[4,20]{1,0:T(4,128)S(1)} %copy-done.6, bf16[128,8192]{1,0:T(8,128)(2,1)S(1)} %copy-done.2), custom_call_target="tpu_custom_call" | custom-call | bytes 65536 | tf_op jit(solution)/shard_map/pack/pallas_call | solution.py:94
  30.3 0.0 collective-permute-done.3.refs_0_
  30.3 1.6 %add_early.2.refs_2_ = f32[8192,80]{1,0:T(8,128)S(1)} custom-call(s32[4,20]{1,0:T(4,128)S(1)} %bitcast.10, f32[8192,80]{1,0:T(8,128)S(1)} %get-tuple-element.85.acc, f32[8192,80]{1,0:T(8,128)S(1)} %get-tuple-element.86.inverse.refs_3_.refs_2_, bf16[80,128,128]{2,1,0:T(8,128)(2,1)S(1)} %bitcast.5, bf16[20,80,128]{2,1,0:T(8,128)(2,1)S(1)} %collective-permute-done.3.refs_0_), custom_call_target="tpu_custom_call" | custom-call | bytes 65536 | tf_op jit(solution)/shard_map/add_early/pallas_call | solution.py:33
  31.9 8.9 %collective-permute-done.4.refs_5_ = bf16[20,80,128]{2,1,0:T(8,128)(2,1)} collective-permute-done((bf16[20,80,128]{2,1,0:T(8,128)(2,1)}, bf16[20,80,128]{2,1,0:T(8,128)(2,1)}, u32[]{:S(2)}, u32[]{:S(2)}) %collective-permute-start.4) | collective-permute-done | bytes 409632 | tf_op jit(solution)/shard_map/ppermute | solution.py:48
  40.8 0.0 collective-permute-done.5.refs_6_
  40.8 14.0 %collective-permute-start.6 = (bf16[20,48,128]{2,1,0:T(8,128)(2,1)S(1)}, bf16[20,48,128]{2,1,0:T(8,128)(2,1)S(1)}, u32[]{:S(2)}, u32[]{:S(2)}) collective-permute-start(bf16[20,48,128]{2,1,0:T(8,128)(2,1)S(1)} %get-tuple-element.96), channel_id=1, source_target_pairs={{0,4},{4,8},{8,12},{12,0},{1,5},{5,9},{9,13},{13,1},{2,6},{6,10},{... | collective-permute-start | bytes 737288 | tf_op jit(solution)/shard_map/ppermute | solution.py:48
  54.8 0.0 collective-permute-start.7
  54.8 2.4 %collective-permute-start.8 = (bf16[20,48,128]{2,1,0:T(8,128)(2,1)S(1)}, bf16[20,48,128]{2,1,0:T(8,128)(2,1)S(1)}, u32[]{:S(2)}, u32[]{:S(2)}) collective-permute-start(bf16[20,48,128]{2,1,0:T(8,128)(2,1)S(1)} %get-tuple-element.98), channel_id=1, source_target_pairs={{0,12},{4,0},{8,4},{12,8},{1,13},{5,1},{9,5},{13,9},{2,14},{6,2},{... | collective-permute-start | bytes 737288 | tf_op jit(solution)/shard_map/ppermute | solution.py:48
  57.2 7.1 %gather_far.2 = (f32[8192,80]{1,0:T(8,128)S(1)}, bf16[80,2048]{1,0:T(8,128)(2,1)S(1)}, bf16[80,2048]{1,0:T(8,128)(2,1)S(1)}) custom-call(s32[4,20]{1,0:T(4,128)S(1)} %bitcast.11, s32[2048]{0:T(1024)S(1)} %get-tuple-element.68.refs_0_, s32[2048]{0:T(1024)S(1)} %get-tuple-element.69.refs_1_.refs_0_, f32[8192,80]{1,0:T(8,128)S(1)} %add_early.2.refs_2_, ...), custom_call_target="tpu_custom_call" | custom-call | bytes 1048576 | tf_op jit(solution)/shard_map/gather_far/pallas_call | solution.py:33
  64.3 0.1 collective-permute-start.12
  64.4 1.6 %collective-permute-start.13 = (bf16[80,2048]{1,0:T(8,128)(2,1)S(1)}, bf16[80,2048]{1,0:T(8,128)(2,1)S(1)}, u32[]{:S(2)}, u32[]{:S(2)}) collective-permute-start(bf16[80,2048]{1,0:T(8,128)(2,1)S(1)} %get-tuple-element.108), channel_id=1, source_target_pairs={{0,2},{1,3},{2,0},{3,1},{4,6},{5,7},{6,4},{7,5},{8,10},{9,11},{10,... | collective-permute-start | bytes 983048 | tf_op jit(solution)/shard_map/ppermute | solution.py:52
  65.9 4.9 %gather_next.4 = (bf16[80,1024]{1,0:T(8,128)(2,1)S(1)}, bf16[80,1024]{1,0:T(8,128)(2,1)S(1)}, bf16[80,2048]{1,0:T(8,128)(2,1)S(1)}) custom-call(s32[2048]{0:T(1024)S(1)} %get-tuple-element.66.refs_0_, s32[2048]{0:T(1024)S(1)} %get-tuple-element.67.refs_1_.refs_0_, f32[8192,80]{1,0:T(8,128)S(1)} %get-tuple-element.91.refs_2_), custom_call_target="tpu_custom_call" | custom-call | bytes 65536 | tf_op jit(solution)/shard_map/gather_next/pallas_call | solution.py:33
  70.9 0.0 collective-permute-done.6.refs_0_
  70.9 1.6 %add_early.3.refs_1_ = f32[8192,48]{1,0:T(8,128)S(1)} custom-call(s32[4,20]{1,0:T(4,128)S(1)} %bitcast.12, f32[8192,48]{1,0:T(8,128)S(1)} %get-tuple-element.95.acc, f32[8192,80]{1,0:T(8,128)S(1)} %get-tuple-element.86.inverse.refs_3_.refs_2_, bf16[80,128,128]{2,1,0:T(8,128)(2,1)S(1)} %bitcast.7, bf16[20,48,128]{2,1,0:T(8,128)(2,1)S(1)} %collective-permute-done.6.refs_0_), custom_call_target="tpu_custom_call" | custom-call | bytes 65536 | tf_op jit(solution)/shard_map/add_early/pallas_call | solution.py:33
  72.4 0.0 collective-permute-done.7.refs_4_
  72.4 0.0 collective-permute-done.8.refs_5_
  72.5 0.3 collective-permute-start.9
  72.8 0.2 collective-permute-start.10
  73.0 4.4 %gather_far.3 = (f32[8192,48]{1,0:T(8,128)S(1)}, bf16[48,2048]{1,0:T(8,128)(2,1)S(1)}) custom-call(s32[4,20]{1,0:T(4,128)S(1)} %bitcast.13, s32[2048]{0:T(1024)S(1)} %get-tuple-element.68.refs_0_, f32[8192,48]{1,0:T(8,128)S(1)} %add_early.3.refs_1_, f32[8192,80]{1,0:T(8,128)S(1)} %get-tuple-element.86.inverse.refs_3_.refs_2_, ...), custom_call_target="tpu_custom_call" | custom-call | bytes 1048576 | tf_op jit(solution)/shard_map/gather_far/pallas_call | solution.py:33
  77.5 1.4 %collective-permute-start.16 = (bf16[48,2048]{1,0:T(8,128)(2,1)S(1)}, bf16[48,2048]{1,0:T(8,128)(2,1)S(1)}, u32[]{:S(2)}, u32[]{:S(2)}) collective-permute-start(bf16[48,2048]{1,0:T(8,128)(2,1)S(1)} %get-tuple-element.112), channel_id=1, source_target_pairs={{0,3},{1,2},{2,1},{3,0},{4,7},{5,6},{6,5},{7,4},{8,11},{9,10},{10,... | collective-permute-start | bytes 589832 | tf_op jit(solution)/shard_map/ppermute | solution.py:52
  78.9 2.7 %gather_next.5 = bf16[48,2048]{1,0:T(8,128)(2,1)S(1)} custom-call(s32[2048]{0:T(1024)S(1)} %get-tuple-element.69.refs_1_.refs_0_, f32[8192,48]{1,0:T(8,128)S(1)} %get-tuple-element.113.refs_1_), custom_call_target="tpu_custom_call" | custom-call | bytes 65536 | tf_op jit(solution)/shard_map/gather_next/pallas_call | solution.py:33
  81.7 0.6 collective-permute-start.11
  82.3 2.7 %gather_next.6 = (bf16[48,1024]{1,0:T(8,128)(2,1)S(1)}, bf16[48,1024]{1,0:T(8,128)(2,1)S(1)}) custom-call(s32[2048]{0:T(1024)S(1)} %get-tuple-element.66.refs_0_, f32[8192,48]{1,0:T(8,128)S(1)} %get-tuple-element.113.refs_1_), custom_call_target="tpu_custom_call" | custom-call | bytes 65536 | tf_op jit(solution)/shard_map/gather_next/pallas_call | solution.py:33
  85.0 0.1 collective-permute-start.14
  85.1 0.5 collective-permute-start.15
  85.6 0.0 collective-permute-done.16.refs_5_
  85.6 2.7 %gather_next.7.refs_4_ = bf16[48,2048]{1,0:T(8,128)(2,1)S(1)} custom-call(s32[2048]{0:T(1024)S(1)} %get-tuple-element.67.refs_1_.refs_0_, f32[8192,48]{1,0:T(8,128)S(1)} %get-tuple-element.113.refs_1_), custom_call_target="tpu_custom_call" | custom-call | bytes 4194304 | tf_op jit(solution)/shard_map/gather_next/pallas_call | solution.py:33
  88.3 0.0 collective-permute-done.15.refs_3_
  88.3 1.5 %collective-permute-done.11.refs_1_ = bf16[48,2048]{1,0:T(8,128)(2,1)S(1)} collective-permute-done((bf16[48,2048]{1,0:T(8,128)(2,1)S(1)}, bf16[48,2048]{1,0:T(8,128)(2,1)S(1)}, u32[]{:S(2)}, u32[]{:S(2)}) %collective-permute-start.11) | collective-permute-done | bytes 196640 | tf_op jit(solution)/shard_map/ppermute | solution.py:52
  89.8 2.1 %mix.1 = bf16[512,2048]{1,0:T(8,128)(2,1)} custom-call(bf16[512,512]{1,0:T(8,128)(2,1)S(1)} %get-tuple-element.62.weight, f32[512,128]{1,0:T(8,128)S(1)} %get-tuple-element.63.bias, bf16[80,2048]{1,0:T(8,128)(2,1)S(1)} %get-tuple-element.99.refs_0_, bf16[48,2048]{1,0:T(8,128)(2,1)S(1)} %collective-permute-done.11.refs_1_, ...), custom_call_target="tpu_custom_call" | custom-call | flops 1073741824 | bytes 5242880 | tf_op jit(solution)/shard_map/mix/pallas_call | solution.py:314
  (29 shorter events, 0.1 us)
Async XLA Ops:
  0.0 15.6 %copy-start = (bf16[1,4,20,128,128]{4,3,2,1,0:T(8,128)(2,1)S(1)}, bf16[1,4,20,128,128]{4,3,2,1,0:T(8,128)(2,1)}, u32[]{:S(2)}) copy-start(bf16[1,4,20,128,128]{4,3,2,1,0:T(8,128)(2,1)} %param.11) | copy-start | bytes 7864324
  0.0 8.7 %collective-permute-start.2 = (s32[4,20]{1,0:T(4,128)}, s32[4,20]{1,0:T(4,128)S(1)}, u32[]{:S(2)}, u32[]{:S(2)}) collective-permute-start(s32[4,20]{1,0:T(4,128)} %bitcast.14), channel_id=1, source_target_pairs={{0,4},{4,8},{8,12},{12,0},{1,5},{5,9},{9,13},{13,1},{2,6},{6,10},{... | collective-permute-start | bytes 968 | tf_op jit(solution)/shard_map/ppermute | solution.py:48
  3.0 5.7 %collective-permute-start.1 = (s32[4,20]{1,0:T(4,128)}, s32[4,20]{1,0:T(4,128)S(1)}, u32[]{:S(2)}, u32[]{:S(2)}) collective-permute-start(s32[4,20]{1,0:T(4,128)} %bitcast.15), channel_id=1, source_target_pairs={{0,8},{4,12},{8,0},{12,4},{1,9},{5,13},{9,1},{13,5},{2,10},{6,14},... | collective-permute-start | bytes 968 | tf_op jit(solution)/shard_map/ppermute | solution.py:48
  5.6 3.8 %collective-permute-start = (s32[4,20]{1,0:T(4,128)}, s32[4,20]{1,0:T(4,128)S(1)}, u32[]{:S(2)}, u32[]{:S(2)}) collective-permute-start(s32[4,20]{1,0:T(4,128)} %bitcast.16), channel_id=1, source_target_pairs={{0,12},{4,0},{8,4},{12,8},{1,13},{5,1},{9,5},{13,9},{2,14},{6,2},{... | collective-permute-start | bytes 968 | tf_op jit(solution)/shard_map/ppermute | solution.py:48
  7.0 1.6 %copy-start.1 = (bf16[128,8192]{1,0:T(8,128)(2,1)S(1)}, bf16[128,8192]{1,0:T(8,128)(2,1)}, u32[]{:S(2)}) copy-start(bf16[128,8192]{1,0:T(8,128)(2,1)} %refs_3_.1) | copy-start | bytes 6291460
  8.6 7.1 %copy-start.3 = (bf16[512,512]{1,0:T(8,128)(2,1)S(1)}, bf16[512,512]{1,0:T(8,128)(2,1)}, u32[]{:S(2)}) copy-start(bf16[512,512]{1,0:T(8,128)(2,1)} %weight.1) | copy-start | bytes 1572868
  8.7 2.4 %copy-start.5 = (s32[4,20]{1,0:T(4,128)}, s32[4,20]{1,0:T(4,128)S(1)}, u32[]{:S(2)}) copy-start(s32[4,20]{1,0:T(4,128)S(1)} %collective-permute-done.2.refs_2_) | copy-start | bytes 964
  8.7 2.3 %copy-start.7 = (s32[4,20]{1,0:T(4,128)}, s32[4,20]{1,0:T(4,128)S(1)}, u32[]{:S(2)}) copy-start(s32[4,20]{1,0:T(4,128)S(1)} %collective-permute-done.1.refs_1_) | copy-start | bytes 964
  9.4 1.8 %copy-start.9 = (s32[4,20]{1,0:T(4,128)}, s32[4,20]{1,0:T(4,128)S(1)}, u32[]{:S(2)}) copy-start(s32[4,20]{1,0:T(4,128)S(1)} %collective-permute-done.refs_0_) | copy-start | bytes 964
  11.1 19.3 %collective-permute-start.3 = (bf16[20,80,128]{2,1,0:T(8,128)(2,1)}, bf16[20,80,128]{2,1,0:T(8,128)(2,1)S(1)}, u32[]{:S(2)}, u32[]{:S(2)}) collective-permute-start(bf16[20,80,128]{2,1,0:T(8,128)(2,1)} %get-tuple-element.82), channel_id=1, source_target_pairs={{0,4},{4,8},{8,12},{12,0},{1,5},{5,9},{9,13},{13,1},{2,6},{6,10},{... | collective-permute-start | bytes 1228808 | tf_op jit(solution)/shard_map/ppermute | solution.py:48
  11.2 29.6 %collective-permute-start.4 = (bf16[20,80,128]{2,1,0:T(8,128)(2,1)}, bf16[20,80,128]{2,1,0:T(8,128)(2,1)}, u32[]{:S(2)}, u32[]{:S(2)}) collective-permute-start(bf16[20,80,128]{2,1,0:T(8,128)(2,1)} %get-tuple-element.83), channel_id=1, source_target_pairs={{0,8},{4,12},{8,0},{12,4},{1,9},{5,13},{9,1},{13,5},{2,10},{6,14},... | collective-permute-start | bytes 1228808 | tf_op jit(solution)/shard_map/ppermute | solution.py:48
  14.8 26.0 %collective-permute-start.5 = (bf16[20,80,128]{2,1,0:T(8,128)(2,1)}, bf16[20,80,128]{2,1,0:T(8,128)(2,1)}, u32[]{:S(2)}, u32[]{:S(2)}) collective-permute-start(bf16[20,80,128]{2,1,0:T(8,128)(2,1)} %get-tuple-element.84), channel_id=1, source_target_pairs={{0,12},{4,0},{8,4},{12,8},{1,13},{5,1},{9,5},{13,9},{2,14},{6,2},{... | collective-permute-start | bytes 1228808 | tf_op jit(solution)/shard_map/ppermute | solution.py:48
  15.0 13.9 %copy-start.6 = (s32[4,20]{1,0:T(4,128)S(1)}, s32[4,20]{1,0:T(4,128)}, u32[]{:S(2)}) copy-start(s32[4,20]{1,0:T(4,128)} %copy-done.5) | copy-start | bytes 964
  15.0 13.9 %copy-start.8 = (s32[4,20]{1,0:T(4,128)S(1)}, s32[4,20]{1,0:T(4,128)}, u32[]{:S(2)}) copy-start(s32[4,20]{1,0:T(4,128)} %copy-done.7) | copy-start | bytes 964
  15.0 13.9 %copy-start.10 = (s32[4,20]{1,0:T(4,128)S(1)}, s32[4,20]{1,0:T(4,128)}, u32[]{:S(2)}) copy-start(s32[4,20]{1,0:T(4,128)} %copy-done.9) | copy-start | bytes 964
  15.6 1.6 %copy-start.2 = (bf16[128,8192]{1,0:T(8,128)(2,1)S(1)}, bf16[128,8192]{1,0:T(8,128)(2,1)}, u32[]{:S(2)}) copy-start(bf16[128,8192]{1,0:T(8,128)(2,1)} %refs_3_.1) | copy-start | bytes 6291460
  17.2 0.7 copy-start.4
  17.9 0.7 copy-start.11
  18.6 0.7 copy-start.12
  19.3 9.6 %copy-start.13 = (s32[8192]{0:T(1024)S(1)}, s32[8192]{0:T(1024)}, u32[]{:S(2)}) copy-start(s32[8192]{0:T(1024)} %param.12) | copy-start | bytes 98308
  40.8 30.1 %collective-permute-start.6 = (bf16[20,48,128]{2,1,0:T(8,128)(2,1)S(1)}, bf16[20,48,128]{2,1,0:T(8,128)(2,1)S(1)}, u32[]{:S(2)}, u32[]{:S(2)}) collective-permute-start(bf16[20,48,128]{2,1,0:T(8,128)(2,1)S(1)} %get-tuple-element.96), channel_id=1, source_target_pairs={{0,4},{4,8},{8,12},{12,0},{1,5},{5,9},{9,13},{13,1},{2,6},{6,10},{... | collective-permute-start | bytes 737288 | tf_op jit(solution)/shard_map/ppermute | solution.py:48
  54.8 17.6 %collective-permute-start.7 = (bf16[20,48,128]{2,1,0:T(8,128)(2,1)S(1)}, bf16[20,48,128]{2,1,0:T(8,128)(2,1)S(1)}, u32[]{:S(2)}, u32[]{:S(2)}) collective-permute-start(bf16[20,48,128]{2,1,0:T(8,128)(2,1)S(1)} %get-tuple-element.97), channel_id=1, source_target_pairs={{0,8},{4,12},{8,0},{12,4},{1,9},{5,13},{9,1},{13,5},{2,10},{6,14},... | collective-permute-start | bytes 737288 | tf_op jit(solution)/shard_map/ppermute | solution.py:48
  54.8 17.6 %collective-permute-start.8 = (bf16[20,48,128]{2,1,0:T(8,128)(2,1)S(1)}, bf16[20,48,128]{2,1,0:T(8,128)(2,1)S(1)}, u32[]{:S(2)}, u32[]{:S(2)}) collective-permute-start(bf16[20,48,128]{2,1,0:T(8,128)(2,1)S(1)} %get-tuple-element.98), channel_id=1, source_target_pairs={{0,12},{4,0},{8,4},{12,8},{1,13},{5,1},{9,5},{13,9},{2,14},{6,2},{... | collective-permute-start | bytes 737288 | tf_op jit(solution)/shard_map/ppermute | solution.py:48
  64.3 18.0 %collective-permute-start.12 = (bf16[80,2048]{1,0:T(8,128)(2,1)S(1)}, bf16[80,2048]{1,0:T(8,128)(2,1)S(1)}, u32[]{:S(2)}, u32[]{:S(2)}) collective-permute-start(bf16[80,2048]{1,0:T(8,128)(2,1)S(1)} %get-tuple-element.107), channel_id=1, source_target_pairs={{0,3},{1,2},{2,1},{3,0},{4,7},{5,6},{6,5},{7,4},{8,11},{9,10},{10,... | collective-permute-start | bytes 983048 | tf_op jit(solution)/shard_map/ppermute | solution.py:52
  64.4 17.9 %collective-permute-start.13 = (bf16[80,2048]{1,0:T(8,128)(2,1)S(1)}, bf16[80,2048]{1,0:T(8,128)(2,1)S(1)}, u32[]{:S(2)}, u32[]{:S(2)}) collective-permute-start(bf16[80,2048]{1,0:T(8,128)(2,1)S(1)} %get-tuple-element.108), channel_id=1, source_target_pairs={{0,2},{1,3},{2,0},{3,1},{4,6},{5,7},{6,4},{7,5},{8,10},{9,11},{10,... | collective-permute-start | bytes 983048 | tf_op jit(solution)/shard_map/ppermute | solution.py:52
  72.5 6.5 %collective-permute-start.9 = (bf16[80,1024]{1,0:T(8,128)(2,1)S(1)}, bf16[80,1024]{1,0:T(8,128)(2,1)S(1)}, u32[]{:S(2)}, u32[]{:S(2)}) collective-permute-start(bf16[80,1024]{1,0:T(8,128)(2,1)S(1)} %get-tuple-element.104), channel_id=1, source_target_pairs={{0,1},{1,0},{2,3},{3,2},{4,5},{5,4},{6,7},{7,6},{8,9},{9,8},{10,11... | collective-permute-start | bytes 491528 | tf_op jit(solution)/shard_map/ppermute | solution.py:52
  72.8 6.1 %collective-permute-start.10 = (bf16[80,1024]{1,0:T(8,128)(2,1)S(1)}, bf16[80,1024]{1,0:T(8,128)(2,1)S(1)}, u32[]{:S(2)}, u32[]{:S(2)}) collective-permute-start(bf16[80,1024]{1,0:T(8,128)(2,1)S(1)} %get-tuple-element.105), channel_id=1, source_target_pairs={{0,1},{1,0},{2,3},{3,2},{4,5},{5,4},{6,7},{7,6},{8,9},{9,8},{10,11... | collective-permute-start | bytes 491528 | tf_op jit(solution)/shard_map/ppermute | solution.py:52
  77.5 8.1 %collective-permute-start.16 = (bf16[48,2048]{1,0:T(8,128)(2,1)S(1)}, bf16[48,2048]{1,0:T(8,128)(2,1)S(1)}, u32[]{:S(2)}, u32[]{:S(2)}) collective-permute-start(bf16[48,2048]{1,0:T(8,128)(2,1)S(1)} %get-tuple-element.112), channel_id=1, source_target_pairs={{0,3},{1,2},{2,1},{3,0},{4,7},{5,6},{6,5},{7,4},{8,11},{9,10},{10,... | collective-permute-start | bytes 589832 | tf_op jit(solution)/shard_map/ppermute | solution.py:52
  81.7 8.2 %collective-permute-start.11 = (bf16[48,2048]{1,0:T(8,128)(2,1)S(1)}, bf16[48,2048]{1,0:T(8,128)(2,1)S(1)}, u32[]{:S(2)}, u32[]{:S(2)}) collective-permute-start(bf16[48,2048]{1,0:T(8,128)(2,1)S(1)} %gather_next.5), channel_id=1, source_target_pairs={{0,2},{1,3},{2,0},{3,1},{4,6},{5,7},{6,4},{7,5},{8,10},{9,11},{10,... | collective-permute-start | bytes 589832 | tf_op jit(solution)/shard_map/ppermute | solution.py:52
  85.0 3.3 %collective-permute-start.14 = (bf16[48,1024]{1,0:T(8,128)(2,1)S(1)}, bf16[48,1024]{1,0:T(8,128)(2,1)S(1)}, u32[]{:S(2)}, u32[]{:S(2)}) collective-permute-start(bf16[48,1024]{1,0:T(8,128)(2,1)S(1)} %get-tuple-element.110), channel_id=1, source_target_pairs={{0,1},{1,0},{2,3},{3,2},{4,5},{5,4},{6,7},{7,6},{8,9},{9,8},{10,11... | collective-permute-start | bytes 294920 | tf_op jit(solution)/shard_map/ppermute | solution.py:52
  85.1 3.2 %collective-permute-start.15 = (bf16[48,1024]{1,0:T(8,128)(2,1)S(1)}, bf16[48,1024]{1,0:T(8,128)(2,1)S(1)}, u32[]{:S(2)}, u32[]{:S(2)}) collective-permute-start(bf16[48,1024]{1,0:T(8,128)(2,1)S(1)} %get-tuple-element.111), channel_id=1, source_target_pairs={{0,1},{1,0},{2,3},{3,2},{4,5},{5,4},{6,7},{7,6},{8,9},{9,8},{10,11... | collective-permute-start | bytes 294920 | tf_op jit(solution)/shard_map/ppermute | solution.py:52
